TPU v7x, 32 devices: a whole 2x2x4 slice. The times are simulated.
32 devices in a mesh: pair: 2 (over x), row: 4 (over y, core), col: 4 (over z).
Axes of the slice: x: 2, y: 2, z: 4, core: 2. Of those that a mesh axis runs over, the one named last changes fastest.
Arguments:
- queries: bfloat16 [4, 8, 8, 32, 2304], P('pair', None, 'row', 'col'), may hold values from -5 to 5
- key_states: bfloat16 [4, 8, 8, 32, 2304], P('pair', None, 'row', 'col'), may hold values from -5 to 5
- value_states: bfloat16 [4, 8, 8, 32, 2304], P('pair', None, 'row', 'col'), may hold values from -6 to 6
- tile_mask: int32 [2, 4, 4, 9], P('pair', 'row', 'col'), may hold values 0 or 1
- frame_reach: int32 [18], replicated, may hold values from 0 to 7
- out_weight: bfloat16 [2, 2304, 3072], P(None, 'pair'), may hold values from -0.125 to 0.125
Outputs:
- attended: bfloat16 [4, 8, 8, 32, 3072], P('pair', None, 'row', 'col')
All inputs are finite; a program needn't handle non-finite values. No bound on the sum of `tile_mask` on one device may be relied on, other than what follows from the above.
Results may differ from a plain program's by a relative error of at most 0.0095.
Values may be sent and summed in bfloat16 or wider, within the bound.
No kernel may reach another device: no remote copies, remote signals or barrier semaphores. Data moves between devices by JAX's collectives and lax.ppermute only.
A program may use at most 256 MiB of HBM per device.

v0:
```python
import jax
import jax.numpy as jnp
from jax import lax
from jax.sharding import PartitionSpec as P


def extended(value, sides, width):
    for axis, dim in sides:
        devices, length = (lax.axis_size(axis), value.shape[dim])
        up = [(i, (i + 1) % devices) for i in range(devices - 1)]
        down = [(j, i) for i, j in up]
        last = lax.slice_in_dim(value, length - width, length, axis=dim)
        leading = lax.slice_in_dim(value, 0, width, axis=dim)
        before = lax.ppermute(last, axis, up)
        after = lax.ppermute(leading, axis, down)
        value = jnp.concatenate([before, value, after], axis=dim)
    return value


def softmax_rows(scores):
    row_max = jnp.max(scores, axis=-1, keepdims=True)
    weights = jnp.exp(scores - row_max)
    row_total = jnp.sum(weights, axis=-1, keepdims=True)
    return (weights / row_total).astype(jnp.bfloat16)


def window_attend(query_rows, key_rows, value_rows, tile_ok, frame_reach):
    S, F, R, C, width = query_rows.shape
    head_count = frame_reach.shape[0]
    head_size = width // head_count
    query_heads = query_rows.reshape(S, F * R * C, head_count, head_size)
    key_heads = key_rows.reshape(S, -1, head_count, head_size)
    value_heads = value_rows.reshape(S, -1, head_count, head_size)
    scores = jnp.einsum(
        "sqhd,skhd->shqk", query_heads, key_heads, preferred_element_type=jnp.float32
    ) * head_size ** (-0.5)
    frames = jnp.arange(F, dtype=jnp.int32)
    frame_gap = jnp.abs(frames[:, None] - frames[None, :])
    close = frame_gap[None, :, :] <= frame_reach[:, None, None]
    allowed = (
        close[:, :, None, :, None, None, None, None]
        & tile_ok[None, None, None, None, :, None, :, None]
    )
    allowed = jnp.broadcast_to(allowed, (head_count, F, R * C, F, 3, R, 3, C)).reshape(
        head_count, F * R * C, -1
    )
    scores = jnp.where(allowed[None], scores, -1e30)
    weights_bf = softmax_rows(scores)
    result = jnp.einsum(
        "shqk,skhd->sqhd", weights_bf, value_heads, preferred_element_type=jnp.float32
    )
    return result.reshape(S, F, R, C, width)


def axial_attend(query_rows, key_rows, value_rows, head_count):
    S, F, R, C, width = query_rows.shape
    head_size = width // head_count
    query_heads = query_rows.reshape(S, F, R, C, head_count, head_size)
    key_heads = key_rows.reshape(S, F, R, -1, head_count, head_size)
    value_heads = value_rows.reshape(S, F, R, -1, head_count, head_size)
    scores = jnp.einsum(
        "sfrchd,sfrwhd->sfrhcw", query_heads, key_heads, preferred_element_type=jnp.float32
    ) * head_size ** (-0.5)
    weights_bf = softmax_rows(scores)
    result = jnp.einsum(
        "sfrhcw,sfrwhd->sfrchd", weights_bf, value_heads, preferred_element_type=jnp.float32
    )
    return result.reshape(S, F, R, C, width)


def per_device(queries, key_states, value_states, tile_mask, frame_reach, out_weight):
    S, F, R, C, width = queries.shape
    paired = jnp.stack([key_states, value_states])
    tiled_kv = paired.reshape(2, S, F, 1, R, 1, C, width)
    row_strip = lax.all_gather(tiled_kv, "col", axis=5, tiled=True)
    row_index = lax.axis_index("row")
    col_index = lax.axis_index("col")
    window_kv = extended(tiled_kv, (("row", 3), ("col", 5)), 1)
    offsets = jnp.arange(3, dtype=jnp.int32) - 1
    row_inside = (row_index + offsets >= 0) & (row_index + offsets < lax.axis_size("row"))
    col_inside = (col_index + offsets >= 0) & (col_index + offsets < lax.axis_size("col"))
    listed = tile_mask.reshape(3, 3) > 0
    center = (offsets[:, None] == 0) & (offsets[None, :] == 0)
    tile_ok = (listed | center) & row_inside[:, None] & col_inside[None, :]
    window_out = window_attend(queries, window_kv[0], window_kv[1], tile_ok, frame_reach)
    strip_width = row_strip.shape[5] * C
    row_keys = row_strip[0].reshape(S, F, R, strip_width, width)
    row_values = row_strip[1].reshape(S, F, R, strip_width, width)
    axial_out = axial_attend(queries, row_keys, row_values, frame_reach.shape[0])
    combined = (window_out + axial_out).astype(jnp.bfloat16).reshape(S, F * R * C, width)
    model_width = out_weight.shape[2]
    attended = jnp.einsum(
        "mtk,mkd->mtd",
        combined,
        lax.all_gather(out_weight, "pair", axis=1, tiled=True),
        preferred_element_type=jnp.float32,
    )
    return attended.astype(jnp.bfloat16).reshape(S, F, R, C, model_width)


def solution(mesh):
    return jax.shard_map(
        per_device,
        mesh=mesh,
        in_specs=(
            P("pair", None, "row", "col", None),
            P("pair", None, "row", "col", None),
            P("pair", None, "row", "col", None),
            P("pair", "row", "col", None),
            P(),
            P(None, "pair", None),
        ),
        out_specs=P("pair", None, "row", "col", None),
        check_vma=False,
    )
```

profile of v0, /device:TPU:0, one launch (start us, length us, event | category | flops | bytes accessed | tf_op | source)
XLA Modules:
  0.0 667.0 jit_solution(12531804892449266455)
XLA Ops:
  6.5 3.3 pad_maximum_fusion.2
  10.0 0.7 all-gather.4.cloned.1.call-update
  10.7 2.5 collective-permute-start
  13.2 1.3 collective-permute-start.1
  14.5 2.7 collective-permute-done
  17.2 4.4 collective-permute-done.1
  21.6 3.7 pad_maximum_fusion.1
  25.3 0.3 copy-done.1
  25.6 6.4 collective-permute-start.2
  32.0 1.3 collective-permute-start.3
  33.9 8.1 %broadcast_in_dim.12 = pred[18,8,16,8,3,2,3,8]{2,1,7,6,5,4,3,0:T(8,128)(4,1)} broadcast(pred[18,8,8,3,3]{1,4,3,2,0:T(4,128)(4,1)S(1)} %broadcast_and_fusion), dimensions={0,1,3,4,6} | broadcast | bytes 2664576 | tf_op jit(solution)/shard_map/broadcast_in_dim | solution.py:44
  42.0 41.1 %broadcast_in_dim.13 = pred[18,128,1152]{1,2,0:T(8,128)(4,1)} reshape(pred[18,8,16,8,3,2,3,8]{2,1,7,6,5,4,3,0:T(8,128)(4,1)} %broadcast_in_dim.12) | data formatting | bytes 5308416 | tf_op jit(solution)/shard_map/jit(_where)/broadcast_in_dim | solution.py:47
  83.1 1.5 reshape.140
  84.6 234.1 %collective-permute-done.2 = bf16[2,2,8,3,2,1,8,2304]{7,6,4,2,1,0,5,3:T(8,128)(2,1)} collective-permute-done((bf16[2,2,8,3,2,1,8,2304]{7,6,4,2,1,0,5,3:T(8,128)(2,1)}, bf16[2,2,8,3,2,1,8,2304]{7,6,4,2,1,0,5,3:T(8,128)(2,1)}, u32[]{:S(2)}, u32[]{:S(2)}) %collective-permute-start.2) | collective-permute-done | bytes 7077920 | tf_op jit(solution)/shard_map/ppermute | solution.py:14
  318.8 5.8 collective-permute-done.3
  324.6 13.9 %pad_maximum_fusion = bf16[2,2,8,3,2,3,8,2304]{7,6,4,2,1,0,5,3:T(8,128)(2,1)S(1)} fusion(bf16[2,2,8,3,2,1,8,2304]{7,6,4,2,1,0,5,3:T(8,128)(2,1)} %collective-permute-done.3, bf16[2,2,8,1,2,1,8,2304]{7,6,4,2,1,0,5,3:T(8,128)(2,1)} %copy-done.1, bf16[2,2,8,1,2,1,8,2304]{7,6,4,2,1,0,5,3:T(8,128)(2,1)S(1)} %get-tuple-element.10, ...), kind=kLoop, calls=%fused_computation.2 | loop fusion | flops 42467328 | bytes 42467328 | tf_op jit(solution)/shard_map/concatenate | solution.py:16
  338.5 5.4 fusion.28
  343.9 4.6 copy.12
  348.6 19.1 %reshape_squeeze.7 = bf16[2,1152,18,128]{3,2,1,0:T(8,128)(2,1)} reshape(bf16[1,2,8,3,2,3,8,2304]{7,6,5,4,3,2,1,0:T(8,128)(2,1)} %copy.12) | data formatting | bytes 21233664 | tf_op jit(solution)/shard_map/reshape;squeeze | solution.py:32
  367.6 9.3 %copy.11 = bf16[1,2,8,3,2,3,8,2304]{7,6,5,4,3,2,1,0:T(8,128)(2,1)} copy(bf16[1,2,8,3,2,3,8,2304]{7,6,4,2,1,0,5,3:T(8,128)(2,1)} %get-tuple-element.6) | data formatting | bytes 21233664 | tf_op jit(solution)/shard_map/slice | solution.py:85
  377.0 19.0 %reshape_squeeze.6 = bf16[2,1152,18,128]{3,2,1,0:T(8,128)(2,1)} reshape(bf16[1,2,8,3,2,3,8,2304]{7,6,5,4,3,2,1,0:T(8,128)(2,1)} %copy.11) | data formatting | bytes 21233664 | tf_op jit(solution)/shard_map/reshape;squeeze | solution.py:33
  395.9 20.3 %fusion.30 = (f32[2,18,128]{2,1,0:T(8,128)S(1)}, f32[2,18,128,1152]{2,3,1,0:T(8,128)}) fusion(pred[18,128,1152]{1,2,0:T(8,128)(4,1)} %broadcast_in_dim.13, bf16[2,1152,18,128]{3,2,1,0:T(8,128)(2,1)} %reshape_squeeze.7, bf16[2,128,18,128]{3,2,1,0:T(8,128)(2,1)S(1)} %copy-done.4), kind=kOutput, calls=%fused_computation.47 | convolution fusion | flops 1380189312 | bytes 35702784 | tf_op jit(solution)/shard_map/sub | solution.py:22
  416.2 15.2 %fusion.3 = f32[2,18,128,128]{3,2,1,0:T(8,128)} fusion(bf16[2,1152,18,128]{3,2,1,0:T(8,128)(2,1)} %reshape_squeeze.6, f32[2,18,128,1152]{2,3,1,0:T(8,128)} %get-tuple-element.12, f32[2,18,128]{2,1,0:T(8,128)S(1)} %get-tuple-element.11), kind=kOutput, calls=%fused_computation.7 | convolution fusion | flops 1369571328 | bytes 34228224 | tf_op jit(solution)/shard_map/shqk,skhd->sqhd/dot_general | solution.py:49
  431.4 2.0 copy.19
  433.5 8.3 %fusion.29 = (bf16[1,2,8,2,32,2304]{5,4,3,2,1,0:T(8,128)(2,1)}, bf16[1,2,8,2,32,2304]{5,4,3,2,1,0:T(8,128)(2,1)}) fusion(bf16[2,2,8,2,32,2304]{5,4,3,2,1,0:T(8,128)(2,1)} %all-gather.6.cloned.1.call-done), kind=kLoop, calls=%fused_computation.46 | loop fusion | bytes 18874368 | tf_op jit(solution)/shard_map/slice | solution.py:87
  441.8 9.1 %reshape_reshape_squeeze.7 = bf16[2,8,2,32,18,128]{5,4,3,2,1,0:T(8,128)(2,1)} reshape(bf16[1,2,8,2,32,2304]{5,4,3,2,1,0:T(8,128)(2,1)} %get-tuple-element.7) | data formatting | bytes 9437184 | tf_op jit(solution)/shard_map/reshape;reshape;squeeze | solution.py:59
  450.9 9.0 %reshape_reshape_squeeze.6 = bf16[2,8,2,32,18,128]{5,4,3,2,1,0:T(8,128)(2,1)} reshape(bf16[1,2,8,2,32,2304]{5,4,3,2,1,0:T(8,128)(2,1)} %get-tuple-element.8) | data formatting | bytes 9437184 | tf_op jit(solution)/shard_map/reshape;reshape;squeeze | solution.py:60
  459.9 4.7 fusion.12
  464.6 94.7 %fusion.31 = (f32[2,8,2,18,8]{4,3,2,1,0:T(8,128)S(1)}, f32[2,8,2,18,8,32]{5,4,3,2,1,0:T(8,128)S(1)}) fusion(f32[2,8,2,18,32,8]{4,5,3,2,1,0:T(8,128)S(1)} %fusion.12), kind=kOutput, calls=%fused_computation.48 | output fusion | flops 589855 | bytes 1198080 | tf_op jit(solution)/shard_map/sub | solution.py:22
  559.3 2.7 fusion.10
  562.0 83.4 %all-gather.4.cloned.1.call-done = bf16[2,2304,3072]{2,1,0:T(8,128)(2,1)} async-done(((bf16[2,1152,3072]{2,1,0:T(8,128)(2,1)}), bf16[2,2304,3072]{2,1,0:T(8,128)(2,1)}) %all-gather.4.cloned.1.call-update) | async-done | bytes 28311568 | tf_op jit(solution)/shard_map/all_gather | solution.py:95
  645.4 14.7 %convolution_convert_fusion = bf16[2,128,3072]{2,1,0:T(8,128)(2,1)} fusion(bf16[2,2304,3072]{2,1,0:T(8,128)(2,1)} %all-gather.4.cloned.1.call-done, f32[2,128,2304]{2,1,0:T(8,128)S(1)} %copy.19, f32[2,128,2304]{2,1,0:T(8,128)} %bitcast.47), kind=kOutput, calls=%fused_computation.19 | convolution fusion | flops 3625844736 | bytes 34603008 | tf_op jit(solution)/shard_map/mtk,mkd->mtd/dot_general | solution.py:92
  (25 shorter events, 0.7 us)
Async XLA Ops:
  6.5 427.0 %all-gather.6.cloned.1.call-start = ((), (), s32[]{:S(2)}) async-start(), calls=%async_computation.1 | async-start | bytes 11796480 | tf_op jit(solution)/shard_map/all_gather | solution.py:75
  9.9 635.5 %all-gather.4.cloned.1.call-start = ((), (), s32[]{:S(2)}) async-start(), calls=%async_computation | async-start | bytes 42467328 | tf_op jit(solution)/shard_map/all_gather | solution.py:95
  10.7 22.7 %copy-start.6 = (s32[1,1,1,9]{3,2,1,0:T(1,128)S(1)}, s32[1,1,1,9]{3,2,1,0:T(1,128)}, u32[]{:S(2)}) copy-start(s32[1,1,1,9]{3,2,1,0:T(1,128)} %param.9) | copy-start | bytes 112
  10.7 22.9 %copy-start.5 = (s32[18]{0:T(128)S(1)}, s32[18]{0:T(128)}, u32[]{:S(2)}) copy-start(s32[18]{0:T(128)} %param.10) | copy-start | bytes 220
  10.7 6.5 collective-permute-start
  13.2 8.4 %collective-permute-start.1 = (bf16[2,2,8,1,2,1,8,2304]{7,6,4,2,1,0,5,3:T(8,128)(2,1)S(1)}, bf16[2,2,8,1,2,1,8,2304]{7,6,4,2,1,0,5,3:T(8,128)(2,1)S(1)}, u32[]{:S(2)}, u32[]{:S(2)}) collective-permute-start(bf16[2,2,8,1,2,1,8,2304]{7,6,4,2,1,0,5,3:T(8,128)(2,1)S(1)} %get-tuple-element.10), channel_id=1, source_target_pairs={{4,0},{8,4},{12,8},{5,1},{9,5},{13,9},{6,2},{10,6},{14,10},{7,3},{... | collective-permute-start | bytes 7077896 | tf_op jit(solution)/shard_map/ppermute | solution.py:15
  17.2 8.1 %copy-start = (bf16[2,2,8,1,2,1,8,2304]{7,6,4,2,1,0,5,3:T(8,128)(2,1)}, bf16[2,2,8,1,2,1,8,2304]{7,6,4,2,1,0,5,3:T(8,128)(2,1)S(1)}, u32[]{:S(2)}) copy-start(bf16[2,2,8,1,2,1,8,2304]{7,6,4,2,1,0,5,3:T(8,128)(2,1)S(1)} %collective-permute-done) | copy-start | bytes 7077892
  21.6 4.0 copy-start.1
  25.6 293.2 %collective-permute-start.2 = (bf16[2,2,8,3,2,1,8,2304]{7,6,4,2,1,0,5,3:T(8,128)(2,1)}, bf16[2,2,8,3,2,1,8,2304]{7,6,4,2,1,0,5,3:T(8,128)(2,1)}, u32[]{:S(2)}, u32[]{:S(2)}) collective-permute-start(bf16[2,2,8,3,2,1,8,2304]{7,6,4,2,1,0,5,3:T(8,128)(2,1)} %pad_maximum_fusion.1), channel_id=1, source_target_pairs={{0,1},{1,2},{2,3},{4,5},{5,6},{6,7},{8,9},{9,10},{10,11},{12,13},{... | collective-permute-start | bytes 21233672 | tf_op jit(solution)/shard_map/ppermute | solution.py:14
  32.0 292.5 %collective-permute-start.3 = (bf16[2,2,8,3,2,1,8,2304]{7,6,4,2,1,0,5,3:T(8,128)(2,1)}, bf16[2,2,8,3,2,1,8,2304]{7,6,4,2,1,0,5,3:T(8,128)(2,1)}, u32[]{:S(2)}, u32[]{:S(2)}) collective-permute-start(bf16[2,2,8,3,2,1,8,2304]{7,6,4,2,1,0,5,3:T(8,128)(2,1)} %pad_maximum_fusion.1), channel_id=1, source_target_pairs={{1,0},{2,1},{3,2},{5,4},{6,5},{7,6},{9,8},{10,9},{11,10},{13,12},{... | collective-permute-start | bytes 21233672 | tf_op jit(solution)/shard_map/ppermute | solution.py:15
  42.0 41.1 %copy-start.3 = (bf16[2,8,2,8,2304]{4,3,2,1,0:T(8,128)(2,1)S(1)}, bf16[2,8,2,8,2304]{4,3,2,1,0:T(8,128)(2,1)}, u32[]{:S(2)}) copy-start(bf16[2,8,2,8,2304]{4,3,2,1,0:T(8,128)(2,1)} %param.6) | copy-start | bytes 3538948
  377.0 19.0 %copy-start.4 = (bf16[2,128,18,128]{3,2,1,0:T(8,128)(2,1)S(1)}, bf16[2,128,18,128]{3,2,1,0:T(8,128)(2,1)}, u32[]{:S(2)}) copy-start(bf16[2,128,18,128]{3,2,1,0:T(8,128)(2,1)} %reshape.140) | copy-start | bytes 3538948
  459.9 99.4 %copy-start.2 = (bf16[2,8,2,32,18,128]{5,4,3,2,1,0:T(8,128)(2,1)S(1)}, bf16[2,8,2,32,18,128]{5,4,3,2,1,0:T(8,128)(2,1)}, u32[]{:S(2)}) copy-start(bf16[2,8,2,32,18,128]{5,4,3,2,1,0:T(8,128)(2,1)} %reshape_reshape_squeeze.6) | copy-start | bytes 14155780
Sparse Core Ops, SparseCore 0:
  10.0 301.4 all-gather.5
  313.1 332.3 all-gather.3
where the time goes:
time: 670 us; the launch traced here: 667 us
  waiting for transfers between devices  331 us (49%)
  local copies, waits for them, and re-layouts  137 us (20%)
  other arithmetic  116 us (17%)
  matrix products  57.7 us (9%)
  between operations  13.5 us (2%)
  starting transfers between devices  11.5 us (2%)
    ppermute x2, waiting for transfers between devices, extended(): before = lax.ppermute(last, axis, up)  237 us
    sub x1, other arithmetic, softmax_rows(): weights = jnp.exp(scores - row_max)  94.7 us
    all_gather x1, waiting for transfers between devices, per_device(): lax.all_gather(out_weight, 'pair', axis=1, tiled=True)  83.4 us
    broadcast_in_dim x1, local copies, waits for them, and re-layouts, window_attend(): scores = jnp.where(allowed[None], scores, -1e+30)  41.1 us
    sub x1, matrix products, softmax_rows(): weights = jnp.exp(scores - row_max)  20.3 us
    another operation x1, local copies, waits for them, and re-layouts, window_attend(): key_heads = key_rows.reshape(S, -1, head_count, head_size)  19.1 us
    another operation x1, local copies, waits for them, and re-layouts, window_attend(): value_heads = value_rows.reshape(S, -1, head_count, head_size)  19 us
    concatenate x2, other arithmetic, extended(): value = jnp.concatenate([before, value, after], axis=dim)  17.6 us
  transfers between devices with their start and end apart: 6, of which 5 were waited for; matrix products, arithmetic and copies ran while one was open for 44% of the time, Pallas kernels for 0%

commit v1 on v0

v1 whole, which is shorter than its diff:
```python
import functools
import math

import jax
import jax.numpy as jnp
from jax import lax
from jax.experimental import pallas as pl
from jax.experimental.pallas import tpu as pltpu
from jax.sharding import PartitionSpec as P

NEG = -1e30
VMEM_LIMIT = 48 * 1024 * 1024


def dot_nt(a, b):
    return lax.dot_general(a, b, (((1,), (1,)), ((), ())), preferred_element_type=jnp.float32)


def dot_nn(a, b):
    return lax.dot_general(a, b, (((1,), (0,)), ((), ())), preferred_element_type=jnp.float32)


def token_grids(tokens, group):
    q = lax.broadcasted_iota(jnp.int32, (tokens, tokens), 0)
    k = lax.broadcasted_iota(jnp.int32, (tokens, tokens), 1)
    return jnp.abs(q // group - k // group)


def edge_kernel(flags, q_ref, left_ref, right_ref, far_ref, out_ref, *, heads, cols_tile):
    tokens = q_ref.shape[0]
    d = 128
    scale = d ** (-0.5)

    @pl.when(flags[0] > 0)
    def _():
        use_right = flags[1] > 0
        same = token_grids(tokens, cols_tile) == 0
        lane = lax.broadcasted_iota(jnp.int32, (tokens, d), 1)
        stats = jnp.zeros((tokens, d), jnp.float32)
        for n in range(heads):
            cut = slice(n * d, (n + 1) * d)
            q = q_ref[:, cut]
            near_k = jnp.where(use_right, right_ref[0, :, cut], left_ref[0, :, cut])
            near_v = jnp.where(use_right, right_ref[1, :, cut], left_ref[1, :, cut])
            s0 = jnp.where(same, dot_nt(q, near_k) * scale, NEG)
            s1 = jnp.where(same, dot_nt(q, far_ref[0, :, cut]) * scale, NEG)
            top = jnp.max(jnp.maximum(s0, s1), axis=1, keepdims=True)
            e0 = jnp.exp(s0 - top)
            e1 = jnp.exp(s1 - top)
            total = jnp.sum(e0 + e1, axis=1, keepdims=True)
            o = dot_nn(e0.astype(jnp.bfloat16), near_v) + dot_nn(
                e1.astype(jnp.bfloat16), far_ref[1, :, cut]
            )
            out_ref[:, cut] = (o / total).astype(jnp.bfloat16)
            lse = top + jnp.log(total)
            high = lse.astype(jnp.bfloat16).astype(jnp.float32)
            mid = (lse - high).astype(jnp.bfloat16).astype(jnp.float32)
            low = lse - high - mid
            stats = jnp.where(lane == 3 * n, high, stats)
            stats = jnp.where(lane == 3 * n + 1, mid, stats)
            stats = jnp.where(lane == 3 * n + 2, low, stats)
        out_ref[:, heads * d:] = stats.astype(jnp.bfloat16)


def main_kernel(flags, reach, q_ref, *refs, heads, cols_tile, frame_tokens):
    tiles = refs[:10]
    remote_ref, stats_ref, out_ref = refs[10:]
    tokens = q_ref.shape[0]
    d = 128
    scale = d ** (-0.5)
    step = pl.program_id(0)
    frame_gap = token_grids(tokens, frame_tokens)
    row_gap = token_grids(tokens, cols_tile)
    lane = lax.broadcasted_iota(jnp.int32, (tokens, d), 1)
    stats = stats_ref[...].astype(jnp.float32)
    for n in range(heads):
        cut = slice(n * d, (n + 1) * d)
        head = step * heads + n
        q = q_ref[:, cut]
        keys = jnp.concatenate([t[0, :, cut] for t in tiles], axis=0)
        values = jnp.concatenate([t[1, :, cut] for t in tiles], axis=0)
        scores = dot_nt(q, keys) * scale
        raw = [scores[:, t * tokens:(t + 1) * tokens] for t in range(10)]
        masked = []
        for t in range(9):
            limit = jnp.where(flags[t] > 0, reach[head], -1)
            masked.append(jnp.where(frame_gap <= limit, raw[t], NEG))
        top = functools.reduce(jnp.maximum, masked)
        top = jnp.max(top, axis=1, keepdims=True)
        weights = [jnp.exp(m - top) for m in masked]
        total = jnp.sum(functools.reduce(jnp.add, weights), axis=1, keepdims=True)
        probs = jnp.concatenate([w.astype(jnp.bfloat16) for w in weights], axis=1)
        window = dot_nn(probs, values[:9 * tokens]) / total

        row_tiles = [(3, flags[9]), (4, None), (5, flags[10]), (9, flags[11])]
        row_masked = []
        for t, valid in row_tiles:
            limit = 0 if valid is None else jnp.where(valid > 0, 0, -1)
            row_masked.append(jnp.where(row_gap <= limit, raw[t], NEG))
        row_top = jnp.max(functools.reduce(jnp.maximum, row_masked), axis=1, keepdims=True)
        row_weights = [jnp.exp(m - row_top) for m in row_masked]
        row_total = jnp.sum(functools.reduce(jnp.add, row_weights), axis=1, keepdims=True)
        row_probs = jnp.concatenate([w.astype(jnp.bfloat16) for w in row_weights], axis=1)
        row_values = jnp.concatenate([values[3 * tokens:6 * tokens], values[9 * tokens:]], axis=0)
        row = dot_nn(row_probs, row_values)

        mine = (lane >= 3 * head) & (lane < 3 * head + 3)
        lse = jnp.sum(jnp.where(mine, stats, 0.0), axis=1, keepdims=True)
        lse = jnp.where(flags[12] > 0, lse, NEG)
        both = jnp.maximum(row_top, lse)
        here = jnp.exp(row_top - both)
        there = jnp.exp(lse - both)
        whole = here * row_total + there
        axial = row * (here / whole) + remote_ref[:, cut].astype(jnp.float32) * (there / whole)
        out_ref[:, cut] = (window + axial).astype(jnp.bfloat16)


def edge_attend(flags, q, left, right, far, half, stream, cols_tile):
    tokens, width = far.shape[1:]
    heads = width // 128
    kv_spec = pl.BlockSpec((2, None, tokens, width), lambda g: (0, stream, 0, 0))
    return pl.pallas_call(
        functools.partial(edge_kernel, heads=heads, cols_tile=cols_tile),
        out_shape=jax.ShapeDtypeStruct((tokens, width + 128), jnp.bfloat16),
        grid=(1,),
        in_specs=[
            pl.BlockSpec(memory_space=pltpu.SMEM),
            pl.BlockSpec((None, None, tokens, width), lambda g: (half, stream, 0, 0)),
            kv_spec,
            kv_spec,
            pl.BlockSpec((2, tokens, width), lambda g: (0, 0, 0)),
        ],
        out_specs=pl.BlockSpec((tokens, width + 128), lambda g: (0, 0)),
        compiler_params=pltpu.CompilerParams(vmem_limit_bytes=VMEM_LIMIT),
        cost_estimate=pl.CostEstimate(
            flops=8 * tokens * tokens * width,
            bytes_accessed=16 * tokens * width,
            transcendentals=2 * tokens * tokens * heads,
        ),
        name="edge_rows",
    )(flags, q, left, right, far)


def main_attend(flags, reach, q, tiles, far, remote, half, stream, cols_tile, frame_tokens, block_heads=3):
    tokens, width = far.shape[1:]
    heads = width // 128
    lanes = block_heads * 128
    kv_spec = pl.BlockSpec((2, None, tokens, lanes), lambda g: (0, stream, 0, g))
    smem = pl.BlockSpec(memory_space=pltpu.SMEM)
    return pl.pallas_call(
        functools.partial(
            main_kernel, heads=block_heads, cols_tile=cols_tile, frame_tokens=frame_tokens
        ),
        out_shape=jax.ShapeDtypeStruct((tokens, width), jnp.bfloat16),
        grid=(heads // block_heads,),
        in_specs=[
            smem,
            smem,
            pl.BlockSpec((None, None, tokens, lanes), lambda g: (half, stream, 0, g)),
        ]
        + [kv_spec] * 9
        + [
            pl.BlockSpec((2, tokens, lanes), lambda g: (0, 0, g)),
            pl.BlockSpec((tokens, lanes), lambda g: (0, g)),
            pl.BlockSpec((tokens, 128), lambda g: (0, heads)),
        ],
        out_specs=pl.BlockSpec((tokens, lanes), lambda g: (0, g)),
        compiler_params=pltpu.CompilerParams(vmem_limit_bytes=VMEM_LIMIT),
        cost_estimate=pl.CostEstimate(
            flops=46 * tokens * tokens * width,
            bytes_accessed=46 * tokens * width,
            transcendentals=13 * tokens * tokens * heads,
        ),
        name="tile_rows",
    )(flags, reach, q, *tiles, far, remote, remote)


def per_device(queries, key_states, value_states, tile_mask, frame_reach, out_weight):
    S, F, R, C, width = queries.shape
    tokens = F * R * C
    half = width // 2
    pair = lax.axis_index("pair")
    rows, cols = lax.axis_size("row"), lax.axis_size("col")
    row, col = lax.axis_index("row"), lax.axis_index("col")
    last = cols - 1
    up = [(i, i + 1) for i in range(rows - 1)]
    down = [(i + 1, i) for i in range(rows - 1)]
    right = [(i, i + 1) for i in range(cols - 1)]
    left = [(i + 1, i) for i in range(cols - 1)]
    swap = [(0, 1), (1, 0)]
    inward = [(0, 1), (last, last - 1)]
    outward = [(1, 0), (last - 1, last)]
    middle = [(1, 2), (2, 1)]

    flat = [a.reshape(S, tokens, width) for a in (queries, key_states, value_states)]
    first = pair == 0

    def halves(value):
        low, high = value[:, :, :half], value[:, :, half:]
        return jnp.where(first, high, low), jnp.where(first, low, high)

    q_halves, k_halves, v_halves = [halves(a) for a in flat]
    kv = [jnp.stack([k, v]) for k, v in zip(k_halves, v_halves)]
    q = jnp.stack(q_halves)

    offsets = jnp.arange(3, dtype=jnp.int32) - 1
    row_inside = (row + offsets >= 0) & (row + offsets < rows)
    col_inside = (col + offsets >= 0) & (col + offsets < cols)
    listed = tile_mask.reshape(3, 3) > 0
    center = (offsets[:, None] == 0) & (offsets[None, :] == 0)
    tile_ok = (listed | center) & row_inside[:, None] & col_inside[None, :]
    inner = (col > 0) & (col < last)
    flags = jnp.concatenate(
        [tile_ok.reshape(9), jnp.stack([col > 0, col < last, inner, ~inner])]
    ).astype(jnp.int32)
    edge_flags = jnp.stack([inner, col == 1]).astype(jnp.int32)
    heads_half = half // 128
    reach_low, reach_high = frame_reach[:heads_half], frame_reach[heads_half:]
    reach = [jnp.where(first, reach_high, reach_low), jnp.where(first, reach_low, reach_high)]

    edge_q = lax.ppermute(q, "col", inward)
    combined = [[None] * S for _ in range(2)]
    for h in range(2):
        own = kv[h]
        from_left = lax.ppermute(own, "col", right)
        from_right = lax.ppermute(own, "col", left)
        strip = (from_left, own, from_right)
        above = [lax.ppermute(x, "row", up) for x in strip]
        below = [lax.ppermute(x, "row", down) for x in strip]
        tiles = above + list(strip) + below
        for s in range(S):
            passed = jnp.where(col == 1, from_left[:, s], from_right[:, s])
            far = lax.ppermute(passed, "col", middle)
            partial = edge_attend(edge_flags, edge_q, from_left, from_right, far, h, s, C)
            remote = lax.ppermute(partial, "col", outward)
            combined[h][s] = main_attend(
                flags, reach[h], q, tiles, far, remote, h, s, C, R * C
            )
    outs = []
    for s in range(S):
        theirs = lax.ppermute(combined[0][s], "pair", swap)
        product = dot_nn(theirs, out_weight[s]).astype(jnp.bfloat16)
        mine = lax.ppermute(product, "pair", swap)
        outs.append(
            (dot_nn(combined[1][s], out_weight[s]) + mine.astype(jnp.float32)).astype(jnp.bfloat16)
        )
    return jnp.stack(outs).reshape(S, F, R, C, out_weight.shape[2])


def solution(mesh):
    return jax.shard_map(
        per_device,
        mesh=mesh,
        in_specs=(
            P("pair", None, "row", "col", None),
            P("pair", None, "row", "col", None),
            P("pair", None, "row", "col", None),
            P("pair", "row", "col", None),
            P(),
            P(None, "pair", None),
        ),
        out_specs=P("pair", None, "row", "col", None),
        check_vma=False,
    )
```

time: 670 us -> 231 us (0.34)
  the two profiles are of different devices: /device:TPU:0 before, /device:TPU:17 now
where the time goes in v1:
time: 231 us; the launch traced here: 229 us
  starting transfers between devices  74.3 us (32%)
  waiting for transfers between devices  61.7 us (27%)
  Pallas kernels  43.6 us (19%)
  local copies, waits for them, and re-layouts  21.7 us (9%)
  matrix products  17 us (7%)
  other arithmetic  10.5 us (5%)
    ppermute x2, waiting for transfers between devices, per_device(): from_right = lax.ppermute(own, 'col', left)  36.7 us
    pallas_call x4, Pallas kernels, main_attend(): pl.pallas_call(functools.partial(main_kernel, heads=block_heads, cols_til...  27 us
    ppermute x6, starting transfers between devices, per_device(): below = [lax.ppermute(x, 'row', down) for x in strip]  21 us
    ppermute x6, starting transfers between devices, per_device(): above = [lax.ppermute(x, 'row', up) for x in strip]  19 us
    dot_general x4, matrix products, dot_nn(): lax.dot_general(a, b, (((1,), (0,)), ((), ())), preferred_element_type=jn...  17 us
    pallas_call x4, Pallas kernels, edge_attend(): pl.pallas_call(functools.partial(edge_kernel, heads=heads, cols_tile=cols...  16.6 us
    ppermute x4, starting transfers between devices, per_device(): far = lax.ppermute(passed, 'col', middle)  14.4 us
    ppermute x1, waiting for transfers between devices, per_device(): edge_q = lax.ppermute(q, 'col', inward)  11.8 us
  transfers between devices with their start and end apart: 29, of which 5 were waited for; matrix products, arithmetic and copies ran while one was open for 17% of the time, Pallas kernels for 19%

profile of v1, /device:TPU:17, one launch (start us, length us, event | category | flops | bytes accessed | tf_op | source)
XLA Modules:
  0.0 229.3 jit_solution(295813659204911198)
XLA Ops:
  8.2 4.4 %collective-permute-start.11 = (bf16[2,2,128,1152]{3,2,0,1:T(8,128)(2,1)}, bf16[2,2,128,1152]{3,2,0,1:T(8,128)(2,1)}, u32[]{:S(2)}, u32[]{:S(2)}) collective-permute-start(bf16[2,2,128,1152]{3,2,0,1:T(8,128)(2,1)} %pad_maximum_fusion.3), channel_id=1, source_target_pairs={{0,1},{1,2},{2,3},{4,5},{5,6},{6,7},{8,9},{9,10},{10,11},{12,13},{... | collective-permute-start | bytes 3538952 | tf_op jit(solution)/shard_map/ppermute | solution.py:225
  16.1 15.9 %collective-permute-done.3.right_ref.refs_5_ = bf16[2,2,128,1152]{3,2,1,0:T(8,128)(2,1)S(1)} collective-permute-done((bf16[2,2,128,1152]{3,2,1,0:T(8,128)(2,1)}, bf16[2,2,128,1152]{3,2,1,0:T(8,128)(2,1)S(1)}, u32[]{:S(2)}, u32[]{:S(2)}) %collective-permute-start.3) | collective-permute-done | bytes 1179680 | tf_op jit(solution)/shard_map/ppermute | solution.py:226
  32.0 4.5 %collective-permute-start.6 = (bf16[2,2,128,1152]{3,2,1,0:T(8,128)(2,1)}, bf16[2,2,128,1152]{3,2,1,0:T(8,128)(2,1)}, u32[]{:S(2)}, u32[]{:S(2)}) collective-permute-start(bf16[2,2,128,1152]{3,2,1,0:T(8,128)(2,1)} %pad_maximum_fusion.2.refs_4_), channel_id=1, source_target_pairs={{4,0},{8,4},{12,8},{5,1},{9,5},{13,9},{6,2},{10,6},{14,10},{7,3},{... | collective-permute-start | bytes 3538952 | tf_op jit(solution)/shard_map/ppermute | solution.py:229
  36.5 20.8 %collective-permute-done.14 = bf16[2,2,128,1152]{3,2,0,1:T(8,128)(2,1)} collective-permute-done((bf16[2,2,128,1152]{3,2,0,1:T(8,128)(2,1)}, bf16[2,2,128,1152]{3,2,0,1:T(8,128)(2,1)}, u32[]{:S(2)}, u32[]{:S(2)}) %collective-permute-start.14) | collective-permute-done | bytes 1179680 | tf_op jit(solution)/shard_map/ppermute | solution.py:226
  57.3 4.6 %collective-permute-start.17 = (bf16[2,2,128,1152]{3,2,0,1:T(8,128)(2,1)}, bf16[2,2,128,1152]{3,2,0,1:T(8,128)(2,1)}, u32[]{:S(2)}, u32[]{:S(2)}) collective-permute-start(bf16[2,2,128,1152]{3,2,0,1:T(8,128)(2,1)} %pad_maximum_fusion.3), channel_id=1, source_target_pairs={{4,0},{8,4},{12,8},{5,1},{9,5},{13,9},{6,2},{10,6},{14,10},{7,3},{... | collective-permute-start | bytes 3538952 | tf_op jit(solution)/shard_map/ppermute | solution.py:229
  61.9 3.0 %collective-permute-start.13 = (bf16[2,2,128,1152]{3,2,0,1:T(8,128)(2,1)}, bf16[2,2,128,1152]{3,2,0,1:T(8,128)(2,1)}, u32[]{:S(2)}, u32[]{:S(2)}) collective-permute-start(bf16[2,2,128,1152]{3,2,0,1:T(8,128)(2,1)} %pad_maximum_fusion.3), channel_id=1, source_target_pairs={{0,4},{4,8},{8,12},{1,5},{5,9},{9,13},{2,6},{6,10},{10,14},{3,7},{... | collective-permute-start | bytes 3538952 | tf_op jit(solution)/shard_map/ppermute | solution.py:228
  64.9 2.8 %fusion.30 = (bf16[2,128,1152]{2,1,0:T(8,128)(2,1)}, bf16[2,128,1152]{2,1,0:T(8,128)(2,1)}) fusion(bf16[2,2,128,1152]{3,2,0,1:T(8,128)(2,1)} %collective-permute-done.14, bf16[2,2,128,1152]{3,2,0,1:T(8,128)(2,1)} %collective-permute-done.11, pred[]{:T(512)} %eq.26), kind=kLoop, calls=%fused_computation.24 | loop fusion | flops 589824 | bytes 3538945 | tf_op jit(solution)/shard_map/jit(_where)/select_n | solution.py:232
  70.8 11.8 %collective-permute-done.9.q_ref = bf16[2,2,128,1152]{3,2,1,0:T(8,128)(2,1)} collective-permute-done((bf16[2,2,128,1152]{3,2,1,0:T(8,128)(2,1)S(1)}, bf16[2,2,128,1152]{3,2,1,0:T(8,128)(2,1)}, u32[]{:S(2)}, u32[]{:S(2)}) %collective-permute-start.9) | collective-permute-done | bytes 1179680 | tf_op jit(solution)/shard_map/ppermute | solution.py:221
  82.6 7.2 %collective-permute-start.23 = (bf16[2,128,1152]{2,1,0:T(8,128)(2,1)}, bf16[2,128,1152]{2,1,0:T(8,128)(2,1)}, u32[]{:S(2)}, u32[]{:S(2)}) collective-permute-start(bf16[2,128,1152]{2,1,0:T(8,128)(2,1)} %get-tuple-element.8), channel_id=1, source_target_pairs={{1,2},{2,1},{5,6},{6,5},{9,10},{10,9},{13,14},{14,13},{17,18},{18,... | collective-permute-start | bytes 1769480 | tf_op jit(solution)/shard_map/ppermute | solution.py:233
  91.7 3.7 %collective-permute-start.18 = (bf16[2,2,128,1152]{3,2,0,1:T(8,128)(2,1)}, bf16[2,2,128,1152]{3,2,0,1:T(8,128)(2,1)}, u32[]{:S(2)}, u32[]{:S(2)}) collective-permute-start(bf16[2,2,128,1152]{3,2,0,1:T(8,128)(2,1)} %collective-permute-done.14), channel_id=1, source_target_pairs={{4,0},{8,4},{12,8},{5,1},{9,5},{13,9},{6,2},{10,6},{14,10},{7,3},{... | collective-permute-start | bytes 3538952 | tf_op jit(solution)/shard_map/ppermute | solution.py:229
  98.7 3.3 %collective-permute-start.15 = (bf16[2,2,128,1152]{3,2,0,1:T(8,128)(2,1)}, bf16[2,2,128,1152]{3,2,0,1:T(8,128)(2,1)}, u32[]{:S(2)}, u32[]{:S(2)}) collective-permute-start(bf16[2,2,128,1152]{3,2,0,1:T(8,128)(2,1)} %collective-permute-done.14), channel_id=1, source_target_pairs={{0,4},{4,8},{8,12},{1,5},{5,9},{9,13},{2,6},{6,10},{10,14},{3,7},{... | collective-permute-start | bytes 3538952 | tf_op jit(solution)/shard_map/ppermute | solution.py:228
  102.1 3.8 %edge_rows.5 = bf16[128,1280]{1,0:T(8,128)(2,1)S(1)} custom-call(s32[2]{0:T(128)S(1)} %add_convert_fusion.flags, bf16[2,2,128,1152]{3,2,1,0:T(8,128)(2,1)} %collective-permute-done.9.q_ref, bf16[2,2,128,1152]{3,2,1,0:T(8,128)(2,1)S(1)} %copy.14.left_ref.refs_3_, bf16[2,2,128,1152]{3,2,1,0:T(8,128)(2,1)S(1)} %copy.16.right_ref.refs_5_, ...), custom_call_target="tpu_custom_call" | custom-call | flops 150994944 | bytes 2359296 | tf_op jit(solution)/shard_map/edge_rows/pallas_call | solution.py:122
  109.3 5.4 %collective-permute-done.25.far_ref.refs_9_ = bf16[2,128,1152]{2,1,0:T(8,128)(2,1)} collective-permute-done((bf16[2,128,1152]{2,1,0:T(8,128)(2,1)}, bf16[2,128,1152]{2,1,0:T(8,128)(2,1)}, u32[]{:S(2)}, u32[]{:S(2)}) %collective-permute-start.25) | collective-permute-done | bytes 589856 | tf_op jit(solution)/shard_map/ppermute | solution.py:233
  114.8 5.1 %collective-permute-start.12 = (bf16[2,2,128,1152]{3,2,0,1:T(8,128)(2,1)}, bf16[2,2,128,1152]{3,2,0,1:T(8,128)(2,1)}, u32[]{:S(2)}, u32[]{:S(2)}) collective-permute-start(bf16[2,2,128,1152]{3,2,0,1:T(8,128)(2,1)} %collective-permute-done.11), channel_id=1, source_target_pairs={{0,4},{4,8},{8,12},{1,5},{5,9},{9,13},{2,6},{6,10},{10,14},{3,7},{... | collective-permute-start | bytes 3538952 | tf_op jit(solution)/shard_map/ppermute | solution.py:228
  125.2 3.4 %collective-permute-start.8 = (bf16[2,128,1152]{2,1,0:T(8,128)(2,1)}, bf16[2,128,1152]{2,1,0:T(8,128)(2,1)}, u32[]{:S(2)}, u32[]{:S(2)}) collective-permute-start(bf16[2,128,1152]{2,1,0:T(8,128)(2,1)} %get-tuple-element.7), channel_id=1, source_target_pairs={{1,2},{2,1},{5,6},{6,5},{9,10},{10,9},{13,14},{14,13},{17,18},{18,... | collective-permute-start | bytes 1769480 | tf_op jit(solution)/shard_map/ppermute | solution.py:233
  129.2 3.8 %collective-permute-start.7 = (bf16[2,2,128,1152]{3,2,1,0:T(8,128)(2,1)S(1)}, bf16[2,2,128,1152]{3,2,1,0:T(8,128)(2,1)}, u32[]{:S(2)}, u32[]{:S(2)}) collective-permute-start(bf16[2,2,128,1152]{3,2,1,0:T(8,128)(2,1)S(1)} %collective-permute-done.3.right_ref.refs_5_), channel_id=1, source_target_pairs={{4,0},{8,4},{12,8},{5,1},{9,5},{13,9},{6,2},{10,6},{14,10},{7,3},{... | collective-permute-start | bytes 3538952 | tf_op jit(solution)/shard_map/ppermute | solution.py:229
  133.1 4.5 %edge_rows.6 = bf16[128,1280]{1,0:T(8,128)(2,1)} custom-call(s32[2]{0:T(128)S(1)} %add_convert_fusion.flags, bf16[2,2,128,1152]{3,2,1,0:T(8,128)(2,1)} %collective-permute-done.9.q_ref, bf16[2,2,128,1152]{3,2,1,0:T(8,128)(2,1)S(1)} %collective-permute-done.left_ref.refs_3_, bf16[2,2,128,1152]{3,2,1,0:T(8,128)(2,1)S(1)} %collective-permute-done.3.right_ref.refs_5_, ...), custom_call_target="tpu_custom_call" | custom-call | flops 150994944 | bytes 2359296 | tf_op jit(solution)/shard_map/edge_rows/pallas_call | solution.py:122
  137.6 4.5 %edge_rows.7 = bf16[128,1280]{1,0:T(8,128)(2,1)} custom-call(s32[2]{0:T(128)S(1)} %add_convert_fusion.flags, bf16[2,2,128,1152]{3,2,1,0:T(8,128)(2,1)} %collective-permute-done.9.q_ref, bf16[2,2,128,1152]{3,2,1,0:T(8,128)(2,1)S(1)} %copy-done.4, bf16[2,2,128,1152]{3,2,1,0:T(8,128)(2,1)S(1)} %copy.16.right_ref.refs_5_, ...), custom_call_target="tpu_custom_call" | custom-call | flops 150994944 | bytes 2359296 | tf_op jit(solution)/shard_map/edge_rows/pallas_call | solution.py:122
  144.8 2.4 %copy.15.refs_4_ = bf16[2,2,128,1152]{3,2,1,0:T(8,128)(2,1)} copy(bf16[2,2,128,1152]{3,2,0,1:T(8,128)(2,1)} %pad_maximum_fusion.3) | data formatting | bytes 2359296 | tf_op jit(solution)/shard_map/stack | solution.py:203
  147.3 2.5 %copy.18.refs_7_ = bf16[2,2,128,1152]{3,2,1,0:T(8,128)(2,1)} copy(bf16[2,2,128,1152]{3,2,0,1:T(8,128)(2,1)} %collective-permute-done.17) | data formatting | bytes 2359296 | tf_op jit(solution)/shard_map/ppermute | solution.py:229
  151.1 2.4 %copy.19.refs_8_ = bf16[2,2,128,1152]{3,2,1,0:T(8,128)(2,1)} copy(bf16[2,2,128,1152]{3,2,0,1:T(8,128)(2,1)} %collective-permute-done.18) | data formatting | bytes 2359296 | tf_op jit(solution)/shard_map/ppermute | solution.py:229
  159.0 6.7 %tile_rows.5 = bf16[128,1152]{1,0:T(8,128)(2,1)S(1)} custom-call(s32[13]{0:T(128)S(1)} %convert_element_type.24.flags, s32[9]{0:T(128)S(1)} %get-tuple-element.15.reach, bf16[2,2,128,1152]{3,2,1,0:T(8,128)(2,1)S(1)} %copy-done.6, bf16[2,2,128,1152]{3,2,1,0:T(8,128)(2,1)S(1)} %copy.11.refs_0_, bf16[2,2,128,1152]{3,2,1,0:T(8,128)(2,1)S(1)} %copy.12.refs_1_, ...), custom_call_target="tpu_custom_call" | custom-call | flops 868220928 | bytes 6782976 | tf_op jit(solution)/shard_map/tile_rows/pallas_call | solution.py:150
  171.4 3.5 %collective-permute-start.1 = (bf16[2,2,128,1152]{3,2,1,0:T(8,128)(2,1)S(1)}, bf16[2,2,128,1152]{3,2,1,0:T(8,128)(2,1)S(1)}, u32[]{:S(2)}, u32[]{:S(2)}) collective-permute-start(bf16[2,2,128,1152]{3,2,1,0:T(8,128)(2,1)S(1)} %collective-permute-done.left_ref.refs_3_), channel_id=1, source_target_pairs={{0,4},{4,8},{8,12},{1,5},{5,9},{9,13},{2,6},{6,10},{10,14},{3,7},{... | collective-permute-start | bytes 3538952 | tf_op jit(solution)/shard_map/ppermute | solution.py:228
  174.9 6.8 %tile_rows.7 = bf16[128,1152]{1,0:T(8,128)(2,1)S(1)} custom-call(s32[13]{0:T(128)S(1)} %convert_element_type.24.flags, s32[9]{0:T(128)S(1)} %get-tuple-element.15.reach, bf16[2,2,128,1152]{3,2,1,0:T(8,128)(2,1)S(1)} %copy-done.6, bf16[2,2,128,1152]{3,2,1,0:T(8,128)(2,1)S(1)} %copy.11.refs_0_, bf16[2,2,128,1152]{3,2,1,0:T(8,128)(2,1)S(1)} %copy.12.refs_1_, ...), custom_call_target="tpu_custom_call" | custom-call | flops 868220928 | bytes 6782976 | tf_op jit(solution)/shard_map/tile_rows/pallas_call | solution.py:150
  182.0 4.3 %fusion.24 = bf16[128,3072]{1,0:T(8,128)(2,1)S(1)} fusion(bf16[128,1152]{1,0:T(8,128)(2,1)S(1)} %collective-permute-done.21, bf16[2,1152,3072]{2,1,0:T(8,128)(2,1)} %param.11), kind=kOutput, calls=%fused_computation.16 | convolution fusion | flops 906362880 | bytes 8159232 | tf_op jit(solution)/shard_map/dot_general | solution.py:20
  187.6 3.8 %edge_rows.4 = bf16[128,1280]{1,0:T(8,128)(2,1)S(1)} custom-call(s32[2]{0:T(128)S(1)} %add_convert_fusion.flags, bf16[2,2,128,1152]{3,2,1,0:T(8,128)(2,1)} %collective-permute-done.9.q_ref, bf16[2,2,128,1152]{3,2,1,0:T(8,128)(2,1)S(1)} %collective-permute-done.left_ref.refs_3_, bf16[2,2,128,1152]{3,2,1,0:T(8,128)(2,1)S(1)} %collective-permute-done.3.right_ref.refs_5_, ...), custom_call_target="tpu_custom_call" | custom-call | flops 150994944 | bytes 2359296 | tf_op jit(solution)/shard_map/edge_rows/pallas_call | solution.py:122
  192.7 4.3 %fusion.27 = bf16[128,3072]{1,0:T(8,128)(2,1)S(1)} fusion(bf16[128,1152]{1,0:T(8,128)(2,1)S(1)} %collective-permute-done.27, bf16[2,1152,3072]{2,1,0:T(8,128)(2,1)} %param.11), kind=kOutput, calls=%fused_computation.17 | convolution fusion | flops 906362880 | bytes 8159232 | tf_op jit(solution)/shard_map/dot_general | solution.py:20
  198.3 6.7 %tile_rows.6 = bf16[128,1152]{1,0:T(8,128)(2,1)S(1)} custom-call(s32[13]{0:T(128)S(1)} %convert_element_type.24.flags, s32[9]{0:T(128)S(1)} %get-tuple-element.16.reach, bf16[2,2,128,1152]{3,2,1,0:T(8,128)(2,1)S(1)} %copy-done.6, bf16[2,2,128,1152]{3,2,1,0:T(8,128)(2,1)S(1)} %collective-permute-done.1.refs_0_, ...), custom_call_target="tpu_custom_call" | custom-call | flops 868220928 | bytes 6782976 | tf_op jit(solution)/shard_map/tile_rows/pallas_call | solution.py:150
  205.1 6.8 %tile_rows.4 = bf16[128,1152]{1,0:T(8,128)(2,1)S(1)} custom-call(s32[13]{0:T(128)S(1)} %convert_element_type.24.flags, s32[9]{0:T(128)S(1)} %get-tuple-element.16.reach, bf16[2,2,128,1152]{3,2,1,0:T(8,128)(2,1)S(1)} %copy-done.6, bf16[2,2,128,1152]{3,2,1,0:T(8,128)(2,1)S(1)} %collective-permute-done.1.refs_0_, ...), custom_call_target="tpu_custom_call" | custom-call | flops 868220928 | bytes 6782976 | tf_op jit(solution)/shard_map/tile_rows/pallas_call | solution.py:150
  211.8 4.2 %fusion.21 = bf16[128,3072]{1,0:T(8,128)(2,1)S(1)} fusion(bf16[128,1152]{1,0:T(8,128)(2,1)S(1)} %tile_rows.4, bf16[2,1152,3072]{2,1,0:T(8,128)(2,1)} %param.11, bf16[128,3072]{1,0:T(8,128)(2,1)S(1)} %collective-permute-done.22), kind=kOutput, calls=%fused_computation.15 | convolution fusion | flops 907149312 | bytes 8945664 | tf_op jit(solution)/shard_map/dot_general | solution.py:20
  216.1 7.7 %collective-permute-done.28 = bf16[128,3072]{1,0:T(8,128)(2,1)S(1)} collective-permute-done((bf16[128,3072]{1,0:T(8,128)(2,1)S(1)}, bf16[128,3072]{1,0:T(8,128)(2,1)S(1)}, u32[]{:S(2)}, u32[]{:S(2)}) %collective-permute-start.28) | collective-permute-done | bytes 786464 | tf_op jit(solution)/shard_map/ppermute | solution.py:243
  223.8 4.2 %fusion.18 = bf16[128,3072]{1,0:T(8,128)(2,1)S(1)} fusion(bf16[128,1152]{1,0:T(8,128)(2,1)S(1)} %tile_rows.6, bf16[2,1152,3072]{2,1,0:T(8,128)(2,1)} %param.11, bf16[128,3072]{1,0:T(8,128)(2,1)S(1)} %collective-permute-done.28), kind=kOutput, calls=%fused_computation.14 | convolution fusion | flops 907149312 | bytes 8945664 | tf_op jit(solution)/shard_map/dot_general | solution.py:20
  (95 shorter events, 50.1 us)
Async XLA Ops:
  3.0 29.0 %collective-permute-start.3 = (bf16[2,2,128,1152]{3,2,1,0:T(8,128)(2,1)}, bf16[2,2,128,1152]{3,2,1,0:T(8,128)(2,1)S(1)}, u32[]{:S(2)}, u32[]{:S(2)}) collective-permute-start(bf16[2,2,128,1152]{3,2,1,0:T(8,128)(2,1)} %pad_maximum_fusion.2.refs_4_), channel_id=1, source_target_pairs={{1,0},{2,1},{3,2},{5,4},{6,5},{7,6},{9,8},{10,9},{11,10},{13,12},{... | collective-permute-start | bytes 3538952 | tf_op jit(solution)/shard_map/ppermute | solution.py:226
  6.3 51.0 %collective-permute-start.14 = (bf16[2,2,128,1152]{3,2,0,1:T(8,128)(2,1)}, bf16[2,2,128,1152]{3,2,0,1:T(8,128)(2,1)}, u32[]{:S(2)}, u32[]{:S(2)}) collective-permute-start(bf16[2,2,128,1152]{3,2,0,1:T(8,128)(2,1)} %pad_maximum_fusion.3), channel_id=1, source_target_pairs={{1,0},{2,1},{3,2},{5,4},{6,5},{7,6},{9,8},{10,9},{11,10},{13,12},{... | collective-permute-start | bytes 3538952 | tf_op jit(solution)/shard_map/ppermute | solution.py:226
  8.2 53.7 %collective-permute-start.11 = (bf16[2,2,128,1152]{3,2,0,1:T(8,128)(2,1)}, bf16[2,2,128,1152]{3,2,0,1:T(8,128)(2,1)}, u32[]{:S(2)}, u32[]{:S(2)}) collective-permute-start(bf16[2,2,128,1152]{3,2,0,1:T(8,128)(2,1)} %pad_maximum_fusion.3), channel_id=1, source_target_pairs={{0,1},{1,2},{2,3},{4,5},{5,6},{6,7},{8,9},{9,10},{10,11},{12,13},{... | collective-permute-start | bytes 3538952 | tf_op jit(solution)/shard_map/ppermute | solution.py:225
  12.6 55.1 %collective-permute-start = (bf16[2,2,128,1152]{3,2,1,0:T(8,128)(2,1)}, bf16[2,2,128,1152]{3,2,1,0:T(8,128)(2,1)S(1)}, u32[]{:S(2)}, u32[]{:S(2)}) collective-permute-start(bf16[2,2,128,1152]{3,2,1,0:T(8,128)(2,1)} %pad_maximum_fusion.2.refs_4_), channel_id=1, source_target_pairs={{0,1},{1,2},{2,3},{4,5},{5,6},{6,7},{8,9},{9,10},{10,11},{12,13},{... | collective-permute-start | bytes 3538952 | tf_op jit(solution)/shard_map/ppermute | solution.py:225
  14.8 52.9 %copy-start.5 = (bf16[2,2,128,1152]{3,2,1,0:T(8,128)(2,1)}, bf16[2,2,128,1152]{3,2,1,0:T(8,128)(2,1)S(1)}, u32[]{:S(2)}) copy-start(bf16[2,2,128,1152]{3,2,1,0:T(8,128)(2,1)S(1)} %pad_maximum_fusion.1.q_ref) | copy-start | bytes 3538948
  14.8 67.8 %collective-permute-start.9 = (bf16[2,2,128,1152]{3,2,1,0:T(8,128)(2,1)S(1)}, bf16[2,2,128,1152]{3,2,1,0:T(8,128)(2,1)}, u32[]{:S(2)}, u32[]{:S(2)}) collective-permute-start(bf16[2,2,128,1152]{3,2,1,0:T(8,128)(2,1)S(1)} %pad_maximum_fusion.1.q_ref), channel_id=1, source_target_pairs={{0,1},{3,2},{4,5},{7,6},{8,9},{11,10},{12,13},{15,14},{16,17},{19,... | collective-permute-start | bytes 3538952 | tf_op jit(solution)/shard_map/ppermute | solution.py:221
  32.0 155.6 %copy-start = (bf16[2,2,128,1152]{3,2,1,0:T(8,128)(2,1)}, bf16[2,2,128,1152]{3,2,1,0:T(8,128)(2,1)S(1)}, u32[]{:S(2)}) copy-start(bf16[2,2,128,1152]{3,2,1,0:T(8,128)(2,1)S(1)} %collective-permute-done.3.right_ref.refs_5_) | copy-start | bytes 3538948
  32.0 57.7 %collective-permute-start.6 = (bf16[2,2,128,1152]{3,2,1,0:T(8,128)(2,1)}, bf16[2,2,128,1152]{3,2,1,0:T(8,128)(2,1)}, u32[]{:S(2)}, u32[]{:S(2)}) collective-permute-start(bf16[2,2,128,1152]{3,2,1,0:T(8,128)(2,1)} %pad_maximum_fusion.2.refs_4_), channel_id=1, source_target_pairs={{4,0},{8,4},{12,8},{5,1},{9,5},{13,9},{6,2},{10,6},{14,10},{7,3},{... | collective-permute-start | bytes 3538952 | tf_op jit(solution)/shard_map/ppermute | solution.py:229
  57.3 34.4 %collective-permute-start.17 = (bf16[2,2,128,1152]{3,2,0,1:T(8,128)(2,1)}, bf16[2,2,128,1152]{3,2,0,1:T(8,128)(2,1)}, u32[]{:S(2)}, u32[]{:S(2)}) collective-permute-start(bf16[2,2,128,1152]{3,2,0,1:T(8,128)(2,1)} %pad_maximum_fusion.3), channel_id=1, source_target_pairs={{4,0},{8,4},{12,8},{5,1},{9,5},{13,9},{6,2},{10,6},{14,10},{7,3},{... | collective-permute-start | bytes 3538952 | tf_op jit(solution)/shard_map/ppermute | solution.py:229
  61.9 44.0 %collective-permute-start.13 = (bf16[2,2,128,1152]{3,2,0,1:T(8,128)(2,1)}, bf16[2,2,128,1152]{3,2,0,1:T(8,128)(2,1)}, u32[]{:S(2)}, u32[]{:S(2)}) collective-permute-start(bf16[2,2,128,1152]{3,2,0,1:T(8,128)(2,1)} %pad_maximum_fusion.3), channel_id=1, source_target_pairs={{0,4},{4,8},{8,12},{1,5},{5,9},{9,13},{2,6},{6,10},{10,14},{3,7},{... | collective-permute-start | bytes 3538952 | tf_op jit(solution)/shard_map/ppermute | solution.py:228
  67.7 119.9 %copy-start.1 = (bf16[2,2,128,1152]{3,2,1,0:T(8,128)(2,1)}, bf16[2,2,128,1152]{3,2,1,0:T(8,128)(2,1)S(1)}, u32[]{:S(2)}) copy-start(bf16[2,2,128,1152]{3,2,1,0:T(8,128)(2,1)S(1)} %collective-permute-done.left_ref.refs_3_) | copy-start | bytes 3538948
  67.7 31.0 %collective-permute-start.19 = (bf16[2,128,1152]{2,1,0:T(8,128)(2,1)}, bf16[2,128,1152]{2,1,0:T(8,128)(2,1)}, u32[]{:S(2)}, u32[]{:S(2)}) collective-permute-start(bf16[2,128,1152]{2,1,0:T(8,128)(2,1)} %get-tuple-element.5), channel_id=1, source_target_pairs={{1,2},{2,1},{5,6},{6,5},{9,10},{10,9},{13,14},{14,13},{17,18},{18,... | collective-permute-start | bytes 1769480 | tf_op jit(solution)/shard_map/ppermute | solution.py:233
  82.6 24.6 %collective-permute-start.23 = (bf16[2,128,1152]{2,1,0:T(8,128)(2,1)}, bf16[2,128,1152]{2,1,0:T(8,128)(2,1)}, u32[]{:S(2)}, u32[]{:S(2)}) collective-permute-start(bf16[2,128,1152]{2,1,0:T(8,128)(2,1)} %get-tuple-element.8), channel_id=1, source_target_pairs={{1,2},{2,1},{5,6},{6,5},{9,10},{10,9},{13,14},{14,13},{17,18},{18,... | collective-permute-start | bytes 1769480 | tf_op jit(solution)/shard_map/ppermute | solution.py:233
  89.7 25.0 %collective-permute-start.25 = (bf16[2,128,1152]{2,1,0:T(8,128)(2,1)}, bf16[2,128,1152]{2,1,0:T(8,128)(2,1)}, u32[]{:S(2)}, u32[]{:S(2)}) collective-permute-start(bf16[2,128,1152]{2,1,0:T(8,128)(2,1)} %get-tuple-element.6), channel_id=1, source_target_pairs={{1,2},{2,1},{5,6},{6,5},{9,10},{10,9},{13,14},{14,13},{17,18},{18,... | collective-permute-start | bytes 1769480 | tf_op jit(solution)/shard_map/ppermute | solution.py:233
  91.7 33.5 %collective-permute-start.18 = (bf16[2,2,128,1152]{3,2,0,1:T(8,128)(2,1)}, bf16[2,2,128,1152]{3,2,0,1:T(8,128)(2,1)}, u32[]{:S(2)}, u32[]{:S(2)}) collective-permute-start(bf16[2,2,128,1152]{3,2,0,1:T(8,128)(2,1)} %collective-permute-done.14), channel_id=1, source_target_pairs={{4,0},{8,4},{12,8},{5,1},{9,5},{13,9},{6,2},{10,6},{14,10},{7,3},{... | collective-permute-start | bytes 3538952 | tf_op jit(solution)/shard_map/ppermute | solution.py:229
  98.7 30.5 %collective-permute-start.15 = (bf16[2,2,128,1152]{3,2,0,1:T(8,128)(2,1)}, bf16[2,2,128,1152]{3,2,0,1:T(8,128)(2,1)}, u32[]{:S(2)}, u32[]{:S(2)}) collective-permute-start(bf16[2,2,128,1152]{3,2,0,1:T(8,128)(2,1)} %collective-permute-done.14), channel_id=1, source_target_pairs={{0,4},{4,8},{8,12},{1,5},{5,9},{9,13},{2,6},{6,10},{10,14},{3,7},{... | collective-permute-start | bytes 3538952 | tf_op jit(solution)/shard_map/ppermute | solution.py:228
  105.9 14.0 %collective-permute-start.20 = (bf16[128,1280]{1,0:T(8,128)(2,1)S(1)}, bf16[128,1280]{1,0:T(8,128)(2,1)S(1)}, u32[]{:S(2)}, u32[]{:S(2)}) collective-permute-start(bf16[128,1280]{1,0:T(8,128)(2,1)S(1)} %edge_rows.5), channel_id=1, source_target_pairs={{1,0},{2,3},{5,4},{6,7},{9,8},{10,11},{13,12},{14,15},{17,16},{18,... | collective-permute-start | bytes 983048 | tf_op jit(solution)/shard_map/ppermute | solution.py:235
  107.2 34.9 %collective-permute-start.16 = (bf16[2,2,128,1152]{3,2,0,1:T(8,128)(2,1)}, bf16[2,2,128,1152]{3,2,0,1:T(8,128)(2,1)}, u32[]{:S(2)}, u32[]{:S(2)}) collective-permute-start(bf16[2,2,128,1152]{3,2,0,1:T(8,128)(2,1)} %collective-permute-done.11), channel_id=1, source_target_pairs={{4,0},{8,4},{12,8},{5,1},{9,5},{13,9},{6,2},{10,6},{14,10},{7,3},{... | collective-permute-start | bytes 3538952 | tf_op jit(solution)/shard_map/ppermute | solution.py:229
  114.8 28.6 %collective-permute-start.12 = (bf16[2,2,128,1152]{3,2,0,1:T(8,128)(2,1)}, bf16[2,2,128,1152]{3,2,0,1:T(8,128)(2,1)}, u32[]{:S(2)}, u32[]{:S(2)}) collective-permute-start(bf16[2,2,128,1152]{3,2,0,1:T(8,128)(2,1)} %collective-permute-done.11), channel_id=1, source_target_pairs={{0,4},{4,8},{8,12},{1,5},{5,9},{9,13},{2,6},{6,10},{10,14},{3,7},{... | collective-permute-start | bytes 3538952 | tf_op jit(solution)/shard_map/ppermute | solution.py:228
  120.6 45.1 %collective-permute-start.2 = (bf16[2,2,128,1152]{3,2,1,0:T(8,128)(2,1)}, bf16[2,2,128,1152]{3,2,1,0:T(8,128)(2,1)}, u32[]{:S(2)}, u32[]{:S(2)}) collective-permute-start(bf16[2,2,128,1152]{3,2,1,0:T(8,128)(2,1)} %pad_maximum_fusion.2.refs_4_), channel_id=1, source_target_pairs={{0,4},{4,8},{8,12},{1,5},{5,9},{9,13},{2,6},{6,10},{10,14},{3,7},{... | collective-permute-start | bytes 3538952 | tf_op jit(solution)/shard_map/ppermute | solution.py:228
  125.2 41.7 %collective-permute-start.8 = (bf16[2,128,1152]{2,1,0:T(8,128)(2,1)}, bf16[2,128,1152]{2,1,0:T(8,128)(2,1)}, u32[]{:S(2)}, u32[]{:S(2)}) collective-permute-start(bf16[2,128,1152]{2,1,0:T(8,128)(2,1)} %get-tuple-element.7), channel_id=1, source_target_pairs={{1,2},{2,1},{5,6},{6,5},{9,10},{10,9},{13,14},{14,13},{17,18},{18,... | collective-permute-start | bytes 1769480 | tf_op jit(solution)/shard_map/ppermute | solution.py:233
  129.2 57.0 %collective-permute-start.7 = (bf16[2,2,128,1152]{3,2,1,0:T(8,128)(2,1)S(1)}, bf16[2,2,128,1152]{3,2,1,0:T(8,128)(2,1)}, u32[]{:S(2)}, u32[]{:S(2)}) collective-permute-start(bf16[2,2,128,1152]{3,2,1,0:T(8,128)(2,1)S(1)} %collective-permute-done.3.right_ref.refs_5_), channel_id=1, source_target_pairs={{4,0},{8,4},{12,8},{5,1},{9,5},{13,9},{6,2},{10,6},{14,10},{7,3},{... | collective-permute-start | bytes 3538952 | tf_op jit(solution)/shard_map/ppermute | solution.py:229
  142.1 27.0 %collective-permute-start.24 = (bf16[128,1280]{1,0:T(8,128)(2,1)}, bf16[128,1280]{1,0:T(8,128)(2,1)S(1)}, u32[]{:S(2)}, u32[]{:S(2)}) collective-permute-start(bf16[128,1280]{1,0:T(8,128)(2,1)} %edge_rows.6), channel_id=1, source_target_pairs={{1,0},{2,3},{5,4},{6,7},{9,8},{10,11},{13,12},{14,15},{17,16},{18,... | collective-permute-start | bytes 983048 | tf_op jit(solution)/shard_map/ppermute | solution.py:235
  143.4 28.0 %collective-permute-start.26 = (bf16[128,1280]{1,0:T(8,128)(2,1)}, bf16[128,1280]{1,0:T(8,128)(2,1)S(1)}, u32[]{:S(2)}, u32[]{:S(2)}) collective-permute-start(bf16[128,1280]{1,0:T(8,128)(2,1)} %edge_rows.7), channel_id=1, source_target_pairs={{1,0},{2,3},{5,4},{6,7},{9,8},{10,11},{13,12},{14,15},{17,16},{18,... | collective-permute-start | bytes 983048 | tf_op jit(solution)/shard_map/ppermute | solution.py:235
  165.7 16.0 %collective-permute-start.21 = (bf16[128,1152]{1,0:T(8,128)(2,1)S(1)}, bf16[128,1152]{1,0:T(8,128)(2,1)S(1)}, u32[]{:S(2)}, u32[]{:S(2)}) collective-permute-start(bf16[128,1152]{1,0:T(8,128)(2,1)S(1)} %tile_rows.5), channel_id=1, source_target_pairs={{0,16},{16,0},{1,17},{17,1},{2,18},{18,2},{3,19},{19,3},{4,20},{20... | collective-permute-start | bytes 884744 | tf_op jit(solution)/shard_map/ppermute | solution.py:241
  167.0 30.0 %collective-permute-start.4 = (bf16[2,2,128,1152]{3,2,1,0:T(8,128)(2,1)S(1)}, bf16[2,2,128,1152]{3,2,1,0:T(8,128)(2,1)S(1)}, u32[]{:S(2)}, u32[]{:S(2)}) collective-permute-start(bf16[2,2,128,1152]{3,2,1,0:T(8,128)(2,1)S(1)} %collective-permute-done.3.right_ref.refs_5_), channel_id=1, source_target_pairs={{0,4},{4,8},{8,12},{1,5},{5,9},{9,13},{2,6},{6,10},{10,14},{3,7},{... | collective-permute-start | bytes 3538952 | tf_op jit(solution)/shard_map/ppermute | solution.py:228
  169.1 28.2 %collective-permute-start.5 = (bf16[2,2,128,1152]{3,2,1,0:T(8,128)(2,1)S(1)}, bf16[2,2,128,1152]{3,2,1,0:T(8,128)(2,1)S(1)}, u32[]{:S(2)}, u32[]{:S(2)}) collective-permute-start(bf16[2,2,128,1152]{3,2,1,0:T(8,128)(2,1)S(1)} %collective-permute-done.left_ref.refs_3_), channel_id=1, source_target_pairs={{4,0},{8,4},{12,8},{5,1},{9,5},{13,9},{6,2},{10,6},{14,10},{7,3},{... | collective-permute-start | bytes 3538952 | tf_op jit(solution)/shard_map/ppermute | solution.py:229
  171.4 25.9 %collective-permute-start.1 = (bf16[2,2,128,1152]{3,2,1,0:T(8,128)(2,1)S(1)}, bf16[2,2,128,1152]{3,2,1,0:T(8,128)(2,1)S(1)}, u32[]{:S(2)}, u32[]{:S(2)}) collective-permute-start(bf16[2,2,128,1152]{3,2,1,0:T(8,128)(2,1)S(1)} %collective-permute-done.left_ref.refs_3_), channel_id=1, source_target_pairs={{0,4},{4,8},{8,12},{1,5},{5,9},{9,13},{2,6},{6,10},{10,14},{3,7},{... | collective-permute-start | bytes 3538952 | tf_op jit(solution)/shard_map/ppermute | solution.py:228
  181.7 9.7 %collective-permute-start.27 = (bf16[128,1152]{1,0:T(8,128)(2,1)S(1)}, bf16[128,1152]{1,0:T(8,128)(2,1)S(1)}, u32[]{:S(2)}, u32[]{:S(2)}) collective-permute-start(bf16[128,1152]{1,0:T(8,128)(2,1)S(1)} %tile_rows.7), channel_id=1, source_target_pairs={{0,16},{16,0},{1,17},{17,1},{2,18},{18,2},{3,19},{19,3},{4,20},{20... | collective-permute-start | bytes 884744 | tf_op jit(solution)/shard_map/ppermute | solution.py:241
  186.3 25.6 %collective-permute-start.22 = (bf16[128,3072]{1,0:T(8,128)(2,1)S(1)}, bf16[128,3072]{1,0:T(8,128)(2,1)S(1)}, u32[]{:S(2)}, u32[]{:S(2)}) collective-permute-start(bf16[128,3072]{1,0:T(8,128)(2,1)S(1)} %fusion.24), channel_id=1, source_target_pairs={{0,16},{16,0},{1,17},{17,1},{2,18},{18,2},{3,19},{19,3},{4,20},{20... | collective-permute-start | bytes 2359304 | tf_op jit(solution)/shard_map/ppermute | solution.py:243
  191.4 13.7 %collective-permute-start.10 = (bf16[128,1280]{1,0:T(8,128)(2,1)S(1)}, bf16[128,1280]{1,0:T(8,128)(2,1)S(1)}, u32[]{:S(2)}, u32[]{:S(2)}) collective-permute-start(bf16[128,1280]{1,0:T(8,128)(2,1)S(1)} %edge_rows.4), channel_id=1, source_target_pairs={{1,0},{2,3},{5,4},{6,7},{9,8},{10,11},{13,12},{14,15},{17,16},{18,... | collective-permute-start | bytes 983048 | tf_op jit(solution)/shard_map/ppermute | solution.py:235
  197.0 26.8 %collective-permute-start.28 = (bf16[128,3072]{1,0:T(8,128)(2,1)S(1)}, bf16[128,3072]{1,0:T(8,128)(2,1)S(1)}, u32[]{:S(2)}, u32[]{:S(2)}) collective-permute-start(bf16[128,3072]{1,0:T(8,128)(2,1)S(1)} %fusion.27), channel_id=1, source_target_pairs={{0,16},{16,0},{1,17},{17,1},{2,18},{18,2},{3,19},{19,3},{4,20},{20... | collective-permute-start | bytes 2359304 | tf_op jit(solution)/shard_map/ppermute | solution.py:243
  (10 other events, 107.8 us)

commit v2 on v0

v2 whole, which is shorter than its diff:
```python
import functools
import math

import jax
import jax.numpy as jnp
from jax import lax
from jax.experimental import pallas as pl
from jax.experimental.pallas import tpu as pltpu
from jax.sharding import PartitionSpec as P

NEG = -1e30
VMEM_LIMIT = 24 * 1024 * 1024
HEAD = 128
TO_LOG2 = HEAD ** (-0.5) * math.log2(math.e)
ANY = pl.BlockSpec(memory_space=pl.ANY)
SMEM = pl.BlockSpec(memory_space=pltpu.SMEM)


def dot_nt(a, b):
    return lax.dot_general(a, b, (((1,), (1,)), ((), ())), preferred_element_type=jnp.float32)


def dot_nn(a, b):
    return lax.dot_general(a, b, (((1,), (0,)), ((), ())), preferred_element_type=jnp.float32)


def group_gap(tokens, group):
    q = lax.broadcasted_iota(jnp.int32, (tokens, tokens), 0)
    k = lax.broadcasted_iota(jnp.int32, (tokens, tokens), 1)
    return jnp.abs(q // group - k // group)


def with_ones(values):
    return jnp.concatenate([values, jnp.ones_like(values)], axis=1)


def softmax_sums(scores, values):
    top = jnp.max(functools.reduce(jnp.maximum, scores), axis=1, keepdims=True)
    weights = [jnp.exp2((s - top) * TO_LOG2).astype(jnp.bfloat16) for s in scores]
    sums = dot_nn(jnp.concatenate(weights, axis=1), with_ones(jnp.concatenate(values, axis=0)))
    return top * TO_LOG2, sums[:, :HEAD], sums[:, HEAD:]


def edge_kernel(place, q_ref, near_ref, far_ref, out_ref, *, heads, cols_tile, cols):
    tokens = q_ref.shape[0]

    @pl.when((place[2] > 0) & (place[2] < cols - 1))
    def _():
        bias = jnp.where(group_gap(tokens, cols_tile) == 0, 0.0, NEG)
        lane = lax.broadcasted_iota(jnp.int32, (tokens, HEAD), 1)
        stats = jnp.zeros((tokens, HEAD), jnp.float32)
        for n in range(heads):
            cut = slice(n * HEAD, (n + 1) * HEAD)
            q = q_ref[:, cut]
            scores = [dot_nt(q, t[0, :, cut]) + bias for t in (near_ref, far_ref)]
            top, total, weight = softmax_sums(scores, [near_ref[1, :, cut], far_ref[1, :, cut]])
            out_ref[:, cut] = (total / weight).astype(jnp.bfloat16)
            lse = top + jnp.log2(weight)
            high = lse.astype(jnp.bfloat16).astype(jnp.float32)
            mid = (lse - high).astype(jnp.bfloat16).astype(jnp.float32)
            low = lse - high - mid
            stats = jnp.where(lane == 3 * n, high, stats)
            stats = jnp.where(lane == 3 * n + 1, mid, stats)
            stats = jnp.where(lane == 3 * n + 2, low, stats)
        out_ref[:, heads * HEAD:] = stats.astype(jnp.bfloat16)


def fill_bias(bias_ref, frame_tokens, cols_tile):
    tokens = bias_ref.shape[1]
    frames = tokens // frame_tokens
    gap = group_gap(tokens, frame_tokens)
    for reach in range(frames):
        bias_ref[reach] = jnp.where(gap <= reach, 0.0, NEG)
    bias_ref[frames] = jnp.full((tokens, tokens), NEG, jnp.float32)
    bias_ref[frames + 1] = jnp.where(group_gap(tokens, cols_tile) == 0, 0.0, NEG)


def combined_heads(place, mask, reach, q_ref, tiles, remote_ref, stats_ref, bias_ref, heads, half, grid):
    tokens = q_ref.shape[0]
    none = bias_ref.shape[0] - 2
    step = pl.program_id(0)
    rows, cols = grid
    row, col = place[1], place[2]
    row_sign, col_sign = 1 - 2 * (row % 2), 1 - 2 * (col % 2)
    row_steps, col_steps = (row_sign, 0, -row_sign), (0, col_sign, -col_sign)
    listed = []
    for a in row_steps:
        for b in col_steps:
            inside = (row + a >= 0) & (row + a < rows) & (col + b >= 0) & (col + b < cols)
            listed.append(inside & ((mask[3 * (a + 1) + b + 1] > 0) | ((a == 0) & (b == 0))))
    inner = (col > 0) & (col < cols - 1)
    first_head = (half + (1 - 2 * half) * (1 - place[0])) * heads * pl.num_programs(0)
    lane = lax.broadcasted_iota(jnp.int32, (tokens, HEAD), 1)
    stats = stats_ref[...].astype(jnp.float32)
    results = []
    for n in range(heads):
        cut = slice(n * HEAD, (n + 1) * HEAD)
        head = step * heads + n
        limit = reach[first_head + head]
        q = q_ref[:, cut]
        scores = dot_nt(q, jnp.concatenate([t[0, :, cut] for t in tiles], axis=0))
        raw = [scores[:, t * tokens:(t + 1) * tokens] for t in range(10)]
        values = [t[1, :, cut] for t in tiles]
        window = [raw[t] + bias_ref[jnp.where(listed[t], limit, none)] for t in range(9)]
        _, window_total, window_weight = softmax_sums(window, values[:9])
        row_bias = bias_ref[none + 1]
        outer_bias = bias_ref[jnp.where(inner, none + 1, none)]
        row_scores = [raw[3] + row_bias, raw[4] + row_bias, raw[5] + outer_bias, raw[9] + outer_bias]
        row_top, row_total, row_weight = softmax_sums(row_scores, values[3:6] + values[9:])
        mine = (lane >= 3 * head) & (lane < 3 * head + 3)
        lse = jnp.sum(jnp.where(mine, stats, 0.0), axis=1, keepdims=True)
        lse = jnp.where(inner, NEG, lse)
        both = jnp.maximum(row_top, lse)
        here = jnp.exp2(row_top - both)
        there = jnp.exp2(lse - both)
        whole = here * row_weight + there
        axial = (row_total * here + remote_ref[:, cut].astype(jnp.float32) * there) / whole
        results.append((window_total / window_weight + axial).astype(jnp.bfloat16))
    return jnp.concatenate(results, axis=1)


def first_kernel(place, mask, reach, q_ref, *refs, cols_tile, frame_tokens, **sizes):
    tiles = refs[:10]
    remote_ref, stats_ref, out_ref, bias_ref = refs[10:]

    @pl.when(pl.program_id(0) == 0)
    def _():
        fill_bias(bias_ref, frame_tokens, cols_tile)

    out_ref[...] = combined_heads(
        place, mask, reach, q_ref, tiles, remote_ref, stats_ref, bias_ref, **sizes
    )


def add_product(total_ref, rows, weight_ref, lanes=512):
    for start in range(0, total_ref.shape[1], lanes):
        cut = slice(start, start + lanes)
        total_ref[:, cut] += dot_nn(rows, weight_ref[:, cut])


def second_kernel(place, mask, reach, q_ref, *refs, cols_tile, frame_tokens, **sizes):
    tiles = refs[:10]
    remote_ref, stats_ref, weight_ref, other_ref = refs[10:14]
    out_ref, bias_ref, total_ref = refs[-3:]

    @pl.when(pl.program_id(0) == 0)
    def _():
        fill_bias(bias_ref, frame_tokens, cols_tile)
        total_ref[...] = other_ref[...].astype(jnp.float32)

    rows = combined_heads(
        place, mask, reach, q_ref, tiles, remote_ref, stats_ref, bias_ref, **sizes
    )
    add_product(total_ref, rows, weight_ref)

    @pl.when(pl.program_id(0) == pl.num_programs(0) - 1)
    def _():
        out_ref[...] = total_ref[...].astype(jnp.bfloat16)


def product_kernel(rows_ref, weight_ref, out_ref, total_ref):
    @pl.when(pl.program_id(0) == 0)
    def _():
        total_ref[...] = jnp.zeros_like(total_ref)

    add_product(total_ref, rows_ref[...], weight_ref)

    @pl.when(pl.program_id(0) == pl.num_programs(0) - 1)
    def _():
        out_ref[...] = total_ref[...].astype(jnp.bfloat16)


def params():
    return pltpu.CompilerParams(vmem_limit_bytes=VMEM_LIMIT)


def side(half, place):
    return half + (1 - 2 * half) * (1 - place[0])


def pack(place, keys, values, half, *earlier):
    S, tokens, width = keys.shape
    spec = pl.BlockSpec((None, tokens, width // 2), lambda s, p: (s, 0, side(half, p)))

    def kernel(place, k_ref, v_ref, *refs):
        refs[-1][0] = k_ref[...]
        refs[-1][1] = v_ref[...]

    return pl.pallas_call(
        kernel,
        out_shape=jax.ShapeDtypeStruct((S, 2, tokens, width // 2), keys.dtype),
        grid_spec=pltpu.PrefetchScalarGridSpec(
            num_scalar_prefetch=1,
            grid=(S,),
            in_specs=[spec, spec, *[ANY] * len(earlier)],
            out_specs=pl.BlockSpec((None, 2, tokens, width // 2), lambda s, p: (s, 0, 0, 0)),
        ),
        compiler_params=params(),
        cost_estimate=pl.CostEstimate(
            flops=0, bytes_accessed=4 * S * tokens * width, transcendentals=0
        ),
        name="pack",
    )(place, keys, values, *earlier)


def edge_attend(place, q, near, far, half, stream, cols_tile, cols):
    tokens, width = far.shape[1:]
    heads = width // HEAD
    return pl.pallas_call(
        functools.partial(edge_kernel, heads=heads, cols_tile=cols_tile, cols=cols),
        out_shape=jax.ShapeDtypeStruct((tokens, width + HEAD), jnp.bfloat16),
        grid_spec=pltpu.PrefetchScalarGridSpec(
            num_scalar_prefetch=1,
            grid=(1,),
            in_specs=[
                pl.BlockSpec((None, tokens, width), lambda g, p: (stream, 0, side(half, p))),
                pl.BlockSpec((None, 2, tokens, width), lambda g, p: (stream, 0, 0, 0)),
                pl.BlockSpec((2, tokens, width), lambda g, p: (0, 0, 0)),
            ],
            out_specs=pl.BlockSpec((tokens, width + HEAD), lambda g, p: (0, 0)),
        ),
        compiler_params=params(),
        cost_estimate=pl.CostEstimate(
            flops=8 * tokens * tokens * width,
            bytes_accessed=14 * tokens * width,
            transcendentals=2 * tokens * tokens * heads,
        ),
        name="edge_rows",
    )(place, q, near, far)


def main_attend(place, mask, reach, q, tiles, far, remote, half, stream, cols_tile, frame_tokens, grid,
                project=None, block=3):
    tokens, width = far.shape[1:]
    heads = width // HEAD
    lanes = block * HEAD
    steps = heads // block
    sizes = dict(heads=block, half=half, grid=grid, cols_tile=cols_tile, frame_tokens=frame_tokens)
    in_specs = [
        SMEM,
        SMEM,
        pl.BlockSpec((None, tokens, lanes), lambda g, p: (stream, 0, side(half, p) * steps + g)),
        *[pl.BlockSpec((None, 2, tokens, lanes), lambda g, p: (stream, 0, 0, g))] * 9,
        pl.BlockSpec((2, tokens, lanes), lambda g, p: (0, 0, g)),
        pl.BlockSpec((tokens, lanes), lambda g, p: (0, g)),
        pl.BlockSpec((tokens, HEAD), lambda g, p: (0, heads)),
    ]
    args = [place, mask, reach, q, *tiles, far, remote, remote]
    scratch = [pltpu.VMEM((tokens // frame_tokens + 2, tokens, tokens), jnp.float32)]
    flops, moved = 46 * tokens * tokens * width, 46 * tokens * width
    exps = 13 * tokens * tokens * heads
    if project is None:
        return pl.pallas_call(
            functools.partial(first_kernel, **sizes),
            out_shape=jax.ShapeDtypeStruct((tokens, width), jnp.bfloat16),
            grid_spec=pltpu.PrefetchScalarGridSpec(
                num_scalar_prefetch=1,
                grid=(steps,),
                in_specs=in_specs,
                out_specs=pl.BlockSpec((tokens, lanes), lambda g, p: (0, g)),
                scratch_shapes=scratch,
            ),
            compiler_params=params(),
            cost_estimate=pl.CostEstimate(
                flops=flops, bytes_accessed=moved, transcendentals=exps
            ),
            name="first_rows",
        )(*args)
    weight, other, output = project
    model = weight.shape[2]
    earlier = [] if output is None else [output]
    return pl.pallas_call(
        functools.partial(second_kernel, **sizes),
        out_shape=jax.ShapeDtypeStruct((q.shape[0], tokens, model), jnp.bfloat16),
        grid_spec=pltpu.PrefetchScalarGridSpec(
            num_scalar_prefetch=1,
            grid=(steps,),
            in_specs=[
                *in_specs,
                pl.BlockSpec((None, lanes, model), lambda g, p: (stream, g, 0)),
                pl.BlockSpec((tokens, model), lambda g, p: (0, 0)),
                *[ANY] * len(earlier),
            ],
            out_specs=pl.BlockSpec((None, tokens, model), lambda g, p: (stream, 0, 0)),
            scratch_shapes=[*scratch, pltpu.VMEM((tokens, model), jnp.float32)],
        ),
        input_output_aliases={len(args) + 2: 0} if earlier else {},
        compiler_params=params(),
        cost_estimate=pl.CostEstimate(
            flops=flops + 2 * tokens * width * model,
            bytes_accessed=moved + 2 * width * model,
            transcendentals=exps,
        ),
        name="second_rows",
    )(*args, weight, other, *earlier)


def product(rows, weight, stream, block=3):
    tokens, width = rows.shape
    model = weight.shape[2]
    lanes = block * HEAD
    return pl.pallas_call(
        product_kernel,
        out_shape=jax.ShapeDtypeStruct((tokens, model), jnp.bfloat16),
        grid=(width // lanes,),
        in_specs=[
            pl.BlockSpec((tokens, lanes), lambda g: (0, g)),
            pl.BlockSpec((None, lanes, model), lambda g: (stream, g, 0)),
        ],
        out_specs=pl.BlockSpec((tokens, model), lambda g: (0, 0)),
        scratch_shapes=[pltpu.VMEM((tokens, model), jnp.float32)],
        compiler_params=params(),
        cost_estimate=pl.CostEstimate(
            flops=2 * tokens * width * model, bytes_accessed=2 * width * model, transcendentals=0
        ),
        name="product",
    )(rows, weight)


def swaps(size, start):
    pairs = [(i, i + 1) for i in range(start, size - 1, 2)]
    return pairs + [(j, i) for i, j in pairs]


def per_device(queries, key_states, value_states, tile_mask, frame_reach, out_weight):
    S, F, R, C, width = queries.shape
    tokens = F * R * C
    model = out_weight.shape[2]
    rows, cols = lax.axis_size("row"), lax.axis_size("col")
    inward = [(0, 1), (cols - 1, cols - 2)]
    outward = [(j, i) for i, j in inward]
    place = jnp.stack([lax.axis_index(a) for a in ("pair", "row", "col")]).astype(jnp.int32)
    q, k, v = [a.reshape(S, tokens, width) for a in (queries, key_states, value_states)]
    mask = tile_mask.reshape(9)

    output, near = None, None
    others = []
    for h in range(2):
        own = pack(place, k, v, h, *([] if h == 0 else [near]))
        near = lax.ppermute(own, "col", swaps(cols, 0))
        other = lax.ppermute(own, "col", swaps(cols, 1))
        if h == 0:
            edge_q = lax.ppermute(q, "col", inward)
        strip = (own, near, other)
        above = [lax.ppermute(x, "row", swaps(rows, 0)) for x in strip]
        below = [lax.ppermute(x, "row", swaps(rows, 1)) for x in strip]
        tiles = above + list(strip) + below
        for s in range(S):
            far = lax.ppermute(near[s], "col", swaps(cols, 1))
            partial = edge_attend(place, edge_q, other, far, h, s, C, cols)
            remote = lax.ppermute(partial, "col", outward)
            args = (place, mask, frame_reach, q, tiles, far, remote, h, s, C, R * C, (rows, cols))
            if h == 0:
                theirs = lax.ppermute(main_attend(*args), "pair", swaps(2, 0))
                others.append(lax.ppermute(product(theirs, out_weight, s), "pair", swaps(2, 0)))
            else:
                output = main_attend(*args, project=(out_weight, others[s], output))
    return output.reshape(S, F, R, C, model)


def solution(mesh):
    return jax.shard_map(
        per_device,
        mesh=mesh,
        in_specs=(
            P("pair", None, "row", "col", None),
            P("pair", None, "row", "col", None),
            P("pair", None, "row", "col", None),
            P("pair", "row", "col", None),
            P(),
            P(None, "pair", None),
        ),
        out_specs=P("pair", None, "row", "col", None),
        check_vma=False,
    )
```

time: 670 us -> 194 us (0.29)
  the two profiles are of different devices: /device:TPU:0 before, /device:TPU:19 now
where the time goes in v2:
time: 194 us; the launch traced here: 193 us
  waiting for transfers between devices  81.2 us (42%)
  starting transfers between devices  57.2 us (29%)
  Pallas kernels  49.5 us (26%)
  local copies, waits for them, and re-layouts  4.84 us (2%)
    ppermute x2, waiting for transfers between devices, per_device(): other = lax.ppermute(own, 'col', swaps(cols, 1))  30.5 us
    ppermute x6, starting transfers between devices, per_device(): below = [lax.ppermute(x, 'row', swaps(rows, 1)) for x in strip]  26.4 us
    pallas_call x2, Pallas kernels, main_attend(): pl.pallas_call(functools.partial(second_kernel, **sizes), out_shape=jax.S...  18.5 us
    ppermute x1, waiting for transfers between devices, per_device(): edge_q = lax.ppermute(q, 'col', inward)  17.4 us
    pallas_call x2, Pallas kernels, main_attend(): pl.pallas_call(functools.partial(first_kernel, **sizes), out_shape=jax.Sh...  13.5 us
    ppermute x4, waiting for transfers between devices, per_device(): far = lax.ppermute(near[s], 'col', swaps(cols, 1))  13 us
    pallas_call x4, Pallas kernels, edge_attend(): pl.pallas_call(functools.partial(edge_kernel, heads=heads, cols_tile=cols...  11.7 us
    ppermute x4, starting transfers between devices, per_device(): far = lax.ppermute(near[s], 'col', swaps(cols, 1))  10.9 us
  transfers between devices with their start and end apart: 29, of which 8 were waited for; matrix products, arithmetic and copies ran while one was open for 0% of the time, Pallas kernels for 20%

profile of v2, /device:TPU:19, one launch (start us, length us, event | category | flops | bytes accessed | tf_op | source)
XLA Modules:
  0.0 193.4 jit_solution(15764810462395101655)
XLA Ops:
  3.4 2.1 %collective-permute-start.14 = (bf16[2,2,128,1152]{3,2,1,0:T(8,128)(2,1)S(1)}, bf16[2,2,128,1152]{3,2,1,0:T(8,128)(2,1)S(1)}, u32[]{:S(2)}, u32[]{:S(2)}) collective-permute-start(bf16[2,2,128,1152]{3,2,1,0:T(8,128)(2,1)S(1)} %pack.2.refs_3_), channel_id=1, source_target_pairs={{1,2},{2,1},{5,6},{6,5},{9,10},{10,9},{13,14},{14,13},{17,18},{18,... | collective-permute-start | bytes 3538952 | tf_op jit(solution)/shard_map/ppermute | solution.py:341
  5.6 4.0 %collective-permute-start.16 = (bf16[2,2,128,1152]{3,2,1,0:T(8,128)(2,1)S(1)}, bf16[2,2,128,1152]{3,2,1,0:T(8,128)(2,1)S(1)}, u32[]{:S(2)}, u32[]{:S(2)}) collective-permute-start(bf16[2,2,128,1152]{3,2,1,0:T(8,128)(2,1)S(1)} %pack.2.refs_3_), channel_id=1, source_target_pairs={{4,8},{8,4},{5,9},{9,5},{6,10},{10,6},{7,11},{11,7},{20,24},{24,20... | collective-permute-start | bytes 3538952 | tf_op jit(solution)/shard_map/ppermute | solution.py:346
  9.7 1.4 collective-permute-start.10
  11.1 21.0 %collective-permute-done.14.near_ref.refs_5_ = bf16[2,2,128,1152]{3,2,1,0:T(8,128)(2,1)S(1)} collective-permute-done((bf16[2,2,128,1152]{3,2,1,0:T(8,128)(2,1)S(1)}, bf16[2,2,128,1152]{3,2,1,0:T(8,128)(2,1)S(1)}, u32[]{:S(2)}, u32[]{:S(2)}) %collective-permute-start.14) | collective-permute-done | bytes 1179680 | tf_op jit(solution)/shard_map/ppermute | solution.py:341
  32.2 4.6 %collective-permute-start.18 = (bf16[2,2,128,1152]{3,2,1,0:T(8,128)(2,1)S(1)}, bf16[2,2,128,1152]{3,2,1,0:T(8,128)(2,1)S(1)}, u32[]{:S(2)}, u32[]{:S(2)}) collective-permute-start(bf16[2,2,128,1152]{3,2,1,0:T(8,128)(2,1)S(1)} %collective-permute-done.14.near_ref.refs_5_), channel_id=1, source_target_pairs={{4,8},{8,4},{5,9},{9,5},{6,10},{10,6},{7,11},{11,7},{20,24},{24,20... | collective-permute-start | bytes 3538952 | tf_op jit(solution)/shard_map/ppermute | solution.py:346
  36.9 2.1 %collective-permute-start.25 = (bf16[2,128,1152]{2,1,0:T(8,128)(2,1)S(1)}, bf16[2,128,1152]{2,1,0:T(8,128)(2,1)S(1)}, u32[]{:S(2)}, u32[]{:S(2)}) collective-permute-start(bf16[2,128,1152]{2,1,0:T(8,128)(2,1)S(1)} %get-tuple-element.5), channel_id=1, source_target_pairs={{1,2},{2,1},{5,6},{6,5},{9,10},{10,9},{13,14},{14,13},{17,18},{18,... | collective-permute-start | bytes 1769480 | tf_op jit(solution)/shard_map/ppermute | solution.py:349
  40.0 17.4 %collective-permute-done.10.q_ref = bf16[2,128,2304]{2,1,0:T(8,128)(2,1)S(1)} collective-permute-done((bf16[2,128,2304]{2,1,0:T(8,128)(2,1)S(1)}, bf16[2,128,2304]{2,1,0:T(8,128)(2,1)S(1)}, u32[]{:S(2)}, u32[]{:S(2)}) %collective-permute-start.10) | collective-permute-done | bytes 1179680 | tf_op jit(solution)/shard_map/ppermute | solution.py:343
  57.4 3.2 %collective-permute-start.19 = (bf16[2,128,1152]{2,1,0:T(8,128)(2,1)S(1)}, bf16[2,128,1152]{2,1,0:T(8,128)(2,1)S(1)}, u32[]{:S(2)}, u32[]{:S(2)}) collective-permute-start(bf16[2,128,1152]{2,1,0:T(8,128)(2,1)S(1)} %get-tuple-element.6), channel_id=1, source_target_pairs={{1,2},{2,1},{5,6},{6,5},{9,10},{10,9},{13,14},{14,13},{17,18},{18,... | collective-permute-start | bytes 1769480 | tf_op jit(solution)/shard_map/ppermute | solution.py:349
  60.6 6.6 %collective-permute-start.17 = (bf16[2,2,128,1152]{3,2,1,0:T(8,128)(2,1)S(1)}, bf16[2,2,128,1152]{3,2,1,0:T(8,128)(2,1)S(1)}, u32[]{:S(2)}, u32[]{:S(2)}) collective-permute-start(bf16[2,2,128,1152]{3,2,1,0:T(8,128)(2,1)S(1)} %collective-permute-done.refs_0_.refs_4_), channel_id=1, source_target_pairs={{4,8},{8,4},{5,9},{9,5},{6,10},{10,6},{7,11},{11,7},{20,24},{24,20... | collective-permute-start | bytes 3538952 | tf_op jit(solution)/shard_map/ppermute | solution.py:346
  67.3 2.9 %edge_rows.7 = bf16[128,1280]{1,0:T(8,128)(2,1)S(1)} custom-call(s32[3]{0:T(128)S(1)} %pad_add_fusion.place, bf16[2,128,2304]{2,1,0:T(8,128)(2,1)S(1)} %collective-permute-done.10.q_ref, bf16[2,2,128,1152]{3,2,1,0:T(8,128)(2,1)S(1)} %collective-permute-done.14.near_ref.refs_5_, bf16[2,128,1152]{2,1,0:T(8,128)(2,1)S(1)} %collective-permute-done.25.far_ref.refs_9_), custom_call_target="tpu_custom_call" | custom-call | flops 150994944 | bytes 2064384 | tf_op jit(solution)/shard_map/edge_rows/pallas_call | solution.py:209
  72.1 4.0 %collective-permute-done.26.refs_10_.refs_11_ = bf16[128,1280]{1,0:T(8,128)(2,1)S(1)} collective-permute-done((bf16[128,1280]{1,0:T(8,128)(2,1)S(1)}, bf16[128,1280]{1,0:T(8,128)(2,1)S(1)}, u32[]{:S(2)}, u32[]{:S(2)}) %collective-permute-start.26) | collective-permute-done | bytes 327712 | tf_op jit(solution)/shard_map/ppermute | solution.py:351
  76.1 4.8 %collective-permute-start.13 = (bf16[2,2,128,1152]{3,2,1,0:T(8,128)(2,1)S(1)}, bf16[2,2,128,1152]{3,2,1,0:T(8,128)(2,1)S(1)}, u32[]{:S(2)}, u32[]{:S(2)}) collective-permute-start(bf16[2,2,128,1152]{3,2,1,0:T(8,128)(2,1)S(1)} %collective-permute-done.refs_0_.refs_4_), channel_id=1, source_target_pairs={{0,4},{8,12},{4,0},{12,8},{1,5},{9,13},{5,1},{13,9},{2,6},{10,14},... | collective-permute-start | bytes 3538952 | tf_op jit(solution)/shard_map/ppermute | solution.py:345
  80.9 3.2 %collective-permute-start.4 = (bf16[2,2,128,1152]{3,2,1,0:T(8,128)(2,1)S(1)}, bf16[2,2,128,1152]{3,2,1,0:T(8,128)(2,1)S(1)}, u32[]{:S(2)}, u32[]{:S(2)}) collective-permute-start(bf16[2,2,128,1152]{3,2,1,0:T(8,128)(2,1)S(1)} %pack.3.refs_3_), channel_id=1, source_target_pairs={{1,2},{2,1},{5,6},{6,5},{9,10},{10,9},{13,14},{14,13},{17,18},{18,... | collective-permute-start | bytes 3538952 | tf_op jit(solution)/shard_map/ppermute | solution.py:341
  84.1 3.3 %collective-permute-start.6 = (bf16[2,2,128,1152]{3,2,1,0:T(8,128)(2,1)S(1)}, bf16[2,2,128,1152]{3,2,1,0:T(8,128)(2,1)S(1)}, u32[]{:S(2)}, u32[]{:S(2)}) collective-permute-start(bf16[2,2,128,1152]{3,2,1,0:T(8,128)(2,1)S(1)} %pack.3.refs_3_), channel_id=1, source_target_pairs={{4,8},{8,4},{5,9},{9,5},{6,10},{10,6},{7,11},{11,7},{20,24},{24,20... | collective-permute-start | bytes 3538952 | tf_op jit(solution)/shard_map/ppermute | solution.py:346
  87.7 2.2 %collective-permute-start.23 = (bf16[2,128,1152]{2,1,0:T(8,128)(2,1)S(1)}, bf16[2,128,1152]{2,1,0:T(8,128)(2,1)S(1)}, u32[]{:S(2)}, u32[]{:S(2)}) collective-permute-start(bf16[2,128,1152]{2,1,0:T(8,128)(2,1)S(1)} %get-tuple-element.7), channel_id=1, source_target_pairs={{1,2},{2,1},{5,6},{6,5},{9,10},{10,9},{13,14},{14,13},{17,18},{18,... | collective-permute-start | bytes 1769480 | tf_op jit(solution)/shard_map/ppermute | solution.py:349
  89.9 2.9 %edge_rows.5 = bf16[128,1280]{1,0:T(8,128)(2,1)S(1)} custom-call(s32[3]{0:T(128)S(1)} %pad_add_fusion.place, bf16[2,128,2304]{2,1,0:T(8,128)(2,1)S(1)} %collective-permute-done.10.q_ref, bf16[2,2,128,1152]{3,2,1,0:T(8,128)(2,1)S(1)} %collective-permute-done.14.near_ref.refs_5_, bf16[2,128,1152]{2,1,0:T(8,128)(2,1)S(1)} %collective-permute-done.19.far_ref.refs_9_), custom_call_target="tpu_custom_call" | custom-call | flops 150994944 | bytes 2064384 | tf_op jit(solution)/shard_map/edge_rows/pallas_call | solution.py:209
  94.2 6.7 %first_rows.3 = bf16[128,1152]{1,0:T(8,128)(2,1)S(1)} custom-call(s32[3]{0:T(128)S(1)} %pad_add_fusion.place, s32[9]{0:T(128)S(1)} %bitcast.27, s32[18]{0:T(128)S(1)} %copy-done.13, bf16[2,128,2304]{2,1,0:T(8,128)(2,1)S(1)} %bitcast.19, bf16[2,2,128,1152]{3,2,1,0:T(8,128)(2,1)S(1)} %collective-permute-done.12.refs_0_, ...), custom_call_target="tpu_custom_call" | custom-call | flops 868220928 | bytes 6782976 | tf_op jit(solution)/shard_map/first_rows/pallas_call | solution.py:253
  100.9 9.4 %collective-permute-done.4.near_ref.refs_5_ = bf16[2,2,128,1152]{3,2,1,0:T(8,128)(2,1)S(1)} collective-permute-done((bf16[2,2,128,1152]{3,2,1,0:T(8,128)(2,1)S(1)}, bf16[2,2,128,1152]{3,2,1,0:T(8,128)(2,1)S(1)}, u32[]{:S(2)}, u32[]{:S(2)}) %collective-permute-start.4) | collective-permute-done | bytes 1179680 | tf_op jit(solution)/shard_map/ppermute | solution.py:341
  110.6 12.4 %collective-permute-done.23.far_ref.refs_9_ = bf16[2,128,1152]{2,1,0:T(8,128)(2,1)S(1)} collective-permute-done((bf16[2,128,1152]{2,1,0:T(8,128)(2,1)S(1)}, bf16[2,128,1152]{2,1,0:T(8,128)(2,1)S(1)}, u32[]{:S(2)}, u32[]{:S(2)}) %collective-permute-start.23) | collective-permute-done | bytes 589856 | tf_op jit(solution)/shard_map/ppermute | solution.py:349
  123.0 3.5 %collective-permute-start.9 = (bf16[2,128,1152]{2,1,0:T(8,128)(2,1)S(1)}, bf16[2,128,1152]{2,1,0:T(8,128)(2,1)S(1)}, u32[]{:S(2)}, u32[]{:S(2)}) collective-permute-start(bf16[2,128,1152]{2,1,0:T(8,128)(2,1)S(1)} %get-tuple-element.8), channel_id=1, source_target_pairs={{1,2},{2,1},{5,6},{6,5},{9,10},{10,9},{13,14},{14,13},{17,18},{18,... | collective-permute-start | bytes 1769480 | tf_op jit(solution)/shard_map/ppermute | solution.py:349
  126.5 2.9 %edge_rows.6 = bf16[128,1280]{1,0:T(8,128)(2,1)S(1)} custom-call(s32[3]{0:T(128)S(1)} %pad_add_fusion.place, bf16[2,128,2304]{2,1,0:T(8,128)(2,1)S(1)} %collective-permute-done.10.q_ref, bf16[2,2,128,1152]{3,2,1,0:T(8,128)(2,1)S(1)} %collective-permute-done.4.near_ref.refs_5_, bf16[2,128,1152]{2,1,0:T(8,128)(2,1)S(1)} %collective-permute-done.23.far_ref.refs_9_), custom_call_target="tpu_custom_call" | custom-call | flops 150994944 | bytes 2064384 | tf_op jit(solution)/shard_map/edge_rows/pallas_call | solution.py:209
  129.4 1.4 collective-permute-start.24
  130.9 6.7 %first_rows.2 = bf16[128,1152]{1,0:T(8,128)(2,1)S(1)} custom-call(s32[3]{0:T(128)S(1)} %pad_add_fusion.place, s32[9]{0:T(128)S(1)} %bitcast.28, s32[18]{0:T(128)S(1)} %copy-done.13, bf16[2,128,2304]{2,1,0:T(8,128)(2,1)S(1)} %bitcast.20, bf16[2,2,128,1152]{3,2,1,0:T(8,128)(2,1)S(1)} %collective-permute-done.12.refs_0_, ...), custom_call_target="tpu_custom_call" | custom-call | flops 868220928 | bytes 6782976 | tf_op jit(solution)/shard_map/first_rows/pallas_call | solution.py:253
  138.0 2.1 %product.3 = bf16[128,3072]{1,0:T(8,128)(2,1)S(1)} custom-call(bf16[128,1152]{1,0:T(8,128)(2,1)S(1)} %collective-permute-done.27.rows_ref, bf16[2,1152,3072]{2,1,0:T(8,128)(2,1)S(1)} %bitcast.17), custom_call_target="tpu_custom_call" | custom-call | flops 905969664 | bytes 7077888 | tf_op jit(solution)/shard_map/product/pallas_call | solution.py:302
  143.3 4.8 %collective-permute-start.8 = (bf16[2,2,128,1152]{3,2,1,0:T(8,128)(2,1)S(1)}, bf16[2,2,128,1152]{3,2,1,0:T(8,128)(2,1)S(1)}, u32[]{:S(2)}, u32[]{:S(2)}) collective-permute-start(bf16[2,2,128,1152]{3,2,1,0:T(8,128)(2,1)S(1)} %collective-permute-done.4.near_ref.refs_5_), channel_id=1, source_target_pairs={{4,8},{8,4},{5,9},{9,5},{6,10},{10,6},{7,11},{11,7},{20,24},{24,20... | collective-permute-start | bytes 3538952 | tf_op jit(solution)/shard_map/ppermute | solution.py:346
  148.7 3.0 %collective-permute-start.7 = (bf16[2,2,128,1152]{3,2,1,0:T(8,128)(2,1)S(1)}, bf16[2,2,128,1152]{3,2,1,0:T(8,128)(2,1)S(1)}, u32[]{:S(2)}, u32[]{:S(2)}) collective-permute-start(bf16[2,2,128,1152]{3,2,1,0:T(8,128)(2,1)S(1)} %collective-permute-done.2.refs_4_), channel_id=1, source_target_pairs={{4,8},{8,4},{5,9},{9,5},{6,10},{10,6},{7,11},{11,7},{20,24},{24,20... | collective-permute-start | bytes 3538952 | tf_op jit(solution)/shard_map/ppermute | solution.py:346
  151.9 2.1 %product.2 = bf16[128,3072]{1,0:T(8,128)(2,1)S(1)} custom-call(bf16[128,1152]{1,0:T(8,128)(2,1)S(1)} %collective-permute-done.21.rows_ref, bf16[2,1152,3072]{2,1,0:T(8,128)(2,1)S(1)} %bitcast.17), custom_call_target="tpu_custom_call" | custom-call | flops 905969664 | bytes 7077888 | tf_op jit(solution)/shard_map/product/pallas_call | solution.py:302
  154.0 8.0 %collective-permute-done.28.refs_13_ = bf16[128,3072]{1,0:T(8,128)(2,1)S(1)} collective-permute-done((bf16[128,3072]{1,0:T(8,128)(2,1)S(1)}, bf16[128,3072]{1,0:T(8,128)(2,1)S(1)}, u32[]{:S(2)}, u32[]{:S(2)}) %collective-permute-start.28) | collective-permute-done | bytes 786464 | tf_op jit(solution)/shard_map/ppermute | solution.py:355
  162.2 2.9 %edge_rows.4 = bf16[128,1280]{1,0:T(8,128)(2,1)S(1)} custom-call(s32[3]{0:T(128)S(1)} %pad_add_fusion.place, bf16[2,128,2304]{2,1,0:T(8,128)(2,1)S(1)} %collective-permute-done.10.q_ref, bf16[2,2,128,1152]{3,2,1,0:T(8,128)(2,1)S(1)} %collective-permute-done.4.near_ref.refs_5_, bf16[2,128,1152]{2,1,0:T(8,128)(2,1)S(1)} %collective-permute-done.9.far_ref.refs_9_), custom_call_target="tpu_custom_call" | custom-call | flops 150994944 | bytes 2064384 | tf_op jit(solution)/shard_map/edge_rows/pallas_call | solution.py:209
  166.5 8.3 %collective-permute-done.7.refs_7_ = bf16[2,2,128,1152]{3,2,1,0:T(8,128)(2,1)S(1)} collective-permute-done((bf16[2,2,128,1152]{3,2,1,0:T(8,128)(2,1)S(1)}, bf16[2,2,128,1152]{3,2,1,0:T(8,128)(2,1)S(1)}, u32[]{:S(2)}, u32[]{:S(2)}) %collective-permute-start.7) | collective-permute-done | bytes 1179680 | tf_op jit(solution)/shard_map/ppermute | solution.py:346
  174.9 9.3 %second_rows.2.refs_14_ = bf16[2,128,3072]{2,1,0:T(8,128)(2,1)} custom-call(s32[3]{0:T(128)S(1)} %pad_add_fusion.place, s32[9]{0:T(128)S(1)} %bitcast.29, s32[18]{0:T(128)S(1)} %copy-done.13, bf16[2,128,2304]{2,1,0:T(8,128)(2,1)S(1)} %bitcast.21, bf16[2,2,128,1152]{3,2,1,0:T(8,128)(2,1)S(1)} %copy-done.8, ...), custom_call_target="tpu_custom_call" | custom-call | flops 1774190592 | bytes 13860864 | tf_op jit(solution)/shard_map/second_rows/pallas_call | solution.py:272
  184.1 9.2 %second_rows.3 = bf16[2,128,3072]{2,1,0:T(8,128)(2,1)} custom-call(s32[3]{0:T(128)S(1)} %pad_add_fusion.place, s32[9]{0:T(128)S(1)} %bitcast.30, s32[18]{0:T(128)S(1)} %copy-done.13, bf16[2,128,2304]{2,1,0:T(8,128)(2,1)S(1)} %bitcast.22, bf16[2,2,128,1152]{3,2,1,0:T(8,128)(2,1)S(1)} %copy-done.8, ...), custom_call_target="tpu_custom_call", output_to_operand_aliasing={{}: (18, {})} | custom-call | flops 1774190592 | bytes 13860864 | tf_op jit(solution)/shard_map/second_rows/pallas_call | solution.py:272
  (78 shorter events, 14.1 us)
Async XLA Ops:
  3.4 28.7 %collective-permute-start.14 = (bf16[2,2,128,1152]{3,2,1,0:T(8,128)(2,1)S(1)}, bf16[2,2,128,1152]{3,2,1,0:T(8,128)(2,1)S(1)}, u32[]{:S(2)}, u32[]{:S(2)}) collective-permute-start(bf16[2,2,128,1152]{3,2,1,0:T(8,128)(2,1)S(1)} %pack.2.refs_3_), channel_id=1, source_target_pairs={{1,2},{2,1},{5,6},{6,5},{9,10},{10,9},{13,14},{14,13},{17,18},{18,... | collective-permute-start | bytes 3538952 | tf_op jit(solution)/shard_map/ppermute | solution.py:341
  5.5 31.2 %collective-permute-start = (bf16[2,2,128,1152]{3,2,1,0:T(8,128)(2,1)S(1)}, bf16[2,2,128,1152]{3,2,1,0:T(8,128)(2,1)S(1)}, u32[]{:S(2)}, u32[]{:S(2)}) collective-permute-start(bf16[2,2,128,1152]{3,2,1,0:T(8,128)(2,1)S(1)} %pack.2.refs_3_), channel_id=1, source_target_pairs={{0,1},{2,3},{1,0},{3,2},{4,5},{6,7},{5,4},{7,6},{8,9},{10,11},{9,8... | collective-permute-start | bytes 3538952 | tf_op jit(solution)/shard_map/ppermute | solution.py:340
  5.6 34.2 %collective-permute-start.16 = (bf16[2,2,128,1152]{3,2,1,0:T(8,128)(2,1)S(1)}, bf16[2,2,128,1152]{3,2,1,0:T(8,128)(2,1)S(1)}, u32[]{:S(2)}, u32[]{:S(2)}) collective-permute-start(bf16[2,2,128,1152]{3,2,1,0:T(8,128)(2,1)S(1)} %pack.2.refs_3_), channel_id=1, source_target_pairs={{4,8},{8,4},{5,9},{9,5},{6,10},{10,6},{7,11},{11,7},{20,24},{24,20... | collective-permute-start | bytes 3538952 | tf_op jit(solution)/shard_map/ppermute | solution.py:346
  9.6 30.3 %collective-permute-start.12 = (bf16[2,2,128,1152]{3,2,1,0:T(8,128)(2,1)S(1)}, bf16[2,2,128,1152]{3,2,1,0:T(8,128)(2,1)S(1)}, u32[]{:S(2)}, u32[]{:S(2)}) collective-permute-start(bf16[2,2,128,1152]{3,2,1,0:T(8,128)(2,1)S(1)} %pack.2.refs_3_), channel_id=1, source_target_pairs={{0,4},{8,12},{4,0},{12,8},{1,5},{9,13},{5,1},{13,9},{2,6},{10,14},... | collective-permute-start | bytes 3538952 | tf_op jit(solution)/shard_map/ppermute | solution.py:345
  9.7 47.7 %collective-permute-start.10 = (bf16[2,128,2304]{2,1,0:T(8,128)(2,1)S(1)}, bf16[2,128,2304]{2,1,0:T(8,128)(2,1)S(1)}, u32[]{:S(2)}, u32[]{:S(2)}) collective-permute-start(bf16[2,128,2304]{2,1,0:T(8,128)(2,1)S(1)} %bitcast.18), channel_id=1, source_target_pairs={{0,1},{3,2},{4,5},{7,6},{8,9},{11,10},{12,13},{15,14},{16,17},{19,... | collective-permute-start | bytes 3538952 | tf_op jit(solution)/shard_map/ppermute | solution.py:343
  32.2 48.7 %collective-permute-start.18 = (bf16[2,2,128,1152]{3,2,1,0:T(8,128)(2,1)S(1)}, bf16[2,2,128,1152]{3,2,1,0:T(8,128)(2,1)S(1)}, u32[]{:S(2)}, u32[]{:S(2)}) collective-permute-start(bf16[2,2,128,1152]{3,2,1,0:T(8,128)(2,1)S(1)} %collective-permute-done.14.near_ref.refs_5_), channel_id=1, source_target_pairs={{4,8},{8,4},{5,9},{9,5},{6,10},{10,6},{7,11},{11,7},{20,24},{24,20... | collective-permute-start | bytes 3538952 | tf_op jit(solution)/shard_map/ppermute | solution.py:346
  36.9 23.7 %collective-permute-start.25 = (bf16[2,128,1152]{2,1,0:T(8,128)(2,1)S(1)}, bf16[2,128,1152]{2,1,0:T(8,128)(2,1)S(1)}, u32[]{:S(2)}, u32[]{:S(2)}) collective-permute-start(bf16[2,128,1152]{2,1,0:T(8,128)(2,1)S(1)} %get-tuple-element.5), channel_id=1, source_target_pairs={{1,2},{2,1},{5,6},{6,5},{9,10},{10,9},{13,14},{14,13},{17,18},{18,... | collective-permute-start | bytes 1769480 | tf_op jit(solution)/shard_map/ppermute | solution.py:349
  39.8 47.7 %copy-start.1 = (bf16[2,2,128,1152]{3,2,1,0:T(8,128)(2,1)}, bf16[2,2,128,1152]{3,2,1,0:T(8,128)(2,1)S(1)}, u32[]{:S(2)}) copy-start(bf16[2,2,128,1152]{3,2,1,0:T(8,128)(2,1)S(1)} %pack.3.refs_3_) | copy-start | bytes 3538948
  39.8 44.3 %collective-permute-start.15 = (bf16[2,2,128,1152]{3,2,1,0:T(8,128)(2,1)S(1)}, bf16[2,2,128,1152]{3,2,1,0:T(8,128)(2,1)S(1)}, u32[]{:S(2)}, u32[]{:S(2)}) collective-permute-start(bf16[2,2,128,1152]{3,2,1,0:T(8,128)(2,1)S(1)} %collective-permute-done.14.near_ref.refs_5_), channel_id=1, source_target_pairs={{0,4},{8,12},{4,0},{12,8},{1,5},{9,13},{5,1},{13,9},{2,6},{10,14},... | collective-permute-start | bytes 3538952 | tf_op jit(solution)/shard_map/ppermute | solution.py:345
  40.0 47.5 %collective-permute-start.2 = (bf16[2,2,128,1152]{3,2,1,0:T(8,128)(2,1)S(1)}, bf16[2,2,128,1152]{3,2,1,0:T(8,128)(2,1)S(1)}, u32[]{:S(2)}, u32[]{:S(2)}) collective-permute-start(bf16[2,2,128,1152]{3,2,1,0:T(8,128)(2,1)S(1)} %pack.3.refs_3_), channel_id=1, source_target_pairs={{0,1},{2,3},{1,0},{3,2},{4,5},{6,7},{5,4},{7,6},{8,9},{10,11},{9,8... | collective-permute-start | bytes 3538952 | tf_op jit(solution)/shard_map/ppermute | solution.py:340
  57.4 13.4 %collective-permute-start.19 = (bf16[2,128,1152]{2,1,0:T(8,128)(2,1)S(1)}, bf16[2,128,1152]{2,1,0:T(8,128)(2,1)S(1)}, u32[]{:S(2)}, u32[]{:S(2)}) collective-permute-start(bf16[2,128,1152]{2,1,0:T(8,128)(2,1)S(1)} %get-tuple-element.6), channel_id=1, source_target_pairs={{1,2},{2,1},{5,6},{6,5},{9,10},{10,9},{13,14},{14,13},{17,18},{18,... | collective-permute-start | bytes 1769480 | tf_op jit(solution)/shard_map/ppermute | solution.py:349
  60.6 27.0 %collective-permute-start.17 = (bf16[2,2,128,1152]{3,2,1,0:T(8,128)(2,1)S(1)}, bf16[2,2,128,1152]{3,2,1,0:T(8,128)(2,1)S(1)}, u32[]{:S(2)}, u32[]{:S(2)}) collective-permute-start(bf16[2,2,128,1152]{3,2,1,0:T(8,128)(2,1)S(1)} %collective-permute-done.refs_0_.refs_4_), channel_id=1, source_target_pairs={{4,8},{8,4},{5,9},{9,5},{6,10},{10,6},{7,11},{11,7},{20,24},{24,20... | collective-permute-start | bytes 3538952 | tf_op jit(solution)/shard_map/ppermute | solution.py:346
  70.8 5.3 %collective-permute-start.26 = (bf16[128,1280]{1,0:T(8,128)(2,1)S(1)}, bf16[128,1280]{1,0:T(8,128)(2,1)S(1)}, u32[]{:S(2)}, u32[]{:S(2)}) collective-permute-start(bf16[128,1280]{1,0:T(8,128)(2,1)S(1)} %edge_rows.7), channel_id=1, source_target_pairs={{1,0},{2,3},{5,4},{6,7},{9,8},{10,11},{13,12},{14,15},{17,16},{18,... | collective-permute-start | bytes 983048 | tf_op jit(solution)/shard_map/ppermute | solution.py:351
  76.1 16.8 %collective-permute-start.13 = (bf16[2,2,128,1152]{3,2,1,0:T(8,128)(2,1)S(1)}, bf16[2,2,128,1152]{3,2,1,0:T(8,128)(2,1)S(1)}, u32[]{:S(2)}, u32[]{:S(2)}) collective-permute-start(bf16[2,2,128,1152]{3,2,1,0:T(8,128)(2,1)S(1)} %collective-permute-done.refs_0_.refs_4_), channel_id=1, source_target_pairs={{0,4},{8,12},{4,0},{12,8},{1,5},{9,13},{5,1},{13,9},{2,6},{10,14},... | collective-permute-start | bytes 3538952 | tf_op jit(solution)/shard_map/ppermute | solution.py:345
  80.9 29.5 %collective-permute-start.4 = (bf16[2,2,128,1152]{3,2,1,0:T(8,128)(2,1)S(1)}, bf16[2,2,128,1152]{3,2,1,0:T(8,128)(2,1)S(1)}, u32[]{:S(2)}, u32[]{:S(2)}) collective-permute-start(bf16[2,2,128,1152]{3,2,1,0:T(8,128)(2,1)S(1)} %pack.3.refs_3_), channel_id=1, source_target_pairs={{1,2},{2,1},{5,6},{6,5},{9,10},{10,9},{13,14},{14,13},{17,18},{18,... | collective-permute-start | bytes 3538952 | tf_op jit(solution)/shard_map/ppermute | solution.py:341
  84.1 56.0 %collective-permute-start.6 = (bf16[2,2,128,1152]{3,2,1,0:T(8,128)(2,1)S(1)}, bf16[2,2,128,1152]{3,2,1,0:T(8,128)(2,1)S(1)}, u32[]{:S(2)}, u32[]{:S(2)}) collective-permute-start(bf16[2,2,128,1152]{3,2,1,0:T(8,128)(2,1)S(1)} %pack.3.refs_3_), channel_id=1, source_target_pairs={{4,8},{8,4},{5,9},{9,5},{6,10},{10,6},{7,11},{11,7},{20,24},{24,20... | collective-permute-start | bytes 3538952 | tf_op jit(solution)/shard_map/ppermute | solution.py:346
  87.4 64.3 %copy-start.3 = (bf16[2,2,128,1152]{3,2,1,0:T(8,128)(2,1)}, bf16[2,2,128,1152]{3,2,1,0:T(8,128)(2,1)S(1)}, u32[]{:S(2)}) copy-start(bf16[2,2,128,1152]{3,2,1,0:T(8,128)(2,1)S(1)} %collective-permute-done.2.refs_4_) | copy-start | bytes 3538948
  87.5 54.9 %collective-permute-start.1 = (bf16[2,2,128,1152]{3,2,1,0:T(8,128)(2,1)S(1)}, bf16[2,2,128,1152]{3,2,1,0:T(8,128)(2,1)S(1)}, u32[]{:S(2)}, u32[]{:S(2)}) collective-permute-start(bf16[2,2,128,1152]{3,2,1,0:T(8,128)(2,1)S(1)} %pack.3.refs_3_), channel_id=1, source_target_pairs={{0,4},{8,12},{4,0},{12,8},{1,5},{9,13},{5,1},{13,9},{2,6},{10,14},... | collective-permute-start | bytes 3538952 | tf_op jit(solution)/shard_map/ppermute | solution.py:345
  87.7 35.3 %collective-permute-start.23 = (bf16[2,128,1152]{2,1,0:T(8,128)(2,1)S(1)}, bf16[2,128,1152]{2,1,0:T(8,128)(2,1)S(1)}, u32[]{:S(2)}, u32[]{:S(2)}) collective-permute-start(bf16[2,128,1152]{2,1,0:T(8,128)(2,1)S(1)} %get-tuple-element.7), channel_id=1, source_target_pairs={{1,2},{2,1},{5,6},{6,5},{9,10},{10,9},{13,14},{14,13},{17,18},{18,... | collective-permute-start | bytes 1769480 | tf_op jit(solution)/shard_map/ppermute | solution.py:349
  92.8 36.6 %collective-permute-start.20 = (bf16[128,1280]{1,0:T(8,128)(2,1)S(1)}, bf16[128,1280]{1,0:T(8,128)(2,1)S(1)}, u32[]{:S(2)}, u32[]{:S(2)}) collective-permute-start(bf16[128,1280]{1,0:T(8,128)(2,1)S(1)} %edge_rows.5), channel_id=1, source_target_pairs={{1,0},{2,3},{5,4},{6,7},{9,8},{10,11},{13,12},{14,15},{17,16},{18,... | collective-permute-start | bytes 983048 | tf_op jit(solution)/shard_map/ppermute | solution.py:351
  94.2 43.8 %slice-start = ((s8[14155776]{0:T(1024)(128)(4,1)}), s8[4194304]{0:T(1024)(128)(4,1)S(1)}, s32[]{:S(2)}) async-start(s8[14155776]{0:T(1024)(128)(4,1)} %bitcast.16), calls=%async_computation | async-start | bytes 8388608
  110.4 27.3 %collective-permute-start.27 = (bf16[128,1152]{1,0:T(8,128)(2,1)S(1)}, bf16[128,1152]{1,0:T(8,128)(2,1)S(1)}, u32[]{:S(2)}, u32[]{:S(2)}) collective-permute-start(bf16[128,1152]{1,0:T(8,128)(2,1)S(1)} %first_rows.3), channel_id=1, source_target_pairs={{0,16},{16,0},{1,17},{17,1},{2,18},{18,2},{3,19},{19,3},{4,20},{20... | collective-permute-start | bytes 884744 | tf_op jit(solution)/shard_map/ppermute | solution.py:354
  123.0 25.7 %collective-permute-start.9 = (bf16[2,128,1152]{2,1,0:T(8,128)(2,1)S(1)}, bf16[2,128,1152]{2,1,0:T(8,128)(2,1)S(1)}, u32[]{:S(2)}, u32[]{:S(2)}) collective-permute-start(bf16[2,128,1152]{2,1,0:T(8,128)(2,1)S(1)} %get-tuple-element.8), channel_id=1, source_target_pairs={{1,2},{2,1},{5,6},{6,5},{9,10},{10,9},{13,14},{14,13},{17,18},{18,... | collective-permute-start | bytes 1769480 | tf_op jit(solution)/shard_map/ppermute | solution.py:349
  129.4 22.3 %collective-permute-start.24 = (bf16[128,1280]{1,0:T(8,128)(2,1)S(1)}, bf16[128,1280]{1,0:T(8,128)(2,1)S(1)}, u32[]{:S(2)}, u32[]{:S(2)}) collective-permute-start(bf16[128,1280]{1,0:T(8,128)(2,1)S(1)} %edge_rows.6), channel_id=1, source_target_pairs={{1,0},{2,3},{5,4},{6,7},{9,8},{10,11},{13,12},{14,15},{17,16},{18,... | collective-permute-start | bytes 983048 | tf_op jit(solution)/shard_map/ppermute | solution.py:351
  137.6 10.6 %collective-permute-start.21 = (bf16[128,1152]{1,0:T(8,128)(2,1)S(1)}, bf16[128,1152]{1,0:T(8,128)(2,1)S(1)}, u32[]{:S(2)}, u32[]{:S(2)}) collective-permute-start(bf16[128,1152]{1,0:T(8,128)(2,1)S(1)} %first_rows.2), channel_id=1, source_target_pairs={{0,16},{16,0},{1,17},{17,1},{2,18},{18,2},{3,19},{19,3},{4,20},{20... | collective-permute-start | bytes 884744 | tf_op jit(solution)/shard_map/ppermute | solution.py:354
  141.1 20.9 %collective-permute-start.28 = (bf16[128,3072]{1,0:T(8,128)(2,1)S(1)}, bf16[128,3072]{1,0:T(8,128)(2,1)S(1)}, u32[]{:S(2)}, u32[]{:S(2)}) collective-permute-start(bf16[128,3072]{1,0:T(8,128)(2,1)S(1)} %product.3), channel_id=1, source_target_pairs={{0,16},{16,0},{1,17},{17,1},{2,18},{18,2},{3,19},{19,3},{4,20},{20... | collective-permute-start | bytes 2359304 | tf_op jit(solution)/shard_map/ppermute | solution.py:355
  143.3 21.8 %collective-permute-start.8 = (bf16[2,2,128,1152]{3,2,1,0:T(8,128)(2,1)S(1)}, bf16[2,2,128,1152]{3,2,1,0:T(8,128)(2,1)S(1)}, u32[]{:S(2)}, u32[]{:S(2)}) collective-permute-start(bf16[2,2,128,1152]{3,2,1,0:T(8,128)(2,1)S(1)} %collective-permute-done.4.near_ref.refs_5_), channel_id=1, source_target_pairs={{4,8},{8,4},{5,9},{9,5},{6,10},{10,6},{7,11},{11,7},{20,24},{24,20... | collective-permute-start | bytes 3538952 | tf_op jit(solution)/shard_map/ppermute | solution.py:346
  148.2 18.3 %collective-permute-start.5 = (bf16[2,2,128,1152]{3,2,1,0:T(8,128)(2,1)S(1)}, bf16[2,2,128,1152]{3,2,1,0:T(8,128)(2,1)S(1)}, u32[]{:S(2)}, u32[]{:S(2)}) collective-permute-start(bf16[2,2,128,1152]{3,2,1,0:T(8,128)(2,1)S(1)} %collective-permute-done.4.near_ref.refs_5_), channel_id=1, source_target_pairs={{0,4},{8,12},{4,0},{12,8},{1,5},{9,13},{5,1},{13,9},{2,6},{10,14},... | collective-permute-start | bytes 3538952 | tf_op jit(solution)/shard_map/ppermute | solution.py:345
  148.7 26.1 %collective-permute-start.7 = (bf16[2,2,128,1152]{3,2,1,0:T(8,128)(2,1)S(1)}, bf16[2,2,128,1152]{3,2,1,0:T(8,128)(2,1)S(1)}, u32[]{:S(2)}, u32[]{:S(2)}) collective-permute-start(bf16[2,2,128,1152]{3,2,1,0:T(8,128)(2,1)S(1)} %collective-permute-done.2.refs_4_), channel_id=1, source_target_pairs={{4,8},{8,4},{5,9},{9,5},{6,10},{10,6},{7,11},{11,7},{20,24},{24,20... | collective-permute-start | bytes 3538952 | tf_op jit(solution)/shard_map/ppermute | solution.py:346
  151.8 23.1 %collective-permute-start.3 = (bf16[2,2,128,1152]{3,2,1,0:T(8,128)(2,1)S(1)}, bf16[2,2,128,1152]{3,2,1,0:T(8,128)(2,1)S(1)}, u32[]{:S(2)}, u32[]{:S(2)}) collective-permute-start(bf16[2,2,128,1152]{3,2,1,0:T(8,128)(2,1)S(1)} %collective-permute-done.2.refs_4_), channel_id=1, source_target_pairs={{0,4},{8,12},{4,0},{12,8},{1,5},{9,13},{5,1},{13,9},{2,6},{10,14},... | collective-permute-start | bytes 3538952 | tf_op jit(solution)/shard_map/ppermute | solution.py:345
  162.0 22.1 %collective-permute-start.22 = (bf16[128,3072]{1,0:T(8,128)(2,1)S(1)}, bf16[128,3072]{1,0:T(8,128)(2,1)S(1)}, u32[]{:S(2)}, u32[]{:S(2)}) collective-permute-start(bf16[128,3072]{1,0:T(8,128)(2,1)S(1)} %product.2), channel_id=1, source_target_pairs={{0,16},{16,0},{1,17},{17,1},{2,18},{18,2},{3,19},{19,3},{4,20},{20... | collective-permute-start | bytes 2359304 | tf_op jit(solution)/shard_map/ppermute | solution.py:355
  165.2 18.9 %collective-permute-start.11 = (bf16[128,1280]{1,0:T(8,128)(2,1)S(1)}, bf16[128,1280]{1,0:T(8,128)(2,1)S(1)}, u32[]{:S(2)}, u32[]{:S(2)}) collective-permute-start(bf16[128,1280]{1,0:T(8,128)(2,1)S(1)} %edge_rows.4), channel_id=1, source_target_pairs={{1,0},{2,3},{5,4},{6,7},{9,8},{10,11},{13,12},{14,15},{17,16},{18,... | collective-permute-start | bytes 983048 | tf_op jit(solution)/shard_map/ppermute | solution.py:351
  (15 other events, 208.9 us)

commit v3 on v2

--- a/solution.py
+++ b/solution.py
@@ -16,10 +16,6 @@
 SMEM = pl.BlockSpec(memory_space=pltpu.SMEM)
 
 
-def dot_nt(a, b):
-    return lax.dot_general(a, b, (((1,), (1,)), ((), ())), preferred_element_type=jnp.float32)
-
-
 def dot_nn(a, b):
     return lax.dot_general(a, b, (((1,), (0,)), ((), ())), preferred_element_type=jnp.float32)
 
@@ -35,10 +31,17 @@
 
 
 def softmax_sums(scores, values):
-    top = jnp.max(functools.reduce(jnp.maximum, scores), axis=1, keepdims=True)
-    weights = [jnp.exp2((s - top) * TO_LOG2).astype(jnp.bfloat16) for s in scores]
-    sums = dot_nn(jnp.concatenate(weights, axis=1), with_ones(jnp.concatenate(values, axis=0)))
-    return top * TO_LOG2, sums[:, :HEAD], sums[:, HEAD:]
+    tops = [jnp.max(functools.reduce(jnp.maximum, tiles), axis=1, keepdims=True) for tiles in scores]
+    weights = [
+        jnp.concatenate(
+            [jnp.exp2((s - top) * TO_LOG2).astype(jnp.bfloat16) for s in tiles], axis=1
+        )
+        for tiles, top in zip(scores, tops)
+    ]
+    sums = [
+        dot_nn(w, with_ones(jnp.concatenate(tiles, axis=0))) for w, tiles in zip(weights, values)
+    ]
+    return [top * TO_LOG2 for top in tops], [x[:, :HEAD] for x in sums], [x[:, HEAD:] for x in sums]
 
 
 def edge_kernel(place, q_ref, near_ref, far_ref, out_ref, *, heads, cols_tile, cols):
@@ -48,20 +51,23 @@
     def _():
         bias = jnp.where(group_gap(tokens, cols_tile) == 0, 0.0, NEG)
         lane = lax.broadcasted_iota(jnp.int32, (tokens, HEAD), 1)
+        cuts = [slice(n * HEAD, (n + 1) * HEAD) for n in range(heads)]
+        tiles = (near_ref, far_ref)
+        scores = [[dot_nn(q_ref[:, c], t[0, :, c]) + bias for t in tiles] for c in cuts]
+        values = [[t[1, :, c] for t in tiles] for c in cuts]
+        tops, totals, weights = softmax_sums(scores, values)
         stats = jnp.zeros((tokens, HEAD), jnp.float32)
         for n in range(heads):
-            cut = slice(n * HEAD, (n + 1) * HEAD)
-            q = q_ref[:, cut]
-            scores = [dot_nt(q, t[0, :, cut]) + bias for t in (near_ref, far_ref)]
-            top, total, weight = softmax_sums(scores, [near_ref[1, :, cut], far_ref[1, :, cut]])
-            out_ref[:, cut] = (total / weight).astype(jnp.bfloat16)
-            lse = top + jnp.log2(weight)
+            lse = tops[n] + jnp.log2(weights[n])
             high = lse.astype(jnp.bfloat16).astype(jnp.float32)
             mid = (lse - high).astype(jnp.bfloat16).astype(jnp.float32)
             low = lse - high - mid
             stats = jnp.where(lane == 3 * n, high, stats)
             stats = jnp.where(lane == 3 * n + 1, mid, stats)
             stats = jnp.where(lane == 3 * n + 2, low, stats)
+        out_ref[:, :heads * HEAD] = jnp.concatenate(
+            [(t / w).astype(jnp.bfloat16) for t, w in zip(totals, weights)], axis=1
+        )
         out_ref[:, heads * HEAD:] = stats.astype(jnp.bfloat16)
 
 
@@ -92,30 +98,37 @@
     first_head = (half + (1 - 2 * half) * (1 - place[0])) * heads * pl.num_programs(0)
     lane = lax.broadcasted_iota(jnp.int32, (tokens, HEAD), 1)
     stats = stats_ref[...].astype(jnp.float32)
+    cuts = [slice(n * HEAD, (n + 1) * HEAD) for n in range(heads)]
+    raw = []
+    for c in cuts:
+        scores = dot_nn(q_ref[:, c], jnp.concatenate([t[0, :, c] for t in tiles], axis=1))
+        raw.append([scores[:, t * tokens:(t + 1) * tokens] for t in range(10)])
+    values = [[t[1, :, c] for t in tiles] for c in cuts]
+    window, row_scores = [], []
+    row_bias = bias_ref[none + 1]
+    outer_bias = bias_ref[jnp.where(inner, none + 1, none)]
+    for n in range(heads):
+        limit = reach[first_head + step * heads + n]
+        window.append(
+            [raw[n][t] + bias_ref[jnp.where(listed[t], limit, none)] for t in range(9)]
+        )
+        row_scores.append(
+            [raw[n][3] + row_bias, raw[n][4] + row_bias, raw[n][5] + outer_bias, raw[n][9] + outer_bias]
+        )
+    _, window_totals, window_weights = softmax_sums(window, [v[:9] for v in values])
+    tops, totals, weights = softmax_sums(row_scores, [v[3:6] + v[9:] for v in values])
     results = []
-    for n in range(heads):
-        cut = slice(n * HEAD, (n + 1) * HEAD)
+    for n, c in enumerate(cuts):
         head = step * heads + n
-        limit = reach[first_head + head]
-        q = q_ref[:, cut]
-        scores = dot_nt(q, jnp.concatenate([t[0, :, cut] for t in tiles], axis=0))
-        raw = [scores[:, t * tokens:(t + 1) * tokens] for t in range(10)]
-        values = [t[1, :, cut] for t in tiles]
-        window = [raw[t] + bias_ref[jnp.where(listed[t], limit, none)] for t in range(9)]
-        _, window_total, window_weight = softmax_sums(window, values[:9])
-        row_bias = bias_ref[none + 1]
-        outer_bias = bias_ref[jnp.where(inner, none + 1, none)]
-        row_scores = [raw[3] + row_bias, raw[4] + row_bias, raw[5] + outer_bias, raw[9] + outer_bias]
-        row_top, row_total, row_weight = softmax_sums(row_scores, values[3:6] + values[9:])
         mine = (lane >= 3 * head) & (lane < 3 * head + 3)
         lse = jnp.sum(jnp.where(mine, stats, 0.0), axis=1, keepdims=True)
         lse = jnp.where(inner, NEG, lse)
-        both = jnp.maximum(row_top, lse)
-        here = jnp.exp2(row_top - both)
+        both = jnp.maximum(tops[n], lse)
+        here = jnp.exp2(tops[n] - both)
         there = jnp.exp2(lse - both)
-        whole = here * row_weight + there
-        axial = (row_total * here + remote_ref[:, cut].astype(jnp.float32) * there) / whole
-        results.append((window_total / window_weight + axial).astype(jnp.bfloat16))
+        whole = here * weights[n] + there
+        axial = (totals[n] * here + remote_ref[:, c].astype(jnp.float32) * there) / whole
+        results.append((window_totals[n] / window_weights[n] + axial).astype(jnp.bfloat16))
     return jnp.concatenate(results, axis=1)
 
 
@@ -170,6 +183,10 @@
         out_ref[...] = total_ref[...].astype(jnp.bfloat16)
 
 
+def hbm(*values):
+    return [pltpu.with_memory_space_constraint(v, pltpu.HBM) for v in values]
+
+
 def params():
     return pltpu.CompilerParams(vmem_limit_bytes=VMEM_LIMIT)
 
@@ -180,50 +197,97 @@
 
 def pack(place, keys, values, half, *earlier):
     S, tokens, width = keys.shape
-    spec = pl.BlockSpec((None, tokens, width // 2), lambda s, p: (s, 0, side(half, p)))
+    width //= 2
 
     def kernel(place, k_ref, v_ref, *refs):
-        refs[-1][0] = k_ref[...]
-        refs[-1][1] = v_ref[...]
+        out_ref, rows, turned, sems = refs[-4:]
+        start = pl.multiple_of(side(half, place) * width, HEAD)
+        loads, moves = [], []
+        for s in range(S):
+            loads.append(
+                pltpu.make_async_copy(k_ref.at[s, :, pl.ds(start, width)], rows.at[s], sems.at[0, s])
+            )
+            moves.append(
+                pltpu.make_async_copy(
+                    v_ref.at[s, :, pl.ds(start, width)], out_ref.at[s, 1], sems.at[1, s]
+                )
+            )
+            moves.append(pltpu.make_async_copy(turned.at[s], out_ref.at[s, 0], sems.at[2, s]))
+        for s in range(S):
+            loads[s].start()
+            moves[2 * s].start()
+        for s in range(S):
+            loads[s].wait()
+            for n in range(width // HEAD):
+                cut = slice(n * HEAD, (n + 1) * HEAD)
+                turned[s, :, cut] = rows[s, :, cut].T
+            moves[2 * s + 1].start()
+        for move in moves:
+            move.wait()
 
     return pl.pallas_call(
         kernel,
-        out_shape=jax.ShapeDtypeStruct((S, 2, tokens, width // 2), keys.dtype),
-        grid_spec=pltpu.PrefetchScalarGridSpec(
-            num_scalar_prefetch=1,
-            grid=(S,),
-            in_specs=[spec, spec, *[ANY] * len(earlier)],
-            out_specs=pl.BlockSpec((None, 2, tokens, width // 2), lambda s, p: (s, 0, 0, 0)),
-        ),
+        out_shape=jax.ShapeDtypeStruct((S, 2, tokens, width), keys.dtype),
+        in_specs=[SMEM, ANY, ANY, *[ANY] * len(earlier)],
+        out_specs=ANY,
+        scratch_shapes=[
+            pltpu.VMEM((S, tokens, width), keys.dtype),
+            pltpu.VMEM((S, tokens, width), keys.dtype),
+            pltpu.SemaphoreType.DMA((3, S)),
+        ],
+        compiler_params=params(),
+        cost_estimate=pl.CostEstimate(
+            flops=0, bytes_accessed=8 * S * tokens * width, transcendentals=0
+        ),
+        name="pack",
+    )(place, *hbm(keys, values), *earlier)
+
+
+def pick(place, value, half):
+    S, tokens, width = value.shape
+    width //= 2
+
+    def kernel(place, in_ref, out_ref, sem):
+        start = pl.multiple_of(side(half, place) * width, HEAD)
+        move = pltpu.make_async_copy(in_ref.at[:, :, pl.ds(start, width)], out_ref, sem)
+        move.start()
+        move.wait()
+
+    return pl.pallas_call(
+        kernel,
+        out_shape=jax.ShapeDtypeStruct((S, tokens, width), value.dtype),
+        in_specs=[SMEM, ANY],
+        out_specs=ANY,
+        scratch_shapes=[pltpu.SemaphoreType.DMA],
         compiler_params=params(),
         cost_estimate=pl.CostEstimate(
             flops=0, bytes_accessed=4 * S * tokens * width, transcendentals=0
         ),
-        name="pack",
-    )(place, keys, values, *earlier)
-
-
-def edge_attend(place, q, near, far, half, stream, cols_tile, cols):
-    tokens, width = far.shape[1:]
+        name="pick",
+    )(place, *hbm(value))
+
+
+def edge_attend(place, q, near, far, start, cols_tile, cols):
+    count, _, tokens, width = far.shape
     heads = width // HEAD
     return pl.pallas_call(
         functools.partial(edge_kernel, heads=heads, cols_tile=cols_tile, cols=cols),
-        out_shape=jax.ShapeDtypeStruct((tokens, width + HEAD), jnp.bfloat16),
+        out_shape=jax.ShapeDtypeStruct((count, tokens, width + HEAD), jnp.bfloat16),
         grid_spec=pltpu.PrefetchScalarGridSpec(
             num_scalar_prefetch=1,
-            grid=(1,),
+            grid=(count,),
             in_specs=[
-                pl.BlockSpec((None, tokens, width), lambda g, p: (stream, 0, side(half, p))),
-                pl.BlockSpec((None, 2, tokens, width), lambda g, p: (stream, 0, 0, 0)),
-                pl.BlockSpec((2, tokens, width), lambda g, p: (0, 0, 0)),
+                pl.BlockSpec((None, tokens, width), lambda g, p: (start + g, 0, 0)),
+                pl.BlockSpec((None, 2, tokens, width), lambda g, p: (start + g, 0, 0, 0)),
+                pl.BlockSpec((None, 2, tokens, width), lambda g, p: (g, 0, 0, 0)),
             ],
-            out_specs=pl.BlockSpec((tokens, width + HEAD), lambda g, p: (0, 0)),
+            out_specs=pl.BlockSpec((None, tokens, width + HEAD), lambda g, p: (g, 0, 0)),
         ),
         compiler_params=params(),
         cost_estimate=pl.CostEstimate(
-            flops=8 * tokens * tokens * width,
-            bytes_accessed=14 * tokens * width,
-            transcendentals=2 * tokens * tokens * heads,
+            flops=8 * count * tokens * tokens * width,
+            bytes_accessed=14 * count * tokens * width,
+            transcendentals=2 * count * tokens * tokens * heads,
         ),
         name="edge_rows",
     )(place, q, near, far)
@@ -231,7 +295,8 @@
 
 def main_attend(place, mask, reach, q, tiles, far, remote, half, stream, cols_tile, frame_tokens, grid,
                 project=None, block=3):
-    tokens, width = far.shape[1:]
+    tokens, width = far.shape[2:]
+    at = stream if far.shape[0] > 1 else 0
     heads = width // HEAD
     lanes = block * HEAD
     steps = heads // block
@@ -240,12 +305,13 @@
         SMEM,
         SMEM,
         pl.BlockSpec((None, tokens, lanes), lambda g, p: (stream, 0, side(half, p) * steps + g)),
-        *[pl.BlockSpec((None, 2, tokens, lanes), lambda g, p: (stream, 0, 0, g))] * 9,
-        pl.BlockSpec((2, tokens, lanes), lambda g, p: (0, 0, g)),
-        pl.BlockSpec((tokens, lanes), lambda g, p: (0, g)),
-        pl.BlockSpec((tokens, HEAD), lambda g, p: (0, heads)),
+        *[pl.BlockSpec((None, None, 2, tokens, lanes), lambda g, p: (1 - p[1] % 2, stream, 0, 0, g))] * 3,
+        *[pl.BlockSpec((None, 2, tokens, lanes), lambda g, p: (stream, 0, 0, g))] * 6,
+        pl.BlockSpec((None, 2, tokens, lanes), lambda g, p: (at, 0, 0, g)),
+        pl.BlockSpec((None, tokens, lanes), lambda g, p: (at, 0, g)),
+        pl.BlockSpec((None, tokens, HEAD), lambda g, p: (at, 0, heads)),
     ]
-    args = [place, mask, reach, q, *tiles, far, remote, remote]
+    args = [place, mask, reach, *hbm(q), *tiles, far, remote, remote]
     scratch = [pltpu.VMEM((tokens // frame_tokens + 2, tokens, tokens), jnp.float32)]
     flops, moved = 46 * tokens * tokens * width, 46 * tokens * width
     exps = 13 * tokens * tokens * heads
@@ -333,28 +399,83 @@
     q, k, v = [a.reshape(S, tokens, width) for a in (queries, key_states, value_states)]
     mask = tile_mask.reshape(9)
 
-    output, near = None, None
-    others = []
-    for h in range(2):
-        own = pack(place, k, v, h, *([] if h == 0 else [near]))
-        near = lax.ppermute(own, "col", swaps(cols, 0))
-        other = lax.ppermute(own, "col", swaps(cols, 1))
-        if h == 0:
-            edge_q = lax.ppermute(q, "col", inward)
-        strip = (own, near, other)
-        above = [lax.ppermute(x, "row", swaps(rows, 0)) for x in strip]
-        below = [lax.ppermute(x, "row", swaps(rows, 1)) for x in strip]
-        tiles = above + list(strip) + below
-        for s in range(S):
-            far = lax.ppermute(near[s], "col", swaps(cols, 1))
-            partial = edge_attend(place, edge_q, other, far, h, s, C, cols)
-            remote = lax.ppermute(partial, "col", outward)
-            args = (place, mask, frame_reach, q, tiles, far, remote, h, s, C, R * C, (rows, cols))
-            if h == 0:
-                theirs = lax.ppermute(main_attend(*args), "pair", swaps(2, 0))
-                others.append(lax.ppermute(product(theirs, out_weight, s), "pair", swaps(2, 0)))
-            else:
-                output = main_attend(*args, project=(out_weight, others[s], output))
+    sent = {}
+
+    def tied(value, after):
+        return lax.optimization_barrier((value, *[sent[n] for n in after]))[0] if after else value
+
+    def send(name, value, axis, pairs, *after):
+        sent[name] = lax.ppermute(tied(value, after), axis, pairs)
+
+    col_pairs, col_others = swaps(cols, 0), swaps(cols, 1)
+    row_pairs, row_others = swaps(rows, 0), swaps(rows, 1)
+    own = [pack(place, k, v, h) for h in range(2)]
+    picked = [pick(place, q, h) for h in range(2)]
+
+    def gather(name, value, *after):
+        groups = [[i, i + 1] for i in range(0, rows, 2)]
+        sent[name] = lax.all_gather(tied(value, after), "row", axis_index_groups=groups)
+
+    def edge(h, start, name, *after):
+        sent[f"part{name}"] = edge_attend(
+            place, tied(sent[f"q{h}"], after), sent[f"other{h}"], sent[f"far{name}"], start, C, cols
+        )
+
+    def main(h, s, name, *after, project=None):
+        tiles = [
+            *[sent[f"pair_{n}{h}"] for n in ("own", "near", "other")],
+            own[h],
+            sent[f"near{h}"],
+            sent[f"other{h}"],
+            *[sent[f"next_{n}{h}"] for n in ("own", "near", "other")],
+        ]
+        return main_attend(
+            place, mask, frame_reach, tied(q, after), tiles, sent[f"far{name}"], sent[f"rest{name}"],
+            h, s, C, R * C, (rows, cols), project=project,
+        )
+
+    pair_swap = swaps(2, 0)
+    send("near0", own[0], "col", col_pairs)
+    send("other0", own[0], "col", col_others)
+    send("next_own0", own[0], "row", row_others)
+    send("q0", picked[0], "col", inward)
+    gather("pair_own0", own[0])
+    second = ("near0", "other0", "next_own0")
+    send("far00", sent["near0"][:1], "col", col_others, *second)
+    send("far01", sent["near0"][1:], "col", col_others, *second)
+    send("next_near0", sent["near0"], "row", row_others, *second)
+    gather("pair_near0", sent["near0"], "pair_own0")
+    edge(0, 0, "00")
+    send("rest00", sent["part00"], "col", outward)
+    send("near1", own[1], "col", col_pairs, "rest00")
+    send("next_other0", sent["other0"], "row", row_others, "next_near0", "q0")
+    send("other1", own[1], "col", col_others, "next_near0")
+    gather("pair_other0", sent["other0"], "pair_near0")
+    edge(0, 1, "01")
+    send("rest01", sent["part01"], "col", outward)
+    send("next_own1", own[1], "row", row_others, "next_other0", "far01")
+    sent["rows0"] = main(0, 0, "00")
+    send("theirs0", sent["rows0"], "pair", pair_swap)
+    sent["product0"] = product(sent["theirs0"], out_weight, 0)
+    send("back0", sent["product0"], "pair", pair_swap)
+    gather("pair_own1", own[1], "pair_other0")
+    send("q1", picked[1], "col", inward, "rest00")
+    send("far10", sent["near1"][:1], "col", col_others, "next_own1")
+    send("next_near1", sent["near1"], "row", row_others, "next_own1", "q1")
+    sent["rows1"] = main(0, 1, "01", "rows0")
+    send("theirs1", sent["rows1"], "pair", pair_swap)
+    sent["product1"] = product(sent["theirs1"], out_weight, 1)
+    send("back1", sent["product1"], "pair", pair_swap)
+    send("far11", sent["near1"][1:], "col", col_others, "other1")
+    gather("pair_near1", sent["near1"], "pair_own1")
+    send("next_other1", sent["other1"], "row", row_others)
+    gather("pair_other1", sent["other1"], "pair_near1")
+    edge(1, 0, "10")
+    send("rest10", sent["part10"], "col", outward)
+    edge(1, 1, "11")
+    send("rest11", sent["part11"], "col", outward)
+    output = main(1, 0, "10", project=(out_weight, sent["back0"], None))
+    output = main(1, 1, "11", project=(out_weight, sent["back1"], output))
     return output.reshape(S, F, R, C, model)
 
 

time: 194 us -> 349 us (1.80)
  the two profiles are of different devices: /device:TPU:19 before, /device:TPU:0 now
where the time goes in v3:
time: 349 us; the launch traced here: 345 us
  waiting for transfers between devices  108 us (31%)
  Pallas kernels  99.7 us (29%)
  starting transfers between devices  86.5 us (25%)
  local copies, waits for them, and re-layouts  37.2 us (11%)
  between operations  14.1 us (4%)
    ppermute x24, waiting for transfers between devices, send(): sent[name] = lax.ppermute(tied(value, after), axis, pairs)  91.4 us
    ppermute x24, starting transfers between devices, send(): sent[name] = lax.ppermute(tied(value, after), axis, pairs)  86.3 us
    pallas_call x2, Pallas kernels, pack(): pl.pallas_call(kernel, out_shape=jax.ShapeDtypeStruct((S, 2, tokens, widt...  39.1 us
    unnamed x92, local copies, waits for them, and re-layouts  36.2 us
    pallas_call x2, Pallas kernels, pick(): pl.pallas_call(kernel, out_shape=jax.ShapeDtypeStruct((S, tokens, width),...  21.3 us
    pallas_call x2, Pallas kernels, main_attend(): pl.pallas_call(functools.partial(second_kernel, **sizes), out_shape=jax.S...  16.9 us
    all_gather x6, waiting for transfers between devices, gather(): lax.all_gather(tied(value, after), 'row', axis_index_groups=groups)  16.2 us
    pallas_call x2, Pallas kernels, main_attend(): pl.pallas_call(functools.partial(first_kernel, **sizes), out_shape=jax.Sh...  12.2 us
  transfers between devices with their start and end apart: 30, of which 7 were waited for; matrix products, arithmetic and copies ran while one was open for 0% of the time, Pallas kernels for 21%

profile of v3, /device:TPU:0, one launch (start us, length us, event | category | flops | bytes accessed | tf_op | source)
XLA Modules:
  0.0 345.2 jit_solution(17789732069234412447)
XLA Ops:
  6.6 19.6 %pack.3.refs_3_ = bf16[2,2,128,1152]{3,2,1,0:T(8,128)(2,1)} custom-call(s32[3]{0:T(128)S(1)} %pad_add_fusion.place, bf16[2,128,2304]{2,1,0:T(8,128)(2,1)} %bitcast.38, bf16[2,128,2304]{2,1,0:T(8,128)(2,1)} %bitcast.40), custom_call_target="tpu_custom_call" | custom-call | bytes 2359296 | tf_op jit(solution)/shard_map/pack/pallas_call | solution.py:228
  26.3 3.1 collective-permute-start.1
  29.4 26.2 %collective-permute-done.1.refs_4_ = bf16[2,2,128,1152]{3,2,1,0:T(8,128)(2,1)S(1)} collective-permute-done((bf16[2,2,128,1152]{3,2,1,0:T(8,128)(2,1)}, bf16[2,2,128,1152]{3,2,1,0:T(8,128)(2,1)S(1)}, u32[]{:S(2)}, u32[]{:S(2)}) %collective-permute-start.1) | collective-permute-done | bytes 1179680 | tf_op jit(solution)/shard_map/ppermute | solution.py:408
  57.4 11.7 %all-gather.15.cloned.1.call-done = bf16[4,2,128,1152]{3,2,1,0:T(8,128)(2,1)} async-done(((bf16[2,2,128,1152]{3,2,1,0:T(8,128)(2,1)}), bf16[4,2,128,1152]{3,2,1,0:T(8,128)(2,1)}) %all-gather.15.cloned.1.call-update) | async-done | bytes 2359312 | tf_op jit(solution)/shard_map/all_gather | solution.py:417
  69.9 19.5 %pick.2 = bf16[2,128,1152]{2,1,0:T(8,128)(2,1)} custom-call(s32[3]{0:T(128)S(1)} %pad_add_fusion.place, bf16[2,128,2304]{2,1,0:T(8,128)(2,1)} %bitcast.32), custom_call_target="tpu_custom_call" | custom-call | bytes 1179648 | tf_op jit(solution)/shard_map/pick/pallas_call | solution.py:256
  89.5 21.9 %collective-permute-start.2 = (bf16[2,128,1152]{2,1,0:T(8,128)(2,1)}, bf16[2,128,1152]{2,1,0:T(8,128)(2,1)}, u32[]{:S(2)}, u32[]{:S(2)}) collective-permute-start(bf16[2,128,1152]{2,1,0:T(8,128)(2,1)} %pick.2), channel_id=1, source_target_pairs={{0,1},{3,2},{4,5},{7,6},{8,9},{11,10},{12,13},{15,14},{16,17},{19,... | collective-permute-start | bytes 1769480 | tf_op jit(solution)/shard_map/ppermute | solution.py:408
  111.4 19.6 %pack.2.refs_3_ = bf16[2,2,128,1152]{3,2,1,0:T(8,128)(2,1)} custom-call(s32[3]{0:T(128)S(1)} %pad_add_fusion.place, bf16[2,128,2304]{2,1,0:T(8,128)(2,1)} %bitcast.39, bf16[2,128,2304]{2,1,0:T(8,128)(2,1)} %bitcast.41), custom_call_target="tpu_custom_call" | custom-call | bytes 2359296 | tf_op jit(solution)/shard_map/pack/pallas_call | solution.py:228
  133.9 1.5 edge_rows.4
  136.7 22.3 %collective-permute-done.5.refs_10_.refs_11_ = bf16[1,128,1280]{2,1,0:T(8,128)(2,1)S(1)} collective-permute-done((bf16[1,128,1280]{2,1,0:T(8,128)(2,1)S(1)}, bf16[1,128,1280]{2,1,0:T(8,128)(2,1)S(1)}, u32[]{:S(2)}, u32[]{:S(2)}) %collective-permute-start.5) | collective-permute-done | bytes 327712 | tf_op jit(solution)/shard_map/ppermute | solution.py:408
  159.7 1.7 collective-permute-start.7
  161.5 27.2 %collective-permute-done.6.refs_4_ = bf16[2,2,128,1152]{3,2,1,0:T(8,128)(2,1)S(1)} collective-permute-done((bf16[2,2,128,1152]{3,2,1,0:T(8,128)(2,1)}, bf16[2,2,128,1152]{3,2,1,0:T(8,128)(2,1)S(1)}, u32[]{:S(2)}, u32[]{:S(2)}) %collective-permute-start.6) | collective-permute-done | bytes 1179680 | tf_op jit(solution)/shard_map/ppermute | solution.py:408
  193.8 1.7 collective-permute-start.11
  195.5 4.5 %all-gather.21.cloned.1.call-done = bf16[4,2,128,1152]{3,2,1,0:T(8,128)(2,1)} async-done(((bf16[2,2,128,1152]{3,2,1,0:T(8,128)(2,1)}), bf16[4,2,128,1152]{3,2,1,0:T(8,128)(2,1)}) %all-gather.21.cloned.1.call-update) | async-done | bytes 2359312 | tf_op jit(solution)/shard_map/all_gather | solution.py:417
  200.0 1.8 pick.3
  202.9 1.6 edge_rows.6
  205.8 41.0 %collective-permute-start.12 = (bf16[2,128,1152]{2,1,0:T(8,128)(2,1)S(1)}, bf16[2,128,1152]{2,1,0:T(8,128)(2,1)S(1)}, u32[]{:S(2)}, u32[]{:S(2)}) collective-permute-start(bf16[2,128,1152]{2,1,0:T(8,128)(2,1)S(1)} %pick.3), channel_id=1, source_target_pairs={{0,1},{3,2},{4,5},{7,6},{8,9},{11,10},{12,13},{15,14},{16,17},{19,... | collective-permute-start | bytes 1769480 | tf_op jit(solution)/shard_map/ppermute | solution.py:408
  247.6 1.7 copy-done.12
  249.3 1.7 copy-done.14
  253.5 6.5 %first_rows.2 = bf16[128,1152]{1,0:T(8,128)(2,1)S(1)} custom-call(s32[3]{0:T(128)S(1)} %pad_add_fusion.place, s32[9]{0:T(128)S(1)} %bitcast.28, s32[18]{0:T(128)S(1)} %copy-done.41, bf16[2,128,2304]{2,1,0:T(8,128)(2,1)} %bitcast.34, bf16[2,2,2,128,1152]{4,3,2,1,0:T(8,128)(2,1)S(1)} %bitcast.16, bf16[2,2,2,128,1152]{4,3,2,1,0:T(8,128)(2,1)S(1)} %bitcast.18, ...), custom_call_target="tpu_custom_call" | custom-call | flops 868220928 | bytes 6782976 | tf_op jit(solution)/shard_map/first_rows/pallas_call | solution.py:319
  260.0 1.6 collective-permute-start.22
  263.3 5.8 %first_rows.3 = bf16[128,1152]{1,0:T(8,128)(2,1)S(1)} custom-call(s32[3]{0:T(128)S(1)} %pad_add_fusion.place, s32[9]{0:T(128)S(1)} %bitcast.29, s32[18]{0:T(128)S(1)} %copy-done.41, bf16[2,128,2304]{2,1,0:T(8,128)(2,1)} %bitcast.35, bf16[2,2,2,128,1152]{4,3,2,1,0:T(8,128)(2,1)S(1)} %bitcast.17, bf16[2,2,2,128,1152]{4,3,2,1,0:T(8,128)(2,1)S(1)} %bitcast.19, ...), custom_call_target="tpu_custom_call" | custom-call | flops 868220928 | bytes 6782976 | tf_op jit(solution)/shard_map/first_rows/pallas_call | solution.py:319
  270.6 2.1 product.3
  272.7 3.2 collective-permute-done.18.rows_ref
  276.6 2.9 product.2
  286.7 12.4 %collective-permute-done.21.refs_10_.refs_11_ = bf16[1,128,1280]{2,1,0:T(8,128)(2,1)S(1)} collective-permute-done((bf16[1,128,1280]{2,1,0:T(8,128)(2,1)S(1)}, bf16[1,128,1280]{2,1,0:T(8,128)(2,1)S(1)}, u32[]{:S(2)}, u32[]{:S(2)}) %collective-permute-start.21) | collective-permute-done | bytes 327712 | tf_op jit(solution)/shard_map/ppermute | solution.py:408
  301.8 5.0 %copy-done = bf16[2,1152,3072]{2,1,0:T(8,128)(2,1)S(1)} copy-done((bf16[2,1152,3072]{2,1,0:T(8,128)(2,1)S(1)}, bf16[2,1152,3072]{2,1,0:T(8,128)(2,1)}, u32[]{:S(2)}) %copy-start) | copy-done | bytes 14155800
  306.9 1.7 copy-done.15
  308.5 1.7 copy-done.16
  310.2 1.7 copy-done.17
  316.5 8.2 %second_rows.2.refs_14_ = bf16[2,128,3072]{2,1,0:T(8,128)(2,1)} custom-call(s32[3]{0:T(128)S(1)} %pad_add_fusion.place, s32[9]{0:T(128)S(1)} %bitcast.30, s32[18]{0:T(128)S(1)} %copy-done.41, bf16[2,128,2304]{2,1,0:T(8,128)(2,1)} %bitcast.36, bf16[2,2,2,128,1152]{4,3,2,1,0:T(8,128)(2,1)S(1)} %bitcast.22, bf16[2,2,2,128,1152]{4,3,2,1,0:T(8,128)(2,1)S(1)} %bitcast.24, ...), custom_call_target="tpu_custom_call" | custom-call | flops 1774190592 | bytes 13860864 | tf_op jit(solution)/shard_map/second_rows/pallas_call | solution.py:338
  324.8 5.0 %copy-done.1 = bf16[2,1152,3072]{2,1,0:T(8,128)(2,1)S(1)} copy-done((bf16[2,1152,3072]{2,1,0:T(8,128)(2,1)S(1)}, bf16[2,1152,3072]{2,1,0:T(8,128)(2,1)}, u32[]{:S(2)}) %copy-start.1) | copy-done | bytes 14155800
  329.8 8.6 %second_rows.3 = bf16[2,128,3072]{2,1,0:T(8,128)(2,1)} custom-call(s32[3]{0:T(128)S(1)} %pad_add_fusion.place, s32[9]{0:T(128)S(1)} %bitcast.31, s32[18]{0:T(128)S(1)} %copy-done.41, bf16[2,128,2304]{2,1,0:T(8,128)(2,1)} %bitcast.37, bf16[2,2,2,128,1152]{4,3,2,1,0:T(8,128)(2,1)S(1)} %bitcast.23, ...), custom_call_target="tpu_custom_call", output_to_operand_aliasing={{}: (18, {})} | custom-call | flops 1774190592 | bytes 13860864 | tf_op jit(solution)/shard_map/second_rows/pallas_call | solution.py:338
  (144 shorter events, 36.7 us)
Async XLA Ops:
  6.5 49.0 %all-gather.13.cloned.1.call-start = ((), (), s32[]{:S(2)}) async-start(), calls=%async_computation | async-start | bytes 3538944 | tf_op jit(solution)/shard_map/all_gather | solution.py:417
  26.2 42.9 %all-gather.15.cloned.1.call-start = ((), (), s32[]{:S(2)}) async-start(), calls=%async_computation.1 | async-start | bytes 3538944 | tf_op jit(solution)/shard_map/all_gather | solution.py:417
  26.3 29.3 %collective-permute-start.1 = (bf16[2,2,128,1152]{3,2,1,0:T(8,128)(2,1)}, bf16[2,2,128,1152]{3,2,1,0:T(8,128)(2,1)S(1)}, u32[]{:S(2)}, u32[]{:S(2)}) collective-permute-start(bf16[2,2,128,1152]{3,2,1,0:T(8,128)(2,1)} %pack.3.refs_3_), channel_id=1, source_target_pairs={{0,1},{2,3},{1,0},{3,2},{4,5},{6,7},{5,4},{7,6},{8,9},{10,11},{9,8... | collective-permute-start | bytes 3538952 | tf_op jit(solution)/shard_map/ppermute | solution.py:408
  56.6 74.4 %all-gather.17.cloned.1.call-start = ((), (), s32[]{:S(2)}) async-start(), calls=%async_computation.2 | async-start | bytes 3538944 | tf_op jit(solution)/shard_map/all_gather | solution.py:417
  56.6 0.7 collective-permute-start
  69.1 119.5 %all-gather.19.cloned.1.call-start = ((), (), s32[]{:S(2)}) async-start(), calls=%async_computation.3 | async-start | bytes 3538944 | tf_op jit(solution)/shard_map/all_gather | solution.py:417
  69.2 64.0 %collective-permute-start.3 = (bf16[2,2,128,1152]{3,2,1,0:T(8,128)(2,1)}, bf16[2,2,128,1152]{3,2,1,0:T(8,128)(2,1)S(1)}, u32[]{:S(2)}, u32[]{:S(2)}) collective-permute-start(bf16[2,2,128,1152]{3,2,1,0:T(8,128)(2,1)} %pack.3.refs_3_), channel_id=1, source_target_pairs={{4,8},{8,4},{5,9},{9,5},{6,10},{10,6},{7,11},{11,7},{20,24},{24,20... | collective-permute-start | bytes 3538952 | tf_op jit(solution)/shard_map/ppermute | solution.py:408
  89.5 44.4 %collective-permute-start.2 = (bf16[2,128,1152]{2,1,0:T(8,128)(2,1)}, bf16[2,128,1152]{2,1,0:T(8,128)(2,1)}, u32[]{:S(2)}, u32[]{:S(2)}) collective-permute-start(bf16[2,128,1152]{2,1,0:T(8,128)(2,1)} %pick.2), channel_id=1, source_target_pairs={{0,1},{3,2},{4,5},{7,6},{8,9},{11,10},{12,13},{15,14},{16,17},{19,... | collective-permute-start | bytes 1769480 | tf_op jit(solution)/shard_map/ppermute | solution.py:408
  131.0 69.0 %all-gather.21.cloned.1.call-start = ((), (), s32[]{:S(2)}) async-start(), calls=%async_computation.4 | async-start | bytes 3538944 | tf_op jit(solution)/shard_map/all_gather | solution.py:417
  133.2 0.7 collective-permute-start.4
  135.4 23.6 %collective-permute-start.5 = (bf16[1,128,1280]{2,1,0:T(8,128)(2,1)S(1)}, bf16[1,128,1280]{2,1,0:T(8,128)(2,1)S(1)}, u32[]{:S(2)}, u32[]{:S(2)}) collective-permute-start(bf16[1,128,1280]{2,1,0:T(8,128)(2,1)S(1)} %edge_rows.4), channel_id=1, source_target_pairs={{1,0},{2,3},{5,4},{6,7},{9,8},{10,11},{13,12},{14,15},{17,16},{18,... | collective-permute-start | bytes 983048 | tf_op jit(solution)/shard_map/ppermute | solution.py:408
  159.7 28.9 %collective-permute-start.6 = (bf16[2,2,128,1152]{3,2,1,0:T(8,128)(2,1)}, bf16[2,2,128,1152]{3,2,1,0:T(8,128)(2,1)S(1)}, u32[]{:S(2)}, u32[]{:S(2)}) collective-permute-start(bf16[2,2,128,1152]{3,2,1,0:T(8,128)(2,1)} %pack.2.refs_3_), channel_id=1, source_target_pairs={{0,1},{2,3},{1,0},{3,2},{4,5},{6,7},{5,4},{7,6},{8,9},{10,11},{9,8... | collective-permute-start | bytes 3538952 | tf_op jit(solution)/shard_map/ppermute | solution.py:408
  159.7 30.0 %collective-permute-start.7 = (bf16[2,2,128,1152]{3,2,1,0:T(8,128)(2,1)S(1)}, bf16[2,2,128,1152]{3,2,1,0:T(8,128)(2,1)}, u32[]{:S(2)}, u32[]{:S(2)}) collective-permute-start(bf16[2,2,128,1152]{3,2,1,0:T(8,128)(2,1)S(1)} %copy-done.7), channel_id=1, source_target_pairs={{4,8},{8,4},{5,9},{9,5},{6,10},{10,6},{7,11},{11,7},{20,24},{24,20... | collective-permute-start | bytes 3538952 | tf_op jit(solution)/shard_map/ppermute | solution.py:408
  189.7 112.1 %all-gather.23.cloned.1.call-start = ((), (), s32[]{:S(2)}) async-start(), calls=%async_computation.5 | async-start | bytes 3538944 | tf_op jit(solution)/shard_map/all_gather | solution.py:417
  189.8 3.0 collective-permute-start.9
  190.5 5.0 %collective-permute-start.8 = (bf16[2,2,128,1152]{3,2,1,0:T(8,128)(2,1)}, bf16[2,2,128,1152]{3,2,1,0:T(8,128)(2,1)S(1)}, u32[]{:S(2)}, u32[]{:S(2)}) collective-permute-start(bf16[2,2,128,1152]{3,2,1,0:T(8,128)(2,1)} %pack.2.refs_3_), channel_id=1, source_target_pairs={{1,2},{2,1},{5,6},{6,5},{9,10},{10,9},{13,14},{14,13},{17,18},{18,... | collective-permute-start | bytes 3538952 | tf_op jit(solution)/shard_map/ppermute | solution.py:408
  191.3 0.7 collective-permute-start.10
  193.8 67.9 %collective-permute-start.11 = (bf16[2,2,128,1152]{3,2,1,0:T(8,128)(2,1)}, bf16[2,2,128,1152]{3,2,1,0:T(8,128)(2,1)}, u32[]{:S(2)}, u32[]{:S(2)}) collective-permute-start(bf16[2,2,128,1152]{3,2,1,0:T(8,128)(2,1)} %pack.2.refs_3_), channel_id=1, source_target_pairs={{4,8},{8,4},{5,9},{9,5},{6,10},{10,6},{7,11},{11,7},{20,24},{24,20... | collective-permute-start | bytes 3538952 | tf_op jit(solution)/shard_map/ppermute | solution.py:408
  200.0 47.5 %copy-start.11 = (bf16[4,2,128,1152]{3,2,1,0:T(8,128)(2,1)S(1)}, bf16[4,2,128,1152]{3,2,1,0:T(8,128)(2,1)}, u32[]{:S(2)}) copy-start(bf16[4,2,128,1152]{3,2,1,0:T(8,128)(2,1)} %all-gather.13.cloned.1.call-done) | copy-start | bytes 7077892
  202.9 44.7 %copy-start.41 = (s32[18]{0:T(128)S(1)}, s32[18]{0:T(128)}, u32[]{:S(2)}) copy-start(s32[18]{0:T(128)} %reach.7) | copy-start | bytes 220
  204.5 58.8 %collective-permute-start.17 = (bf16[1,128,1280]{2,1,0:T(8,128)(2,1)S(1)}, bf16[1,128,1280]{2,1,0:T(8,128)(2,1)S(1)}, u32[]{:S(2)}, u32[]{:S(2)}) collective-permute-start(bf16[1,128,1280]{2,1,0:T(8,128)(2,1)S(1)} %edge_rows.6), channel_id=1, source_target_pairs={{1,0},{2,3},{5,4},{6,7},{9,8},{10,11},{13,12},{14,15},{17,16},{18,... | collective-permute-start | bytes 983048 | tf_op jit(solution)/shard_map/ppermute | solution.py:408
  205.8 56.7 %collective-permute-start.12 = (bf16[2,128,1152]{2,1,0:T(8,128)(2,1)S(1)}, bf16[2,128,1152]{2,1,0:T(8,128)(2,1)S(1)}, u32[]{:S(2)}, u32[]{:S(2)}) collective-permute-start(bf16[2,128,1152]{2,1,0:T(8,128)(2,1)S(1)} %pick.3), channel_id=1, source_target_pairs={{0,1},{3,2},{4,5},{7,6},{8,9},{11,10},{12,13},{15,14},{16,17},{19,... | collective-permute-start | bytes 1769480 | tf_op jit(solution)/shard_map/ppermute | solution.py:408
  246.8 37.6 %collective-permute-start.14 = (bf16[2,2,128,1152]{3,2,1,0:T(8,128)(2,1)S(1)}, bf16[2,2,128,1152]{3,2,1,0:T(8,128)(2,1)S(1)}, u32[]{:S(2)}, u32[]{:S(2)}) collective-permute-start(bf16[2,2,128,1152]{3,2,1,0:T(8,128)(2,1)S(1)} %copy-done.5), channel_id=1, source_target_pairs={{4,8},{8,4},{5,9},{9,5},{6,10},{10,6},{7,11},{11,7},{20,24},{24,20... | collective-permute-start | bytes 3538952 | tf_op jit(solution)/shard_map/ppermute | solution.py:408
  260.0 9.8 %collective-permute-start.22 = (bf16[128,1152]{1,0:T(8,128)(2,1)S(1)}, bf16[128,1152]{1,0:T(8,128)(2,1)S(1)}, u32[]{:S(2)}, u32[]{:S(2)}) collective-permute-start(bf16[128,1152]{1,0:T(8,128)(2,1)S(1)} %first_rows.2), channel_id=1, source_target_pairs={{0,16},{16,0},{1,17},{17,1},{2,18},{18,2},{3,19},{19,3},{4,20},{20... | collective-permute-start | bytes 884744 | tf_op jit(solution)/shard_map/ppermute | solution.py:408
  261.7 17.8 %collective-permute-start.20 = (bf16[1,2,128,1152]{3,2,1,0:T(8,128)(2,1)S(1)}, bf16[1,2,128,1152]{3,2,1,0:T(8,128)(2,1)S(1)}, u32[]{:S(2)}, u32[]{:S(2)}) collective-permute-start(bf16[1,2,128,1152]{3,2,1,0:T(8,128)(2,1)S(1)} %get-tuple-element.38), channel_id=1, source_target_pairs={{1,2},{2,1},{5,6},{6,5},{9,10},{10,9},{13,14},{14,13},{17,18},{18,... | collective-permute-start | bytes 1769480 | tf_op jit(solution)/shard_map/ppermute | solution.py:408
  262.6 37.3 %collective-permute-start.13 = (bf16[2,2,128,1152]{3,2,1,0:T(8,128)(2,1)S(1)}, bf16[2,2,128,1152]{3,2,1,0:T(8,128)(2,1)S(1)}, u32[]{:S(2)}, u32[]{:S(2)}) collective-permute-start(bf16[2,2,128,1152]{3,2,1,0:T(8,128)(2,1)S(1)} %copy-done.9), channel_id=1, source_target_pairs={{4,8},{8,4},{5,9},{9,5},{6,10},{10,6},{7,11},{11,7},{20,24},{24,20... | collective-permute-start | bytes 3538952 | tf_op jit(solution)/shard_map/ppermute | solution.py:408
  269.1 6.8 %collective-permute-start.18 = (bf16[128,1152]{1,0:T(8,128)(2,1)S(1)}, bf16[128,1152]{1,0:T(8,128)(2,1)S(1)}, u32[]{:S(2)}, u32[]{:S(2)}) collective-permute-start(bf16[128,1152]{1,0:T(8,128)(2,1)S(1)} %first_rows.3), channel_id=1, source_target_pairs={{0,16},{16,0},{1,17},{17,1},{2,18},{18,2},{3,19},{19,3},{4,20},{20... | collective-permute-start | bytes 884744 | tf_op jit(solution)/shard_map/ppermute | solution.py:408
  269.8 11.6 %collective-permute-start.15 = (bf16[1,2,128,1152]{3,2,1,0:T(8,128)(2,1)S(1)}, bf16[1,2,128,1152]{3,2,1,0:T(8,128)(2,1)S(1)}, u32[]{:S(2)}, u32[]{:S(2)}) collective-permute-start(bf16[1,2,128,1152]{3,2,1,0:T(8,128)(2,1)S(1)} %get-tuple-element.36), channel_id=1, source_target_pairs={{1,2},{2,1},{5,6},{6,5},{9,10},{10,9},{13,14},{14,13},{17,18},{18,... | collective-permute-start | bytes 1769480 | tf_op jit(solution)/shard_map/ppermute | solution.py:408
  275.9 25.0 %collective-permute-start.23 = (bf16[128,3072]{1,0:T(8,128)(2,1)S(1)}, bf16[128,3072]{1,0:T(8,128)(2,1)S(1)}, u32[]{:S(2)}, u32[]{:S(2)}) collective-permute-start(bf16[128,3072]{1,0:T(8,128)(2,1)S(1)} %product.3), channel_id=1, source_target_pairs={{0,16},{16,0},{1,17},{17,1},{2,18},{18,2},{3,19},{19,3},{4,20},{20... | collective-permute-start | bytes 2359304 | tf_op jit(solution)/shard_map/ppermute | solution.py:408
  279.5 45.2 %collective-permute-start.19 = (bf16[128,3072]{1,0:T(8,128)(2,1)}, bf16[128,3072]{1,0:T(8,128)(2,1)}, u32[]{:S(2)}, u32[]{:S(2)}) collective-permute-start(bf16[128,3072]{1,0:T(8,128)(2,1)} %product.2), channel_id=1, source_target_pairs={{0,16},{16,0},{1,17},{17,1},{2,18},{18,2},{3,19},{19,3},{4,20},{20... | collective-permute-start | bytes 2359304 | tf_op jit(solution)/shard_map/ppermute | solution.py:408
  281.5 17.7 %collective-permute-start.21 = (bf16[1,128,1280]{2,1,0:T(8,128)(2,1)S(1)}, bf16[1,128,1280]{2,1,0:T(8,128)(2,1)S(1)}, u32[]{:S(2)}, u32[]{:S(2)}) collective-permute-start(bf16[1,128,1280]{2,1,0:T(8,128)(2,1)S(1)} %edge_rows.7), channel_id=1, source_target_pairs={{1,0},{2,3},{5,4},{6,7},{9,8},{10,11},{13,12},{14,15},{17,16},{18,... | collective-permute-start | bytes 983048 | tf_op jit(solution)/shard_map/ppermute | solution.py:408
  285.4 39.3 %collective-permute-start.16 = (bf16[1,128,1280]{2,1,0:T(8,128)(2,1)}, bf16[1,128,1280]{2,1,0:T(8,128)(2,1)}, u32[]{:S(2)}, u32[]{:S(2)}) collective-permute-start(bf16[1,128,1280]{2,1,0:T(8,128)(2,1)} %edge_rows.5), channel_id=1, source_target_pairs={{1,0},{2,3},{5,4},{6,7},{9,8},{10,11},{13,12},{14,15},{17,16},{18,... | collective-permute-start | bytes 983048 | tf_op jit(solution)/shard_map/ppermute | solution.py:408
  (44 other events, 370.8 us)
Sparse Core Ops, SparseCore 0:
  26.3 13.6 all-gather.12
  56.7 12.3 all-gather.14
  70.7 27.4 all-gather.16
  131.2 12.2 all-gather.18
  189.8 10.1 all-gather.20
  201.4 47.1 all-gather.22

commit v4 on v3

v4 whole, which is shorter than its diff:
```python
import functools
import math

import jax
import jax.numpy as jnp
from jax import lax
from jax.experimental import pallas as pl
from jax.experimental.pallas import tpu as pltpu
from jax.sharding import PartitionSpec as P

NEG = -1e30
VMEM_LIMIT = 24 * 1024 * 1024
HEAD = 128
TO_LOG2 = HEAD ** (-0.5) * math.log2(math.e)
ANY = pl.BlockSpec(memory_space=pl.ANY)
SMEM = pl.BlockSpec(memory_space=pltpu.SMEM)


def dot_nn(a, b):
    return lax.dot_general(a, b, (((1,), (0,)), ((), ())), preferred_element_type=jnp.float32)


def group_gap(tokens, group):
    q = lax.broadcasted_iota(jnp.int32, (tokens, tokens), 0)
    k = lax.broadcasted_iota(jnp.int32, (tokens, tokens), 1)
    return jnp.abs(q // group - k // group)


def with_ones(values):
    return jnp.concatenate([values, jnp.ones_like(values)], axis=1)


def softmax_sums(scores, values):
    tops = [jnp.max(functools.reduce(jnp.maximum, tiles), axis=1, keepdims=True) for tiles in scores]
    weights = [
        jnp.concatenate(
            [jnp.exp2((s - top) * TO_LOG2).astype(jnp.bfloat16) for s in tiles], axis=1
        )
        for tiles, top in zip(scores, tops)
    ]
    sums = [
        dot_nn(w, with_ones(jnp.concatenate(tiles, axis=0))) for w, tiles in zip(weights, values)
    ]
    return [top * TO_LOG2 for top in tops], [x[:, :HEAD] for x in sums], [x[:, HEAD:] for x in sums]


def edge_kernel(place, q_ref, near_ref, far_ref, out_ref, *, heads, cols_tile, cols):
    tokens = q_ref.shape[0]

    @pl.when((place[2] > 0) & (place[2] < cols - 1))
    def _():
        bias = jnp.where(group_gap(tokens, cols_tile) == 0, 0.0, NEG)
        lane = lax.broadcasted_iota(jnp.int32, (tokens, HEAD), 1)
        cuts = [slice(n * HEAD, (n + 1) * HEAD) for n in range(heads)]
        tiles = (near_ref, far_ref)
        scores = [[dot_nn(q_ref[:, c], t[0, :, c]) + bias for t in tiles] for c in cuts]
        values = [[t[1, :, c] for t in tiles] for c in cuts]
        tops, totals, weights = softmax_sums(scores, values)
        stats = jnp.zeros((tokens, HEAD), jnp.float32)
        for n in range(heads):
            lse = tops[n] + jnp.log2(weights[n])
            high = lse.astype(jnp.bfloat16).astype(jnp.float32)
            mid = (lse - high).astype(jnp.bfloat16).astype(jnp.float32)
            low = lse - high - mid
            stats = jnp.where(lane == 3 * n, high, stats)
            stats = jnp.where(lane == 3 * n + 1, mid, stats)
            stats = jnp.where(lane == 3 * n + 2, low, stats)
        out_ref[:, :heads * HEAD] = jnp.concatenate(
            [(t / w).astype(jnp.bfloat16) for t, w in zip(totals, weights)], axis=1
        )
        out_ref[:, heads * HEAD:] = stats.astype(jnp.bfloat16)


def fill_bias(bias_ref, frame_tokens, cols_tile):
    tokens = bias_ref.shape[1]
    frames = tokens // frame_tokens
    gap = group_gap(tokens, frame_tokens)
    for reach in range(frames):
        bias_ref[reach] = jnp.where(gap <= reach, 0.0, NEG)
    bias_ref[frames] = jnp.full((tokens, tokens), NEG, jnp.float32)
    bias_ref[frames + 1] = jnp.where(group_gap(tokens, cols_tile) == 0, 0.0, NEG)


def rows_kernel(place, mask, reach, q_ref, *refs, heads, half, grid, cols_tile, frame_tokens):
    tiles = refs[:10]
    window_ref, row_ref, sums_ref, bias_ref = refs[10:]
    tokens = q_ref.shape[0]
    none = bias_ref.shape[0] - 2
    step = pl.program_id(0)

    @pl.when(step == 0)
    def _():
        fill_bias(bias_ref, frame_tokens, cols_tile)
        sums_ref[...] = jnp.zeros_like(sums_ref)

    rows, cols = grid
    row, col = place[1], place[2]
    row_sign, col_sign = 1 - 2 * (row % 2), 1 - 2 * (col % 2)
    row_steps, col_steps = (row_sign, 0, -row_sign), (0, col_sign, -col_sign)
    listed = []
    for a in row_steps:
        for b in col_steps:
            inside = (row + a >= 0) & (row + a < rows) & (col + b >= 0) & (col + b < cols)
            listed.append(inside & ((mask[3 * (a + 1) + b + 1] > 0) | ((a == 0) & (b == 0))))
    inner = (col > 0) & (col < cols - 1)
    first_head = side(half, place) * heads * pl.num_programs(0)
    cuts = [slice(n * HEAD, (n + 1) * HEAD) for n in range(heads)]
    raw = []
    for c in cuts:
        scores = dot_nn(q_ref[:, c], jnp.concatenate([t[0, :, c] for t in tiles], axis=1))
        raw.append([scores[:, t * tokens:(t + 1) * tokens] for t in range(10)])
    values = [[t[1, :, c] for t in tiles] for c in cuts]
    window, row_scores = [], []
    row_bias = bias_ref[none + 1]
    outer_bias = bias_ref[jnp.where(inner, none + 1, none)]
    for n in range(heads):
        limit = reach[first_head + step * heads + n]
        window.append(
            [raw[n][t] + bias_ref[jnp.where(listed[t], limit, none)] for t in range(9)]
        )
        row_scores.append(
            [raw[n][3] + row_bias, raw[n][4] + row_bias, raw[n][5] + outer_bias, raw[n][9] + outer_bias]
        )
    _, totals, weights = softmax_sums(window, [v[:9] for v in values])
    window_ref[...] = jnp.concatenate([t / w for t, w in zip(totals, weights)], axis=1)
    tops, totals, weights = softmax_sums(row_scores, [v[3:6] + v[9:] for v in values])
    row_ref[...] = jnp.concatenate([t / w for t, w in zip(totals, weights)], axis=1)
    lane = lax.broadcasted_iota(jnp.int32, (tokens, HEAD), 1)
    sums = sums_ref[...]
    for n in range(heads):
        sums = jnp.where(lane == step * heads + n, tops[n] + jnp.log2(weights[n]), sums)
    sums_ref[...] = sums


def merged(place, window, row, sums, rest, stats, cols, step, heads):
    inner = (place[2] > 0) & (place[2] < cols - 1)
    lane = lax.broadcasted_iota(jnp.int32, sums.shape, 1)
    results = []
    for n in range(heads):
        cut = slice(n * HEAD, (n + 1) * HEAD)
        head = step * heads + n
        near = jnp.sum(jnp.where(lane == head, sums, 0.0), axis=1, keepdims=True)
        mine = (lane >= 3 * head) & (lane < 3 * head + 3)
        far = jnp.sum(jnp.where(mine, stats, 0.0), axis=1, keepdims=True)
        far = jnp.where(inner, NEG, far)
        both = jnp.maximum(near, far)
        near, far = jnp.exp2(near - both), jnp.exp2(far - both)
        share = far / (near + far)
        axial = row[:, cut] * (1.0 - share) + rest[:, cut].astype(jnp.float32) * share
        results.append((window[:, cut] + axial).astype(jnp.bfloat16))
    return jnp.concatenate(results, axis=1)


def merge_kernel(place, window_ref, row_ref, sums_ref, rest_ref, stats_ref, out_ref, *, cols):
    out_ref[...] = merged(
        place, window_ref[...], row_ref[...], sums_ref[...], rest_ref[...],
        stats_ref[...].astype(jnp.float32), cols, 0, out_ref.shape[1] // HEAD,
    )


def add_product(total_ref, rows, weight_ref, lanes=512):
    for start in range(0, total_ref.shape[1], lanes):
        cut = slice(start, start + lanes)
        total_ref[:, cut] += dot_nn(rows, weight_ref[:, cut])


def project_kernel(place, window_ref, row_ref, sums_ref, rest_ref, stats_ref, weight_ref, other_ref, *refs, cols):
    out_ref, total_ref = refs[-2:]

    @pl.when(pl.program_id(0) == 0)
    def _():
        total_ref[...] = other_ref[...].astype(jnp.float32)

    rows = merged(
        place, window_ref[...], row_ref[...], sums_ref[...], rest_ref[...],
        stats_ref[...].astype(jnp.float32), cols, pl.program_id(0), window_ref.shape[1] // HEAD,
    )
    add_product(total_ref, rows, weight_ref)

    @pl.when(pl.program_id(0) == pl.num_programs(0) - 1)
    def _():
        out_ref[...] = total_ref[...].astype(jnp.bfloat16)


def product_kernel(rows_ref, weight_ref, out_ref, total_ref):
    @pl.when(pl.program_id(0) == 0)
    def _():
        total_ref[...] = jnp.zeros_like(total_ref)

    add_product(total_ref, rows_ref[...], weight_ref)

    @pl.when(pl.program_id(0) == pl.num_programs(0) - 1)
    def _():
        out_ref[...] = total_ref[...].astype(jnp.bfloat16)


def hbm(*values):
    return [pltpu.with_memory_space_constraint(v, pltpu.HBM) for v in values]


def params():
    return pltpu.CompilerParams(vmem_limit_bytes=VMEM_LIMIT)


def side(half, place):
    return half + (1 - 2 * half) * (1 - place[0])


def pack(place, keys, values, half):
    S, tokens, width = keys.shape
    width //= 2
    spec = pl.BlockSpec((None, tokens, width), lambda s, p: (s, 0, side(half, p)))

    def kernel(place, k_ref, v_ref, out_ref):
        for start in range(0, width, HEAD):
            cut = slice(start, start + HEAD)
            out_ref[0, :, cut] = k_ref[:, cut].T
        out_ref[1] = v_ref[...]

    return pl.pallas_call(
        kernel,
        out_shape=jax.ShapeDtypeStruct((S, 2, tokens, width), keys.dtype),
        grid_spec=pltpu.PrefetchScalarGridSpec(
            num_scalar_prefetch=1,
            grid=(S,),
            in_specs=[spec, spec],
            out_specs=pl.BlockSpec((None, 2, tokens, width), lambda s, p: (s, 0, 0, 0)),
        ),
        compiler_params=params(),
        cost_estimate=pl.CostEstimate(
            flops=0, bytes_accessed=8 * S * tokens * width, transcendentals=0
        ),
        name="pack",
    )(place, *hbm(keys, values))


def pick(place, value, half):
    S, tokens, width = value.shape
    width //= 2

    def kernel(place, in_ref, out_ref):
        out_ref[...] = in_ref[...]

    return pl.pallas_call(
        kernel,
        out_shape=jax.ShapeDtypeStruct((S, tokens, width), value.dtype),
        grid_spec=pltpu.PrefetchScalarGridSpec(
            num_scalar_prefetch=1,
            grid=(S,),
            in_specs=[pl.BlockSpec((None, tokens, width), lambda s, p: (s, 0, side(half, p)))],
            out_specs=pl.BlockSpec((None, tokens, width), lambda s, p: (s, 0, 0)),
        ),
        compiler_params=params(),
        cost_estimate=pl.CostEstimate(
            flops=0, bytes_accessed=4 * S * tokens * width, transcendentals=0
        ),
        name="pick",
    )(place, *hbm(value))


def edge_attend(place, q, near, far, start, cols_tile, cols):
    count, _, tokens, width = far.shape
    heads = width // HEAD
    return pl.pallas_call(
        functools.partial(edge_kernel, heads=heads, cols_tile=cols_tile, cols=cols),
        out_shape=jax.ShapeDtypeStruct((count, tokens, width + HEAD), jnp.bfloat16),
        grid_spec=pltpu.PrefetchScalarGridSpec(
            num_scalar_prefetch=1,
            grid=(count,),
            in_specs=[
                pl.BlockSpec((None, tokens, width), lambda g, p: (start + g, 0, 0)),
                pl.BlockSpec((None, 2, tokens, width), lambda g, p: (start + g, 0, 0, 0)),
                pl.BlockSpec((None, 2, tokens, width), lambda g, p: (g, 0, 0, 0)),
            ],
            out_specs=pl.BlockSpec((None, tokens, width + HEAD), lambda g, p: (g, 0, 0)),
        ),
        compiler_params=params(),
        cost_estimate=pl.CostEstimate(
            flops=8 * count * tokens * tokens * width,
            bytes_accessed=14 * count * tokens * width,
            transcendentals=2 * count * tokens * tokens * heads,
        ),
        name="edge_rows",
    )(place, q, near, far)


def rows_attend(place, mask, reach, q, tiles, sides, far, half, stream, cols_tile, frame_tokens, grid, block=3):
    tokens, width = far.shape[2:]
    at = stream if far.shape[0] > 1 else 0
    heads = width // HEAD
    lanes = block * HEAD
    steps = heads // block
    own = pl.BlockSpec((None, 2, tokens, lanes), lambda g, p: (stream, 0, 0, g))
    near = pl.BlockSpec((None, None, 2, tokens, lanes), lambda g, p: (0, stream, 0, 0, g))
    other = pl.BlockSpec((None, None, 2, tokens, lanes), lambda g, p: (1, stream, 0, 0, g))
    args = [x for tile, pair in zip(tiles, sides) for x in (tile, pair, pair)]
    kernel = functools.partial(
        rows_kernel, heads=block, half=half, grid=grid, cols_tile=cols_tile, frame_tokens=frame_tokens
    )
    return pl.pallas_call(
        kernel,
        out_shape=(
            jax.ShapeDtypeStruct((tokens, width), jnp.float32),
            jax.ShapeDtypeStruct((tokens, width), jnp.float32),
            jax.ShapeDtypeStruct((tokens, HEAD), jnp.float32),
        ),
        grid_spec=pltpu.PrefetchScalarGridSpec(
            num_scalar_prefetch=1,
            grid=(steps,),
            in_specs=[
                SMEM,
                SMEM,
                pl.BlockSpec((None, tokens, lanes), lambda g, p: (stream, 0, side(half, p) * steps + g)),
                *[own, near, other] * 3,
                pl.BlockSpec((None, 2, tokens, lanes), lambda g, p: (at, 0, 0, g)),
            ],
            out_specs=(
                pl.BlockSpec((tokens, lanes), lambda g, p: (0, g)),
                pl.BlockSpec((tokens, lanes), lambda g, p: (0, g)),
                pl.BlockSpec((tokens, HEAD), lambda g, p: (0, 0)),
            ),
            scratch_shapes=[
                pltpu.VMEM((tokens // frame_tokens + 2, tokens, tokens), jnp.float32)
            ],
        ),
        compiler_params=params(),
        cost_estimate=pl.CostEstimate(
            flops=46 * tokens * tokens * width,
            bytes_accessed=54 * tokens * width,
            transcendentals=13 * tokens * tokens * heads,
        ),
        name="rows",
    )(place, mask, reach, *hbm(q), *args, far)


def merge(place, parts, rest, stream, cols):
    tokens, width = parts[0].shape
    at = stream if rest.shape[0] > 1 else 0
    whole = pl.BlockSpec((tokens, width), lambda g, p: (0, 0))
    return pl.pallas_call(
        functools.partial(merge_kernel, cols=cols),
        out_shape=jax.ShapeDtypeStruct((tokens, width), jnp.bfloat16),
        grid_spec=pltpu.PrefetchScalarGridSpec(
            num_scalar_prefetch=1,
            grid=(1,),
            in_specs=[
                whole,
                whole,
                pl.BlockSpec((tokens, HEAD), lambda g, p: (0, 0)),
                pl.BlockSpec((None, tokens, width), lambda g, p: (at, 0, 0)),
                pl.BlockSpec((None, tokens, HEAD), lambda g, p: (at, 0, width // HEAD)),
            ],
            out_specs=whole,
        ),
        compiler_params=params(),
        cost_estimate=pl.CostEstimate(
            flops=8 * tokens * width, bytes_accessed=12 * tokens * width, transcendentals=0
        ),
        name="merge",
    )(place, *parts, rest, rest)


def project(place, parts, rest, weight, other, output, stream, cols, block=3):
    tokens, width = parts[0].shape
    at = stream if rest.shape[0] > 1 else 0
    lanes = block * HEAD
    streams, _, model = weight.shape
    earlier = [] if output is None else [output]
    cut = pl.BlockSpec((tokens, lanes), lambda g, p: (0, g))
    args = [place, *parts, rest, rest, weight, other]
    return pl.pallas_call(
        functools.partial(project_kernel, cols=cols),
        out_shape=jax.ShapeDtypeStruct((streams, tokens, model), jnp.bfloat16),
        grid_spec=pltpu.PrefetchScalarGridSpec(
            num_scalar_prefetch=1,
            grid=(width // lanes,),
            in_specs=[
                cut,
                cut,
                pl.BlockSpec((tokens, HEAD), lambda g, p: (0, 0)),
                pl.BlockSpec((None, tokens, lanes), lambda g, p: (at, 0, g)),
                pl.BlockSpec((None, tokens, HEAD), lambda g, p: (at, 0, width // HEAD)),
                pl.BlockSpec((None, lanes, model), lambda g, p: (stream, g, 0)),
                pl.BlockSpec((tokens, model), lambda g, p: (0, 0)),
                *[ANY] * len(earlier),
            ],
            out_specs=pl.BlockSpec((None, tokens, model), lambda g, p: (stream, 0, 0)),
            scratch_shapes=[pltpu.VMEM((tokens, model), jnp.float32)],
        ),
        input_output_aliases={len(args): 0} if earlier else {},
        compiler_params=params(),
        cost_estimate=pl.CostEstimate(
            flops=2 * tokens * width * model, bytes_accessed=2 * width * model, transcendentals=0
        ),
        name="project",
    )(*args, *earlier)


def product(rows, weight, stream, block=3):
    tokens, width = rows.shape
    model = weight.shape[2]
    lanes = block * HEAD
    return pl.pallas_call(
        product_kernel,
        out_shape=jax.ShapeDtypeStruct((tokens, model), jnp.bfloat16),
        grid=(width // lanes,),
        in_specs=[
            pl.BlockSpec((tokens, lanes), lambda g: (0, g)),
            pl.BlockSpec((None, lanes, model), lambda g: (stream, g, 0)),
        ],
        out_specs=pl.BlockSpec((tokens, model), lambda g: (0, 0)),
        scratch_shapes=[pltpu.VMEM((tokens, model), jnp.float32)],
        compiler_params=params(),
        cost_estimate=pl.CostEstimate(
            flops=2 * tokens * width * model, bytes_accessed=2 * width * model, transcendentals=0
        ),
        name="product",
    )(rows, weight)


def swaps(size, start):
    pairs = [(i, i + 1) for i in range(start, size - 1, 2)]
    return pairs + [(j, i) for i, j in pairs]


def per_device(queries, key_states, value_states, tile_mask, frame_reach, out_weight):
    S, F, R, C, width = queries.shape
    tokens = F * R * C
    model = out_weight.shape[2]
    rows, cols = lax.axis_size("row"), lax.axis_size("col")
    inward = [(0, 1), (cols - 1, cols - 2)]
    outward = [(j, i) for i, j in inward]
    place = jnp.stack([lax.axis_index(a) for a in ("pair", "row", "col")]).astype(jnp.int32)
    q, k, v = [a.reshape(S, tokens, width) for a in (queries, key_states, value_states)]
    mask = tile_mask.reshape(9)

    sent = {}

    def tied(value, after):
        return lax.optimization_barrier((value, *[sent[n] for n in after]))[0] if after else value

    def send(name, value, axis, pairs, *after):
        sent[name] = lax.ppermute(tied(value, after), axis, pairs)

    col_pairs, col_others = swaps(cols, 0), swaps(cols, 1)
    row_pairs, row_others = swaps(rows, 0), swaps(rows, 1)
    pair_swap = swaps(2, 0)
    own = [pack(place, k, v, h) for h in range(2)]
    picked = [pick(place, q, h) for h in range(2)]

    def edge(name, h, start, *after):
        sent[f"part{name}"] = edge_attend(
            place, tied(sent[f"q{h}"], after), sent[f"other{h}"], sent[f"far{name}"], start, C, cols
        )

    def rows_of(name, h, s, *after):
        tiles = [sent[f"pair_own{h}"], own[h], sent[f"next_own{h}"]]
        sides = [sent[f"pair_sides{h}"], sent[f"sides{h}"], sent[f"next_sides{h}"]]
        sent[f"rows{h}{s}"] = rows_attend(
            place, tied(mask, after), frame_reach, q, tiles, sides, sent[f"far{name}"], h, s, C, R * C, (rows, cols)
        )

    send("near0", own[0], "col", col_pairs)
    send("other0", own[0], "col", col_others)
    send("next_own0", own[0], "row", row_others)
    send("pair_own0", own[0], "row", row_pairs)
    send("q0", picked[0], "col", inward)
    send("far00", sent["near0"][:1], "col", col_others, "other0", "next_own0")
    send("far01", sent["near0"][1:], "col", col_others, "other0", "next_own0")
    sent["sides0"] = jnp.stack([sent["near0"], sent["other0"]])
    send("next_sides0", sent["sides0"], "row", row_others)
    send("pair_sides0", sent["sides0"], "row", row_pairs, "pair_own0")
    edge("00", 0, 0)
    send("rest00", sent["part00"], "col", outward)
    send("near1", own[1], "col", col_pairs, "rest00")
    send("other1", own[1], "col", col_others, "far00")
    edge("01", 0, 1)
    send("rest01", sent["part01"], "col", outward)
    rows_of("00", 0, 0)
    rows_of("01", 0, 1)
    sent["merged0"] = merge(tied(place, []), sent["rows00"], sent["rest00"], 0, cols)
    send("theirs0", sent["merged0"], "pair", pair_swap)
    sent["merged1"] = merge(tied(place, []), sent["rows01"], sent["rest01"], 1, cols)
    send("theirs1", sent["merged1"], "pair", pair_swap)
    send("next_own1", own[1], "row", row_others, "next_sides0")
    send("pair_own1", own[1], "row", row_pairs)
    send("q1", picked[1], "col", inward, "rest01")
    sent["product0"] = product(tied(sent["theirs0"], []), out_weight, 0)
    send("back0", sent["product0"], "pair", pair_swap)
    sent["product1"] = product(tied(sent["theirs1"], []), out_weight, 1)
    send("back1", sent["product1"], "pair", pair_swap)
    send("far10", sent["near1"][:1], "col", col_others, "far01")
    send("far11", sent["near1"][1:], "col", col_others, "other1")
    sent["sides1"] = jnp.stack([sent["near1"], sent["other1"]])
    send("next_sides1", sent["sides1"], "row", row_others)
    send("pair_sides1", sent["sides1"], "row", row_pairs)
    edge("10", 1, 0)
    send("rest10", sent["part10"], "col", outward)
    edge("11", 1, 1)
    send("rest11", sent["part11"], "col", outward)
    rows_of("10", 1, 0)
    rows_of("11", 1, 1)
    output = project(tied(place, []), sent["rows10"], sent["rest10"], out_weight, sent["back0"], None, 0, cols)
    output = project(place, sent["rows11"], sent["rest11"], out_weight, sent["back1"], output, 1, cols)
    return output.reshape(S, F, R, C, model)


def solution(mesh):
    return jax.shard_map(
        per_device,
        mesh=mesh,
        in_specs=(
            P("pair", None, "row", "col", None),
            P("pair", None, "row", "col", None),
            P("pair", None, "row", "col", None),
            P("pair", "row", "col", None),
            P(),
            P(None, "pair", None),
        ),
        out_specs=P("pair", None, "row", "col", None),
        check_vma=False,
    )
```

time: 349 us -> 188 us (0.54)
  starting transfers between devices: 86.5 us -> 30.7 us
  Pallas kernels: 99.7 us -> 46.6 us
  local copies, waits for them, and re-layouts: 37.2 us -> 0.99 us
  between operations: 14.1 us -> 0.51 us
    ppermute x24 -> x26, starting transfers between devices: 86.3 us -> 30.7 us  [send(): sent[name] = lax.ppermute(tied(value, after), axis, pairs)]
    unnamed x92 -> x16, local copies, waits for them, and re-layouts: 36.2 us -> 0.81 us
    pallas_call x2, Pallas kernels: 39.1 us -> 3.93 us  [pack(): pl.pallas_call(kernel, out_shape=jax.ShapeDtypeStruct((S, 2, tokens, widt...]
    pallas_call x2, Pallas kernels: 21.3 us -> 3.29 us  [pick(): pl.pallas_call(kernel, out_shape=jax.ShapeDtypeStruct((S, tokens, width),...]
    all_gather x6 -> x0, waiting for transfers between devices: 16.2 us -> none  [gather(): lax.all_gather(tied(value, after), 'row', axis_index_groups=groups)]
    ppermute x24 -> x26, waiting for transfers between devices: 91.4 us -> 106 us  [send(): sent[name] = lax.ppermute(tied(value, after), axis, pairs)]
    pallas_call x4 -> x8, Pallas kernels: 29.1 us -> 32.8 us  [the longest x4 22.8 us: rows_attend(): pl.pallas_call(kernel, out_shape=(jax.ShapeDtypeStruct((tokens, width), j...]
  transfers between devices with their start and end apart: 30 -> 26, of which waited for: 7 -> 8; matrix products, arithmetic and copies ran while one was open for 0% -> 0% of each run, Pallas kernels for 21% -> 22%
where the time goes in v4:
time: 188 us; the launch traced here: 186 us
  waiting for transfers between devices  106 us (56%)
  Pallas kernels  46.6 us (25%)
  starting transfers between devices  30.7 us (16%)
    ppermute x26, waiting for transfers between devices, send(): sent[name] = lax.ppermute(tied(value, after), axis, pairs)  106 us
    ppermute x26, starting transfers between devices, send(): sent[name] = lax.ppermute(tied(value, after), axis, pairs)  30.7 us
    pallas_call x4, Pallas kernels, rows_attend(): pl.pallas_call(kernel, out_shape=(jax.ShapeDtypeStruct((tokens, width), j...  22.8 us
    pallas_call x2, Pallas kernels, project(): pl.pallas_call(functools.partial(project_kernel, cols=cols), out_shape=ja...  7.96 us
    pallas_call x2, Pallas kernels, product(): pl.pallas_call(product_kernel, out_shape=jax.ShapeDtypeStruct((tokens, mo...  4.17 us
    pallas_call x2, Pallas kernels, pack(): pl.pallas_call(kernel, out_shape=jax.ShapeDtypeStruct((S, 2, tokens, widt...  3.93 us
  transfers between devices with their start and end apart: 26, of which 8 were waited for; matrix products, arithmetic and copies ran while one was open for 0% of the time, Pallas kernels for 22%

profile of v4, /device:TPU:0, one launch (start us, length us, event | category | flops | bytes accessed | tf_op | source)
XLA Modules:
  0.0 185.6 jit_solution(7735971520889034287)
XLA Ops:
  0.1 2.0 %pack.3.refs_3_ = bf16[2,2,128,1152]{3,2,1,0:T(8,128)(2,1)S(1)} custom-call(s32[3]{0:T(128)S(1)} %pad_add_fusion.place, bf16[2,128,2304]{2,1,0:T(8,128)(2,1)} %bitcast.28, bf16[2,128,2304]{2,1,0:T(8,128)(2,1)} %bitcast.30), custom_call_target="tpu_custom_call" | custom-call | bytes 2359296 | tf_op jit(solution)/shard_map/pack/pallas_call | solution.py:220
  2.0 3.1 %collective-permute-start.3 = (bf16[2,2,128,1152]{3,2,1,0:T(8,128)(2,1)S(1)}, bf16[2,2,128,1152]{3,2,1,0:T(8,128)(2,1)S(1)}, u32[]{:S(2)}, u32[]{:S(2)}) collective-permute-start(bf16[2,2,128,1152]{3,2,1,0:T(8,128)(2,1)S(1)} %pack.3.refs_3_), channel_id=1, source_target_pairs={{0,1},{2,3},{1,0},{3,2},{4,5},{6,7},{5,4},{7,6},{8,9},{10,11},{9,8... | collective-permute-start | bytes 3538952 | tf_op jit(solution)/shard_map/ppermute | solution.py:443
  6.6 2.9 %collective-permute-start.18 = (bf16[2,2,128,1152]{3,2,1,0:T(8,128)(2,1)S(1)}, bf16[2,2,128,1152]{3,2,1,0:T(8,128)(2,1)S(1)}, u32[]{:S(2)}, u32[]{:S(2)}) collective-permute-start(bf16[2,2,128,1152]{3,2,1,0:T(8,128)(2,1)S(1)} %pack.3.refs_3_), channel_id=1, source_target_pairs={{0,4},{8,12},{4,0},{12,8},{1,5},{9,13},{5,1},{13,9},{2,6},{10,14},... | collective-permute-start | bytes 3538952 | tf_op jit(solution)/shard_map/ppermute | solution.py:443
  9.5 1.6 pick.2
  11.1 6.0 %collective-permute-start.1 = (bf16[2,128,1152]{2,1,0:T(8,128)(2,1)S(1)}, bf16[2,128,1152]{2,1,0:T(8,128)(2,1)S(1)}, u32[]{:S(2)}, u32[]{:S(2)}) collective-permute-start(bf16[2,128,1152]{2,1,0:T(8,128)(2,1)S(1)} %pick.2), channel_id=1, source_target_pairs={{0,1},{3,2},{4,5},{7,6},{8,9},{11,10},{12,13},{15,14},{16,17},{19,... | collective-permute-start | bytes 1769480 | tf_op jit(solution)/shard_map/ppermute | solution.py:443
  17.1 14.4 %collective-permute-done.3 = bf16[2,2,128,1152]{3,2,1,0:T(8,128)(2,1)S(1)} collective-permute-done((bf16[2,2,128,1152]{3,2,1,0:T(8,128)(2,1)S(1)}, bf16[2,2,128,1152]{3,2,1,0:T(8,128)(2,1)S(1)}, u32[]{:S(2)}, u32[]{:S(2)}) %collective-permute-start.3) | collective-permute-done | bytes 1179680 | tf_op jit(solution)/shard_map/ppermute | solution.py:443
  33.4 9.6 %collective-permute-done.1.q_ref = bf16[2,128,1152]{2,1,0:T(8,128)(2,1)S(1)} collective-permute-done((bf16[2,128,1152]{2,1,0:T(8,128)(2,1)S(1)}, bf16[2,128,1152]{2,1,0:T(8,128)(2,1)S(1)}, u32[]{:S(2)}, u32[]{:S(2)}) %collective-permute-start.1) | collective-permute-done | bytes 589856 | tf_op jit(solution)/shard_map/ppermute | solution.py:443
  43.6 1.3 collective-permute-start.6
  45.0 2.0 %pack.2.refs_3_ = bf16[2,2,128,1152]{3,2,1,0:T(8,128)(2,1)S(1)} custom-call(s32[3]{0:T(128)S(1)} %pad_add_fusion.place, bf16[2,128,2304]{2,1,0:T(8,128)(2,1)} %bitcast.29, bf16[2,128,2304]{2,1,0:T(8,128)(2,1)} %bitcast.31), custom_call_target="tpu_custom_call" | custom-call | bytes 2359296 | tf_op jit(solution)/shard_map/pack/pallas_call | solution.py:220
  47.7 15.6 %collective-permute-done.6.rest_ref.stats_ref = bf16[1,128,1280]{2,1,0:T(8,128)(2,1)S(1)} collective-permute-done((bf16[1,128,1280]{2,1,0:T(8,128)(2,1)S(1)}, bf16[1,128,1280]{2,1,0:T(8,128)(2,1)S(1)}, u32[]{:S(2)}, u32[]{:S(2)}) %collective-permute-start.6) | collective-permute-done | bytes 327712 | tf_op jit(solution)/shard_map/ppermute | solution.py:443
  64.8 1.3 collective-permute-start.15
  66.1 25.2 %collective-permute-done.7 = bf16[2,2,128,1152]{3,2,1,0:T(8,128)(2,1)S(1)} collective-permute-done((bf16[2,2,128,1152]{3,2,1,0:T(8,128)(2,1)S(1)}, bf16[2,2,128,1152]{3,2,1,0:T(8,128)(2,1)S(1)}, u32[]{:S(2)}, u32[]{:S(2)}) %collective-permute-start.7) | collective-permute-done | bytes 1179680 | tf_op jit(solution)/shard_map/ppermute | solution.py:443
  93.3 18.7 %collective-permute-done.15.rest_ref.stats_ref = bf16[1,128,1280]{2,1,0:T(8,128)(2,1)S(1)} collective-permute-done((bf16[1,128,1280]{2,1,0:T(8,128)(2,1)S(1)}, bf16[1,128,1280]{2,1,0:T(8,128)(2,1)S(1)}, u32[]{:S(2)}, u32[]{:S(2)}) %collective-permute-start.15) | collective-permute-done | bytes 327712 | tf_op jit(solution)/shard_map/ppermute | solution.py:443
  112.1 1.6 pick.3
  113.7 1.5 collective-permute-start.16
  115.3 5.5 %rows.7 = (f32[128,1152]{1,0:T(8,128)S(1)}, f32[128,1152]{1,0:T(8,128)S(1)}, f32[128,128]{1,0:T(8,128)S(1)}) custom-call(s32[3]{0:T(128)S(1)} %pad_add_fusion.place, s32[9]{0:T(128)S(1)} %bitcast.16, s32[18]{0:T(128)S(1)} %copy-done.1, bf16[2,128,2304]{2,1,0:T(8,128)(2,1)} %bitcast.22, bf16[2,2,128,1152]{3,2,1,0:T(8,128)(2,1)S(1)} %collective-permute-done.18.refs_0_, ...), custom_call_target="tpu_custom_call" | custom-call | flops 868220928 | bytes 7962624 | tf_op jit(solution)/shard_map/rows/pallas_call | solution.py:300
  120.8 1.0 merge.3
  121.9 1.6 collective-permute-start.24
  123.4 6.3 %rows.5 = (f32[128,1152]{1,0:T(8,128)S(1)}, f32[128,1152]{1,0:T(8,128)S(1)}, f32[128,128]{1,0:T(8,128)S(1)}) custom-call(s32[3]{0:T(128)S(1)} %pad_add_fusion.place, s32[9]{0:T(128)S(1)} %bitcast.17, s32[18]{0:T(128)S(1)} %copy-done.1, bf16[2,128,2304]{2,1,0:T(8,128)(2,1)} %bitcast.23, bf16[2,2,128,1152]{3,2,1,0:T(8,128)(2,1)S(1)} %collective-permute-done.18.refs_0_, ...), custom_call_target="tpu_custom_call" | custom-call | flops 868220928 | bytes 7962624 | tf_op jit(solution)/shard_map/rows/pallas_call | solution.py:300
  129.7 1.0 merge.2
  132.8 7.0 %collective-permute-done.20.rows_ref = bf16[128,1152]{1,0:T(8,128)(2,1)S(1)} collective-permute-done((bf16[128,1152]{1,0:T(8,128)(2,1)S(1)}, bf16[128,1152]{1,0:T(8,128)(2,1)S(1)}, u32[]{:S(2)}, u32[]{:S(2)}) %collective-permute-start.20) | collective-permute-done | bytes 294944 | tf_op jit(solution)/shard_map/ppermute | solution.py:443
  140.5 2.1 %product.3 = bf16[128,3072]{1,0:T(8,128)(2,1)S(1)} custom-call(bf16[128,1152]{1,0:T(8,128)(2,1)S(1)} %collective-permute-done.24.rows_ref, bf16[2,1152,3072]{2,1,0:T(8,128)(2,1)S(1)} %bitcast.13), custom_call_target="tpu_custom_call" | custom-call | flops 905969664 | bytes 7077888 | tf_op jit(solution)/shard_map/product/pallas_call | solution.py:403
  143.1 2.1 %product.2 = bf16[128,3072]{1,0:T(8,128)(2,1)S(1)} custom-call(bf16[128,1152]{1,0:T(8,128)(2,1)S(1)} %collective-permute-done.20.rows_ref, bf16[2,1152,3072]{2,1,0:T(8,128)(2,1)S(1)} %bitcast.13), custom_call_target="tpu_custom_call" | custom-call | flops 905969664 | bytes 7077888 | tf_op jit(solution)/shard_map/product/pallas_call | solution.py:403
  145.2 1.7 collective-permute-start.21
  147.7 1.3 collective-permute-start.23
  149.5 1.3 collective-permute-start.17
  150.8 5.5 %rows.6 = (f32[128,1152]{1,0:T(8,128)S(1)}, f32[128,1152]{1,0:T(8,128)S(1)}, f32[128,128]{1,0:T(8,128)S(1)}) custom-call(s32[3]{0:T(128)S(1)} %pad_add_fusion.place, s32[9]{0:T(128)S(1)} %bitcast.18, s32[18]{0:T(128)S(1)} %copy-done.1, bf16[2,128,2304]{2,1,0:T(8,128)(2,1)} %bitcast.24, bf16[2,2,128,1152]{3,2,1,0:T(8,128)(2,1)S(1)} %collective-permute-done.refs_0_, ...), custom_call_target="tpu_custom_call" | custom-call | flops 868220928 | bytes 7962624 | tf_op jit(solution)/shard_map/rows/pallas_call | solution.py:300
  156.4 5.5 %rows.4 = (f32[128,1152]{1,0:T(8,128)S(1)}, f32[128,1152]{1,0:T(8,128)S(1)}, f32[128,128]{1,0:T(8,128)S(1)}) custom-call(s32[3]{0:T(128)S(1)} %pad_add_fusion.place, s32[9]{0:T(128)S(1)} %bitcast.19, s32[18]{0:T(128)S(1)} %copy-done.1, bf16[2,128,2304]{2,1,0:T(8,128)(2,1)} %bitcast.25, bf16[2,2,128,1152]{3,2,1,0:T(8,128)(2,1)S(1)} %collective-permute-done.refs_0_, ...), custom_call_target="tpu_custom_call" | custom-call | flops 868220928 | bytes 7962624 | tf_op jit(solution)/shard_map/rows/pallas_call | solution.py:300
  161.9 13.5 %collective-permute-done.23.rest_ref.stats_ref = bf16[1,128,1280]{2,1,0:T(8,128)(2,1)S(1)} collective-permute-done((bf16[1,128,1280]{2,1,0:T(8,128)(2,1)S(1)}, bf16[1,128,1280]{2,1,0:T(8,128)(2,1)S(1)}, u32[]{:S(2)}, u32[]{:S(2)}) %collective-permute-start.23) | collective-permute-done | bytes 327712 | tf_op jit(solution)/shard_map/ppermute | solution.py:443
  175.4 4.0 %project.2.refs_0_ = bf16[2,128,3072]{2,1,0:T(8,128)(2,1)} custom-call(s32[3]{0:T(128)S(1)} %pad_add_fusion.place, f32[128,1152]{1,0:T(8,128)S(1)} %get-tuple-element.41.window_ref, f32[128,1152]{1,0:T(8,128)S(1)} %get-tuple-element.42.row_ref, f32[128,128]{1,0:T(8,128)S(1)} %get-tuple-element.43.sums_ref, ...), custom_call_target="tpu_custom_call" | custom-call | flops 905969664 | bytes 7077888 | tf_op jit(solution)/shard_map/project/pallas_call | solution.py:371
  179.4 2.2 %collective-permute-done.17.rest_ref.stats_ref = bf16[1,128,1280]{2,1,0:T(8,128)(2,1)S(1)} collective-permute-done((bf16[1,128,1280]{2,1,0:T(8,128)(2,1)S(1)}, bf16[1,128,1280]{2,1,0:T(8,128)(2,1)S(1)}, u32[]{:S(2)}, u32[]{:S(2)}) %collective-permute-start.17) | collective-permute-done | bytes 327712 | tf_op jit(solution)/shard_map/ppermute | solution.py:443
  181.6 4.0 %project.3 = bf16[2,128,3072]{2,1,0:T(8,128)(2,1)} custom-call(s32[3]{0:T(128)S(1)} %pad_add_fusion.place, f32[128,1152]{1,0:T(8,128)S(1)} %get-tuple-element.31.window_ref, f32[128,1152]{1,0:T(8,128)S(1)} %get-tuple-element.32.row_ref, f32[128,128]{1,0:T(8,128)S(1)} %get-tuple-element.33.sums_ref, ...), custom_call_target="tpu_custom_call", output_to_operand_aliasing={{}: (8, {})} | custom-call | flops 905969664 | bytes 7077888 | tf_op jit(solution)/shard_map/project/pallas_call | solution.py:371
  (60 shorter events, 12.7 us)
Async XLA Ops:
  2.0 29.5 %collective-permute-start.3 = (bf16[2,2,128,1152]{3,2,1,0:T(8,128)(2,1)S(1)}, bf16[2,2,128,1152]{3,2,1,0:T(8,128)(2,1)S(1)}, u32[]{:S(2)}, u32[]{:S(2)}) collective-permute-start(bf16[2,2,128,1152]{3,2,1,0:T(8,128)(2,1)S(1)} %pack.3.refs_3_), channel_id=1, source_target_pairs={{0,1},{2,3},{1,0},{3,2},{4,5},{6,7},{5,4},{7,6},{8,9},{10,11},{9,8... | collective-permute-start | bytes 3538952 | tf_op jit(solution)/shard_map/ppermute | solution.py:443
  5.1 26.5 %collective-permute-start.4 = (bf16[2,2,128,1152]{3,2,1,0:T(8,128)(2,1)S(1)}, bf16[2,2,128,1152]{3,2,1,0:T(8,128)(2,1)S(1)}, u32[]{:S(2)}, u32[]{:S(2)}) collective-permute-start(bf16[2,2,128,1152]{3,2,1,0:T(8,128)(2,1)S(1)} %pack.3.refs_3_), channel_id=1, source_target_pairs={{4,8},{8,4},{5,9},{9,5},{6,10},{10,6},{7,11},{11,7},{20,24},{24,20... | collective-permute-start | bytes 3538952 | tf_op jit(solution)/shard_map/ppermute | solution.py:443
  5.9 25.7 %collective-permute-start.2 = (bf16[2,2,128,1152]{3,2,1,0:T(8,128)(2,1)S(1)}, bf16[2,2,128,1152]{3,2,1,0:T(8,128)(2,1)S(1)}, u32[]{:S(2)}, u32[]{:S(2)}) collective-permute-start(bf16[2,2,128,1152]{3,2,1,0:T(8,128)(2,1)S(1)} %pack.3.refs_3_), channel_id=1, source_target_pairs={{1,2},{2,1},{5,6},{6,5},{9,10},{10,9},{13,14},{14,13},{17,18},{18,... | collective-permute-start | bytes 3538952 | tf_op jit(solution)/shard_map/ppermute | solution.py:443
  6.6 38.3 %collective-permute-start.18 = (bf16[2,2,128,1152]{3,2,1,0:T(8,128)(2,1)S(1)}, bf16[2,2,128,1152]{3,2,1,0:T(8,128)(2,1)S(1)}, u32[]{:S(2)}, u32[]{:S(2)}) collective-permute-start(bf16[2,2,128,1152]{3,2,1,0:T(8,128)(2,1)S(1)} %pack.3.refs_3_), channel_id=1, source_target_pairs={{0,4},{8,12},{4,0},{12,8},{1,5},{9,13},{5,1},{13,9},{2,6},{10,14},... | collective-permute-start | bytes 3538952 | tf_op jit(solution)/shard_map/ppermute | solution.py:443
  11.1 31.9 %collective-permute-start.1 = (bf16[2,128,1152]{2,1,0:T(8,128)(2,1)S(1)}, bf16[2,128,1152]{2,1,0:T(8,128)(2,1)S(1)}, u32[]{:S(2)}, u32[]{:S(2)}) collective-permute-start(bf16[2,128,1152]{2,1,0:T(8,128)(2,1)S(1)} %pick.2), channel_id=1, source_target_pairs={{0,1},{3,2},{4,5},{7,6},{8,9},{11,10},{12,13},{15,14},{16,17},{19,... | collective-permute-start | bytes 1769480 | tf_op jit(solution)/shard_map/ppermute | solution.py:443
  31.6 11.4 %collective-permute-start.5 = (bf16[1,2,128,1152]{3,2,1,0:T(8,128)(2,1)S(1)}, bf16[1,2,128,1152]{3,2,1,0:T(8,128)(2,1)S(1)}, u32[]{:S(2)}, u32[]{:S(2)}) collective-permute-start(bf16[1,2,128,1152]{3,2,1,0:T(8,128)(2,1)S(1)} %get-tuple-element.26), channel_id=1, source_target_pairs={{1,2},{2,1},{5,6},{6,5},{9,10},{10,9},{13,14},{14,13},{17,18},{18,... | collective-permute-start | bytes 1769480 | tf_op jit(solution)/shard_map/ppermute | solution.py:443
  32.6 81.1 %collective-permute-start.10 = (bf16[2,2,2,128,1152]{4,3,2,1,0:T(8,128)(2,1)S(1)}, bf16[2,2,2,128,1152]{4,3,2,1,0:T(8,128)(2,1)S(1)}, u32[]{:S(2)}, u32[]{:S(2)}) collective-permute-start(bf16[2,2,2,128,1152]{4,3,2,1,0:T(8,128)(2,1)S(1)} %pad_maximum_fusion.1.refs_4_.refs_5_), channel_id=1, source_target_pairs={{4,8},{8,4},{5,9},{9,5},{6,10},{10,6},{7,11},{11,7},{20,24},{24,20... | collective-permute-start | bytes 7077896 | tf_op jit(solution)/shard_map/ppermute | solution.py:443
  43.6 19.7 %collective-permute-start.6 = (bf16[1,128,1280]{2,1,0:T(8,128)(2,1)S(1)}, bf16[1,128,1280]{2,1,0:T(8,128)(2,1)S(1)}, u32[]{:S(2)}, u32[]{:S(2)}) collective-permute-start(bf16[1,128,1280]{2,1,0:T(8,128)(2,1)S(1)} %edge_rows.4), channel_id=1, source_target_pairs={{1,0},{2,3},{5,4},{6,7},{9,8},{10,11},{13,12},{14,15},{17,16},{18,... | collective-permute-start | bytes 983048 | tf_op jit(solution)/shard_map/ppermute | solution.py:443
  44.9 70.4 %collective-permute-start.19 = (bf16[2,2,2,128,1152]{4,3,2,1,0:T(8,128)(2,1)S(1)}, bf16[2,2,2,128,1152]{4,3,2,1,0:T(8,128)(2,1)S(1)}, u32[]{:S(2)}, u32[]{:S(2)}) collective-permute-start(bf16[2,2,2,128,1152]{4,3,2,1,0:T(8,128)(2,1)S(1)} %pad_maximum_fusion.1.refs_4_.refs_5_), channel_id=1, source_target_pairs={{0,4},{8,12},{4,0},{12,8},{1,5},{9,13},{5,1},{13,9},{2,6},{10,14},... | collective-permute-start | bytes 7077896 | tf_op jit(solution)/shard_map/ppermute | solution.py:443
  46.9 17.9 %collective-permute-start.8 = (bf16[2,2,128,1152]{3,2,1,0:T(8,128)(2,1)S(1)}, bf16[2,2,128,1152]{3,2,1,0:T(8,128)(2,1)S(1)}, u32[]{:S(2)}, u32[]{:S(2)}) collective-permute-start(bf16[2,2,128,1152]{3,2,1,0:T(8,128)(2,1)S(1)} %pack.2.refs_3_), channel_id=1, source_target_pairs={{1,2},{2,1},{5,6},{6,5},{9,10},{10,9},{13,14},{14,13},{17,18},{18,... | collective-permute-start | bytes 3538952 | tf_op jit(solution)/shard_map/ppermute | solution.py:443
  63.2 28.1 %collective-permute-start.7 = (bf16[2,2,128,1152]{3,2,1,0:T(8,128)(2,1)S(1)}, bf16[2,2,128,1152]{3,2,1,0:T(8,128)(2,1)S(1)}, u32[]{:S(2)}, u32[]{:S(2)}) collective-permute-start(bf16[2,2,128,1152]{3,2,1,0:T(8,128)(2,1)S(1)} %pack.2.refs_3_), channel_id=1, source_target_pairs={{0,1},{2,3},{1,0},{3,2},{4,5},{6,7},{5,4},{7,6},{8,9},{10,11},{9,8... | collective-permute-start | bytes 3538952 | tf_op jit(solution)/shard_map/ppermute | solution.py:443
  63.2 0.7 collective-permute-start.14
  63.9 66.8 %collective-permute-start = (bf16[2,2,128,1152]{3,2,1,0:T(8,128)(2,1)S(1)}, bf16[2,2,128,1152]{3,2,1,0:T(8,128)(2,1)S(1)}, u32[]{:S(2)}, u32[]{:S(2)}) collective-permute-start(bf16[2,2,128,1152]{3,2,1,0:T(8,128)(2,1)S(1)} %pack.2.refs_3_), channel_id=1, source_target_pairs={{0,4},{8,12},{4,0},{12,8},{1,5},{9,13},{5,1},{13,9},{2,6},{10,14},... | collective-permute-start | bytes 3538952 | tf_op jit(solution)/shard_map/ppermute | solution.py:443
  64.8 47.2 %collective-permute-start.15 = (bf16[1,128,1280]{2,1,0:T(8,128)(2,1)S(1)}, bf16[1,128,1280]{2,1,0:T(8,128)(2,1)S(1)}, u32[]{:S(2)}, u32[]{:S(2)}) collective-permute-start(bf16[1,128,1280]{2,1,0:T(8,128)(2,1)S(1)} %edge_rows.5), channel_id=1, source_target_pairs={{1,0},{2,3},{5,4},{6,7},{9,8},{10,11},{13,12},{14,15},{17,16},{18,... | collective-permute-start | bytes 983048 | tf_op jit(solution)/shard_map/ppermute | solution.py:443
  92.4 22.8 %copy-start = (s32[1,1,1,9]{3,2,1,0:T(1,128)S(1)}, s32[1,1,1,9]{3,2,1,0:T(1,128)}, u32[]{:S(2)}) copy-start(s32[1,1,1,9]{3,2,1,0:T(1,128)} %param.9) | copy-start | bytes 112
  92.4 22.9 %copy-start.1 = (s32[18]{0:T(128)S(1)}, s32[18]{0:T(128)}, u32[]{:S(2)}) copy-start(s32[18]{0:T(128)} %reach.7) | copy-start | bytes 220
  92.4 57.1 %collective-permute-start.12 = (bf16[2,2,2,128,1152]{4,3,2,1,0:T(8,128)(2,1)S(1)}, bf16[2,2,2,128,1152]{4,3,2,1,0:T(8,128)(2,1)S(1)}, u32[]{:S(2)}, u32[]{:S(2)}) collective-permute-start(bf16[2,2,2,128,1152]{4,3,2,1,0:T(8,128)(2,1)S(1)} %pad_maximum_fusion.refs_4_.refs_5_), channel_id=1, source_target_pairs={{4,8},{8,4},{5,9},{9,5},{6,10},{10,6},{7,11},{11,7},{20,24},{24,20... | collective-permute-start | bytes 7077896 | tf_op jit(solution)/shard_map/ppermute | solution.py:443
  112.1 38.8 %collective-permute-start.9 = (bf16[2,2,2,128,1152]{4,3,2,1,0:T(8,128)(2,1)S(1)}, bf16[2,2,2,128,1152]{4,3,2,1,0:T(8,128)(2,1)S(1)}, u32[]{:S(2)}, u32[]{:S(2)}) collective-permute-start(bf16[2,2,2,128,1152]{4,3,2,1,0:T(8,128)(2,1)S(1)} %pad_maximum_fusion.refs_4_.refs_5_), channel_id=1, source_target_pairs={{0,4},{8,12},{4,0},{12,8},{1,5},{9,13},{5,1},{13,9},{2,6},{10,14},... | collective-permute-start | bytes 7077896 | tf_op jit(solution)/shard_map/ppermute | solution.py:443
  113.7 17.6 %collective-permute-start.16 = (bf16[2,128,1152]{2,1,0:T(8,128)(2,1)S(1)}, bf16[2,128,1152]{2,1,0:T(8,128)(2,1)S(1)}, u32[]{:S(2)}, u32[]{:S(2)}) collective-permute-start(bf16[2,128,1152]{2,1,0:T(8,128)(2,1)S(1)} %pick.3), channel_id=1, source_target_pairs={{0,1},{3,2},{4,5},{7,6},{8,9},{11,10},{12,13},{15,14},{16,17},{19,... | collective-permute-start | bytes 1769480 | tf_op jit(solution)/shard_map/ppermute | solution.py:443
  120.8 19.7 %slice-start = ((s8[14155776]{0:T(1024)(128)(4,1)}), s8[4194304]{0:T(1024)(128)(4,1)S(1)}, s32[]{:S(2)}) async-start(s8[14155776]{0:T(1024)(128)(4,1)} %bitcast.12), calls=%async_computation | async-start | bytes 8388608
  121.8 18.7 %slice-start.1 = ((s8[14155776]{0:T(1024)(128)(4,1)}), s8[4194304]{0:T(1024)(128)(4,1)S(1)}, s32[]{:S(2)}) async-start(s8[14155776]{0:T(1024)(128)(4,1)} %bitcast.12), calls=%async_computation.1 | async-start | bytes 8388608
  121.8 18.7 %slice-start.2 = ((s8[14155776]{0:T(1024)(128)(4,1)}), s8[4194304]{0:T(1024)(128)(4,1)S(1)}, s32[]{:S(2)}) async-start(s8[14155776]{0:T(1024)(128)(4,1)} %bitcast.12), calls=%async_computation.2 | async-start | bytes 8388608
  121.8 18.7 %slice-start.3 = ((s8[14155776]{0:T(1024)(128)(4,1)}), s8[1572864]{0:T(1024)(128)(4,1)S(1)}, s32[]{:S(2)}) async-start(s8[14155776]{0:T(1024)(128)(4,1)} %bitcast.12), calls=%async_computation.3 | async-start | bytes 3145728
  121.9 10.3 %collective-permute-start.24 = (bf16[128,1152]{1,0:T(8,128)(2,1)S(1)}, bf16[128,1152]{1,0:T(8,128)(2,1)S(1)}, u32[]{:S(2)}, u32[]{:S(2)}) collective-permute-start(bf16[128,1152]{1,0:T(8,128)(2,1)S(1)} %merge.3), channel_id=1, source_target_pairs={{0,16},{16,0},{1,17},{17,1},{2,18},{18,2},{3,19},{19,3},{4,20},{20... | collective-permute-start | bytes 884744 | tf_op jit(solution)/shard_map/ppermute | solution.py:443
  130.8 9.0 %collective-permute-start.20 = (bf16[128,1152]{1,0:T(8,128)(2,1)S(1)}, bf16[128,1152]{1,0:T(8,128)(2,1)S(1)}, u32[]{:S(2)}, u32[]{:S(2)}) collective-permute-start(bf16[128,1152]{1,0:T(8,128)(2,1)S(1)} %merge.2), channel_id=1, source_target_pairs={{0,16},{16,0},{1,17},{17,1},{2,18},{18,2},{3,19},{19,3},{4,20},{20... | collective-permute-start | bytes 884744 | tf_op jit(solution)/shard_map/ppermute | solution.py:443
  131.3 16.4 %collective-permute-start.11 = (bf16[2,2,128,1152]{3,2,1,0:T(8,128)(2,1)S(1)}, bf16[2,2,128,1152]{3,2,1,0:T(8,128)(2,1)S(1)}, u32[]{:S(2)}, u32[]{:S(2)}) collective-permute-start(bf16[2,2,128,1152]{3,2,1,0:T(8,128)(2,1)S(1)} %pack.2.refs_3_), channel_id=1, source_target_pairs={{4,8},{8,4},{5,9},{9,5},{6,10},{10,6},{7,11},{11,7},{20,24},{24,20... | collective-permute-start | bytes 3538952 | tf_op jit(solution)/shard_map/ppermute | solution.py:443
  132.1 10.5 %collective-permute-start.22 = (bf16[1,2,128,1152]{3,2,1,0:T(8,128)(2,1)S(1)}, bf16[1,2,128,1152]{3,2,1,0:T(8,128)(2,1)S(1)}, u32[]{:S(2)}, u32[]{:S(2)}) collective-permute-start(bf16[1,2,128,1152]{3,2,1,0:T(8,128)(2,1)S(1)} %get-tuple-element.40), channel_id=1, source_target_pairs={{1,2},{2,1},{5,6},{6,5},{9,10},{10,9},{13,14},{14,13},{17,18},{18,... | collective-permute-start | bytes 1769480 | tf_op jit(solution)/shard_map/ppermute | solution.py:443
  139.8 5.4 %collective-permute-start.13 = (bf16[1,2,128,1152]{3,2,1,0:T(8,128)(2,1)S(1)}, bf16[1,2,128,1152]{3,2,1,0:T(8,128)(2,1)S(1)}, u32[]{:S(2)}, u32[]{:S(2)}) collective-permute-start(bf16[1,2,128,1152]{3,2,1,0:T(8,128)(2,1)S(1)} %get-tuple-element.30), channel_id=1, source_target_pairs={{1,2},{2,1},{5,6},{6,5},{9,10},{10,9},{13,14},{14,13},{17,18},{18,... | collective-permute-start | bytes 1769480 | tf_op jit(solution)/shard_map/ppermute | solution.py:443
  142.7 32.7 %collective-permute-start.25 = (bf16[128,3072]{1,0:T(8,128)(2,1)S(1)}, bf16[128,3072]{1,0:T(8,128)(2,1)S(1)}, u32[]{:S(2)}, u32[]{:S(2)}) collective-permute-start(bf16[128,3072]{1,0:T(8,128)(2,1)S(1)} %product.3), channel_id=1, source_target_pairs={{0,16},{16,0},{1,17},{17,1},{2,18},{18,2},{3,19},{19,3},{4,20},{20... | collective-permute-start | bytes 2359304 | tf_op jit(solution)/shard_map/ppermute | solution.py:443
  145.2 36.4 %collective-permute-start.21 = (bf16[128,3072]{1,0:T(8,128)(2,1)S(1)}, bf16[128,3072]{1,0:T(8,128)(2,1)S(1)}, u32[]{:S(2)}, u32[]{:S(2)}) collective-permute-start(bf16[128,3072]{1,0:T(8,128)(2,1)S(1)} %product.2), channel_id=1, source_target_pairs={{0,16},{16,0},{1,17},{17,1},{2,18},{18,2},{3,19},{19,3},{4,20},{20... | collective-permute-start | bytes 2359304 | tf_op jit(solution)/shard_map/ppermute | solution.py:443
  147.7 27.7 %collective-permute-start.23 = (bf16[1,128,1280]{2,1,0:T(8,128)(2,1)S(1)}, bf16[1,128,1280]{2,1,0:T(8,128)(2,1)S(1)}, u32[]{:S(2)}, u32[]{:S(2)}) collective-permute-start(bf16[1,128,1280]{2,1,0:T(8,128)(2,1)S(1)} %edge_rows.7), channel_id=1, source_target_pairs={{1,0},{2,3},{5,4},{6,7},{9,8},{10,11},{13,12},{14,15},{17,16},{18,... | collective-permute-start | bytes 983048 | tf_op jit(solution)/shard_map/ppermute | solution.py:443
  149.5 32.0 %collective-permute-start.17 = (bf16[1,128,1280]{2,1,0:T(8,128)(2,1)S(1)}, bf16[1,128,1280]{2,1,0:T(8,128)(2,1)S(1)}, u32[]{:S(2)}, u32[]{:S(2)}) collective-permute-start(bf16[1,128,1280]{2,1,0:T(8,128)(2,1)S(1)} %edge_rows.6), channel_id=1, source_target_pairs={{1,0},{2,3},{5,4},{6,7},{9,8},{10,11},{13,12},{14,15},{17,16},{18,... | collective-permute-start | bytes 983048 | tf_op jit(solution)/shard_map/ppermute | solution.py:443
  (2 other events, 3.3 us)

commit v5 on v4

--- a/solution.py
+++ b/solution.py
@@ -26,22 +26,39 @@
     return jnp.abs(q // group - k // group)
 
 
-def with_ones(values):
-    return jnp.concatenate([values, jnp.ones_like(values)], axis=1)
-
-
 def softmax_sums(scores, values):
     tops = [jnp.max(functools.reduce(jnp.maximum, tiles), axis=1, keepdims=True) for tiles in scores]
     weights = [
-        jnp.concatenate(
-            [jnp.exp2((s - top) * TO_LOG2).astype(jnp.bfloat16) for s in tiles], axis=1
+        [jnp.exp2((s - top) * TO_LOG2) for s in tiles] for tiles, top in zip(scores, tops)
+    ]
+    sums = [jnp.sum(functools.reduce(jnp.add, w), axis=1, keepdims=True) for w in weights]
+    totals = [
+        dot_nn(
+            jnp.concatenate([x.astype(jnp.bfloat16) for x in w], axis=1),
+            jnp.concatenate(tiles, axis=0),
         )
-        for tiles, top in zip(scores, tops)
+        for w, tiles in zip(weights, values)
     ]
-    sums = [
-        dot_nn(w, with_ones(jnp.concatenate(tiles, axis=0))) for w, tiles in zip(weights, values)
-    ]
-    return [top * TO_LOG2 for top in tops], [x[:, :HEAD] for x in sums], [x[:, HEAD:] for x in sums]
+    return [top * TO_LOG2 for top in tops], totals, sums
+
+
+def place_pieces(stats, values, first):
+    lane = lax.broadcasted_iota(jnp.int32, stats.shape, 1)
+    for n, value in enumerate(values):
+        at = 3 * (first + n)
+        high = value.astype(jnp.bfloat16).astype(jnp.float32)
+        mid = (value - high).astype(jnp.bfloat16).astype(jnp.float32)
+        stats = jnp.where(lane == at, high, stats)
+        stats = jnp.where(lane == at + 1, mid, stats)
+        stats = jnp.where(lane == at + 2, value - high - mid, stats)
+    return stats
+
+
+def spread_pieces(stats, first, heads):
+    lane = lax.broadcasted_iota(jnp.int32, (HEAD, heads * HEAD), 0)
+    at = 3 * (first + lax.broadcasted_iota(jnp.int32, (HEAD, heads * HEAD), 1) // HEAD)
+    pick_head = jnp.where((lane >= at) & (lane < at + 3), 1.0, 0.0).astype(jnp.bfloat16)
+    return dot_nn(stats, pick_head)
 
 
 def edge_kernel(place, q_ref, near_ref, far_ref, out_ref, *, heads, cols_tile, cols):
@@ -50,21 +67,13 @@
     @pl.when((place[2] > 0) & (place[2] < cols - 1))
     def _():
         bias = jnp.where(group_gap(tokens, cols_tile) == 0, 0.0, NEG)
-        lane = lax.broadcasted_iota(jnp.int32, (tokens, HEAD), 1)
         cuts = [slice(n * HEAD, (n + 1) * HEAD) for n in range(heads)]
         tiles = (near_ref, far_ref)
         scores = [[dot_nn(q_ref[:, c], t[0, :, c]) + bias for t in tiles] for c in cuts]
         values = [[t[1, :, c] for t in tiles] for c in cuts]
         tops, totals, weights = softmax_sums(scores, values)
-        stats = jnp.zeros((tokens, HEAD), jnp.float32)
-        for n in range(heads):
-            lse = tops[n] + jnp.log2(weights[n])
-            high = lse.astype(jnp.bfloat16).astype(jnp.float32)
-            mid = (lse - high).astype(jnp.bfloat16).astype(jnp.float32)
-            low = lse - high - mid
-            stats = jnp.where(lane == 3 * n, high, stats)
-            stats = jnp.where(lane == 3 * n + 1, mid, stats)
-            stats = jnp.where(lane == 3 * n + 2, low, stats)
+        lse = [top + jnp.log2(w) for top, w in zip(tops, weights)]
+        stats = place_pieces(jnp.zeros((tokens, HEAD), jnp.float32), lse, 0)
         out_ref[:, :heads * HEAD] = jnp.concatenate(
             [(t / w).astype(jnp.bfloat16) for t, w in zip(totals, weights)], axis=1
         )
@@ -125,36 +134,24 @@
     window_ref[...] = jnp.concatenate([t / w for t, w in zip(totals, weights)], axis=1)
     tops, totals, weights = softmax_sums(row_scores, [v[3:6] + v[9:] for v in values])
     row_ref[...] = jnp.concatenate([t / w for t, w in zip(totals, weights)], axis=1)
-    lane = lax.broadcasted_iota(jnp.int32, (tokens, HEAD), 1)
-    sums = sums_ref[...]
-    for n in range(heads):
-        sums = jnp.where(lane == step * heads + n, tops[n] + jnp.log2(weights[n]), sums)
-    sums_ref[...] = sums
-
-
-def merged(place, window, row, sums, rest, stats, cols, step, heads):
+    lse = [top + jnp.log2(w) for top, w in zip(tops, weights)]
+    sums = place_pieces(sums_ref[...].astype(jnp.float32), lse, step * heads)
+    sums_ref[...] = sums.astype(jnp.bfloat16)
+
+
+def merged(place, window, row, sums, rest, stats, cols, first, heads):
     inner = (place[2] > 0) & (place[2] < cols - 1)
-    lane = lax.broadcasted_iota(jnp.int32, sums.shape, 1)
-    results = []
-    for n in range(heads):
-        cut = slice(n * HEAD, (n + 1) * HEAD)
-        head = step * heads + n
-        near = jnp.sum(jnp.where(lane == head, sums, 0.0), axis=1, keepdims=True)
-        mine = (lane >= 3 * head) & (lane < 3 * head + 3)
-        far = jnp.sum(jnp.where(mine, stats, 0.0), axis=1, keepdims=True)
-        far = jnp.where(inner, NEG, far)
-        both = jnp.maximum(near, far)
-        near, far = jnp.exp2(near - both), jnp.exp2(far - both)
-        share = far / (near + far)
-        axial = row[:, cut] * (1.0 - share) + rest[:, cut].astype(jnp.float32) * share
-        results.append((window[:, cut] + axial).astype(jnp.bfloat16))
-    return jnp.concatenate(results, axis=1)
+    near = spread_pieces(sums, first, heads)
+    far = jnp.where(inner, NEG, spread_pieces(stats, first, heads))
+    share = 1.0 / (1.0 + jnp.exp2(near - far))
+    axial = row + (rest.astype(jnp.float32) - row) * share
+    return (window + axial).astype(jnp.bfloat16)
 
 
 def merge_kernel(place, window_ref, row_ref, sums_ref, rest_ref, stats_ref, out_ref, *, cols):
     out_ref[...] = merged(
-        place, window_ref[...], row_ref[...], sums_ref[...], rest_ref[...],
-        stats_ref[...].astype(jnp.float32), cols, 0, out_ref.shape[1] // HEAD,
+        place, window_ref[...], row_ref[...], sums_ref[...], rest_ref[...], stats_ref[...], cols,
+        0, out_ref.shape[1] // HEAD,
     )
 
 
@@ -171,9 +168,10 @@
     def _():
         total_ref[...] = other_ref[...].astype(jnp.float32)
 
+    heads = window_ref.shape[1] // HEAD
     rows = merged(
-        place, window_ref[...], row_ref[...], sums_ref[...], rest_ref[...],
-        stats_ref[...].astype(jnp.float32), cols, pl.program_id(0), window_ref.shape[1] // HEAD,
+        place, window_ref[...], row_ref[...], sums_ref[...], rest_ref[...], stats_ref[...], cols,
+        pl.program_id(0) * heads, heads,
     )
     add_product(total_ref, rows, weight_ref)
 
@@ -302,7 +300,7 @@
         out_shape=(
             jax.ShapeDtypeStruct((tokens, width), jnp.float32),
             jax.ShapeDtypeStruct((tokens, width), jnp.float32),
-            jax.ShapeDtypeStruct((tokens, HEAD), jnp.float32),
+            jax.ShapeDtypeStruct((tokens, HEAD), jnp.bfloat16),
         ),
         grid_spec=pltpu.PrefetchScalarGridSpec(
             num_scalar_prefetch=1,
@@ -465,11 +463,11 @@
     send("next_own0", own[0], "row", row_others)
     send("pair_own0", own[0], "row", row_pairs)
     send("q0", picked[0], "col", inward)
-    send("far00", sent["near0"][:1], "col", col_others, "other0", "next_own0")
+    send("far00", sent["near0"][:1], "col", col_others, "next_own0")
     send("far01", sent["near0"][1:], "col", col_others, "other0", "next_own0")
     sent["sides0"] = jnp.stack([sent["near0"], sent["other0"]])
     send("next_sides0", sent["sides0"], "row", row_others)
-    send("pair_sides0", sent["sides0"], "row", row_pairs, "pair_own0")
+    send("pair_sides0", sent["sides0"], "row", row_pairs, "pair_own0", "far01")
     edge("00", 0, 0)
     send("rest00", sent["part00"], "col", outward)
     send("near1", own[1], "col", col_pairs, "rest00")
@@ -481,8 +479,8 @@
     sent["merged0"] = merge(tied(place, []), sent["rows00"], sent["rest00"], 0, cols)
     send("theirs0", sent["merged0"], "pair", pair_swap)
     sent["merged1"] = merge(tied(place, []), sent["rows01"], sent["rest01"], 1, cols)
-    send("theirs1", sent["merged1"], "pair", pair_swap)
-    send("next_own1", own[1], "row", row_others, "next_sides0")
+    send("theirs1", sent["merged1"], "pair", pair_swap, "rest00")
+    send("next_own1", own[1], "row", row_others)
     send("pair_own1", own[1], "row", row_pairs)
     send("q1", picked[1], "col", inward, "rest01")
     sent["product0"] = product(tied(sent["theirs0"], []), out_weight, 0)

time: 188 us -> 168 us (0.89)
  waiting for transfers between devices: 106 us -> 77.9 us
  starting transfers between devices: 30.7 us -> 39.8 us
    ppermute x26, waiting for transfers between devices: 106 us -> 77.9 us  [send(): sent[name] = lax.ppermute(tied(value, after), axis, pairs)]
    ppermute x26, starting transfers between devices: 30.7 us -> 39.8 us  [send(): sent[name] = lax.ppermute(tied(value, after), axis, pairs)]
  transfers between devices with their start and end apart: 26 -> 26, of which waited for: 8 -> 9; matrix products, arithmetic and copies ran while one was open for 0% -> 1% of each run, Pallas kernels for 22% -> 25%
where the time goes in v5:
time: 168 us; the launch traced here: 167 us
  waiting for transfers between devices  77.9 us (46%)
  Pallas kernels  47.2 us (28%)
  starting transfers between devices  39.8 us (24%)
    ppermute x26, waiting for transfers between devices, send(): sent[name] = lax.ppermute(tied(value, after), axis, pairs)  77.9 us
    ppermute x26, starting transfers between devices, send(): sent[name] = lax.ppermute(tied(value, after), axis, pairs)  39.8 us
    pallas_call x4, Pallas kernels, rows_attend(): pl.pallas_call(kernel, out_shape=(jax.ShapeDtypeStruct((tokens, width), j...  22.7 us
    pallas_call x2, Pallas kernels, project(): pl.pallas_call(functools.partial(project_kernel, cols=cols), out_shape=ja...  8.58 us
    pallas_call x2, Pallas kernels, product(): pl.pallas_call(product_kernel, out_shape=jax.ShapeDtypeStruct((tokens, mo...  4.16 us
    pallas_call x2, Pallas kernels, pack(): pl.pallas_call(kernel, out_shape=jax.ShapeDtypeStruct((S, 2, tokens, widt...  3.93 us
  transfers between devices with their start and end apart: 26, of which 9 were waited for; matrix products, arithmetic and copies ran while one was open for 1% of the time, Pallas kernels for 25%

profile of v5, /device:TPU:0, one launch (start us, length us, event | category | flops | bytes accessed | tf_op | source)
XLA Modules:
  0.0 167.3 jit_solution(1872630071085117000)
XLA Ops:
  0.1 2.0 %pack.3.refs_3_ = bf16[2,2,128,1152]{3,2,1,0:T(8,128)(2,1)S(1)} custom-call(s32[3]{0:T(128)S(1)} %pad_add_fusion.place, bf16[2,128,2304]{2,1,0:T(8,128)(2,1)} %bitcast.28, bf16[2,128,2304]{2,1,0:T(8,128)(2,1)} %bitcast.30), custom_call_target="tpu_custom_call" | custom-call | bytes 2359296 | tf_op jit(solution)/shard_map/pack/pallas_call | solution.py:218
  2.0 3.1 %collective-permute-start.3 = (bf16[2,2,128,1152]{3,2,1,0:T(8,128)(2,1)S(1)}, bf16[2,2,128,1152]{3,2,1,0:T(8,128)(2,1)S(1)}, u32[]{:S(2)}, u32[]{:S(2)}) collective-permute-start(bf16[2,2,128,1152]{3,2,1,0:T(8,128)(2,1)S(1)} %pack.3.refs_3_), channel_id=1, source_target_pairs={{0,1},{2,3},{1,0},{3,2},{4,5},{6,7},{5,4},{7,6},{8,9},{10,11},{9,8... | collective-permute-start | bytes 3538952 | tf_op jit(solution)/shard_map/ppermute | solution.py:441
  6.6 1.6 pick.2
  8.3 6.3 %collective-permute-start.1 = (bf16[2,128,1152]{2,1,0:T(8,128)(2,1)S(1)}, bf16[2,128,1152]{2,1,0:T(8,128)(2,1)S(1)}, u32[]{:S(2)}, u32[]{:S(2)}) collective-permute-start(bf16[2,128,1152]{2,1,0:T(8,128)(2,1)S(1)} %pick.2), channel_id=1, source_target_pairs={{0,1},{3,2},{4,5},{7,6},{8,9},{11,10},{12,13},{15,14},{16,17},{19,... | collective-permute-start | bytes 1769480 | tf_op jit(solution)/shard_map/ppermute | solution.py:441
  14.5 17.0 %collective-permute-done.3 = bf16[2,2,128,1152]{3,2,1,0:T(8,128)(2,1)S(1)} collective-permute-done((bf16[2,2,128,1152]{3,2,1,0:T(8,128)(2,1)S(1)}, bf16[2,2,128,1152]{3,2,1,0:T(8,128)(2,1)S(1)}, u32[]{:S(2)}, u32[]{:S(2)}) %collective-permute-start.3) | collective-permute-done | bytes 1179680 | tf_op jit(solution)/shard_map/ppermute | solution.py:441
  33.1 9.9 %collective-permute-done.1.q_ref = bf16[2,128,1152]{2,1,0:T(8,128)(2,1)S(1)} collective-permute-done((bf16[2,128,1152]{2,1,0:T(8,128)(2,1)S(1)}, bf16[2,128,1152]{2,1,0:T(8,128)(2,1)S(1)}, u32[]{:S(2)}, u32[]{:S(2)}) %collective-permute-start.1) | collective-permute-done | bytes 589856 | tf_op jit(solution)/shard_map/ppermute | solution.py:441
  43.6 1.3 collective-permute-start.6
  45.9 2.0 %pack.2.refs_3_ = bf16[2,2,128,1152]{3,2,1,0:T(8,128)(2,1)S(1)} custom-call(s32[3]{0:T(128)S(1)} %pad_add_fusion.place, bf16[2,128,2304]{2,1,0:T(8,128)(2,1)} %bitcast.29, bf16[2,128,2304]{2,1,0:T(8,128)(2,1)} %bitcast.31), custom_call_target="tpu_custom_call" | custom-call | bytes 2359296 | tf_op jit(solution)/shard_map/pack/pallas_call | solution.py:218
  48.6 11.3 %collective-permute-done.6.rest_ref.stats_ref = bf16[1,128,1280]{2,1,0:T(8,128)(2,1)S(1)} collective-permute-done((bf16[1,128,1280]{2,1,0:T(8,128)(2,1)S(1)}, bf16[1,128,1280]{2,1,0:T(8,128)(2,1)S(1)}, u32[]{:S(2)}, u32[]{:S(2)}) %collective-permute-start.6) | collective-permute-done | bytes 327712 | tf_op jit(solution)/shard_map/ppermute | solution.py:441
  59.9 1.6 collective-permute-start.7
  62.3 4.7 %collective-permute-start.18 = (bf16[2,2,2,128,1152]{4,3,2,1,0:T(8,128)(2,1)S(1)}, bf16[2,2,2,128,1152]{4,3,2,1,0:T(8,128)(2,1)S(1)}, u32[]{:S(2)}, u32[]{:S(2)}) collective-permute-start(bf16[2,2,2,128,1152]{4,3,2,1,0:T(8,128)(2,1)S(1)} %pad_maximum_fusion.1.refs_4_.refs_5_), channel_id=1, source_target_pairs={{0,4},{8,12},{4,0},{12,8},{1,5},{9,13},{5,1},{13,9},{2,6},{10,14},... | collective-permute-start | bytes 7077896 | tf_op jit(solution)/shard_map/ppermute | solution.py:441
  67.6 1.3 collective-permute-start.14
  68.9 18.5 %collective-permute-done.7 = bf16[2,2,128,1152]{3,2,1,0:T(8,128)(2,1)S(1)} collective-permute-done((bf16[2,2,128,1152]{3,2,1,0:T(8,128)(2,1)S(1)}, bf16[2,2,128,1152]{3,2,1,0:T(8,128)(2,1)S(1)}, u32[]{:S(2)}, u32[]{:S(2)}) %collective-permute-start.7) | collective-permute-done | bytes 1179680 | tf_op jit(solution)/shard_map/ppermute | solution.py:441
  88.5 2.4 %collective-permute-start.9 = (bf16[2,2,2,128,1152]{4,3,2,1,0:T(8,128)(2,1)S(1)}, bf16[2,2,2,128,1152]{4,3,2,1,0:T(8,128)(2,1)S(1)}, u32[]{:S(2)}, u32[]{:S(2)}) collective-permute-start(bf16[2,2,2,128,1152]{4,3,2,1,0:T(8,128)(2,1)S(1)} %pad_maximum_fusion.refs_4_.refs_5_), channel_id=1, source_target_pairs={{0,4},{8,12},{4,0},{12,8},{1,5},{9,13},{5,1},{13,9},{2,6},{10,14},... | collective-permute-start | bytes 7077896 | tf_op jit(solution)/shard_map/ppermute | solution.py:441
  90.9 4.6 %collective-permute-done.14.rest_ref.stats_ref = bf16[1,128,1280]{2,1,0:T(8,128)(2,1)S(1)} collective-permute-done((bf16[1,128,1280]{2,1,0:T(8,128)(2,1)S(1)}, bf16[1,128,1280]{2,1,0:T(8,128)(2,1)S(1)}, u32[]{:S(2)}, u32[]{:S(2)}) %collective-permute-start.14) | collective-permute-done | bytes 327712 | tf_op jit(solution)/shard_map/ppermute | solution.py:441
  96.5 1.6 pick.3
  98.2 3.3 %collective-permute-start.15 = (bf16[2,128,1152]{2,1,0:T(8,128)(2,1)S(1)}, bf16[2,128,1152]{2,1,0:T(8,128)(2,1)S(1)}, u32[]{:S(2)}, u32[]{:S(2)}) collective-permute-start(bf16[2,128,1152]{2,1,0:T(8,128)(2,1)S(1)} %pick.3), channel_id=1, source_target_pairs={{0,1},{3,2},{4,5},{7,6},{8,9},{11,10},{12,13},{15,14},{16,17},{19,... | collective-permute-start | bytes 1769480 | tf_op jit(solution)/shard_map/ppermute | solution.py:441
  103.4 5.9 %rows.7 = (f32[128,1152]{1,0:T(8,128)S(1)}, f32[128,1152]{1,0:T(8,128)S(1)}, bf16[128,128]{1,0:T(8,128)(2,1)S(1)}) custom-call(s32[3]{0:T(128)S(1)} %pad_add_fusion.place, s32[9]{0:T(128)S(1)} %bitcast.16, s32[18]{0:T(128)S(1)} %copy-done.1, bf16[2,128,2304]{2,1,0:T(8,128)(2,1)} %bitcast.22, bf16[2,2,128,1152]{3,2,1,0:T(8,128)(2,1)S(1)} %collective-permute-done.17.refs_0_, ...), custom_call_target="tpu_custom_call" | custom-call | flops 868220928 | bytes 7962624 | tf_op jit(solution)/shard_map/rows/pallas_call | solution.py:298
  110.4 1.5 collective-permute-start.24
  112.0 5.6 %rows.5 = (f32[128,1152]{1,0:T(8,128)S(1)}, f32[128,1152]{1,0:T(8,128)S(1)}, bf16[128,128]{1,0:T(8,128)(2,1)S(1)}) custom-call(s32[3]{0:T(128)S(1)} %pad_add_fusion.place, s32[9]{0:T(128)S(1)} %bitcast.17, s32[18]{0:T(128)S(1)} %copy-done.1, bf16[2,128,2304]{2,1,0:T(8,128)(2,1)} %bitcast.23, bf16[2,2,128,1152]{3,2,1,0:T(8,128)(2,1)S(1)} %collective-permute-done.17.refs_0_, ...), custom_call_target="tpu_custom_call" | custom-call | flops 868220928 | bytes 7962624 | tf_op jit(solution)/shard_map/rows/pallas_call | solution.py:298
  118.6 1.1 collective-permute-start.20
  120.5 2.1 %product.3 = bf16[128,3072]{1,0:T(8,128)(2,1)S(1)} custom-call(bf16[128,1152]{1,0:T(8,128)(2,1)S(1)} %collective-permute-done.24.rows_ref, bf16[2,1152,3072]{2,1,0:T(8,128)(2,1)S(1)} %bitcast.13), custom_call_target="tpu_custom_call" | custom-call | flops 905969664 | bytes 7077888 | tf_op jit(solution)/shard_map/product/pallas_call | solution.py:401
  122.6 5.0 %collective-permute-done.20.rows_ref = bf16[128,1152]{1,0:T(8,128)(2,1)S(1)} collective-permute-done((bf16[128,1152]{1,0:T(8,128)(2,1)S(1)}, bf16[128,1152]{1,0:T(8,128)(2,1)S(1)}, u32[]{:S(2)}, u32[]{:S(2)}) %collective-permute-start.20) | collective-permute-done | bytes 294944 | tf_op jit(solution)/shard_map/ppermute | solution.py:441
  128.6 2.1 %product.2 = bf16[128,3072]{1,0:T(8,128)(2,1)S(1)} custom-call(bf16[128,1152]{1,0:T(8,128)(2,1)S(1)} %collective-permute-done.20.rows_ref, bf16[2,1152,3072]{2,1,0:T(8,128)(2,1)S(1)} %bitcast.13), custom_call_target="tpu_custom_call" | custom-call | flops 905969664 | bytes 7077888 | tf_op jit(solution)/shard_map/product/pallas_call | solution.py:401
  132.5 1.3 collective-permute-start.23
  134.4 1.3 collective-permute-start.16
  135.7 5.6 %rows.6 = (f32[128,1152]{1,0:T(8,128)S(1)}, f32[128,1152]{1,0:T(8,128)S(1)}, bf16[128,128]{1,0:T(8,128)(2,1)S(1)}) custom-call(s32[3]{0:T(128)S(1)} %pad_add_fusion.place, s32[9]{0:T(128)S(1)} %bitcast.18, s32[18]{0:T(128)S(1)} %copy-done.1, bf16[2,128,2304]{2,1,0:T(8,128)(2,1)} %bitcast.24, bf16[2,2,128,1152]{3,2,1,0:T(8,128)(2,1)} %collective-permute-done.refs_0_, ...), custom_call_target="tpu_custom_call" | custom-call | flops 868220928 | bytes 7962624 | tf_op jit(solution)/shard_map/rows/pallas_call | solution.py:298
  141.3 5.6 %rows.4 = (f32[128,1152]{1,0:T(8,128)S(1)}, f32[128,1152]{1,0:T(8,128)S(1)}, bf16[128,128]{1,0:T(8,128)(2,1)S(1)}) custom-call(s32[3]{0:T(128)S(1)} %pad_add_fusion.place, s32[9]{0:T(128)S(1)} %bitcast.19, s32[18]{0:T(128)S(1)} %copy-done.1, bf16[2,128,2304]{2,1,0:T(8,128)(2,1)} %bitcast.25, bf16[2,2,128,1152]{3,2,1,0:T(8,128)(2,1)} %collective-permute-done.refs_0_, ...), custom_call_target="tpu_custom_call" | custom-call | flops 868220928 | bytes 7962624 | tf_op jit(solution)/shard_map/rows/pallas_call | solution.py:298
  147.0 1.5 collective-permute-done.23.rest_ref.stats_ref
  148.5 4.3 %project.2.refs_0_ = bf16[2,128,3072]{2,1,0:T(8,128)(2,1)} custom-call(s32[3]{0:T(128)S(1)} %pad_add_fusion.place, f32[128,1152]{1,0:T(8,128)S(1)} %get-tuple-element.41.window_ref, f32[128,1152]{1,0:T(8,128)S(1)} %get-tuple-element.42.row_ref, bf16[128,128]{1,0:T(8,128)(2,1)S(1)} %get-tuple-element.43.sums_ref, ...), custom_call_target="tpu_custom_call" | custom-call | flops 905969664 | bytes 7077888 | tf_op jit(solution)/shard_map/project/pallas_call | solution.py:369
  153.5 9.5 %collective-permute-done.21.other_ref = bf16[128,3072]{1,0:T(8,128)(2,1)S(1)} collective-permute-done((bf16[128,3072]{1,0:T(8,128)(2,1)S(1)}, bf16[128,3072]{1,0:T(8,128)(2,1)S(1)}, u32[]{:S(2)}, u32[]{:S(2)}) %collective-permute-start.21) | collective-permute-done | bytes 786464 | tf_op jit(solution)/shard_map/ppermute | solution.py:441
  163.0 4.3 %project.3 = bf16[2,128,3072]{2,1,0:T(8,128)(2,1)} custom-call(s32[3]{0:T(128)S(1)} %pad_add_fusion.place, f32[128,1152]{1,0:T(8,128)S(1)} %get-tuple-element.30.window_ref, f32[128,1152]{1,0:T(8,128)S(1)} %get-tuple-element.31.row_ref, bf16[128,128]{1,0:T(8,128)(2,1)S(1)} %get-tuple-element.32.sums_ref, ...), custom_call_target="tpu_custom_call", output_to_operand_aliasing={{}: (8, {})} | custom-call | flops 905969664 | bytes 7077888 | tf_op jit(solution)/shard_map/project/pallas_call | solution.py:369
  (58 shorter events, 17.6 us)
Async XLA Ops:
  2.0 29.5 %collective-permute-start.3 = (bf16[2,2,128,1152]{3,2,1,0:T(8,128)(2,1)S(1)}, bf16[2,2,128,1152]{3,2,1,0:T(8,128)(2,1)S(1)}, u32[]{:S(2)}, u32[]{:S(2)}) collective-permute-start(bf16[2,2,128,1152]{3,2,1,0:T(8,128)(2,1)S(1)} %pack.3.refs_3_), channel_id=1, source_target_pairs={{0,1},{2,3},{1,0},{3,2},{4,5},{6,7},{5,4},{7,6},{8,9},{10,11},{9,8... | collective-permute-start | bytes 3538952 | tf_op jit(solution)/shard_map/ppermute | solution.py:441
  5.1 26.5 %collective-permute-start.4 = (bf16[2,2,128,1152]{3,2,1,0:T(8,128)(2,1)S(1)}, bf16[2,2,128,1152]{3,2,1,0:T(8,128)(2,1)S(1)}, u32[]{:S(2)}, u32[]{:S(2)}) collective-permute-start(bf16[2,2,128,1152]{3,2,1,0:T(8,128)(2,1)S(1)} %pack.3.refs_3_), channel_id=1, source_target_pairs={{4,8},{8,4},{5,9},{9,5},{6,10},{10,6},{7,11},{11,7},{20,24},{24,20... | collective-permute-start | bytes 3538952 | tf_op jit(solution)/shard_map/ppermute | solution.py:441
  5.9 26.5 %collective-permute-start.2 = (bf16[2,2,128,1152]{3,2,1,0:T(8,128)(2,1)S(1)}, bf16[2,2,128,1152]{3,2,1,0:T(8,128)(2,1)S(1)}, u32[]{:S(2)}, u32[]{:S(2)}) collective-permute-start(bf16[2,2,128,1152]{3,2,1,0:T(8,128)(2,1)S(1)} %pack.3.refs_3_), channel_id=1, source_target_pairs={{1,2},{2,1},{5,6},{6,5},{9,10},{10,9},{13,14},{14,13},{17,18},{18,... | collective-permute-start | bytes 3538952 | tf_op jit(solution)/shard_map/ppermute | solution.py:441
  8.3 34.7 %collective-permute-start.1 = (bf16[2,128,1152]{2,1,0:T(8,128)(2,1)S(1)}, bf16[2,128,1152]{2,1,0:T(8,128)(2,1)S(1)}, u32[]{:S(2)}, u32[]{:S(2)}) collective-permute-start(bf16[2,128,1152]{2,1,0:T(8,128)(2,1)S(1)} %pick.2), channel_id=1, source_target_pairs={{0,1},{3,2},{4,5},{7,6},{8,9},{11,10},{12,13},{15,14},{16,17},{19,... | collective-permute-start | bytes 1769480 | tf_op jit(solution)/shard_map/ppermute | solution.py:441
  31.6 11.4 %collective-permute-start.5 = (bf16[1,2,128,1152]{3,2,1,0:T(8,128)(2,1)S(1)}, bf16[1,2,128,1152]{3,2,1,0:T(8,128)(2,1)S(1)}, u32[]{:S(2)}, u32[]{:S(2)}) collective-permute-start(bf16[1,2,128,1152]{3,2,1,0:T(8,128)(2,1)S(1)} %get-tuple-element.26), channel_id=1, source_target_pairs={{1,2},{2,1},{5,6},{6,5},{9,10},{10,9},{13,14},{14,13},{17,18},{18,... | collective-permute-start | bytes 1769480 | tf_op jit(solution)/shard_map/ppermute | solution.py:441
  32.3 29.2 %collective-permute-start.17 = (bf16[2,2,128,1152]{3,2,1,0:T(8,128)(2,1)S(1)}, bf16[2,2,128,1152]{3,2,1,0:T(8,128)(2,1)S(1)}, u32[]{:S(2)}, u32[]{:S(2)}) collective-permute-start(bf16[2,2,128,1152]{3,2,1,0:T(8,128)(2,1)S(1)} %pack.3.refs_3_), channel_id=1, source_target_pairs={{0,4},{8,12},{4,0},{12,8},{1,5},{9,13},{5,1},{13,9},{2,6},{10,14},... | collective-permute-start | bytes 3538952 | tf_op jit(solution)/shard_map/ppermute | solution.py:441
  32.4 29.9 %collective-permute-start.13 = (bf16[1,2,128,1152]{3,2,1,0:T(8,128)(2,1)S(1)}, bf16[1,2,128,1152]{3,2,1,0:T(8,128)(2,1)S(1)}, u32[]{:S(2)}, u32[]{:S(2)}) collective-permute-start(bf16[1,2,128,1152]{3,2,1,0:T(8,128)(2,1)S(1)} %get-tuple-element.33), channel_id=1, source_target_pairs={{1,2},{2,1},{5,6},{6,5},{9,10},{10,9},{13,14},{14,13},{17,18},{18,... | collective-permute-start | bytes 1769480 | tf_op jit(solution)/shard_map/ppermute | solution.py:441
  43.6 16.4 %collective-permute-start.6 = (bf16[1,128,1280]{2,1,0:T(8,128)(2,1)S(1)}, bf16[1,128,1280]{2,1,0:T(8,128)(2,1)S(1)}, u32[]{:S(2)}, u32[]{:S(2)}) collective-permute-start(bf16[1,128,1280]{2,1,0:T(8,128)(2,1)S(1)} %edge_rows.4), channel_id=1, source_target_pairs={{1,0},{2,3},{5,4},{6,7},{9,8},{10,11},{13,12},{14,15},{17,16},{18,... | collective-permute-start | bytes 983048 | tf_op jit(solution)/shard_map/ppermute | solution.py:441
  45.1 53.1 %collective-permute-start.19 = (bf16[2,2,2,128,1152]{4,3,2,1,0:T(8,128)(2,1)S(1)}, bf16[2,2,2,128,1152]{4,3,2,1,0:T(8,128)(2,1)S(1)}, u32[]{:S(2)}, u32[]{:S(2)}) collective-permute-start(bf16[2,2,2,128,1152]{4,3,2,1,0:T(8,128)(2,1)S(1)} %pad_maximum_fusion.1.refs_4_.refs_5_), channel_id=1, source_target_pairs={{4,8},{8,4},{5,9},{9,5},{6,10},{10,6},{7,11},{11,7},{20,24},{24,20... | collective-permute-start | bytes 7077896 | tf_op jit(solution)/shard_map/ppermute | solution.py:441
  47.9 19.6 %collective-permute-start.8 = (bf16[2,2,128,1152]{3,2,1,0:T(8,128)(2,1)S(1)}, bf16[2,2,128,1152]{3,2,1,0:T(8,128)(2,1)S(1)}, u32[]{:S(2)}, u32[]{:S(2)}) collective-permute-start(bf16[2,2,128,1152]{3,2,1,0:T(8,128)(2,1)S(1)} %pack.2.refs_3_), channel_id=1, source_target_pairs={{1,2},{2,1},{5,6},{6,5},{9,10},{10,9},{13,14},{14,13},{17,18},{18,... | collective-permute-start | bytes 3538952 | tf_op jit(solution)/shard_map/ppermute | solution.py:441
  59.9 27.5 %collective-permute-start.7 = (bf16[2,2,128,1152]{3,2,1,0:T(8,128)(2,1)S(1)}, bf16[2,2,128,1152]{3,2,1,0:T(8,128)(2,1)S(1)}, u32[]{:S(2)}, u32[]{:S(2)}) collective-permute-start(bf16[2,2,128,1152]{3,2,1,0:T(8,128)(2,1)S(1)} %pack.2.refs_3_), channel_id=1, source_target_pairs={{0,1},{2,3},{1,0},{3,2},{4,5},{6,7},{5,4},{7,6},{8,9},{10,11},{9,8... | collective-permute-start | bytes 3538952 | tf_op jit(solution)/shard_map/ppermute | solution.py:441
  61.5 26.9 %collective-permute-start.10 = (bf16[2,2,128,1152]{3,2,1,0:T(8,128)(2,1)S(1)}, bf16[2,2,128,1152]{3,2,1,0:T(8,128)(2,1)S(1)}, u32[]{:S(2)}, u32[]{:S(2)}) collective-permute-start(bf16[2,2,128,1152]{3,2,1,0:T(8,128)(2,1)S(1)} %pack.2.refs_3_), channel_id=1, source_target_pairs={{4,8},{8,4},{5,9},{9,5},{6,10},{10,6},{7,11},{11,7},{20,24},{24,20... | collective-permute-start | bytes 3538952 | tf_op jit(solution)/shard_map/ppermute | solution.py:441
  62.3 40.4 %collective-permute-start.18 = (bf16[2,2,2,128,1152]{4,3,2,1,0:T(8,128)(2,1)S(1)}, bf16[2,2,2,128,1152]{4,3,2,1,0:T(8,128)(2,1)S(1)}, u32[]{:S(2)}, u32[]{:S(2)}) collective-permute-start(bf16[2,2,2,128,1152]{4,3,2,1,0:T(8,128)(2,1)S(1)} %pad_maximum_fusion.1.refs_4_.refs_5_), channel_id=1, source_target_pairs={{0,4},{8,12},{4,0},{12,8},{1,5},{9,13},{5,1},{13,9},{2,6},{10,14},... | collective-permute-start | bytes 7077896 | tf_op jit(solution)/shard_map/ppermute | solution.py:441
  67.6 27.9 %collective-permute-start.14 = (bf16[1,128,1280]{2,1,0:T(8,128)(2,1)S(1)}, bf16[1,128,1280]{2,1,0:T(8,128)(2,1)S(1)}, u32[]{:S(2)}, u32[]{:S(2)}) collective-permute-start(bf16[1,128,1280]{2,1,0:T(8,128)(2,1)S(1)} %edge_rows.5), channel_id=1, source_target_pairs={{1,0},{2,3},{5,4},{6,7},{9,8},{10,11},{13,12},{14,15},{17,16},{18,... | collective-permute-start | bytes 983048 | tf_op jit(solution)/shard_map/ppermute | solution.py:441
  87.6 46.7 %collective-permute-start.11 = (bf16[2,2,2,128,1152]{4,3,2,1,0:T(8,128)(2,1)S(1)}, bf16[2,2,2,128,1152]{4,3,2,1,0:T(8,128)(2,1)S(1)}, u32[]{:S(2)}, u32[]{:S(2)}) collective-permute-start(bf16[2,2,2,128,1152]{4,3,2,1,0:T(8,128)(2,1)S(1)} %pad_maximum_fusion.refs_4_.refs_5_), channel_id=1, source_target_pairs={{4,8},{8,4},{5,9},{9,5},{6,10},{10,6},{7,11},{11,7},{20,24},{24,20... | collective-permute-start | bytes 7077896 | tf_op jit(solution)/shard_map/ppermute | solution.py:441
  88.5 47.2 %collective-permute-start.9 = (bf16[2,2,2,128,1152]{4,3,2,1,0:T(8,128)(2,1)S(1)}, bf16[2,2,2,128,1152]{4,3,2,1,0:T(8,128)(2,1)S(1)}, u32[]{:S(2)}, u32[]{:S(2)}) collective-permute-start(bf16[2,2,2,128,1152]{4,3,2,1,0:T(8,128)(2,1)S(1)} %pad_maximum_fusion.refs_4_.refs_5_), channel_id=1, source_target_pairs={{0,4},{8,12},{4,0},{12,8},{1,5},{9,13},{5,1},{13,9},{2,6},{10,14},... | collective-permute-start | bytes 7077896 | tf_op jit(solution)/shard_map/ppermute | solution.py:441
  95.4 15.0 %collective-permute-start = (bf16[2,2,128,1152]{3,2,1,0:T(8,128)(2,1)S(1)}, bf16[2,2,128,1152]{3,2,1,0:T(8,128)(2,1)}, u32[]{:S(2)}, u32[]{:S(2)}) collective-permute-start(bf16[2,2,128,1152]{3,2,1,0:T(8,128)(2,1)S(1)} %pack.2.refs_3_), channel_id=1, source_target_pairs={{0,4},{8,12},{4,0},{12,8},{1,5},{9,13},{5,1},{13,9},{2,6},{10,14},... | collective-permute-start | bytes 3538952 | tf_op jit(solution)/shard_map/ppermute | solution.py:441
  98.2 5.2 %copy-start = (s32[1,1,1,9]{3,2,1,0:T(1,128)S(1)}, s32[1,1,1,9]{3,2,1,0:T(1,128)}, u32[]{:S(2)}) copy-start(s32[1,1,1,9]{3,2,1,0:T(1,128)} %param.9) | copy-start | bytes 112
  98.2 5.2 %copy-start.1 = (s32[18]{0:T(128)S(1)}, s32[18]{0:T(128)}, u32[]{:S(2)}) copy-start(s32[18]{0:T(128)} %reach.7) | copy-start | bytes 220
  98.2 20.4 %collective-permute-start.15 = (bf16[2,128,1152]{2,1,0:T(8,128)(2,1)S(1)}, bf16[2,128,1152]{2,1,0:T(8,128)(2,1)S(1)}, u32[]{:S(2)}, u32[]{:S(2)}) collective-permute-start(bf16[2,128,1152]{2,1,0:T(8,128)(2,1)S(1)} %pick.3), channel_id=1, source_target_pairs={{0,1},{3,2},{4,5},{7,6},{8,9},{11,10},{12,13},{15,14},{16,17},{19,... | collective-permute-start | bytes 1769480 | tf_op jit(solution)/shard_map/ppermute | solution.py:441
  102.7 28.0 %collective-permute-start.22 = (bf16[1,2,128,1152]{3,2,1,0:T(8,128)(2,1)}, bf16[1,2,128,1152]{3,2,1,0:T(8,128)(2,1)S(1)}, u32[]{:S(2)}, u32[]{:S(2)}) collective-permute-start(bf16[1,2,128,1152]{3,2,1,0:T(8,128)(2,1)} %get-tuple-element.40), channel_id=1, source_target_pairs={{1,2},{2,1},{5,6},{6,5},{9,10},{10,9},{13,14},{14,13},{17,18},{18,... | collective-permute-start | bytes 1769480 | tf_op jit(solution)/shard_map/ppermute | solution.py:441
  103.4 17.1 %slice-start = ((s8[14155776]{0:T(1024)(128)(4,1)}), s8[4194304]{0:T(1024)(128)(4,1)S(1)}, s32[]{:S(2)}) async-start(s8[14155776]{0:T(1024)(128)(4,1)} %bitcast.12), calls=%async_computation | async-start | bytes 8388608
  103.4 17.1 %slice-start.1 = ((s8[14155776]{0:T(1024)(128)(4,1)}), s8[4194304]{0:T(1024)(128)(4,1)S(1)}, s32[]{:S(2)}) async-start(s8[14155776]{0:T(1024)(128)(4,1)} %bitcast.12), calls=%async_computation.1 | async-start | bytes 8388608
  110.4 10.1 %slice-start.2 = ((s8[14155776]{0:T(1024)(128)(4,1)}), s8[4194304]{0:T(1024)(128)(4,1)S(1)}, s32[]{:S(2)}) async-start(s8[14155776]{0:T(1024)(128)(4,1)} %bitcast.12), calls=%async_computation.2 | async-start | bytes 8388608
  110.4 10.1 %slice-start.3 = ((s8[14155776]{0:T(1024)(128)(4,1)}), s8[1572864]{0:T(1024)(128)(4,1)S(1)}, s32[]{:S(2)}) async-start(s8[14155776]{0:T(1024)(128)(4,1)} %bitcast.12), calls=%async_computation.3 | async-start | bytes 3145728
  110.4 9.4 %collective-permute-start.24 = (bf16[128,1152]{1,0:T(8,128)(2,1)S(1)}, bf16[128,1152]{1,0:T(8,128)(2,1)S(1)}, u32[]{:S(2)}, u32[]{:S(2)}) collective-permute-start(bf16[128,1152]{1,0:T(8,128)(2,1)S(1)} %merge.3), channel_id=1, source_target_pairs={{0,16},{16,0},{1,17},{17,1},{2,18},{18,2},{3,19},{19,3},{4,20},{20... | collective-permute-start | bytes 884744 | tf_op jit(solution)/shard_map/ppermute | solution.py:441
  118.6 8.9 %collective-permute-start.20 = (bf16[128,1152]{1,0:T(8,128)(2,1)S(1)}, bf16[128,1152]{1,0:T(8,128)(2,1)S(1)}, u32[]{:S(2)}, u32[]{:S(2)}) collective-permute-start(bf16[128,1152]{1,0:T(8,128)(2,1)S(1)} %merge.2), channel_id=1, source_target_pairs={{0,16},{16,0},{1,17},{17,1},{2,18},{18,2},{3,19},{19,3},{4,20},{20... | collective-permute-start | bytes 884744 | tf_op jit(solution)/shard_map/ppermute | solution.py:441
  119.8 12.7 %collective-permute-start.12 = (bf16[1,2,128,1152]{3,2,1,0:T(8,128)(2,1)S(1)}, bf16[1,2,128,1152]{3,2,1,0:T(8,128)(2,1)S(1)}, u32[]{:S(2)}, u32[]{:S(2)}) collective-permute-start(bf16[1,2,128,1152]{3,2,1,0:T(8,128)(2,1)S(1)} %copy-done.2), channel_id=1, source_target_pairs={{1,2},{2,1},{5,6},{6,5},{9,10},{10,9},{13,14},{14,13},{17,18},{18,... | collective-permute-start | bytes 1769480 | tf_op jit(solution)/shard_map/ppermute | solution.py:441
  127.6 20.9 %collective-permute-start.25 = (bf16[128,3072]{1,0:T(8,128)(2,1)S(1)}, bf16[128,3072]{1,0:T(8,128)(2,1)S(1)}, u32[]{:S(2)}, u32[]{:S(2)}) collective-permute-start(bf16[128,3072]{1,0:T(8,128)(2,1)S(1)} %product.3), channel_id=1, source_target_pairs={{0,16},{16,0},{1,17},{17,1},{2,18},{18,2},{3,19},{19,3},{4,20},{20... | collective-permute-start | bytes 2359304 | tf_op jit(solution)/shard_map/ppermute | solution.py:441
  130.7 32.3 %collective-permute-start.21 = (bf16[128,3072]{1,0:T(8,128)(2,1)S(1)}, bf16[128,3072]{1,0:T(8,128)(2,1)S(1)}, u32[]{:S(2)}, u32[]{:S(2)}) collective-permute-start(bf16[128,3072]{1,0:T(8,128)(2,1)S(1)} %product.2), channel_id=1, source_target_pairs={{0,16},{16,0},{1,17},{17,1},{2,18},{18,2},{3,19},{19,3},{4,20},{20... | collective-permute-start | bytes 2359304 | tf_op jit(solution)/shard_map/ppermute | solution.py:441
  132.5 16.0 %collective-permute-start.23 = (bf16[1,128,1280]{2,1,0:T(8,128)(2,1)S(1)}, bf16[1,128,1280]{2,1,0:T(8,128)(2,1)S(1)}, u32[]{:S(2)}, u32[]{:S(2)}) collective-permute-start(bf16[1,128,1280]{2,1,0:T(8,128)(2,1)S(1)} %edge_rows.7), channel_id=1, source_target_pairs={{1,0},{2,3},{5,4},{6,7},{9,8},{10,11},{13,12},{14,15},{17,16},{18,... | collective-permute-start | bytes 983048 | tf_op jit(solution)/shard_map/ppermute | solution.py:441
  134.4 19.1 %collective-permute-start.16 = (bf16[1,128,1280]{2,1,0:T(8,128)(2,1)S(1)}, bf16[1,128,1280]{2,1,0:T(8,128)(2,1)S(1)}, u32[]{:S(2)}, u32[]{:S(2)}) collective-permute-start(bf16[1,128,1280]{2,1,0:T(8,128)(2,1)S(1)} %edge_rows.6), channel_id=1, source_target_pairs={{1,0},{2,3},{5,4},{6,7},{9,8},{10,11},{13,12},{14,15},{17,16},{18,... | collective-permute-start | bytes 983048 | tf_op jit(solution)/shard_map/ppermute | solution.py:441
  (1 other events, 2.2 us)

commit v6 on v5

--- a/solution.py
+++ b/solution.py
@@ -11,6 +11,7 @@
 NEG = -1e30
 VMEM_LIMIT = 24 * 1024 * 1024
 HEAD = 128
+FOLD = 16
 TO_LOG2 = HEAD ** (-0.5) * math.log2(math.e)
 ANY = pl.BlockSpec(memory_space=pl.ANY)
 SMEM = pl.BlockSpec(memory_space=pltpu.SMEM)
@@ -61,10 +62,38 @@
     return dot_nn(stats, pick_head)
 
 
-def edge_kernel(place, q_ref, near_ref, far_ref, out_ref, *, heads, cols_tile, cols):
+def fold_stats(stats, width):
+    groups = [stats[start:start + FOLD] for start in range(0, stats.shape[0], FOLD)]
+    rest = width // HEAD - len(groups)
+    return jnp.concatenate(groups + [jnp.zeros_like(groups[0])] * rest, axis=1)
+
+
+def unfold_stats(folded, tokens):
+    return jnp.concatenate(
+        [folded[:, n * HEAD:(n + 1) * HEAD] for n in range(tokens // FOLD)], axis=0
+    )
+
+
+def edge_kernel(place, q_ref, near_ref, far_ref, *refs, heads, cols_tile, cols):
     tokens = q_ref.shape[0]
-
-    @pl.when((place[2] > 0) & (place[2] < cols - 1))
+    out_ref = refs[-1]
+    first = 0
+    if len(refs) > 1:
+        next_ref, next_q_ref = refs[:2]
+        first = 2 * tokens
+        out_ref[:tokens] = next_ref[0]
+        out_ref[tokens:first] = next_ref[1]
+    inner = (place[2] > 0) & (place[2] < cols - 1)
+
+    @pl.when(jnp.logical_not(inner))
+    def _():
+        if first:
+            out_ref[first:first + tokens] = next_q_ref[...]
+        else:
+            out_ref[:tokens] = jnp.zeros((tokens, out_ref.shape[1]), out_ref.dtype)
+        out_ref[first + tokens:] = jnp.zeros((FOLD, out_ref.shape[1]), out_ref.dtype)
+
+    @pl.when(inner)
     def _():
         bias = jnp.where(group_gap(tokens, cols_tile) == 0, 0.0, NEG)
         cuts = [slice(n * HEAD, (n + 1) * HEAD) for n in range(heads)]
@@ -74,10 +103,10 @@
         tops, totals, weights = softmax_sums(scores, values)
         lse = [top + jnp.log2(w) for top, w in zip(tops, weights)]
         stats = place_pieces(jnp.zeros((tokens, HEAD), jnp.float32), lse, 0)
-        out_ref[:, :heads * HEAD] = jnp.concatenate(
+        out_ref[first:first + tokens] = jnp.concatenate(
             [(t / w).astype(jnp.bfloat16) for t, w in zip(totals, weights)], axis=1
         )
-        out_ref[:, heads * HEAD:] = stats.astype(jnp.bfloat16)
+        out_ref[first + tokens:] = fold_stats(stats.astype(jnp.bfloat16), out_ref.shape[1])
 
 
 def fill_bias(bias_ref, frame_tokens, cols_tile):
@@ -150,8 +179,8 @@
 
 def merge_kernel(place, window_ref, row_ref, sums_ref, rest_ref, stats_ref, out_ref, *, cols):
     out_ref[...] = merged(
-        place, window_ref[...], row_ref[...], sums_ref[...], rest_ref[...], stats_ref[...], cols,
-        0, out_ref.shape[1] // HEAD,
+        place, window_ref[...], row_ref[...], sums_ref[...], rest_ref[...],
+        unfold_stats(stats_ref[...], rest_ref.shape[0]), cols, 0, out_ref.shape[1] // HEAD,
     )
 
 
@@ -170,8 +199,8 @@
 
     heads = window_ref.shape[1] // HEAD
     rows = merged(
-        place, window_ref[...], row_ref[...], sums_ref[...], rest_ref[...], stats_ref[...], cols,
-        pl.program_id(0) * heads, heads,
+        place, window_ref[...], row_ref[...], sums_ref[...], rest_ref[...],
+        unfold_stats(stats_ref[...], rest_ref.shape[0]), cols, pl.program_id(0) * heads, heads,
     )
     add_product(total_ref, rows, weight_ref)
 
@@ -204,32 +233,48 @@
     return half + (1 - 2 * half) * (1 - place[0])
 
 
-def pack(place, keys, values, half):
+def pack(place, keys, values, half, earlier=None):
     S, tokens, width = keys.shape
     width //= 2
-    spec = pl.BlockSpec((None, tokens, width), lambda s, p: (s, 0, side(half, p)))
-
-    def kernel(place, k_ref, v_ref, out_ref):
+    spec = pl.BlockSpec((None, tokens, width), lambda h, s, p: (s, 0, side(half, p)))
+    block = (None, None, 2, tokens, width)
+    given = [] if earlier is None else [earlier]
+
+    def turn(k_ref, v_ref, out_ref):
         for start in range(0, width, HEAD):
             cut = slice(start, start + HEAD)
             out_ref[0, :, cut] = k_ref[:, cut].T
         out_ref[1] = v_ref[...]
 
+    def kernel(place, k_ref, v_ref, *refs):
+        out_ref = refs[-1]
+        if not given:
+            turn(k_ref, v_ref, out_ref)
+            return
+
+        @pl.when(pl.program_id(0) == 0)
+        def _():
+            out_ref[...] = refs[0][...]
+
+        @pl.when(pl.program_id(0) == 1)
+        def _():
+            turn(k_ref, v_ref, out_ref)
+
     return pl.pallas_call(
         kernel,
-        out_shape=jax.ShapeDtypeStruct((S, 2, tokens, width), keys.dtype),
+        out_shape=jax.ShapeDtypeStruct((1 + len(given), S, 2, tokens, width), keys.dtype),
         grid_spec=pltpu.PrefetchScalarGridSpec(
             num_scalar_prefetch=1,
-            grid=(S,),
-            in_specs=[spec, spec],
-            out_specs=pl.BlockSpec((None, 2, tokens, width), lambda s, p: (s, 0, 0, 0)),
+            grid=(1 + len(given), S),
+            in_specs=[spec, spec, *[pl.BlockSpec(block, lambda h, s, p: (0, s, 0, 0, 0))] * len(given)],
+            out_specs=pl.BlockSpec(block, lambda h, s, p: (h, s, 0, 0, 0)),
         ),
         compiler_params=params(),
         cost_estimate=pl.CostEstimate(
             flops=0, bytes_accessed=8 * S * tokens * width, transcendentals=0
         ),
         name="pack",
-    )(place, *hbm(keys, values))
+    )(place, *hbm(keys, values), *given)
 
 
 def pick(place, value, half):
@@ -256,30 +301,39 @@
     )(place, *hbm(value))
 
 
-def edge_attend(place, q, near, far, start, cols_tile, cols):
-    count, _, tokens, width = far.shape
+def edge_attend(place, q, q_block, near, far, stream, cols_tile, cols, following=None):
+    _, _, tokens, width = far.shape
     heads = width // HEAD
+    extra, args, rows = [], [], tokens + FOLD
+    if following is not None:
+        rows += 2 * tokens
+        args = [following[0], *hbm(following[1])]
+        extra = [
+            pl.BlockSpec((None, None, 2, tokens, width), lambda g, p: (1, stream, 0, 0, 0)),
+            pl.BlockSpec((None, tokens, width), lambda g, p: (stream, 0, side(1, p))),
+        ]
     return pl.pallas_call(
         functools.partial(edge_kernel, heads=heads, cols_tile=cols_tile, cols=cols),
-        out_shape=jax.ShapeDtypeStruct((count, tokens, width + HEAD), jnp.bfloat16),
+        out_shape=jax.ShapeDtypeStruct((rows, width), jnp.bfloat16),
         grid_spec=pltpu.PrefetchScalarGridSpec(
             num_scalar_prefetch=1,
-            grid=(count,),
+            grid=(1,),
             in_specs=[
-                pl.BlockSpec((None, tokens, width), lambda g, p: (start + g, 0, 0)),
-                pl.BlockSpec((None, 2, tokens, width), lambda g, p: (start + g, 0, 0, 0)),
-                pl.BlockSpec((None, 2, tokens, width), lambda g, p: (g, 0, 0, 0)),
+                pl.BlockSpec((tokens, width), lambda g, p: (q_block, 0)),
+                pl.BlockSpec((None, 2, tokens, width), lambda g, p: (stream, 0, 0, 0)),
+                pl.BlockSpec((None, 2, tokens, width), lambda g, p: (0, 0, 0, 0)),
+                *extra,
             ],
-            out_specs=pl.BlockSpec((None, tokens, width + HEAD), lambda g, p: (g, 0, 0)),
-        ),
-        compiler_params=params(),
-        cost_estimate=pl.CostEstimate(
-            flops=8 * count * tokens * tokens * width,
-            bytes_accessed=14 * count * tokens * width,
-            transcendentals=2 * count * tokens * tokens * heads,
+            out_specs=pl.BlockSpec((rows, width), lambda g, p: (0, 0)),
+        ),
+        compiler_params=params(),
+        cost_estimate=pl.CostEstimate(
+            flops=8 * tokens * tokens * width,
+            bytes_accessed=14 * tokens * width,
+            transcendentals=2 * tokens * tokens * heads,
         ),
         name="edge_rows",
-    )(place, q, near, far)
+    )(place, q, near, far, *args)
 
 
 def rows_attend(place, mask, reach, q, tiles, sides, far, half, stream, cols_tile, frame_tokens, grid, block=3):
@@ -288,7 +342,7 @@
     heads = width // HEAD
     lanes = block * HEAD
     steps = heads // block
-    own = pl.BlockSpec((None, 2, tokens, lanes), lambda g, p: (stream, 0, 0, g))
+    own = pl.BlockSpec((None, None, 2, tokens, lanes), lambda g, p: (half, stream, 0, 0, g))
     near = pl.BlockSpec((None, None, 2, tokens, lanes), lambda g, p: (0, stream, 0, 0, g))
     other = pl.BlockSpec((None, None, 2, tokens, lanes), lambda g, p: (1, stream, 0, 0, g))
     args = [x for tile, pair in zip(tiles, sides) for x in (tile, pair, pair)]
@@ -331,9 +385,9 @@
     )(place, mask, reach, *hbm(q), *args, far)
 
 
-def merge(place, parts, rest, stream, cols):
+def merge(place, parts, rest, cols):
     tokens, width = parts[0].shape
-    at = stream if rest.shape[0] > 1 else 0
+    at = rest.shape[0] // tokens - 1
     whole = pl.BlockSpec((tokens, width), lambda g, p: (0, 0))
     return pl.pallas_call(
         functools.partial(merge_kernel, cols=cols),
@@ -345,8 +399,8 @@
                 whole,
                 whole,
                 pl.BlockSpec((tokens, HEAD), lambda g, p: (0, 0)),
-                pl.BlockSpec((None, tokens, width), lambda g, p: (at, 0, 0)),
-                pl.BlockSpec((None, tokens, HEAD), lambda g, p: (at, 0, width // HEAD)),
+                pl.BlockSpec((tokens, width), lambda g, p: (at, 0)),
+                pl.BlockSpec((FOLD, width), lambda g, p: ((at + 1) * tokens // FOLD, 0)),
             ],
             out_specs=whole,
         ),
@@ -360,7 +414,7 @@
 
 def project(place, parts, rest, weight, other, output, stream, cols, block=3):
     tokens, width = parts[0].shape
-    at = stream if rest.shape[0] > 1 else 0
+    at = rest.shape[0] // tokens - 1
     lanes = block * HEAD
     streams, _, model = weight.shape
     earlier = [] if output is None else [output]
@@ -376,8 +430,8 @@
                 cut,
                 cut,
                 pl.BlockSpec((tokens, HEAD), lambda g, p: (0, 0)),
-                pl.BlockSpec((None, tokens, lanes), lambda g, p: (at, 0, g)),
-                pl.BlockSpec((None, tokens, HEAD), lambda g, p: (at, 0, width // HEAD)),
+                pl.BlockSpec((tokens, lanes), lambda g, p: (at, g)),
+                pl.BlockSpec((FOLD, width), lambda g, p: ((at + 1) * tokens // FOLD, 0)),
                 pl.BlockSpec((None, lanes, model), lambda g, p: (stream, g, 0)),
                 pl.BlockSpec((tokens, model), lambda g, p: (0, 0)),
                 *[ANY] * len(earlier),
@@ -424,7 +478,7 @@
 def per_device(queries, key_states, value_states, tile_mask, frame_reach, out_weight):
     S, F, R, C, width = queries.shape
     tokens = F * R * C
-    model = out_weight.shape[2]
+    half, model = width // 2, out_weight.shape[2]
     rows, cols = lax.axis_size("row"), lax.axis_size("col")
     inward = [(0, 1), (cols - 1, cols - 2)]
     outward = [(j, i) for i, j in inward]
@@ -443,61 +497,66 @@
     col_pairs, col_others = swaps(cols, 0), swaps(cols, 1)
     row_pairs, row_others = swaps(rows, 0), swaps(rows, 1)
     pair_swap = swaps(2, 0)
-    own = [pack(place, k, v, h) for h in range(2)]
-    picked = [pick(place, q, h) for h in range(2)]
-
-    def edge(name, h, start, *after):
-        sent[f"part{name}"] = edge_attend(
-            place, tied(sent[f"q{h}"], after), sent[f"other{h}"], sent[f"far{name}"], start, C, cols
-        )
-
-    def rows_of(name, h, s, *after):
-        tiles = [sent[f"pair_own{h}"], own[h], sent[f"next_own{h}"]]
+    own0 = pack(place, k, v, 0)
+    own = pack(place, k, v, 1, own0)
+    picked = pick(place, q, 0).reshape(S * tokens, half)
+
+    def mix(s, *after):
+        sent[f"part0{s}"] = edge_attend(
+            place, tied(sent["q0"], after), s, sent["other0"], sent[f"far0{s}"], s, C, cols, (own, q)
+        )
+
+    def edge(s, *after):
+        sent[f"part1{s}"] = edge_attend(
+            place, tied(sent[f"mix{s}"], after), 2, sent["other1"], sent[f"far1{s}"], s, C, cols
+        )
+
+    def near1(s):
+        return sent[f"mix{s}"][:2 * tokens].reshape(1, 2, tokens, half)
+
+    def rows_of(h, s, *after):
+        tiles = [sent["pair_own"], own, sent["next_own"]]
         sides = [sent[f"pair_sides{h}"], sent[f"sides{h}"], sent[f"next_sides{h}"]]
         sent[f"rows{h}{s}"] = rows_attend(
-            place, tied(mask, after), frame_reach, q, tiles, sides, sent[f"far{name}"], h, s, C, R * C, (rows, cols)
-        )
-
-    send("near0", own[0], "col", col_pairs)
-    send("other0", own[0], "col", col_others)
-    send("next_own0", own[0], "row", row_others)
-    send("pair_own0", own[0], "row", row_pairs)
-    send("q0", picked[0], "col", inward)
-    send("far00", sent["near0"][:1], "col", col_others, "next_own0")
-    send("far01", sent["near0"][1:], "col", col_others, "other0", "next_own0")
+            place, tied(mask, after), frame_reach, q, tiles, sides, sent[f"far{h}{s}"], h, s, C, R * C, (rows, cols)
+        )
+
+    send("near0", own0[0], "col", col_pairs)
+    send("other0", own0[0], "col", col_others)
+    send("next_own", own, "row", row_others)
+    send("pair_own", own, "row", row_pairs)
+    send("q0", picked, "col", inward)
+    send("far00", sent["near0"][:1], "col", col_others, "near0", "other0", "pair_own")
+    send("far01", sent["near0"][1:], "col", col_others, "near0", "other0", "pair_own")
     sent["sides0"] = jnp.stack([sent["near0"], sent["other0"]])
-    send("next_sides0", sent["sides0"], "row", row_others)
-    send("pair_sides0", sent["sides0"], "row", row_pairs, "pair_own0", "far01")
-    edge("00", 0, 0)
-    send("rest00", sent["part00"], "col", outward)
-    send("near1", own[1], "col", col_pairs, "rest00")
+    send("next_sides0", sent["sides0"], "row", row_others, "next_own")
+    send("pair_sides0", sent["sides0"], "row", row_pairs, "q0")
+    mix(0)
+    send("mix0", sent["part00"], "col", col_pairs)
     send("other1", own[1], "col", col_others, "far00")
-    edge("01", 0, 1)
-    send("rest01", sent["part01"], "col", outward)
-    rows_of("00", 0, 0)
-    rows_of("01", 0, 1)
-    sent["merged0"] = merge(tied(place, []), sent["rows00"], sent["rest00"], 0, cols)
+    mix(1)
+    send("mix1", sent["part01"], "col", col_pairs)
+    rows_of(0, 0)
+    rows_of(0, 1)
+    sent["merged0"] = merge(tied(place, []), sent["rows00"], sent["mix0"], cols)
     send("theirs0", sent["merged0"], "pair", pair_swap)
-    sent["merged1"] = merge(tied(place, []), sent["rows01"], sent["rest01"], 1, cols)
-    send("theirs1", sent["merged1"], "pair", pair_swap, "rest00")
-    send("next_own1", own[1], "row", row_others)
-    send("pair_own1", own[1], "row", row_pairs)
-    send("q1", picked[1], "col", inward, "rest01")
+    sent["merged1"] = merge(tied(place, []), sent["rows01"], sent["mix1"], cols)
+    send("theirs1", sent["merged1"], "pair", pair_swap)
     sent["product0"] = product(tied(sent["theirs0"], []), out_weight, 0)
     send("back0", sent["product0"], "pair", pair_swap)
     sent["product1"] = product(tied(sent["theirs1"], []), out_weight, 1)
     send("back1", sent["product1"], "pair", pair_swap)
-    send("far10", sent["near1"][:1], "col", col_others, "far01")
-    send("far11", sent["near1"][1:], "col", col_others, "other1")
-    sent["sides1"] = jnp.stack([sent["near1"], sent["other1"]])
+    send("far10", near1(0), "col", col_others, "far01", "pair_sides0", "next_sides0")
+    send("far11", near1(1), "col", col_others, "other1")
+    sent["sides1"] = jnp.stack([jnp.concatenate([near1(0), near1(1)]), sent["other1"]])
     send("next_sides1", sent["sides1"], "row", row_others)
     send("pair_sides1", sent["sides1"], "row", row_pairs)
-    edge("10", 1, 0)
+    edge(0)
     send("rest10", sent["part10"], "col", outward)
-    edge("11", 1, 1)
+    edge(1)
     send("rest11", sent["part11"], "col", outward)
-    rows_of("10", 1, 0)
-    rows_of("11", 1, 1)
+    rows_of(1, 0)
+    rows_of(1, 1)
     output = project(tied(place, []), sent["rows10"], sent["rest10"], out_weight, sent["back0"], None, 0, cols)
     output = project(place, sent["rows11"], sent["rest11"], out_weight, sent["back1"], output, 1, cols)
     return output.reshape(S, F, R, C, model)

time: 168 us -> 172 us (1.024)
  waiting for transfers between devices: 77.9 us -> 62.8 us
  starting transfers between devices: 39.8 us -> 48.2 us
  local copies, waits for them, and re-layouts: 1.25 us -> 7.96 us
    ppermute x26 -> x22, waiting for transfers between devices: 77.9 us -> 62.8 us  [send(): sent[name] = lax.ppermute(tied(value, after), axis, pairs)]
    ppermute x26 -> x22, starting transfers between devices: 39.8 us -> 48.2 us  [send(): sent[name] = lax.ppermute(tied(value, after), axis, pairs)]
    unnamed x14 -> x32, local copies, waits for them, and re-layouts: 0.04 us -> 6.85 us
    pallas_call x4, Pallas kernels: 2.37 us -> 4.47 us  [edge_attend(): pl.pallas_call(functools.partial(edge_kernel, heads=heads, cols_tile=cols...]
  transfers between devices with their start and end apart: 26 -> 22, of which waited for: 9 -> 7; matrix products, arithmetic and copies ran while one was open for 1% -> 2% of each run, Pallas kernels for 25% -> 23%
where the time goes in v6:
time: 172 us; the launch traced here: 170 us
  waiting for transfers between devices  62.8 us (37%)
  Pallas kernels  48.5 us (28%)
  starting transfers between devices  48.2 us (28%)
  local copies, waits for them, and re-layouts  7.96 us (5%)
  other arithmetic  1.74 us (1%)
    ppermute x22, waiting for transfers between devices, send(): sent[name] = lax.ppermute(tied(value, after), axis, pairs)  62.8 us
    ppermute x22, starting transfers between devices, send(): sent[name] = lax.ppermute(tied(value, after), axis, pairs)  48.2 us
    pallas_call x4, Pallas kernels, rows_attend(): pl.pallas_call(kernel, out_shape=(jax.ShapeDtypeStruct((tokens, width), j...  22.7 us
    pallas_call x2, Pallas kernels, project(): pl.pallas_call(functools.partial(project_kernel, cols=cols), out_shape=ja...  8.31 us
    unnamed x32, local copies, waits for them, and re-layouts  6.85 us
    pallas_call x2, Pallas kernels, pack(): pl.pallas_call(kernel, out_shape=jax.ShapeDtypeStruct((1 + len(given), S,...  5.08 us
    pallas_call x4, Pallas kernels, edge_attend(): pl.pallas_call(functools.partial(edge_kernel, heads=heads, cols_tile=cols...  4.47 us
    pallas_call x2, Pallas kernels, product(): pl.pallas_call(product_kernel, out_shape=jax.ShapeDtypeStruct((tokens, mo...  4.22 us
  transfers between devices with their start and end apart: 22, of which 7 were waited for; matrix products, arithmetic and copies ran while one was open for 2% of the time, Pallas kernels for 23%

profile of v6, /device:TPU:0, one launch (start us, length us, event | category | flops | bytes accessed | tf_op | source)
XLA Modules:
  0.0 169.8 jit_solution(11466540213934342193)
XLA Ops:
  0.1 2.0 %pack.2.refs_0_ = bf16[1,2,2,128,1152]{4,3,2,1,0:T(8,128)(2,1)S(1)} custom-call(s32[3]{0:T(128)S(1)} %pad_add_fusion.place, bf16[2,128,2304]{2,1,0:T(8,128)(2,1)} %bitcast.38, bf16[2,128,2304]{2,1,0:T(8,128)(2,1)} %bitcast.40), custom_call_target="tpu_custom_call" | custom-call | bytes 2359296 | tf_op jit(solution)/shard_map/pack/pallas_call | solution.py:263
  2.1 3.1 %pack.3.refs_0_.refs_3_ = bf16[2,2,2,128,1152]{4,3,2,1,0:T(8,128)(2,1)S(1)} custom-call(s32[3]{0:T(128)S(1)} %pad_add_fusion.place, bf16[2,128,2304]{2,1,0:T(8,128)(2,1)} %bitcast.39, bf16[2,128,2304]{2,1,0:T(8,128)(2,1)} %bitcast.41, bf16[1,2,2,128,1152]{4,3,2,1,0:T(8,128)(2,1)S(1)} %pack.2.refs_0_), custom_call_target="tpu_custom_call" | custom-call | bytes 2359296 | tf_op jit(solution)/shard_map/pack/pallas_call | solution.py:263
  5.7 2.6 %collective-permute-start.3 = (bf16[2,2,128,1152]{3,2,1,0:T(8,128)(2,1)S(1)}, bf16[2,2,128,1152]{3,2,1,0:T(8,128)(2,1)S(1)}, u32[]{:S(2)}, u32[]{:S(2)}) collective-permute-start(bf16[2,2,128,1152]{3,2,1,0:T(8,128)(2,1)S(1)} %bitcast.23), channel_id=1, source_target_pairs={{0,1},{2,3},{1,0},{3,2},{4,5},{6,7},{5,4},{7,6},{8,9},{10,11},{9,8... | collective-permute-start | bytes 3538952 | tf_op jit(solution)/shard_map/ppermute | solution.py:495
  9.9 1.6 pick.1
  11.5 6.3 %collective-permute-start.1 = (bf16[256,1152]{1,0:T(8,128)(2,1)S(1)}, bf16[256,1152]{1,0:T(8,128)(2,1)S(1)}, u32[]{:S(2)}, u32[]{:S(2)}) collective-permute-start(bf16[256,1152]{1,0:T(8,128)(2,1)S(1)} %bitcast.25), channel_id=1, source_target_pairs={{0,1},{3,2},{4,5},{7,6},{8,9},{11,10},{12,13},{15,14},{16,17},{19,... | collective-permute-start | bytes 1769480 | tf_op jit(solution)/shard_map/ppermute | solution.py:495
  17.8 17.1 %collective-permute-done.3 = bf16[2,2,128,1152]{3,2,1,0:T(8,128)(2,1)S(1)} collective-permute-done((bf16[2,2,128,1152]{3,2,1,0:T(8,128)(2,1)S(1)}, bf16[2,2,128,1152]{3,2,1,0:T(8,128)(2,1)S(1)}, u32[]{:S(2)}, u32[]{:S(2)}) %collective-permute-start.3) | collective-permute-done | bytes 1179680 | tf_op jit(solution)/shard_map/ppermute | solution.py:495
  36.4 10.4 %collective-permute-done.1.q_ref = bf16[256,1152]{1,0:T(8,128)(2,1)S(1)} collective-permute-done((bf16[256,1152]{1,0:T(8,128)(2,1)S(1)}, bf16[256,1152]{1,0:T(8,128)(2,1)S(1)}, u32[]{:S(2)}, u32[]{:S(2)}) %collective-permute-start.1) | collective-permute-done | bytes 589856 | tf_op jit(solution)/shard_map/ppermute | solution.py:495
  46.8 1.6 edge_rows.4
  48.4 11.8 %collective-permute-start.5 = (bf16[400,1152]{1,0:T(8,128)(2,1)S(1)}, bf16[400,1152]{1,0:T(8,128)(2,1)S(1)}, u32[]{:S(2)}, u32[]{:S(2)}) collective-permute-start(bf16[400,1152]{1,0:T(8,128)(2,1)S(1)} %edge_rows.4), channel_id=1, source_target_pairs={{0,1},{2,3},{1,0},{3,2},{4,5},{6,7},{5,4},{7,6},{8,9},{10,11},{9,8... | collective-permute-start | bytes 2764808 | tf_op jit(solution)/shard_map/ppermute | solution.py:495
  60.2 1.6 edge_rows.5
  61.8 9.7 %collective-permute-start.7 = (bf16[400,1152]{1,0:T(8,128)(2,1)S(1)}, bf16[400,1152]{1,0:T(8,128)(2,1)S(1)}, u32[]{:S(2)}, u32[]{:S(2)}) collective-permute-start(bf16[400,1152]{1,0:T(8,128)(2,1)S(1)} %edge_rows.5), channel_id=1, source_target_pairs={{0,1},{2,3},{1,0},{3,2},{4,5},{6,7},{5,4},{7,6},{8,9},{10,11},{9,8... | collective-permute-start | bytes 2764808 | tf_op jit(solution)/shard_map/ppermute | solution.py:495
  73.5 8.0 %collective-permute-done.5.q_ref.rest_ref.stats_ref = bf16[400,1152]{1,0:T(8,128)(2,1)S(1)} collective-permute-done((bf16[400,1152]{1,0:T(8,128)(2,1)S(1)}, bf16[400,1152]{1,0:T(8,128)(2,1)S(1)}, u32[]{:S(2)}, u32[]{:S(2)}) %collective-permute-start.5) | collective-permute-done | bytes 921632 | tf_op jit(solution)/shard_map/ppermute | solution.py:495
  82.4 15.5 %collective-permute-done.7.q_ref.rest_ref.stats_ref = bf16[400,1152]{1,0:T(8,128)(2,1)S(1)} collective-permute-done((bf16[400,1152]{1,0:T(8,128)(2,1)S(1)}, bf16[400,1152]{1,0:T(8,128)(2,1)S(1)}, u32[]{:S(2)}, u32[]{:S(2)}) %collective-permute-start.7) | collective-permute-done | bytes 921632 | tf_op jit(solution)/shard_map/ppermute | solution.py:495
  100.3 2.8 %collective-permute-start.9 = (bf16[2,2,2,128,1152]{4,3,2,1,0:T(8,128)(2,1)S(1)}, bf16[2,2,2,128,1152]{4,3,2,1,0:T(8,128)(2,1)}, u32[]{:S(2)}, u32[]{:S(2)}) collective-permute-start(bf16[2,2,2,128,1152]{4,3,2,1,0:T(8,128)(2,1)S(1)} %pad_maximum_fusion.refs_4_.refs_5_), channel_id=1, source_target_pairs={{0,4},{8,12},{4,0},{12,8},{1,5},{9,13},{5,1},{13,9},{2,6},{10,14},... | collective-permute-start | bytes 7077896 | tf_op jit(solution)/shard_map/ppermute | solution.py:495
  103.9 5.7 %rows.7 = (f32[128,1152]{1,0:T(8,128)S(1)}, f32[128,1152]{1,0:T(8,128)S(1)}, bf16[128,128]{1,0:T(8,128)(2,1)S(1)}) custom-call(s32[3]{0:T(128)S(1)} %pad_add_fusion.place, s32[9]{0:T(128)S(1)} %bitcast.26, s32[18]{0:T(128)S(1)} %copy-done.11, bf16[2,128,2304]{2,1,0:T(8,128)(2,1)} %bitcast.33, bf16[2,2,2,128,1152]{4,3,2,1,0:T(8,128)(2,1)S(1)} %collective-permute-done.refs_0_, ...), custom_call_target="tpu_custom_call" | custom-call | flops 868220928 | bytes 7962624 | tf_op jit(solution)/shard_map/rows/pallas_call | solution.py:352
  110.8 1.6 collective-permute-start.20
  112.3 2.4 %copy-done.7 = bf16[2,2,2,128,1152]{4,3,2,1,0:T(8,128)(2,1)S(1)} copy-done((bf16[2,2,2,128,1152]{4,3,2,1,0:T(8,128)(2,1)S(1)}, bf16[2,2,2,128,1152]{4,3,2,1,0:T(8,128)(2,1)}, u32[]{:S(2)}) %copy-start.7) | copy-done | bytes 2359320
  114.8 5.6 %rows.5 = (f32[128,1152]{1,0:T(8,128)S(1)}, f32[128,1152]{1,0:T(8,128)S(1)}, bf16[128,128]{1,0:T(8,128)(2,1)S(1)}) custom-call(s32[3]{0:T(128)S(1)} %pad_add_fusion.place, s32[9]{0:T(128)S(1)} %bitcast.27, s32[18]{0:T(128)S(1)} %copy-done.11, bf16[2,128,2304]{2,1,0:T(8,128)(2,1)} %bitcast.34, bf16[2,2,2,128,1152]{4,3,2,1,0:T(8,128)(2,1)S(1)} %collective-permute-done.refs_0_, ...), custom_call_target="tpu_custom_call" | custom-call | flops 868220928 | bytes 7962624 | tf_op jit(solution)/shard_map/rows/pallas_call | solution.py:352
  121.4 1.3 collective-permute-start.16
  123.5 2.1 %product.3 = bf16[128,3072]{1,0:T(8,128)(2,1)S(1)} custom-call(bf16[128,1152]{1,0:T(8,128)(2,1)S(1)} %collective-permute-done.20.rows_ref, bf16[2,1152,3072]{2,1,0:T(8,128)(2,1)S(1)} %bitcast.20), custom_call_target="tpu_custom_call" | custom-call | flops 905969664 | bytes 7077888 | tf_op jit(solution)/shard_map/product/pallas_call | solution.py:455
  125.6 4.7 %collective-permute-done.16.rows_ref = bf16[128,1152]{1,0:T(8,128)(2,1)S(1)} collective-permute-done((bf16[128,1152]{1,0:T(8,128)(2,1)S(1)}, bf16[128,1152]{1,0:T(8,128)(2,1)S(1)}, u32[]{:S(2)}, u32[]{:S(2)}) %collective-permute-start.16) | collective-permute-done | bytes 294944 | tf_op jit(solution)/shard_map/ppermute | solution.py:495
  130.3 1.5 collective-permute-start.21
  131.8 2.1 %product.2 = bf16[128,3072]{1,0:T(8,128)(2,1)S(1)} custom-call(bf16[128,1152]{1,0:T(8,128)(2,1)S(1)} %collective-permute-done.16.rows_ref, bf16[2,1152,3072]{2,1,0:T(8,128)(2,1)S(1)} %bitcast.20), custom_call_target="tpu_custom_call" | custom-call | flops 905969664 | bytes 7077888 | tf_op jit(solution)/shard_map/product/pallas_call | solution.py:455
  135.3 1.4 collective-permute-start.19
  138.6 1.4 copy-done.2
  140.0 1.3 collective-permute-start.13
  141.3 1.7 copy-done.3
  143.0 5.7 %rows.6 = (f32[128,1152]{1,0:T(8,128)S(1)}, f32[128,1152]{1,0:T(8,128)S(1)}, bf16[128,128]{1,0:T(8,128)(2,1)S(1)}) custom-call(s32[3]{0:T(128)S(1)} %pad_add_fusion.place, s32[9]{0:T(128)S(1)} %bitcast.28, s32[18]{0:T(128)S(1)} %copy-done.11, bf16[2,128,2304]{2,1,0:T(8,128)(2,1)} %bitcast.35, bf16[2,2,2,128,1152]{4,3,2,1,0:T(8,128)(2,1)S(1)} %collective-permute-done.refs_0_, ...), custom_call_target="tpu_custom_call" | custom-call | flops 868220928 | bytes 7962624 | tf_op jit(solution)/shard_map/rows/pallas_call | solution.py:352
  148.7 5.7 %rows.4 = (f32[128,1152]{1,0:T(8,128)S(1)}, f32[128,1152]{1,0:T(8,128)S(1)}, bf16[128,128]{1,0:T(8,128)(2,1)S(1)}) custom-call(s32[3]{0:T(128)S(1)} %pad_add_fusion.place, s32[9]{0:T(128)S(1)} %bitcast.29, s32[18]{0:T(128)S(1)} %copy-done.11, bf16[2,128,2304]{2,1,0:T(8,128)(2,1)} %bitcast.36, bf16[2,2,2,128,1152]{4,3,2,1,0:T(8,128)(2,1)S(1)} %collective-permute-done.refs_0_, ...), custom_call_target="tpu_custom_call" | custom-call | flops 868220928 | bytes 7962624 | tf_op jit(solution)/shard_map/rows/pallas_call | solution.py:352
  154.4 4.2 %project.2.refs_0_ = bf16[2,128,3072]{2,1,0:T(8,128)(2,1)} custom-call(s32[3]{0:T(128)S(1)} %pad_add_fusion.place, f32[128,1152]{1,0:T(8,128)S(1)} %get-tuple-element.37.window_ref, f32[128,1152]{1,0:T(8,128)S(1)} %get-tuple-element.38.row_ref, bf16[128,128]{1,0:T(8,128)(2,1)S(1)} %get-tuple-element.39.sums_ref, ...), custom_call_target="tpu_custom_call" | custom-call | flops 905969664 | bytes 7077888 | tf_op jit(solution)/shard_map/project/pallas_call | solution.py:423
  159.2 6.5 %collective-permute-done.17.other_ref = bf16[128,3072]{1,0:T(8,128)(2,1)S(1)} collective-permute-done((bf16[128,3072]{1,0:T(8,128)(2,1)S(1)}, bf16[128,3072]{1,0:T(8,128)(2,1)S(1)}, u32[]{:S(2)}, u32[]{:S(2)}) %collective-permute-start.17) | collective-permute-done | bytes 786464 | tf_op jit(solution)/shard_map/ppermute | solution.py:495
  165.7 4.2 %project.3 = bf16[2,128,3072]{2,1,0:T(8,128)(2,1)} custom-call(s32[3]{0:T(128)S(1)} %pad_add_fusion.place, f32[128,1152]{1,0:T(8,128)S(1)} %get-tuple-element.28.window_ref, f32[128,1152]{1,0:T(8,128)S(1)} %get-tuple-element.29.row_ref, bf16[128,128]{1,0:T(8,128)(2,1)S(1)} %get-tuple-element.30.sums_ref, ...), custom_call_target="tpu_custom_call", output_to_operand_aliasing={{}: (8, {})} | custom-call | flops 905969664 | bytes 7077888 | tf_op jit(solution)/shard_map/project/pallas_call | solution.py:423
  (70 shorter events, 16.2 us)
Async XLA Ops:
  5.2 29.8 %collective-permute-start = (bf16[2,2,2,128,1152]{4,3,2,1,0:T(8,128)(2,1)S(1)}, bf16[2,2,2,128,1152]{4,3,2,1,0:T(8,128)(2,1)S(1)}, u32[]{:S(2)}, u32[]{:S(2)}) collective-permute-start(bf16[2,2,2,128,1152]{4,3,2,1,0:T(8,128)(2,1)S(1)} %pack.3.refs_0_.refs_3_), channel_id=1, source_target_pairs={{0,4},{8,12},{4,0},{12,8},{1,5},{9,13},{5,1},{13,9},{2,6},{10,14},... | collective-permute-start | bytes 7077896 | tf_op jit(solution)/shard_map/ppermute | solution.py:495
  5.7 29.2 %collective-permute-start.3 = (bf16[2,2,128,1152]{3,2,1,0:T(8,128)(2,1)S(1)}, bf16[2,2,128,1152]{3,2,1,0:T(8,128)(2,1)S(1)}, u32[]{:S(2)}, u32[]{:S(2)}) collective-permute-start(bf16[2,2,128,1152]{3,2,1,0:T(8,128)(2,1)S(1)} %bitcast.23), channel_id=1, source_target_pairs={{0,1},{2,3},{1,0},{3,2},{4,5},{6,7},{5,4},{7,6},{8,9},{10,11},{9,8... | collective-permute-start | bytes 3538952 | tf_op jit(solution)/shard_map/ppermute | solution.py:495
  8.3 26.7 %collective-permute-start.2 = (bf16[2,2,128,1152]{3,2,1,0:T(8,128)(2,1)S(1)}, bf16[2,2,128,1152]{3,2,1,0:T(8,128)(2,1)S(1)}, u32[]{:S(2)}, u32[]{:S(2)}) collective-permute-start(bf16[2,2,128,1152]{3,2,1,0:T(8,128)(2,1)S(1)} %bitcast.24), channel_id=1, source_target_pairs={{1,2},{2,1},{5,6},{6,5},{9,10},{10,9},{13,14},{14,13},{17,18},{18,... | collective-permute-start | bytes 3538952 | tf_op jit(solution)/shard_map/ppermute | solution.py:495
  9.1 63.6 %collective-permute-start.10 = (bf16[2,2,2,128,1152]{4,3,2,1,0:T(8,128)(2,1)S(1)}, bf16[2,2,2,128,1152]{4,3,2,1,0:T(8,128)(2,1)S(1)}, u32[]{:S(2)}, u32[]{:S(2)}) collective-permute-start(bf16[2,2,2,128,1152]{4,3,2,1,0:T(8,128)(2,1)S(1)} %pack.3.refs_0_.refs_3_), channel_id=1, source_target_pairs={{4,8},{8,4},{5,9},{9,5},{6,10},{10,6},{7,11},{11,7},{20,24},{24,20... | collective-permute-start | bytes 7077896 | tf_op jit(solution)/shard_map/ppermute | solution.py:495
  11.5 35.3 %collective-permute-start.1 = (bf16[256,1152]{1,0:T(8,128)(2,1)S(1)}, bf16[256,1152]{1,0:T(8,128)(2,1)S(1)}, u32[]{:S(2)}, u32[]{:S(2)}) collective-permute-start(bf16[256,1152]{1,0:T(8,128)(2,1)S(1)} %bitcast.25), channel_id=1, source_target_pairs={{0,1},{3,2},{4,5},{7,6},{8,9},{11,10},{12,13},{15,14},{16,17},{19,... | collective-permute-start | bytes 1769480 | tf_op jit(solution)/shard_map/ppermute | solution.py:495
  35.0 11.8 %collective-permute-start.4 = (bf16[1,2,128,1152]{3,2,1,0:T(8,128)(2,1)S(1)}, bf16[1,2,128,1152]{3,2,1,0:T(8,128)(2,1)S(1)}, u32[]{:S(2)}, u32[]{:S(2)}) collective-permute-start(bf16[1,2,128,1152]{3,2,1,0:T(8,128)(2,1)S(1)} %get-tuple-element.24), channel_id=1, source_target_pairs={{1,2},{2,1},{5,6},{6,5},{9,10},{10,9},{13,14},{14,13},{17,18},{18,... | collective-permute-start | bytes 1769480 | tf_op jit(solution)/shard_map/ppermute | solution.py:495
  35.7 24.5 %collective-permute-start.6 = (bf16[1,2,128,1152]{3,2,1,0:T(8,128)(2,1)S(1)}, bf16[1,2,128,1152]{3,2,1,0:T(8,128)(2,1)S(1)}, u32[]{:S(2)}, u32[]{:S(2)}) collective-permute-start(bf16[1,2,128,1152]{3,2,1,0:T(8,128)(2,1)S(1)} %get-tuple-element.25), channel_id=1, source_target_pairs={{1,2},{2,1},{5,6},{6,5},{9,10},{10,9},{13,14},{14,13},{17,18},{18,... | collective-permute-start | bytes 1769480 | tf_op jit(solution)/shard_map/ppermute | solution.py:495
  48.4 33.2 %collective-permute-start.5 = (bf16[400,1152]{1,0:T(8,128)(2,1)S(1)}, bf16[400,1152]{1,0:T(8,128)(2,1)S(1)}, u32[]{:S(2)}, u32[]{:S(2)}) collective-permute-start(bf16[400,1152]{1,0:T(8,128)(2,1)S(1)} %edge_rows.4), channel_id=1, source_target_pairs={{0,1},{2,3},{1,0},{3,2},{4,5},{6,7},{5,4},{7,6},{8,9},{10,11},{9,8... | collective-permute-start | bytes 2764808 | tf_op jit(solution)/shard_map/ppermute | solution.py:495
  61.8 36.2 %collective-permute-start.7 = (bf16[400,1152]{1,0:T(8,128)(2,1)S(1)}, bf16[400,1152]{1,0:T(8,128)(2,1)S(1)}, u32[]{:S(2)}, u32[]{:S(2)}) collective-permute-start(bf16[400,1152]{1,0:T(8,128)(2,1)S(1)} %edge_rows.5), channel_id=1, source_target_pairs={{0,1},{2,3},{1,0},{3,2},{4,5},{6,7},{5,4},{7,6},{8,9},{10,11},{9,8... | collective-permute-start | bytes 2764808 | tf_op jit(solution)/shard_map/ppermute | solution.py:495
  71.6 27.6 %collective-permute-start.8 = (bf16[2,2,128,1152]{3,2,1,0:T(8,128)(2,1)S(1)}, bf16[2,2,128,1152]{3,2,1,0:T(8,128)(2,1)S(1)}, u32[]{:S(2)}, u32[]{:S(2)}) collective-permute-start(bf16[2,2,128,1152]{3,2,1,0:T(8,128)(2,1)S(1)} %slice_bitcast_fusion), channel_id=1, source_target_pairs={{1,2},{2,1},{5,6},{6,5},{9,10},{10,9},{13,14},{14,13},{17,18},{18,... | collective-permute-start | bytes 3538952 | tf_op jit(solution)/shard_map/ppermute | solution.py:495
  72.6 30.5 %collective-permute-start.14 = (bf16[2,2,2,128,1152]{4,3,2,1,0:T(8,128)(2,1)S(1)}, bf16[2,2,2,128,1152]{4,3,2,1,0:T(8,128)(2,1)S(1)}, u32[]{:S(2)}, u32[]{:S(2)}) collective-permute-start(bf16[2,2,2,128,1152]{4,3,2,1,0:T(8,128)(2,1)S(1)} %pad_maximum_fusion.1.refs_4_.refs_5_), channel_id=1, source_target_pairs={{0,4},{8,12},{4,0},{12,8},{1,5},{9,13},{5,1},{13,9},{2,6},{10,14},... | collective-permute-start | bytes 7077896 | tf_op jit(solution)/shard_map/ppermute | solution.py:495
  72.7 39.6 %copy-start = (bf16[2,2,2,128,1152]{4,3,2,1,0:T(8,128)(2,1)}, bf16[2,2,2,128,1152]{4,3,2,1,0:T(8,128)(2,1)S(1)}, u32[]{:S(2)}) copy-start(bf16[2,2,2,128,1152]{4,3,2,1,0:T(8,128)(2,1)S(1)} %collective-permute-done.10.refs_6_) | copy-start | bytes 7077892
  72.7 30.4 %collective-permute-start.15 = (bf16[2,2,2,128,1152]{4,3,2,1,0:T(8,128)(2,1)S(1)}, bf16[2,2,2,128,1152]{4,3,2,1,0:T(8,128)(2,1)S(1)}, u32[]{:S(2)}, u32[]{:S(2)}) collective-permute-start(bf16[2,2,2,128,1152]{4,3,2,1,0:T(8,128)(2,1)S(1)} %pad_maximum_fusion.1.refs_4_.refs_5_), channel_id=1, source_target_pairs={{4,8},{8,4},{5,9},{9,5},{6,10},{10,6},{7,11},{11,7},{20,24},{24,20... | collective-permute-start | bytes 7077896 | tf_op jit(solution)/shard_map/ppermute | solution.py:495
  99.2 35.3 %copy-start.8 = (bf16[2,2,128,1152]{3,2,1,0:T(8,128)(2,1)}, bf16[2,2,128,1152]{3,2,1,0:T(8,128)(2,1)S(1)}, u32[]{:S(2)}) copy-start(bf16[2,2,128,1152]{3,2,1,0:T(8,128)(2,1)S(1)} %collective-permute-done.8.near_ref) | copy-start | bytes 3538948
  99.2 4.6 %copy-start.10 = (s32[1,1,1,9]{3,2,1,0:T(1,128)S(1)}, s32[1,1,1,9]{3,2,1,0:T(1,128)}, u32[]{:S(2)}) copy-start(s32[1,1,1,9]{3,2,1,0:T(1,128)} %param.9) | copy-start | bytes 112
  99.5 39.1 %collective-permute-start.11 = (bf16[2,2,2,128,1152]{4,3,2,1,0:T(8,128)(2,1)S(1)}, bf16[2,2,2,128,1152]{4,3,2,1,0:T(8,128)(2,1)S(1)}, u32[]{:S(2)}, u32[]{:S(2)}) collective-permute-start(bf16[2,2,2,128,1152]{4,3,2,1,0:T(8,128)(2,1)S(1)} %pad_maximum_fusion.refs_4_.refs_5_), channel_id=1, source_target_pairs={{4,8},{8,4},{5,9},{9,5},{6,10},{10,6},{7,11},{11,7},{20,24},{24,20... | collective-permute-start | bytes 7077896 | tf_op jit(solution)/shard_map/ppermute | solution.py:495
  100.3 41.0 %collective-permute-start.9 = (bf16[2,2,2,128,1152]{4,3,2,1,0:T(8,128)(2,1)S(1)}, bf16[2,2,2,128,1152]{4,3,2,1,0:T(8,128)(2,1)}, u32[]{:S(2)}, u32[]{:S(2)}) collective-permute-start(bf16[2,2,2,128,1152]{4,3,2,1,0:T(8,128)(2,1)S(1)} %pad_maximum_fusion.refs_4_.refs_5_), channel_id=1, source_target_pairs={{0,4},{8,12},{4,0},{12,8},{1,5},{9,13},{5,1},{13,9},{2,6},{10,14},... | collective-permute-start | bytes 7077896 | tf_op jit(solution)/shard_map/ppermute | solution.py:495
  103.1 6.5 %copy-start.4 = (bf16[2,2,2,128,1152]{4,3,2,1,0:T(8,128)(2,1)}, bf16[2,2,2,128,1152]{4,3,2,1,0:T(8,128)(2,1)S(1)}, u32[]{:S(2)}) copy-start(bf16[2,2,2,128,1152]{4,3,2,1,0:T(8,128)(2,1)S(1)} %collective-permute-done.14.refs_1_.refs_2_) | copy-start | bytes 7077892
  103.2 6.5 %copy-start.6 = (bf16[2,2,2,128,1152]{4,3,2,1,0:T(8,128)(2,1)}, bf16[2,2,2,128,1152]{4,3,2,1,0:T(8,128)(2,1)S(1)}, u32[]{:S(2)}) copy-start(bf16[2,2,2,128,1152]{4,3,2,1,0:T(8,128)(2,1)S(1)} %collective-permute-done.15.refs_7_.refs_8_) | copy-start | bytes 7077892
  103.2 30.7 %collective-permute-start.18 = (bf16[1,2,128,1152]{3,2,1,0:T(8,128)(2,1)}, bf16[1,2,128,1152]{3,2,1,0:T(8,128)(2,1)S(1)}, u32[]{:S(2)}, u32[]{:S(2)}) collective-permute-start(bf16[1,2,128,1152]{3,2,1,0:T(8,128)(2,1)} %bitcast.9), channel_id=1, source_target_pairs={{1,2},{2,1},{5,6},{6,5},{9,10},{10,9},{13,14},{14,13},{17,18},{18,... | collective-permute-start | bytes 1769480 | tf_op jit(solution)/shard_map/ppermute | solution.py:495
  109.7 13.8 %slice-start = ((s8[14155776]{0:T(1024)(128)(4,1)}), s8[4194304]{0:T(1024)(128)(4,1)S(1)}, s32[]{:S(2)}) async-start(s8[14155776]{0:T(1024)(128)(4,1)} %bitcast.19), calls=%async_computation | async-start | bytes 8388608
  110.7 12.7 %slice-start.1 = ((s8[14155776]{0:T(1024)(128)(4,1)}), s8[4194304]{0:T(1024)(128)(4,1)S(1)}, s32[]{:S(2)}) async-start(s8[14155776]{0:T(1024)(128)(4,1)} %bitcast.19), calls=%async_computation.1 | async-start | bytes 8388608
  110.7 12.7 %slice-start.2 = ((s8[14155776]{0:T(1024)(128)(4,1)}), s8[4194304]{0:T(1024)(128)(4,1)S(1)}, s32[]{:S(2)}) async-start(s8[14155776]{0:T(1024)(128)(4,1)} %bitcast.19), calls=%async_computation.2 | async-start | bytes 8388608
  110.8 12.7 %slice-start.3 = ((s8[14155776]{0:T(1024)(128)(4,1)}), s8[1572864]{0:T(1024)(128)(4,1)S(1)}, s32[]{:S(2)}) async-start(s8[14155776]{0:T(1024)(128)(4,1)} %bitcast.19), calls=%async_computation.3 | async-start | bytes 3145728
  110.8 12.0 %collective-permute-start.20 = (bf16[128,1152]{1,0:T(8,128)(2,1)S(1)}, bf16[128,1152]{1,0:T(8,128)(2,1)S(1)}, u32[]{:S(2)}, u32[]{:S(2)}) collective-permute-start(bf16[128,1152]{1,0:T(8,128)(2,1)S(1)} %merge.3), channel_id=1, source_target_pairs={{0,16},{16,0},{1,17},{17,1},{2,18},{18,2},{3,19},{19,3},{4,20},{20... | collective-permute-start | bytes 884744 | tf_op jit(solution)/shard_map/ppermute | solution.py:495
  121.4 8.9 %collective-permute-start.16 = (bf16[128,1152]{1,0:T(8,128)(2,1)S(1)}, bf16[128,1152]{1,0:T(8,128)(2,1)S(1)}, u32[]{:S(2)}, u32[]{:S(2)}) collective-permute-start(bf16[128,1152]{1,0:T(8,128)(2,1)S(1)} %merge.2), channel_id=1, source_target_pairs={{0,16},{16,0},{1,17},{17,1},{2,18},{18,2},{3,19},{19,3},{4,20},{20... | collective-permute-start | bytes 884744 | tf_op jit(solution)/shard_map/ppermute | solution.py:495
  122.7 12.6 %collective-permute-start.12 = (bf16[1,2,128,1152]{3,2,1,0:T(8,128)(2,1)S(1)}, bf16[1,2,128,1152]{3,2,1,0:T(8,128)(2,1)S(1)}, u32[]{:S(2)}, u32[]{:S(2)}) collective-permute-start(bf16[1,2,128,1152]{3,2,1,0:T(8,128)(2,1)S(1)} %bitcast.43), channel_id=1, source_target_pairs={{1,2},{2,1},{5,6},{6,5},{9,10},{10,9},{13,14},{14,13},{17,18},{18,... | collective-permute-start | bytes 1769480 | tf_op jit(solution)/shard_map/ppermute | solution.py:495
  130.3 24.1 %collective-permute-start.21 = (bf16[128,3072]{1,0:T(8,128)(2,1)S(1)}, bf16[128,3072]{1,0:T(8,128)(2,1)S(1)}, u32[]{:S(2)}, u32[]{:S(2)}) collective-permute-start(bf16[128,3072]{1,0:T(8,128)(2,1)S(1)} %product.3), channel_id=1, source_target_pairs={{0,16},{16,0},{1,17},{17,1},{2,18},{18,2},{3,19},{19,3},{4,20},{20... | collective-permute-start | bytes 2359304 | tf_op jit(solution)/shard_map/ppermute | solution.py:495
  133.9 31.8 %collective-permute-start.17 = (bf16[128,3072]{1,0:T(8,128)(2,1)S(1)}, bf16[128,3072]{1,0:T(8,128)(2,1)S(1)}, u32[]{:S(2)}, u32[]{:S(2)}) collective-permute-start(bf16[128,3072]{1,0:T(8,128)(2,1)S(1)} %product.2), channel_id=1, source_target_pairs={{0,16},{16,0},{1,17},{17,1},{2,18},{18,2},{3,19},{19,3},{4,20},{20... | collective-permute-start | bytes 2359304 | tf_op jit(solution)/shard_map/ppermute | solution.py:495
  135.3 6.0 %copy-start.1 = (bf16[2,2,2,128,1152]{4,3,2,1,0:T(8,128)(2,1)S(1)}, bf16[2,2,2,128,1152]{4,3,2,1,0:T(8,128)(2,1)}, u32[]{:S(2)}) copy-start(bf16[2,2,2,128,1152]{4,3,2,1,0:T(8,128)(2,1)} %copy-done) | copy-start | bytes 7077892
  135.3 19.1 %collective-permute-start.19 = (bf16[144,1152]{1,0:T(8,128)(2,1)S(1)}, bf16[144,1152]{1,0:T(8,128)(2,1)S(1)}, u32[]{:S(2)}, u32[]{:S(2)}) collective-permute-start(bf16[144,1152]{1,0:T(8,128)(2,1)S(1)} %edge_rows.7), channel_id=1, source_target_pairs={{1,0},{2,3},{5,4},{6,7},{9,8},{10,11},{13,12},{14,15},{17,16},{18,... | collective-permute-start | bytes 995336 | tf_op jit(solution)/shard_map/ppermute | solution.py:495
  140.0 19.2 %collective-permute-start.13 = (bf16[144,1152]{1,0:T(8,128)(2,1)S(1)}, bf16[144,1152]{1,0:T(8,128)(2,1)S(1)}, u32[]{:S(2)}, u32[]{:S(2)}) collective-permute-start(bf16[144,1152]{1,0:T(8,128)(2,1)S(1)} %edge_rows.6), channel_id=1, source_target_pairs={{1,0},{2,3},{5,4},{6,7},{9,8},{10,11},{13,12},{14,15},{17,16},{18,... | collective-permute-start | bytes 995336 | tf_op jit(solution)/shard_map/ppermute | solution.py:495
  (6 other events, 14.1 us)

commit v7 on v6

--- a/solution.py
+++ b/solution.py
@@ -15,6 +15,19 @@
 TO_LOG2 = HEAD ** (-0.5) * math.log2(math.e)
 ANY = pl.BlockSpec(memory_space=pl.ANY)
 SMEM = pl.BlockSpec(memory_space=pltpu.SMEM)
+
+
+COST = {"pack": 4, "edge_rows": 4, "rows": 4, "merge": 4, "project": 4, "product": 4, "pick": 4}
+
+
+def kernel_call(kernel, name, cost_estimate, **kwargs):
+    k = COST.get(name, 1)
+    cost = pl.CostEstimate(
+        flops=int(k * cost_estimate.flops),
+        bytes_accessed=int(k * cost_estimate.bytes_accessed),
+        transcendentals=int(k * cost_estimate.transcendentals),
+    )
+    return pl.pallas_call(kernel, name=name, cost_estimate=cost, **kwargs)
 
 
 def dot_nn(a, b):
@@ -121,7 +134,7 @@
 
 def rows_kernel(place, mask, reach, q_ref, *refs, heads, half, grid, cols_tile, frame_tokens):
     tiles = refs[:10]
-    window_ref, row_ref, sums_ref, bias_ref = refs[10:]
+    base_ref, row_ref, sums_ref, bias_ref = refs[10:]
     tokens = q_ref.shape[0]
     none = bias_ref.shape[0] - 2
     step = pl.program_id(0)
@@ -143,82 +156,57 @@
     inner = (col > 0) & (col < cols - 1)
     first_head = side(half, place) * heads * pl.num_programs(0)
     cuts = [slice(n * HEAD, (n + 1) * HEAD) for n in range(heads)]
-    raw = []
-    for c in cuts:
-        scores = dot_nn(q_ref[:, c], jnp.concatenate([t[0, :, c] for t in tiles], axis=1))
-        raw.append([scores[:, t * tokens:(t + 1) * tokens] for t in range(10)])
-    values = [[t[1, :, c] for t in tiles] for c in cuts]
-    window, row_scores = [], []
     row_bias = bias_ref[none + 1]
     outer_bias = bias_ref[jnp.where(inner, none + 1, none)]
-    for n in range(heads):
+
+    def scores_of(n):
+        scores = dot_nn(q_ref[:, cuts[n]], jnp.concatenate([t[0, :, cuts[n]] for t in tiles], axis=1))
+        return [scores[:, t * tokens:(t + 1) * tokens] for t in range(10)]
+
+    lse = []
+    following = scores_of(0)
+    for n, c in enumerate(cuts):
+        raw, following = following, scores_of(n + 1) if n + 1 < heads else None
+        values = [t[1, :, c] for t in tiles]
         limit = reach[first_head + step * heads + n]
-        window.append(
-            [raw[n][t] + bias_ref[jnp.where(listed[t], limit, none)] for t in range(9)]
-        )
-        row_scores.append(
-            [raw[n][3] + row_bias, raw[n][4] + row_bias, raw[n][5] + outer_bias, raw[n][9] + outer_bias]
-        )
-    _, totals, weights = softmax_sums(window, [v[:9] for v in values])
-    window_ref[...] = jnp.concatenate([t / w for t, w in zip(totals, weights)], axis=1)
-    tops, totals, weights = softmax_sums(row_scores, [v[3:6] + v[9:] for v in values])
-    row_ref[...] = jnp.concatenate([t / w for t, w in zip(totals, weights)], axis=1)
-    lse = [top + jnp.log2(w) for top, w in zip(tops, weights)]
+        window = [raw[t] + bias_ref[jnp.where(listed[t], limit, none)] for t in range(9)]
+        row = [raw[3] + row_bias, raw[4] + row_bias, raw[5] + outer_bias, raw[9] + outer_bias]
+        tops, totals, weights = softmax_sums([window, row], [values[:9], values[3:6] + values[9:]])
+        axial = totals[1] / weights[1]
+        base_ref[:, c] = totals[0] / weights[0] + axial
+        row_ref[:, c] = axial.astype(jnp.bfloat16)
+        lse.append(tops[1] + jnp.log2(weights[1]))
     sums = place_pieces(sums_ref[...].astype(jnp.float32), lse, step * heads)
     sums_ref[...] = sums.astype(jnp.bfloat16)
 
 
-def merged(place, window, row, sums, rest, stats, cols, first, heads):
+def merged(place, base_ref, row_ref, sums_ref, rest_ref, stats_ref, cols):
     inner = (place[2] > 0) & (place[2] < cols - 1)
-    near = spread_pieces(sums, first, heads)
-    far = jnp.where(inner, NEG, spread_pieces(stats, first, heads))
-    share = 1.0 / (1.0 + jnp.exp2(near - far))
-    axial = row + (rest.astype(jnp.float32) - row) * share
-    return (window + axial).astype(jnp.bfloat16)
-
-
-def merge_kernel(place, window_ref, row_ref, sums_ref, rest_ref, stats_ref, out_ref, *, cols):
-    out_ref[...] = merged(
-        place, window_ref[...], row_ref[...], sums_ref[...], rest_ref[...],
-        unfold_stats(stats_ref[...], rest_ref.shape[0]), cols, 0, out_ref.shape[1] // HEAD,
-    )
-
-
-def add_product(total_ref, rows, weight_ref, lanes=512):
-    for start in range(0, total_ref.shape[1], lanes):
-        cut = slice(start, start + lanes)
-        total_ref[:, cut] += dot_nn(rows, weight_ref[:, cut])
-
-
-def project_kernel(place, window_ref, row_ref, sums_ref, rest_ref, stats_ref, weight_ref, other_ref, *refs, cols):
-    out_ref, total_ref = refs[-2:]
+    tokens, width = base_ref.shape
+    near = spread_pieces(sums_ref[...], 0, width // HEAD)
+    far = spread_pieces(unfold_stats(stats_ref[...], tokens), 0, width // HEAD)
+    share = 1.0 / (1.0 + jnp.exp2(near - jnp.where(inner, NEG, far)))
+    rest, row = rest_ref[...].astype(jnp.float32), row_ref[...].astype(jnp.float32)
+    return (base_ref[...] + (rest - row) * share).astype(jnp.bfloat16)
+
+
+def merge_kernel(place, base_ref, row_ref, sums_ref, rest_ref, stats_ref, out_ref, *, cols):
+    out_ref[...] = merged(place, base_ref, row_ref, sums_ref, rest_ref, stats_ref, cols)
+
+
+def project_kernel(place, base_ref, row_ref, sums_ref, rest_ref, stats_ref, weight_ref, other_ref, *refs, cols):
+    out_ref, rows_ref = refs[-2:]
 
     @pl.when(pl.program_id(0) == 0)
     def _():
-        total_ref[...] = other_ref[...].astype(jnp.float32)
-
-    heads = window_ref.shape[1] // HEAD
-    rows = merged(
-        place, window_ref[...], row_ref[...], sums_ref[...], rest_ref[...],
-        unfold_stats(stats_ref[...], rest_ref.shape[0]), cols, pl.program_id(0) * heads, heads,
-    )
-    add_product(total_ref, rows, weight_ref)
-
-    @pl.when(pl.program_id(0) == pl.num_programs(0) - 1)
-    def _():
-        out_ref[...] = total_ref[...].astype(jnp.bfloat16)
-
-
-def product_kernel(rows_ref, weight_ref, out_ref, total_ref):
-    @pl.when(pl.program_id(0) == 0)
-    def _():
-        total_ref[...] = jnp.zeros_like(total_ref)
-
-    add_product(total_ref, rows_ref[...], weight_ref)
-
-    @pl.when(pl.program_id(0) == pl.num_programs(0) - 1)
-    def _():
-        out_ref[...] = total_ref[...].astype(jnp.bfloat16)
+        rows_ref[...] = merged(place, base_ref, row_ref, sums_ref, rest_ref, stats_ref, cols)
+
+    total = other_ref[...].astype(jnp.float32) + dot_nn(rows_ref[...], weight_ref[...])
+    out_ref[...] = total.astype(jnp.bfloat16)
+
+
+def product_kernel(rows_ref, weight_ref, out_ref):
+    out_ref[...] = dot_nn(rows_ref[...], weight_ref[...]).astype(jnp.bfloat16)
 
 
 def hbm(*values):
@@ -260,7 +248,7 @@
         def _():
             turn(k_ref, v_ref, out_ref)
 
-    return pl.pallas_call(
+    return kernel_call(
         kernel,
         out_shape=jax.ShapeDtypeStruct((1 + len(given), S, 2, tokens, width), keys.dtype),
         grid_spec=pltpu.PrefetchScalarGridSpec(
@@ -284,7 +272,7 @@
     def kernel(place, in_ref, out_ref):
         out_ref[...] = in_ref[...]
 
-    return pl.pallas_call(
+    return kernel_call(
         kernel,
         out_shape=jax.ShapeDtypeStruct((S, tokens, width), value.dtype),
         grid_spec=pltpu.PrefetchScalarGridSpec(
@@ -312,7 +300,7 @@
             pl.BlockSpec((None, None, 2, tokens, width), lambda g, p: (1, stream, 0, 0, 0)),
             pl.BlockSpec((None, tokens, width), lambda g, p: (stream, 0, side(1, p))),
         ]
-    return pl.pallas_call(
+    return kernel_call(
         functools.partial(edge_kernel, heads=heads, cols_tile=cols_tile, cols=cols),
         out_shape=jax.ShapeDtypeStruct((rows, width), jnp.bfloat16),
         grid_spec=pltpu.PrefetchScalarGridSpec(
@@ -342,18 +330,19 @@
     heads = width // HEAD
     lanes = block * HEAD
     steps = heads // block
+    place_of = stream if sides[0].shape[1] > 1 else 0
     own = pl.BlockSpec((None, None, 2, tokens, lanes), lambda g, p: (half, stream, 0, 0, g))
-    near = pl.BlockSpec((None, None, 2, tokens, lanes), lambda g, p: (0, stream, 0, 0, g))
-    other = pl.BlockSpec((None, None, 2, tokens, lanes), lambda g, p: (1, stream, 0, 0, g))
+    near = pl.BlockSpec((None, None, 2, tokens, lanes), lambda g, p: (0, place_of, 0, 0, g))
+    other = pl.BlockSpec((None, None, 2, tokens, lanes), lambda g, p: (1, place_of, 0, 0, g))
     args = [x for tile, pair in zip(tiles, sides) for x in (tile, pair, pair)]
     kernel = functools.partial(
         rows_kernel, heads=block, half=half, grid=grid, cols_tile=cols_tile, frame_tokens=frame_tokens
     )
-    return pl.pallas_call(
+    return kernel_call(
         kernel,
         out_shape=(
             jax.ShapeDtypeStruct((tokens, width), jnp.float32),
-            jax.ShapeDtypeStruct((tokens, width), jnp.float32),
+            jax.ShapeDtypeStruct((tokens, width), jnp.bfloat16),
             jax.ShapeDtypeStruct((tokens, HEAD), jnp.bfloat16),
         ),
         grid_spec=pltpu.PrefetchScalarGridSpec(
@@ -389,7 +378,7 @@
     tokens, width = parts[0].shape
     at = rest.shape[0] // tokens - 1
     whole = pl.BlockSpec((tokens, width), lambda g, p: (0, 0))
-    return pl.pallas_call(
+    return kernel_call(
         functools.partial(merge_kernel, cols=cols),
         out_shape=jax.ShapeDtypeStruct((tokens, width), jnp.bfloat16),
         grid_spec=pltpu.PrefetchScalarGridSpec(
@@ -412,32 +401,31 @@
     )(place, *parts, rest, rest)
 
 
-def project(place, parts, rest, weight, other, output, stream, cols, block=3):
+def project(place, parts, rest, weight, other, output, stream, cols, lanes=512):
     tokens, width = parts[0].shape
     at = rest.shape[0] // tokens - 1
-    lanes = block * HEAD
     streams, _, model = weight.shape
     earlier = [] if output is None else [output]
-    cut = pl.BlockSpec((tokens, lanes), lambda g, p: (0, g))
+    whole = pl.BlockSpec((tokens, width), lambda g, p: (0, 0))
     args = [place, *parts, rest, rest, weight, other]
-    return pl.pallas_call(
+    return kernel_call(
         functools.partial(project_kernel, cols=cols),
         out_shape=jax.ShapeDtypeStruct((streams, tokens, model), jnp.bfloat16),
         grid_spec=pltpu.PrefetchScalarGridSpec(
             num_scalar_prefetch=1,
-            grid=(width // lanes,),
+            grid=(model // lanes,),
             in_specs=[
-                cut,
-                cut,
+                whole,
+                whole,
                 pl.BlockSpec((tokens, HEAD), lambda g, p: (0, 0)),
-                pl.BlockSpec((tokens, lanes), lambda g, p: (at, g)),
+                pl.BlockSpec((tokens, width), lambda g, p: (at, 0)),
                 pl.BlockSpec((FOLD, width), lambda g, p: ((at + 1) * tokens // FOLD, 0)),
-                pl.BlockSpec((None, lanes, model), lambda g, p: (stream, g, 0)),
-                pl.BlockSpec((tokens, model), lambda g, p: (0, 0)),
+                pl.BlockSpec((None, width, lanes), lambda g, p: (stream, 0, g)),
+                pl.BlockSpec((tokens, lanes), lambda g, p: (0, g)),
                 *[ANY] * len(earlier),
             ],
-            out_specs=pl.BlockSpec((None, tokens, model), lambda g, p: (stream, 0, 0)),
-            scratch_shapes=[pltpu.VMEM((tokens, model), jnp.float32)],
+            out_specs=pl.BlockSpec((None, tokens, lanes), lambda g, p: (stream, 0, g)),
+            scratch_shapes=[pltpu.VMEM((tokens, width), jnp.bfloat16)],
         ),
         input_output_aliases={len(args): 0} if earlier else {},
         compiler_params=params(),
@@ -448,20 +436,18 @@
     )(*args, *earlier)
 
 
-def product(rows, weight, stream, block=3):
+def product(rows, weight, stream, lanes=512):
     tokens, width = rows.shape
     model = weight.shape[2]
-    lanes = block * HEAD
-    return pl.pallas_call(
+    return kernel_call(
         product_kernel,
         out_shape=jax.ShapeDtypeStruct((tokens, model), jnp.bfloat16),
-        grid=(width // lanes,),
+        grid=(model // lanes,),
         in_specs=[
-            pl.BlockSpec((tokens, lanes), lambda g: (0, g)),
-            pl.BlockSpec((None, lanes, model), lambda g: (stream, g, 0)),
+            pl.BlockSpec((tokens, width), lambda g: (0, 0)),
+            pl.BlockSpec((None, width, lanes), lambda g: (stream, 0, g)),
         ],
-        out_specs=pl.BlockSpec((tokens, model), lambda g: (0, 0)),
-        scratch_shapes=[pltpu.VMEM((tokens, model), jnp.float32)],
+        out_specs=pl.BlockSpec((tokens, lanes), lambda g: (0, g)),
         compiler_params=params(),
         cost_estimate=pl.CostEstimate(
             flops=2 * tokens * width * model, bytes_accessed=2 * width * model, transcendentals=0
@@ -489,7 +475,8 @@
     sent = {}
 
     def tied(value, after):
-        return lax.optimization_barrier((value, *[sent[n] for n in after]))[0] if after else value
+        earlier = [sent[n] if isinstance(n, str) else n for n in after]
+        return lax.optimization_barrier((value, *earlier))[0] if earlier else value
 
     def send(name, value, axis, pairs, *after):
         sent[name] = lax.ppermute(tied(value, after), axis, pairs)
@@ -498,8 +485,8 @@
     row_pairs, row_others = swaps(rows, 0), swaps(rows, 1)
     pair_swap = swaps(2, 0)
     own0 = pack(place, k, v, 0)
-    own = pack(place, k, v, 1, own0)
     picked = pick(place, q, 0).reshape(S * tokens, half)
+    own = pack(tied(place, [picked]), k, v, 1, own0)
 
     def mix(s, *after):
         sent[f"part0{s}"] = edge_attend(
@@ -516,7 +503,8 @@
 
     def rows_of(h, s, *after):
         tiles = [sent["pair_own"], own, sent["next_own"]]
-        sides = [sent[f"pair_sides{h}"], sent[f"sides{h}"], sent[f"next_sides{h}"]]
+        part = f"{h}" if h == 0 else f"{h}{s}"
+        sides = [sent[f"pair_sides{part}"], sent[f"sides{part}"], sent[f"next_sides{part}"]]
         sent[f"rows{h}{s}"] = rows_attend(
             place, tied(mask, after), frame_reach, q, tiles, sides, sent[f"far{h}{s}"], h, s, C, R * C, (rows, cols)
         )
@@ -526,37 +514,41 @@
     send("next_own", own, "row", row_others)
     send("pair_own", own, "row", row_pairs)
     send("q0", picked, "col", inward)
-    send("far00", sent["near0"][:1], "col", col_others, "near0", "other0", "pair_own")
-    send("far01", sent["near0"][1:], "col", col_others, "near0", "other0", "pair_own")
+    send("far00", sent["near0"][:1], "col", col_others, "other0", "pair_own", "next_own")
+    send("far01", sent["near0"][1:], "col", col_others, "near0")
     sent["sides0"] = jnp.stack([sent["near0"], sent["other0"]])
-    send("next_sides0", sent["sides0"], "row", row_others, "next_own")
-    send("pair_sides0", sent["sides0"], "row", row_pairs, "q0")
+    send("next_sides0", sent["sides0"], "row", row_others)
+    send("pair_sides0", sent["sides0"], "row", row_pairs, "other0")
     mix(0)
     send("mix0", sent["part00"], "col", col_pairs)
-    send("other1", own[1], "col", col_others, "far00")
-    mix(1)
+    send("other1", own[1], "col", col_others, "far01", "next_sides0", "pair_sides0")
+    mix(1, "part00")
     send("mix1", sent["part01"], "col", col_pairs)
     rows_of(0, 0)
     rows_of(0, 1)
     sent["merged0"] = merge(tied(place, []), sent["rows00"], sent["mix0"], cols)
     send("theirs0", sent["merged0"], "pair", pair_swap)
+    sent["product0"] = product(tied(sent["theirs0"], ["rows01"]), out_weight, 0)
+    send("back0", sent["product0"], "pair", pair_swap)
+    sent["mix1"] = tied(sent["mix1"], ["theirs0"])
     sent["merged1"] = merge(tied(place, []), sent["rows01"], sent["mix1"], cols)
-    send("theirs1", sent["merged1"], "pair", pair_swap)
-    sent["product0"] = product(tied(sent["theirs0"], []), out_weight, 0)
-    send("back0", sent["product0"], "pair", pair_swap)
+    send("theirs1", sent["merged1"], "pair", pair_swap, "back0")
     sent["product1"] = product(tied(sent["theirs1"], []), out_weight, 1)
     send("back1", sent["product1"], "pair", pair_swap)
-    send("far10", near1(0), "col", col_others, "far01", "pair_sides0", "next_sides0")
-    send("far11", near1(1), "col", col_others, "other1")
-    sent["sides1"] = jnp.stack([jnp.concatenate([near1(0), near1(1)]), sent["other1"]])
-    send("next_sides1", sent["sides1"], "row", row_others)
-    send("pair_sides1", sent["sides1"], "row", row_pairs)
+    send("far10", near1(0), "col", col_others, "theirs0")
+    sent["sides10"] = jnp.stack([near1(0), tied(sent["other1"][0:1], ["theirs0"])])
+    send("next_sides10", sent["sides10"], "row", row_others)
+    send("pair_sides10", sent["sides10"], "row", row_pairs)
+    send("far11", near1(1), "col", col_others)
+    sent["sides11"] = jnp.stack([near1(1), tied(sent["other1"][1:2], ["theirs0"])])
+    send("next_sides11", sent["sides11"], "row", row_others)
+    send("pair_sides11", sent["sides11"], "row", row_pairs)
     edge(0)
     send("rest10", sent["part10"], "col", outward)
-    edge(1)
+    edge(1, "part10", "next_sides10")
     send("rest11", sent["part11"], "col", outward)
     rows_of(1, 0)
-    rows_of(1, 1)
+    rows_of(1, 1, "rows10")
     output = project(tied(place, []), sent["rows10"], sent["rest10"], out_weight, sent["back0"], None, 0, cols)
     output = project(place, sent["rows11"], sent["rest11"], out_weight, sent["back1"], output, 1, cols)
     return output.reshape(S, F, R, C, model)

time: 172 us -> 156 us (0.907)
  waiting for transfers between devices: 62.8 us -> 43.3 us
  starting transfers between devices: 48.2 us -> 55.9 us
  local copies, waits for them, and re-layouts: 7.96 us -> 1.42 us
  Pallas kernels: 48.5 us -> 51.4 us
    ppermute x22 -> x24, waiting for transfers between devices: 62.8 us -> 43.3 us  [send(): sent[name] = lax.ppermute(tied(value, after), axis, pairs)]
    ppermute x22 -> x24, starting transfers between devices: 48.2 us -> 55.9 us  [send(): sent[name] = lax.ppermute(tied(value, after), axis, pairs)]
    unnamed x32 -> x16, local copies, waits for them, and re-layouts: 6.85 us -> 0.04 us
    pallas_call x17, Pallas kernels: 48.5 us -> 51.4 us  [the longest x4 23.3 us: rows_attend(): kernel_call(kernel, out_shape=(jax.ShapeDtypeStruct((tokens, width), jnp....]
  transfers between devices with their start and end apart: 22 -> 24, of which waited for: 7 -> 5; matrix products, arithmetic and copies ran while one was open for 2% -> 1% of each run, Pallas kernels for 23% -> 29%
where the time goes in v7:
time: 156 us; the launch traced here: 153 us
  starting transfers between devices  55.9 us (36%)
  Pallas kernels  51.4 us (33%)
  waiting for transfers between devices  43.3 us (28%)
    ppermute x24, starting transfers between devices, send(): sent[name] = lax.ppermute(tied(value, after), axis, pairs)  55.9 us
    ppermute x24, waiting for transfers between devices, send(): sent[name] = lax.ppermute(tied(value, after), axis, pairs)  43.3 us
    pallas_call x4, Pallas kernels, rows_attend(): kernel_call(kernel, out_shape=(jax.ShapeDtypeStruct((tokens, width), jnp....  23.3 us
    pallas_call x2, Pallas kernels, project(): kernel_call(functools.partial(project_kernel, cols=cols), out_shape=jax.S...  9.65 us
    pallas_call x2, Pallas kernels, product(): kernel_call(product_kernel, out_shape=jax.ShapeDtypeStruct((tokens, model...  5.35 us
    pallas_call x2, Pallas kernels, pack(): kernel_call(kernel, out_shape=jax.ShapeDtypeStruct((1 + len(given), S, 2,...  5.08 us
    pallas_call x4, Pallas kernels, edge_attend(): kernel_call(functools.partial(edge_kernel, heads=heads, cols_tile=cols_ti...  4.29 us
  transfers between devices with their start and end apart: 24, of which 5 were waited for; matrix products, arithmetic and copies ran while one was open for 1% of the time, Pallas kernels for 29%

profile of v7, /device:TPU:0, one launch (start us, length us, event | category | flops | bytes accessed | tf_op | source)
XLA Modules:
  0.0 153.1 jit_solution(4594097236501318470)
XLA Ops:
  0.1 2.0 %pack.2.refs_0_ = bf16[1,2,2,128,1152]{4,3,2,1,0:T(8,128)(2,1)S(1)} custom-call(s32[3]{0:T(128)S(1)} %pad_add_fusion.place, bf16[2,128,2304]{2,1,0:T(8,128)(2,1)} %bitcast.38, bf16[2,128,2304]{2,1,0:T(8,128)(2,1)} %bitcast.40), custom_call_target="tpu_custom_call" | custom-call | bytes 9437184 | tf_op jit(solution)/shard_map/pack/pallas_call | solution.py:251
  2.1 3.1 %collective-permute-start.3 = (bf16[2,2,128,1152]{3,2,1,0:T(8,128)(2,1)S(1)}, bf16[2,2,128,1152]{3,2,1,0:T(8,128)(2,1)S(1)}, u32[]{:S(2)}, u32[]{:S(2)}) collective-permute-start(bf16[2,2,128,1152]{3,2,1,0:T(8,128)(2,1)S(1)} %bitcast.23), channel_id=1, source_target_pairs={{0,1},{2,3},{1,0},{3,2},{4,5},{6,7},{5,4},{7,6},{8,9},{10,11},{9,8... | collective-permute-start | bytes 3538952 | tf_op jit(solution)/shard_map/ppermute | solution.py:482
  5.9 1.6 %pick.1 = bf16[2,128,1152]{2,1,0:T(8,128)(2,1)S(1)} custom-call(s32[3]{0:T(128)S(1)} %pad_add_fusion.place, bf16[2,128,2304]{2,1,0:T(8,128)(2,1)} %bitcast.30), custom_call_target="tpu_custom_call" | custom-call | bytes 4718592 | tf_op jit(solution)/shard_map/pick/pallas_call | solution.py:275
  7.5 3.1 %pack.3.refs_0_.refs_3_ = bf16[2,2,2,128,1152]{4,3,2,1,0:T(8,128)(2,1)S(1)} custom-call(s32[3]{0:T(128)S(1)} %pad_add_fusion.place, bf16[2,128,2304]{2,1,0:T(8,128)(2,1)} %bitcast.39, bf16[2,128,2304]{2,1,0:T(8,128)(2,1)} %bitcast.41, bf16[1,2,2,128,1152]{4,3,2,1,0:T(8,128)(2,1)S(1)} %pack.2.refs_0_), custom_call_target="tpu_custom_call" | custom-call | bytes 9437184 | tf_op jit(solution)/shard_map/pack/pallas_call | solution.py:251
  10.6 0.8 collective-permute-start.4
  11.5 2.8 %collective-permute-start = (bf16[2,2,2,128,1152]{4,3,2,1,0:T(8,128)(2,1)S(1)}, bf16[2,2,2,128,1152]{4,3,2,1,0:T(8,128)(2,1)S(1)}, u32[]{:S(2)}, u32[]{:S(2)}) collective-permute-start(bf16[2,2,2,128,1152]{4,3,2,1,0:T(8,128)(2,1)S(1)} %pack.3.refs_0_.refs_3_), channel_id=1, source_target_pairs={{0,4},{8,12},{4,0},{12,8},{1,5},{9,13},{5,1},{13,9},{2,6},{10,14},... | collective-permute-start | bytes 7077896 | tf_op jit(solution)/shard_map/ppermute | solution.py:482
  14.3 16.8 %collective-permute-done.3 = bf16[2,2,128,1152]{3,2,1,0:T(8,128)(2,1)S(1)} collective-permute-done((bf16[2,2,128,1152]{3,2,1,0:T(8,128)(2,1)S(1)}, bf16[2,2,128,1152]{3,2,1,0:T(8,128)(2,1)S(1)}, u32[]{:S(2)}, u32[]{:S(2)}) %collective-permute-start.3) | collective-permute-done | bytes 1179680 | tf_op jit(solution)/shard_map/ppermute | solution.py:482
  32.3 6.7 %collective-permute-start.1 = (bf16[256,1152]{1,0:T(8,128)(2,1)S(1)}, bf16[256,1152]{1,0:T(8,128)(2,1)S(1)}, u32[]{:S(2)}, u32[]{:S(2)}) collective-permute-start(bf16[256,1152]{1,0:T(8,128)(2,1)S(1)} %bitcast.25), channel_id=1, source_target_pairs={{0,1},{3,2},{4,5},{7,6},{8,9},{11,10},{12,13},{15,14},{16,17},{19,... | collective-permute-start | bytes 1769480 | tf_op jit(solution)/shard_map/ppermute | solution.py:482
  40.5 10.3 %collective-permute-done.1.q_ref = bf16[256,1152]{1,0:T(8,128)(2,1)S(1)} collective-permute-done((bf16[256,1152]{1,0:T(8,128)(2,1)S(1)}, bf16[256,1152]{1,0:T(8,128)(2,1)S(1)}, u32[]{:S(2)}, u32[]{:S(2)}) %collective-permute-start.1) | collective-permute-done | bytes 589856 | tf_op jit(solution)/shard_map/ppermute | solution.py:482
  50.8 1.6 %edge_rows.4 = bf16[400,1152]{1,0:T(8,128)(2,1)S(1)} custom-call(s32[3]{0:T(128)S(1)} %pad_add_fusion.place, bf16[256,1152]{1,0:T(8,128)(2,1)S(1)} %collective-permute-done.1.q_ref, bf16[2,2,128,1152]{3,2,1,0:T(8,128)(2,1)S(1)} %collective-permute-done.2.near_ref, bf16[1,2,128,1152]{3,2,1,0:T(8,128)(2,1)S(1)} %collective-permute-done.5.far_ref.refs_9_, ...), custom_call_target="tpu_custom_call" | custom-call | flops 603979776 | bytes 8257536 | tf_op jit(solution)/shard_map/edge_rows/pallas_call | solution.py:303
  52.4 3.3 %collective-permute-start.6 = (bf16[400,1152]{1,0:T(8,128)(2,1)S(1)}, bf16[400,1152]{1,0:T(8,128)(2,1)S(1)}, u32[]{:S(2)}, u32[]{:S(2)}) collective-permute-start(bf16[400,1152]{1,0:T(8,128)(2,1)S(1)} %edge_rows.4), channel_id=1, source_target_pairs={{0,1},{2,3},{1,0},{3,2},{4,5},{6,7},{5,4},{7,6},{8,9},{10,11},{9,8... | collective-permute-start | bytes 2764808 | tf_op jit(solution)/shard_map/ppermute | solution.py:482
  55.7 1.1 slice_bitcast_fusion
  57.6 1.6 %edge_rows.5 = bf16[400,1152]{1,0:T(8,128)(2,1)S(1)} custom-call(s32[3]{0:T(128)S(1)} %pad_add_fusion.place, bf16[256,1152]{1,0:T(8,128)(2,1)S(1)} %collective-permute-done.1.q_ref, bf16[2,2,128,1152]{3,2,1,0:T(8,128)(2,1)S(1)} %collective-permute-done.2.near_ref, bf16[1,2,128,1152]{3,2,1,0:T(8,128)(2,1)S(1)} %collective-permute-done.7.far_ref.refs_9_, ...), custom_call_target="tpu_custom_call" | custom-call | flops 603979776 | bytes 8257536 | tf_op jit(solution)/shard_map/edge_rows/pallas_call | solution.py:303
  59.2 11.5 %collective-permute-start.15 = (bf16[400,1152]{1,0:T(8,128)(2,1)S(1)}, bf16[400,1152]{1,0:T(8,128)(2,1)S(1)}, u32[]{:S(2)}, u32[]{:S(2)}) collective-permute-start(bf16[400,1152]{1,0:T(8,128)(2,1)S(1)} %edge_rows.5), channel_id=1, source_target_pairs={{0,1},{2,3},{1,0},{3,2},{4,5},{6,7},{5,4},{7,6},{8,9},{10,11},{9,8... | collective-permute-start | bytes 2764808 | tf_op jit(solution)/shard_map/ppermute | solution.py:482
  70.7 5.6 %rows.4 = (f32[128,1152]{1,0:T(8,128)S(1)}, bf16[128,1152]{1,0:T(8,128)(2,1)S(1)}, bf16[128,128]{1,0:T(8,128)(2,1)S(1)}) custom-call(s32[3]{0:T(128)S(1)} %pad_add_fusion.place, s32[9]{0:T(128)S(1)} %bitcast.26, s32[18]{0:T(128)S(1)} %copy-done.3, bf16[2,128,2304]{2,1,0:T(8,128)(2,1)} %bitcast.33, ...), custom_call_target="tpu_custom_call" | custom-call | flops 3472883712 | bytes 31850496 | tf_op jit(solution)/shard_map/rows/pallas_call | solution.py:341
  76.4 1.1 merge.2
  77.5 1.5 collective-permute-start.11
  79.0 6.4 %rows.7 = (f32[128,1152]{1,0:T(8,128)S(1)}, bf16[128,1152]{1,0:T(8,128)(2,1)S(1)}, bf16[128,128]{1,0:T(8,128)(2,1)S(1)}) custom-call(s32[3]{0:T(128)S(1)} %pad_add_fusion.place, s32[9]{0:T(128)S(1)} %bitcast.27, s32[18]{0:T(128)S(1)} %copy-done.3, bf16[2,128,2304]{2,1,0:T(8,128)(2,1)} %bitcast.34, ...), custom_call_target="tpu_custom_call" | custom-call | flops 3472883712 | bytes 31850496 | tf_op jit(solution)/shard_map/rows/pallas_call | solution.py:341
  85.5 2.7 %product.2 = bf16[128,3072]{1,0:T(8,128)(2,1)S(1)} custom-call(bf16[128,1152]{1,0:T(8,128)(2,1)S(1)} %collective-permute-done.11.rows_ref, bf16[2,1152,3072]{2,1,0:T(8,128)(2,1)S(1)} %bitcast.21), custom_call_target="tpu_custom_call" | custom-call | flops 3623878656 | bytes 28311552 | tf_op jit(solution)/shard_map/product/pallas_call | solution.py:442
  89.8 11.0 %collective-permute-start.12 = (bf16[2,1,2,128,1152]{4,3,2,1,0:T(8,128)(2,1)S(1)}, bf16[2,1,2,128,1152]{4,3,2,1,0:T(8,128)(2,1)S(1)}, u32[]{:S(2)}, u32[]{:S(2)}) collective-permute-start(bf16[2,1,2,128,1152]{4,3,2,1,0:T(8,128)(2,1)S(1)} %pad_maximum_fusion.1.refs_4_.refs_5_), channel_id=1, source_target_pairs={{0,4},{8,12},{4,0},{12,8},{1,5},{9,13},{5,1},{13,9},{2,6},{10,14},... | collective-permute-start | bytes 3538952 | tf_op jit(solution)/shard_map/ppermute | solution.py:482
  101.5 1.1 merge.3
  102.5 1.9 %collective-permute-done.20.other_ref = bf16[128,3072]{1,0:T(8,128)(2,1)S(1)} collective-permute-done((bf16[128,3072]{1,0:T(8,128)(2,1)S(1)}, bf16[128,3072]{1,0:T(8,128)(2,1)S(1)}, u32[]{:S(2)}, u32[]{:S(2)}) %collective-permute-start.20) | collective-permute-done | bytes 786464 | tf_op jit(solution)/shard_map/ppermute | solution.py:482
  106.4 5.4 %collective-permute-done.21.rows_ref = bf16[128,1152]{1,0:T(8,128)(2,1)S(1)} collective-permute-done((bf16[128,1152]{1,0:T(8,128)(2,1)S(1)}, bf16[128,1152]{1,0:T(8,128)(2,1)S(1)}, u32[]{:S(2)}, u32[]{:S(2)}) %collective-permute-start.21) | collective-permute-done | bytes 294944 | tf_op jit(solution)/shard_map/ppermute | solution.py:482
  111.9 4.7 %collective-permute-start.16 = (bf16[2,1,2,128,1152]{4,3,2,1,0:T(8,128)(2,1)S(1)}, bf16[2,1,2,128,1152]{4,3,2,1,0:T(8,128)(2,1)S(1)}, u32[]{:S(2)}, u32[]{:S(2)}) collective-permute-start(bf16[2,1,2,128,1152]{4,3,2,1,0:T(8,128)(2,1)S(1)} %pad_maximum_fusion.2.refs_4_.refs_5_), channel_id=1, source_target_pairs={{0,4},{8,12},{4,0},{12,8},{1,5},{9,13},{5,1},{13,9},{2,6},{10,14},... | collective-permute-start | bytes 3538952 | tf_op jit(solution)/shard_map/ppermute | solution.py:482
  117.2 2.7 %product.3 = bf16[128,3072]{1,0:T(8,128)(2,1)S(1)} custom-call(bf16[128,1152]{1,0:T(8,128)(2,1)S(1)} %collective-permute-done.21.rows_ref, bf16[2,1152,3072]{2,1,0:T(8,128)(2,1)S(1)} %bitcast.21), custom_call_target="tpu_custom_call" | custom-call | flops 3623878656 | bytes 28311552 | tf_op jit(solution)/shard_map/product/pallas_call | solution.py:442
  119.9 1.5 collective-permute-start.23
  122.1 1.3 collective-permute-start.19
  123.4 5.6 %rows.5 = (f32[128,1152]{1,0:T(8,128)S(1)}, bf16[128,1152]{1,0:T(8,128)(2,1)S(1)}, bf16[128,128]{1,0:T(8,128)(2,1)S(1)}) custom-call(s32[3]{0:T(128)S(1)} %pad_add_fusion.place, s32[9]{0:T(128)S(1)} %bitcast.28, s32[18]{0:T(128)S(1)} %copy-done.3, bf16[2,128,2304]{2,1,0:T(8,128)(2,1)} %bitcast.35, ...), custom_call_target="tpu_custom_call" | custom-call | flops 3472883712 | bytes 31850496 | tf_op jit(solution)/shard_map/rows/pallas_call | solution.py:341
  129.0 8.8 %collective-permute-done.23.rest_ref.stats_ref = bf16[144,1152]{1,0:T(8,128)(2,1)S(1)} collective-permute-done((bf16[144,1152]{1,0:T(8,128)(2,1)S(1)}, bf16[144,1152]{1,0:T(8,128)(2,1)S(1)}, u32[]{:S(2)}, u32[]{:S(2)}) %collective-permute-start.23) | collective-permute-done | bytes 331808 | tf_op jit(solution)/shard_map/ppermute | solution.py:482
  137.8 4.8 %project.2.refs_0_ = bf16[2,128,3072]{2,1,0:T(8,128)(2,1)} custom-call(s32[3]{0:T(128)S(1)} %pad_add_fusion.place, f32[128,1152]{1,0:T(8,128)S(1)} %get-tuple-element.41.base_ref, bf16[128,1152]{1,0:T(8,128)(2,1)S(1)} %get-tuple-element.42.row_ref, bf16[128,128]{1,0:T(8,128)(2,1)S(1)} %get-tuple-element.43.sums_ref, ...), custom_call_target="tpu_custom_call" | custom-call | flops 3623878656 | bytes 28311552 | tf_op jit(solution)/shard_map/project/pallas_call | solution.py:411
  142.6 5.6 %rows.6 = (f32[128,1152]{1,0:T(8,128)S(1)}, bf16[128,1152]{1,0:T(8,128)(2,1)S(1)}, bf16[128,128]{1,0:T(8,128)(2,1)S(1)}) custom-call(s32[3]{0:T(128)S(1)} %pad_add_fusion.place, s32[9]{0:T(128)S(1)} %bitcast.29, s32[18]{0:T(128)S(1)} %copy-done.3, bf16[2,128,2304]{2,1,0:T(8,128)(2,1)} %bitcast.36, ...), custom_call_target="tpu_custom_call" | custom-call | flops 3472883712 | bytes 31850496 | tf_op jit(solution)/shard_map/rows/pallas_call | solution.py:341
  148.3 4.8 %project.3 = bf16[2,128,3072]{2,1,0:T(8,128)(2,1)} custom-call(s32[3]{0:T(128)S(1)} %pad_add_fusion.place, f32[128,1152]{1,0:T(8,128)S(1)} %get-tuple-element.48.base_ref, bf16[128,1152]{1,0:T(8,128)(2,1)S(1)} %get-tuple-element.49.row_ref, bf16[128,128]{1,0:T(8,128)(2,1)S(1)} %get-tuple-element.50.sums_ref, ...), custom_call_target="tpu_custom_call", output_to_operand_aliasing={{}: (8, {})} | custom-call | flops 3623878656 | bytes 28311552 | tf_op jit(solution)/shard_map/project/pallas_call | solution.py:411
  (59 shorter events, 9.8 us)
Async XLA Ops:
  2.1 29.1 %collective-permute-start.3 = (bf16[2,2,128,1152]{3,2,1,0:T(8,128)(2,1)S(1)}, bf16[2,2,128,1152]{3,2,1,0:T(8,128)(2,1)S(1)}, u32[]{:S(2)}, u32[]{:S(2)}) collective-permute-start(bf16[2,2,128,1152]{3,2,1,0:T(8,128)(2,1)S(1)} %bitcast.23), channel_id=1, source_target_pairs={{0,1},{2,3},{1,0},{3,2},{4,5},{6,7},{5,4},{7,6},{8,9},{10,11},{9,8... | collective-permute-start | bytes 3538952 | tf_op jit(solution)/shard_map/ppermute | solution.py:482
  5.1 26.0 %collective-permute-start.2 = (bf16[2,2,128,1152]{3,2,1,0:T(8,128)(2,1)S(1)}, bf16[2,2,128,1152]{3,2,1,0:T(8,128)(2,1)S(1)}, u32[]{:S(2)}, u32[]{:S(2)}) collective-permute-start(bf16[2,2,128,1152]{3,2,1,0:T(8,128)(2,1)S(1)} %bitcast.24), channel_id=1, source_target_pairs={{1,2},{2,1},{5,6},{6,5},{9,10},{10,9},{13,14},{14,13},{17,18},{18,... | collective-permute-start | bytes 3538952 | tf_op jit(solution)/shard_map/ppermute | solution.py:482
  10.6 28.4 %collective-permute-start.4 = (bf16[2,2,2,128,1152]{4,3,2,1,0:T(8,128)(2,1)S(1)}, bf16[2,2,2,128,1152]{4,3,2,1,0:T(8,128)(2,1)S(1)}, u32[]{:S(2)}, u32[]{:S(2)}) collective-permute-start(bf16[2,2,2,128,1152]{4,3,2,1,0:T(8,128)(2,1)S(1)} %pack.3.refs_0_.refs_3_), channel_id=1, source_target_pairs={{4,8},{8,4},{5,9},{9,5},{6,10},{10,6},{7,11},{11,7},{20,24},{24,20... | collective-permute-start | bytes 7077896 | tf_op jit(solution)/shard_map/ppermute | solution.py:482
  11.5 27.6 %collective-permute-start = (bf16[2,2,2,128,1152]{4,3,2,1,0:T(8,128)(2,1)S(1)}, bf16[2,2,2,128,1152]{4,3,2,1,0:T(8,128)(2,1)S(1)}, u32[]{:S(2)}, u32[]{:S(2)}) collective-permute-start(bf16[2,2,2,128,1152]{4,3,2,1,0:T(8,128)(2,1)S(1)} %pack.3.refs_0_.refs_3_), channel_id=1, source_target_pairs={{0,4},{8,12},{4,0},{12,8},{1,5},{9,13},{5,1},{13,9},{2,6},{10,14},... | collective-permute-start | bytes 7077896 | tf_op jit(solution)/shard_map/ppermute | solution.py:482
  31.4 25.4 %collective-permute-start.9 = (bf16[2,2,2,128,1152]{4,3,2,1,0:T(8,128)(2,1)S(1)}, bf16[2,2,2,128,1152]{4,3,2,1,0:T(8,128)(2,1)S(1)}, u32[]{:S(2)}, u32[]{:S(2)}) collective-permute-start(bf16[2,2,2,128,1152]{4,3,2,1,0:T(8,128)(2,1)S(1)} %pad_maximum_fusion.refs_4_.refs_5_), channel_id=1, source_target_pairs={{0,4},{8,12},{4,0},{12,8},{1,5},{9,13},{5,1},{13,9},{2,6},{10,14},... | collective-permute-start | bytes 7077896 | tf_op jit(solution)/shard_map/ppermute | solution.py:482
  31.4 25.4 %collective-permute-start.8 = (bf16[2,2,2,128,1152]{4,3,2,1,0:T(8,128)(2,1)S(1)}, bf16[2,2,2,128,1152]{4,3,2,1,0:T(8,128)(2,1)S(1)}, u32[]{:S(2)}, u32[]{:S(2)}) collective-permute-start(bf16[2,2,2,128,1152]{4,3,2,1,0:T(8,128)(2,1)S(1)} %pad_maximum_fusion.refs_4_.refs_5_), channel_id=1, source_target_pairs={{4,8},{8,4},{5,9},{9,5},{6,10},{10,6},{7,11},{11,7},{20,24},{24,20... | collective-permute-start | bytes 7077896 | tf_op jit(solution)/shard_map/ppermute | solution.py:482
  32.3 18.5 %collective-permute-start.1 = (bf16[256,1152]{1,0:T(8,128)(2,1)S(1)}, bf16[256,1152]{1,0:T(8,128)(2,1)S(1)}, u32[]{:S(2)}, u32[]{:S(2)}) collective-permute-start(bf16[256,1152]{1,0:T(8,128)(2,1)S(1)} %bitcast.25), channel_id=1, source_target_pairs={{0,1},{3,2},{4,5},{7,6},{8,9},{11,10},{12,13},{15,14},{16,17},{19,... | collective-permute-start | bytes 1769480 | tf_op jit(solution)/shard_map/ppermute | solution.py:482
  39.1 11.7 %collective-permute-start.5 = (bf16[1,2,128,1152]{3,2,1,0:T(8,128)(2,1)S(1)}, bf16[1,2,128,1152]{3,2,1,0:T(8,128)(2,1)S(1)}, u32[]{:S(2)}, u32[]{:S(2)}) collective-permute-start(bf16[1,2,128,1152]{3,2,1,0:T(8,128)(2,1)S(1)} %get-tuple-element.32), channel_id=1, source_target_pairs={{1,2},{2,1},{5,6},{6,5},{9,10},{10,9},{13,14},{14,13},{17,18},{18,... | collective-permute-start | bytes 1769480 | tf_op jit(solution)/shard_map/ppermute | solution.py:482
  39.8 17.0 %collective-permute-start.7 = (bf16[1,2,128,1152]{3,2,1,0:T(8,128)(2,1)S(1)}, bf16[1,2,128,1152]{3,2,1,0:T(8,128)(2,1)S(1)}, u32[]{:S(2)}, u32[]{:S(2)}) collective-permute-start(bf16[1,2,128,1152]{3,2,1,0:T(8,128)(2,1)S(1)} %get-tuple-element.33), channel_id=1, source_target_pairs={{1,2},{2,1},{5,6},{6,5},{9,10},{10,9},{13,14},{14,13},{17,18},{18,... | collective-permute-start | bytes 1769480 | tf_op jit(solution)/shard_map/ppermute | solution.py:482
  52.4 24.0 %collective-permute-start.6 = (bf16[400,1152]{1,0:T(8,128)(2,1)S(1)}, bf16[400,1152]{1,0:T(8,128)(2,1)S(1)}, u32[]{:S(2)}, u32[]{:S(2)}) collective-permute-start(bf16[400,1152]{1,0:T(8,128)(2,1)S(1)} %edge_rows.4), channel_id=1, source_target_pairs={{0,1},{2,3},{1,0},{3,2},{4,5},{6,7},{5,4},{7,6},{8,9},{10,11},{9,8... | collective-permute-start | bytes 2764808 | tf_op jit(solution)/shard_map/ppermute | solution.py:482
  56.8 13.9 %copy-start.2 = (s32[1,1,1,9]{3,2,1,0:T(1,128)S(1)}, s32[1,1,1,9]{3,2,1,0:T(1,128)}, u32[]{:S(2)}) copy-start(s32[1,1,1,9]{3,2,1,0:T(1,128)} %param.9) | copy-start | bytes 112
  56.8 13.9 %copy-start.3 = (s32[18]{0:T(128)S(1)}, s32[18]{0:T(128)}, u32[]{:S(2)}) copy-start(s32[18]{0:T(128)} %reach.7) | copy-start | bytes 220
  56.8 13.9 %copy-start = (bf16[2,2,2,128,1152]{4,3,2,1,0:T(8,128)(2,1)}, bf16[2,2,2,128,1152]{4,3,2,1,0:T(8,128)(2,1)S(1)}, u32[]{:S(2)}) copy-start(bf16[2,2,2,128,1152]{4,3,2,1,0:T(8,128)(2,1)S(1)} %collective-permute-done.9.refs_1_.refs_2_) | copy-start | bytes 7077892
  56.8 32.0 %collective-permute-start.10 = (bf16[2,2,128,1152]{3,2,1,0:T(8,128)(2,1)}, bf16[2,2,128,1152]{3,2,1,0:T(8,128)(2,1)S(1)}, u32[]{:S(2)}, u32[]{:S(2)}) collective-permute-start(bf16[2,2,128,1152]{3,2,1,0:T(8,128)(2,1)} %slice_bitcast_fusion), channel_id=1, source_target_pairs={{1,2},{2,1},{5,6},{6,5},{9,10},{10,9},{13,14},{14,13},{17,18},{18,... | collective-permute-start | bytes 3538952 | tf_op jit(solution)/shard_map/ppermute | solution.py:482
  59.2 42.3 %collective-permute-start.15 = (bf16[400,1152]{1,0:T(8,128)(2,1)S(1)}, bf16[400,1152]{1,0:T(8,128)(2,1)S(1)}, u32[]{:S(2)}, u32[]{:S(2)}) collective-permute-start(bf16[400,1152]{1,0:T(8,128)(2,1)S(1)} %edge_rows.5), channel_id=1, source_target_pairs={{0,1},{2,3},{1,0},{3,2},{4,5},{6,7},{5,4},{7,6},{8,9},{10,11},{9,8... | collective-permute-start | bytes 2764808 | tf_op jit(solution)/shard_map/ppermute | solution.py:482
  76.4 2.7 %copy-start.1 = (bf16[2,2,2,128,1152]{4,3,2,1,0:T(8,128)(2,1)S(1)}, bf16[2,2,2,128,1152]{4,3,2,1,0:T(8,128)(2,1)}, u32[]{:S(2)}) copy-start(bf16[2,2,2,128,1152]{4,3,2,1,0:T(8,128)(2,1)} %copy-done) | copy-start | bytes 7077892
  76.4 9.1 %slice-start = ((s8[14155776]{0:T(1024)(128)(4,1)}), s8[4194304]{0:T(1024)(128)(4,1)S(1)}, s32[]{:S(2)}) async-start(s8[14155776]{0:T(1024)(128)(4,1)} %bitcast.20), calls=%async_computation | async-start | bytes 8388608
  77.5 8.0 %slice-start.1 = ((s8[14155776]{0:T(1024)(128)(4,1)}), s8[4194304]{0:T(1024)(128)(4,1)S(1)}, s32[]{:S(2)}) async-start(s8[14155776]{0:T(1024)(128)(4,1)} %bitcast.20), calls=%async_computation.1 | async-start | bytes 8388608
  77.5 8.0 %slice-start.2 = ((s8[14155776]{0:T(1024)(128)(4,1)}), s8[4194304]{0:T(1024)(128)(4,1)S(1)}, s32[]{:S(2)}) async-start(s8[14155776]{0:T(1024)(128)(4,1)} %bitcast.20), calls=%async_computation.2 | async-start | bytes 8388608
  77.5 8.0 %slice-start.3 = ((s8[14155776]{0:T(1024)(128)(4,1)}), s8[1572864]{0:T(1024)(128)(4,1)S(1)}, s32[]{:S(2)}) async-start(s8[14155776]{0:T(1024)(128)(4,1)} %bitcast.20), calls=%async_computation.3 | async-start | bytes 3145728
  77.5 8.0 %collective-permute-start.11 = (bf16[128,1152]{1,0:T(8,128)(2,1)S(1)}, bf16[128,1152]{1,0:T(8,128)(2,1)S(1)}, u32[]{:S(2)}, u32[]{:S(2)}) collective-permute-start(bf16[128,1152]{1,0:T(8,128)(2,1)S(1)} %merge.2), channel_id=1, source_target_pairs={{0,16},{16,0},{1,17},{17,1},{2,18},{18,2},{3,19},{19,3},{4,20},{20... | collective-permute-start | bytes 884744 | tf_op jit(solution)/shard_map/ppermute | solution.py:482
  88.2 16.3 %collective-permute-start.20 = (bf16[128,3072]{1,0:T(8,128)(2,1)S(1)}, bf16[128,3072]{1,0:T(8,128)(2,1)S(1)}, u32[]{:S(2)}, u32[]{:S(2)}) collective-permute-start(bf16[128,3072]{1,0:T(8,128)(2,1)S(1)} %product.2), channel_id=1, source_target_pairs={{0,16},{16,0},{1,17},{17,1},{2,18},{18,2},{3,19},{19,3},{4,20},{20... | collective-permute-start | bytes 2359304 | tf_op jit(solution)/shard_map/ppermute | solution.py:482
  89.1 30.8 %collective-permute-start.13 = (bf16[2,1,2,128,1152]{4,3,2,1,0:T(8,128)(2,1)S(1)}, bf16[2,1,2,128,1152]{4,3,2,1,0:T(8,128)(2,1)S(1)}, u32[]{:S(2)}, u32[]{:S(2)}) collective-permute-start(bf16[2,1,2,128,1152]{4,3,2,1,0:T(8,128)(2,1)S(1)} %pad_maximum_fusion.1.refs_4_.refs_5_), channel_id=1, source_target_pairs={{4,8},{8,4},{5,9},{9,5},{6,10},{10,6},{7,11},{11,7},{20,24},{24,20... | collective-permute-start | bytes 3538952 | tf_op jit(solution)/shard_map/ppermute | solution.py:482
  89.8 32.3 %collective-permute-start.12 = (bf16[2,1,2,128,1152]{4,3,2,1,0:T(8,128)(2,1)S(1)}, bf16[2,1,2,128,1152]{4,3,2,1,0:T(8,128)(2,1)S(1)}, u32[]{:S(2)}, u32[]{:S(2)}) collective-permute-start(bf16[2,1,2,128,1152]{4,3,2,1,0:T(8,128)(2,1)S(1)} %pad_maximum_fusion.1.refs_4_.refs_5_), channel_id=1, source_target_pairs={{0,4},{8,12},{4,0},{12,8},{1,5},{9,13},{5,1},{13,9},{2,6},{10,14},... | collective-permute-start | bytes 3538952 | tf_op jit(solution)/shard_map/ppermute | solution.py:482
  100.7 4.9 %collective-permute-start.14 = (bf16[1,2,128,1152]{3,2,1,0:T(8,128)(2,1)S(1)}, bf16[1,2,128,1152]{3,2,1,0:T(8,128)(2,1)S(1)}, u32[]{:S(2)}, u32[]{:S(2)}) collective-permute-start(bf16[1,2,128,1152]{3,2,1,0:T(8,128)(2,1)S(1)} %bitcast.43), channel_id=1, source_target_pairs={{1,2},{2,1},{5,6},{6,5},{9,10},{10,9},{13,14},{14,13},{17,18},{18,... | collective-permute-start | bytes 1769480 | tf_op jit(solution)/shard_map/ppermute | solution.py:482
  104.5 7.4 %collective-permute-start.21 = (bf16[128,1152]{1,0:T(8,128)(2,1)S(1)}, bf16[128,1152]{1,0:T(8,128)(2,1)S(1)}, u32[]{:S(2)}, u32[]{:S(2)}) collective-permute-start(bf16[128,1152]{1,0:T(8,128)(2,1)S(1)} %merge.3), channel_id=1, source_target_pairs={{0,16},{16,0},{1,17},{17,1},{2,18},{18,2},{3,19},{19,3},{4,20},{20... | collective-permute-start | bytes 884744 | tf_op jit(solution)/shard_map/ppermute | solution.py:482
  104.8 16.5 %collective-permute-start.18 = (bf16[1,2,128,1152]{3,2,1,0:T(8,128)(2,1)S(1)}, bf16[1,2,128,1152]{3,2,1,0:T(8,128)(2,1)S(1)}, u32[]{:S(2)}, u32[]{:S(2)}) collective-permute-start(bf16[1,2,128,1152]{3,2,1,0:T(8,128)(2,1)S(1)} %bitcast.44), channel_id=1, source_target_pairs={{1,2},{2,1},{5,6},{6,5},{9,10},{10,9},{13,14},{14,13},{17,18},{18,... | collective-permute-start | bytes 1769480 | tf_op jit(solution)/shard_map/ppermute | solution.py:482
  105.7 36.9 %collective-permute-start.17 = (bf16[2,1,2,128,1152]{4,3,2,1,0:T(8,128)(2,1)S(1)}, bf16[2,1,2,128,1152]{4,3,2,1,0:T(8,128)(2,1)S(1)}, u32[]{:S(2)}, u32[]{:S(2)}) collective-permute-start(bf16[2,1,2,128,1152]{4,3,2,1,0:T(8,128)(2,1)S(1)} %pad_maximum_fusion.2.refs_4_.refs_5_), channel_id=1, source_target_pairs={{4,8},{8,4},{5,9},{9,5},{6,10},{10,6},{7,11},{11,7},{20,24},{24,20... | collective-permute-start | bytes 3538952 | tf_op jit(solution)/shard_map/ppermute | solution.py:482
  111.9 30.8 %collective-permute-start.16 = (bf16[2,1,2,128,1152]{4,3,2,1,0:T(8,128)(2,1)S(1)}, bf16[2,1,2,128,1152]{4,3,2,1,0:T(8,128)(2,1)S(1)}, u32[]{:S(2)}, u32[]{:S(2)}) collective-permute-start(bf16[2,1,2,128,1152]{4,3,2,1,0:T(8,128)(2,1)S(1)} %pad_maximum_fusion.2.refs_4_.refs_5_), channel_id=1, source_target_pairs={{0,4},{8,12},{4,0},{12,8},{1,5},{9,13},{5,1},{13,9},{2,6},{10,14},... | collective-permute-start | bytes 3538952 | tf_op jit(solution)/shard_map/ppermute | solution.py:482
  119.9 18.0 %collective-permute-start.23 = (bf16[144,1152]{1,0:T(8,128)(2,1)S(1)}, bf16[144,1152]{1,0:T(8,128)(2,1)S(1)}, u32[]{:S(2)}, u32[]{:S(2)}) collective-permute-start(bf16[144,1152]{1,0:T(8,128)(2,1)S(1)} %edge_rows.6), channel_id=1, source_target_pairs={{1,0},{2,3},{5,4},{6,7},{9,8},{10,11},{13,12},{14,15},{17,16},{18,... | collective-permute-start | bytes 995336 | tf_op jit(solution)/shard_map/ppermute | solution.py:482
  121.3 26.9 %collective-permute-start.22 = (bf16[128,3072]{1,0:T(8,128)(2,1)S(1)}, bf16[128,3072]{1,0:T(8,128)(2,1)S(1)}, u32[]{:S(2)}, u32[]{:S(2)}) collective-permute-start(bf16[128,3072]{1,0:T(8,128)(2,1)S(1)} %product.3), channel_id=1, source_target_pairs={{0,16},{16,0},{1,17},{17,1},{2,18},{18,2},{3,19},{19,3},{4,20},{20... | collective-permute-start | bytes 2359304 | tf_op jit(solution)/shard_map/ppermute | solution.py:482
  122.1 26.2 %collective-permute-start.19 = (bf16[144,1152]{1,0:T(8,128)(2,1)S(1)}, bf16[144,1152]{1,0:T(8,128)(2,1)S(1)}, u32[]{:S(2)}, u32[]{:S(2)}) collective-permute-start(bf16[144,1152]{1,0:T(8,128)(2,1)S(1)} %edge_rows.7), channel_id=1, source_target_pairs={{1,0},{2,3},{5,4},{6,7},{9,8},{10,11},{13,12},{14,15},{17,16},{18,... | collective-permute-start | bytes 995336 | tf_op jit(solution)/shard_map/ppermute | solution.py:482

commit v8 on v7

--- a/solution.py
+++ b/solution.py
@@ -17,7 +17,7 @@
 SMEM = pl.BlockSpec(memory_space=pltpu.SMEM)
 
 
-COST = {"pack": 4, "edge_rows": 4, "rows": 4, "merge": 4, "project": 4, "product": 4, "pick": 4}
+COST = {"pack": 1, "edge_rows": 8, "rows": 1, "merge": 4, "project": 1, "product": 4, "pick": 4}
 
 
 def kernel_call(kernel, name, cost_estimate, **kwargs):
@@ -87,24 +87,13 @@
     )
 
 
-def edge_kernel(place, q_ref, near_ref, far_ref, *refs, heads, cols_tile, cols):
+def edge_kernel(place, q_ref, near_ref, far_ref, out_ref, *, heads, cols_tile, cols):
     tokens = q_ref.shape[0]
-    out_ref = refs[-1]
-    first = 0
-    if len(refs) > 1:
-        next_ref, next_q_ref = refs[:2]
-        first = 2 * tokens
-        out_ref[:tokens] = next_ref[0]
-        out_ref[tokens:first] = next_ref[1]
     inner = (place[2] > 0) & (place[2] < cols - 1)
 
     @pl.when(jnp.logical_not(inner))
     def _():
-        if first:
-            out_ref[first:first + tokens] = next_q_ref[...]
-        else:
-            out_ref[:tokens] = jnp.zeros((tokens, out_ref.shape[1]), out_ref.dtype)
-        out_ref[first + tokens:] = jnp.zeros((FOLD, out_ref.shape[1]), out_ref.dtype)
+        out_ref[...] = jnp.zeros_like(out_ref)
 
     @pl.when(inner)
     def _():
@@ -116,10 +105,10 @@
         tops, totals, weights = softmax_sums(scores, values)
         lse = [top + jnp.log2(w) for top, w in zip(tops, weights)]
         stats = place_pieces(jnp.zeros((tokens, HEAD), jnp.float32), lse, 0)
-        out_ref[first:first + tokens] = jnp.concatenate(
+        out_ref[:tokens] = jnp.concatenate(
             [(t / w).astype(jnp.bfloat16) for t, w in zip(totals, weights)], axis=1
         )
-        out_ref[first + tokens:] = fold_stats(stats.astype(jnp.bfloat16), out_ref.shape[1])
+        out_ref[tokens:] = fold_stats(stats.astype(jnp.bfloat16), out_ref.shape[1])
 
 
 def fill_bias(bias_ref, frame_tokens, cols_tile):
@@ -194,19 +183,40 @@
     out_ref[...] = merged(place, base_ref, row_ref, sums_ref, rest_ref, stats_ref, cols)
 
 
+def add_product(total_ref, rows, weight_ref, lanes=512):
+    for start in range(0, total_ref.shape[1], lanes):
+        cut = slice(start, start + lanes)
+        total_ref[:, cut] += dot_nn(rows, weight_ref[:, cut])
+
+
 def project_kernel(place, base_ref, row_ref, sums_ref, rest_ref, stats_ref, weight_ref, other_ref, *refs, cols):
-    out_ref, rows_ref = refs[-2:]
-
+    out_ref, total_ref, rows_ref = refs[-3:]
+    step, lanes = pl.program_id(0), weight_ref.shape[0]
+
+    @pl.when(step == 0)
+    def _():
+        total_ref[...] = other_ref[...].astype(jnp.float32)
+        rows = merged(place, base_ref, row_ref, sums_ref, rest_ref, stats_ref, cols)
+        for n in range(rows_ref.shape[0]):
+            rows_ref[n] = rows[:, n * lanes:(n + 1) * lanes]
+
+    add_product(total_ref, rows_ref[step], weight_ref)
+
+    @pl.when(step == pl.num_programs(0) - 1)
+    def _():
+        out_ref[...] = total_ref[...].astype(jnp.bfloat16)
+
+
+def product_kernel(rows_ref, weight_ref, out_ref, total_ref):
     @pl.when(pl.program_id(0) == 0)
     def _():
-        rows_ref[...] = merged(place, base_ref, row_ref, sums_ref, rest_ref, stats_ref, cols)
-
-    total = other_ref[...].astype(jnp.float32) + dot_nn(rows_ref[...], weight_ref[...])
-    out_ref[...] = total.astype(jnp.bfloat16)
-
-
-def product_kernel(rows_ref, weight_ref, out_ref):
-    out_ref[...] = dot_nn(rows_ref[...], weight_ref[...]).astype(jnp.bfloat16)
+        total_ref[...] = jnp.zeros_like(total_ref)
+
+    add_product(total_ref, rows_ref[...], weight_ref)
+
+    @pl.when(pl.program_id(0) == pl.num_programs(0) - 1)
+    def _():
+        out_ref[...] = total_ref[...].astype(jnp.bfloat16)
 
 
 def hbm(*values):
@@ -289,17 +299,10 @@
     )(place, *hbm(value))
 
 
-def edge_attend(place, q, q_block, near, far, stream, cols_tile, cols, following=None):
+def edge_attend(place, q, q_block, near, far, stream, cols_tile, cols):
     _, _, tokens, width = far.shape
     heads = width // HEAD
-    extra, args, rows = [], [], tokens + FOLD
-    if following is not None:
-        rows += 2 * tokens
-        args = [following[0], *hbm(following[1])]
-        extra = [
-            pl.BlockSpec((None, None, 2, tokens, width), lambda g, p: (1, stream, 0, 0, 0)),
-            pl.BlockSpec((None, tokens, width), lambda g, p: (stream, 0, side(1, p))),
-        ]
+    rows = tokens + FOLD
     return kernel_call(
         functools.partial(edge_kernel, heads=heads, cols_tile=cols_tile, cols=cols),
         out_shape=jax.ShapeDtypeStruct((rows, width), jnp.bfloat16),
@@ -310,7 +313,6 @@
                 pl.BlockSpec((tokens, width), lambda g, p: (q_block, 0)),
                 pl.BlockSpec((None, 2, tokens, width), lambda g, p: (stream, 0, 0, 0)),
                 pl.BlockSpec((None, 2, tokens, width), lambda g, p: (0, 0, 0, 0)),
-                *extra,
             ],
             out_specs=pl.BlockSpec((rows, width), lambda g, p: (0, 0)),
         ),
@@ -321,7 +323,7 @@
             transcendentals=2 * tokens * tokens * heads,
         ),
         name="edge_rows",
-    )(place, q, near, far, *args)
+    )(place, q, near, far)
 
 
 def rows_attend(place, mask, reach, q, tiles, sides, far, half, stream, cols_tile, frame_tokens, grid, block=3):
@@ -401,9 +403,10 @@
     )(place, *parts, rest, rest)
 
 
-def project(place, parts, rest, weight, other, output, stream, cols, lanes=512):
+def project(place, parts, rest, weight, other, output, stream, cols, block=3):
     tokens, width = parts[0].shape
     at = rest.shape[0] // tokens - 1
+    lanes = block * HEAD
     streams, _, model = weight.shape
     earlier = [] if output is None else [output]
     whole = pl.BlockSpec((tokens, width), lambda g, p: (0, 0))
@@ -413,19 +416,22 @@
         out_shape=jax.ShapeDtypeStruct((streams, tokens, model), jnp.bfloat16),
         grid_spec=pltpu.PrefetchScalarGridSpec(
             num_scalar_prefetch=1,
-            grid=(model // lanes,),
+            grid=(width // lanes,),
             in_specs=[
                 whole,
                 whole,
                 pl.BlockSpec((tokens, HEAD), lambda g, p: (0, 0)),
                 pl.BlockSpec((tokens, width), lambda g, p: (at, 0)),
                 pl.BlockSpec((FOLD, width), lambda g, p: ((at + 1) * tokens // FOLD, 0)),
-                pl.BlockSpec((None, width, lanes), lambda g, p: (stream, 0, g)),
-                pl.BlockSpec((tokens, lanes), lambda g, p: (0, g)),
+                pl.BlockSpec((None, lanes, model), lambda g, p: (stream, g, 0)),
+                pl.BlockSpec((tokens, model), lambda g, p: (0, 0)),
                 *[ANY] * len(earlier),
             ],
-            out_specs=pl.BlockSpec((None, tokens, lanes), lambda g, p: (stream, 0, g)),
-            scratch_shapes=[pltpu.VMEM((tokens, width), jnp.bfloat16)],
+            out_specs=pl.BlockSpec((None, tokens, model), lambda g, p: (stream, 0, 0)),
+            scratch_shapes=[
+                pltpu.VMEM((tokens, model), jnp.float32),
+                pltpu.VMEM((width // lanes, tokens, lanes), jnp.bfloat16),
+            ],
         ),
         input_output_aliases={len(args): 0} if earlier else {},
         compiler_params=params(),
@@ -436,18 +442,20 @@
     )(*args, *earlier)
 
 
-def product(rows, weight, stream, lanes=512):
+def product(rows, weight, stream, block=3):
     tokens, width = rows.shape
     model = weight.shape[2]
+    lanes = block * HEAD
     return kernel_call(
         product_kernel,
         out_shape=jax.ShapeDtypeStruct((tokens, model), jnp.bfloat16),
-        grid=(model // lanes,),
+        grid=(width // lanes,),
         in_specs=[
-            pl.BlockSpec((tokens, width), lambda g: (0, 0)),
-            pl.BlockSpec((None, width, lanes), lambda g: (stream, 0, g)),
+            pl.BlockSpec((tokens, lanes), lambda g: (0, g)),
+            pl.BlockSpec((None, lanes, model), lambda g: (stream, g, 0)),
         ],
-        out_specs=pl.BlockSpec((tokens, lanes), lambda g: (0, g)),
+        out_specs=pl.BlockSpec((tokens, model), lambda g: (0, 0)),
+        scratch_shapes=[pltpu.VMEM((tokens, model), jnp.float32)],
         compiler_params=params(),
         cost_estimate=pl.CostEstimate(
             flops=2 * tokens * width * model, bytes_accessed=2 * width * model, transcendentals=0
@@ -487,19 +495,17 @@
     own0 = pack(place, k, v, 0)
     picked = pick(place, q, 0).reshape(S * tokens, half)
     own = pack(tied(place, [picked]), k, v, 1, own0)
-
-    def mix(s, *after):
-        sent[f"part0{s}"] = edge_attend(
-            place, tied(sent["q0"], after), s, sent["other0"], sent[f"far0{s}"], s, C, cols, (own, q)
+    q1 = pick(tied(place, [own]), q, 1)
+    onward = [jnp.concatenate([own[1, s].reshape(2 * tokens, half), q1[s]]) for s in range(S)]
+
+    def edge(h, s, *after):
+        rows_q, block = (sent["q0"], s) if h == 0 else (sent[f"near1{s}"], 2)
+        sent[f"part{h}{s}"] = edge_attend(
+            place, tied(rows_q, after), block, sent[f"other{h}"], sent[f"far{h}{s}"], s, C, cols
         )
 
-    def edge(s, *after):
-        sent[f"part1{s}"] = edge_attend(
-            place, tied(sent[f"mix{s}"], after), 2, sent["other1"], sent[f"far1{s}"], s, C, cols
-        )
-
     def near1(s):
-        return sent[f"mix{s}"][:2 * tokens].reshape(1, 2, tokens, half)
+        return sent[f"near1{s}"][:2 * tokens].reshape(1, 2, tokens, half)
 
     def rows_of(h, s, *after):
         tiles = [sent["pair_own"], own, sent["next_own"]]
@@ -514,40 +520,41 @@
     send("next_own", own, "row", row_others)
     send("pair_own", own, "row", row_pairs)
     send("q0", picked, "col", inward)
-    send("far00", sent["near0"][:1], "col", col_others, "other0", "pair_own", "next_own")
-    send("far01", sent["near0"][1:], "col", col_others, "near0")
+    send("far00", sent["near0"][:1], "col", col_others, "other0", "pair_own")
+    send("far01", sent["near0"][1:], "col", col_others, "near0", "next_own")
     sent["sides0"] = jnp.stack([sent["near0"], sent["other0"]])
+    send("pair_sides0", sent["sides0"], "row", row_pairs)
     send("next_sides0", sent["sides0"], "row", row_others)
-    send("pair_sides0", sent["sides0"], "row", row_pairs, "other0")
-    mix(0)
-    send("mix0", sent["part00"], "col", col_pairs)
-    send("other1", own[1], "col", col_others, "far01", "next_sides0", "pair_sides0")
-    mix(1, "part00")
-    send("mix1", sent["part01"], "col", col_pairs)
-    rows_of(0, 0)
-    rows_of(0, 1)
-    sent["merged0"] = merge(tied(place, []), sent["rows00"], sent["mix0"], cols)
+    send("near10", onward[0], "col", col_pairs, "other0")
+    edge(0, 0)
+    send("rest00", sent["part00"], "col", outward)
+    send("other1", own[1], "col", col_others, "far00")
+    edge(0, 1, "part00")
+    send("rest01", sent["part01"], "col", outward)
+    send("near11", onward[1], "col", col_pairs, "rest00", "part01")
+    rows_of(0, 0, "part01")
+    sent["merged0"] = merge(tied(place, []), sent["rows00"], sent["rest00"], cols)
+    rows_of(0, 1, "merged0")
     send("theirs0", sent["merged0"], "pair", pair_swap)
     sent["product0"] = product(tied(sent["theirs0"], ["rows01"]), out_weight, 0)
     send("back0", sent["product0"], "pair", pair_swap)
-    sent["mix1"] = tied(sent["mix1"], ["theirs0"])
-    sent["merged1"] = merge(tied(place, []), sent["rows01"], sent["mix1"], cols)
-    send("theirs1", sent["merged1"], "pair", pair_swap, "back0")
-    sent["product1"] = product(tied(sent["theirs1"], []), out_weight, 1)
+    sent["merged1"] = merge(tied(place, []), sent["rows01"], sent["rest01"], cols)
+    send("theirs1", sent["merged1"], "pair", pair_swap)
+    send("far10", near1(0), "col", col_others, "product0")
+    sent["sides10"] = jnp.stack([near1(0), tied(sent["other1"][0:1], ["rows01"])])
+    send("next_sides10", sent["sides10"], "row", row_others, "other1")
+    send("pair_sides10", sent["sides10"], "row", row_pairs)
+    edge(1, 0)
+    sent["product1"] = product(tied(sent["theirs1"], ["part10"]), out_weight, 1)
     send("back1", sent["product1"], "pair", pair_swap)
-    send("far10", near1(0), "col", col_others, "theirs0")
-    sent["sides10"] = jnp.stack([near1(0), tied(sent["other1"][0:1], ["theirs0"])])
-    send("next_sides10", sent["sides10"], "row", row_others)
-    send("pair_sides10", sent["sides10"], "row", row_pairs)
-    send("far11", near1(1), "col", col_others)
-    sent["sides11"] = jnp.stack([near1(1), tied(sent["other1"][1:2], ["theirs0"])])
+    send("rest10", sent["part10"], "col", outward)
+    rows_of(1, 0)
+    send("far11", near1(1), "col", col_others, "product0")
+    sent["sides11"] = jnp.stack([near1(1), tied(sent["other1"][1:2], ["merged1", "sides10"])])
     send("next_sides11", sent["sides11"], "row", row_others)
     send("pair_sides11", sent["sides11"], "row", row_pairs)
-    edge(0)
-    send("rest10", sent["part10"], "col", outward)
-    edge(1, "part10", "next_sides10")
+    edge(1, 1, "part10")
     send("rest11", sent["part11"], "col", outward)
-    rows_of(1, 0)
     rows_of(1, 1, "rows10")
     output = project(tied(place, []), sent["rows10"], sent["rest10"], out_weight, sent["back0"], None, 0, cols)
     output = project(place, sent["rows11"], sent["rest11"], out_weight, sent["back1"], output, 1, cols)

time: 156 us -> 154 us (0.987); the launches traced: 153 us -> 153 us
  waiting for transfers between devices: 43.3 us -> 69.3 us
  starting transfers between devices: 55.9 us -> 33.7 us
  Pallas kernels: 51.4 us -> 48.1 us
    ppermute x24 -> x26, waiting for transfers between devices: 43.3 us -> 69.3 us  [send(): sent[name] = lax.ppermute(tied(value, after), axis, pairs)]
    ppermute x24 -> x26, starting transfers between devices: 55.9 us -> 33.7 us  [send(): sent[name] = lax.ppermute(tied(value, after), axis, pairs)]
    pallas_call x4, Pallas kernels: 4.29 us -> 2.48 us  [edge_attend(): kernel_call(functools.partial(edge_kernel, heads=heads, cols_tile=cols_ti...]
    pallas_call x2, Pallas kernels: 9.65 us -> 7.92 us  [project(): kernel_call(functools.partial(project_kernel, cols=cols), out_shape=jax.S...]
    pallas_call x1 -> x2, Pallas kernels: 1.65 us -> 3.29 us  [pick(): kernel_call(kernel, out_shape=jax.ShapeDtypeStruct((S, tokens, width), va...]
  transfers between devices with their start and end apart: 24 -> 26, of which waited for: 5 -> 6; matrix products, arithmetic and copies ran while one was open for 1% -> 1% of each run, Pallas kernels for 29% -> 28%
where the time goes in v8:
time: 154 us; the launch traced here: 153 us
  waiting for transfers between devices  69.3 us (45%)
  Pallas kernels  48.1 us (31%)
  starting transfers between devices  33.7 us (22%)
    ppermute x26, waiting for transfers between devices, send(): sent[name] = lax.ppermute(tied(value, after), axis, pairs)  69.3 us
    ppermute x26, starting transfers between devices, send(): sent[name] = lax.ppermute(tied(value, after), axis, pairs)  33.7 us
    pallas_call x4, Pallas kernels, rows_attend(): kernel_call(kernel, out_shape=(jax.ShapeDtypeStruct((tokens, width), jnp....  23 us
    pallas_call x2, Pallas kernels, project(): kernel_call(functools.partial(project_kernel, cols=cols), out_shape=jax.S...  7.92 us
    pallas_call x2, Pallas kernels, pack(): kernel_call(kernel, out_shape=jax.ShapeDtypeStruct((1 + len(given), S, 2,...  5.08 us
    pallas_call x2, Pallas kernels, product(): kernel_call(product_kernel, out_shape=jax.ShapeDtypeStruct((tokens, model...  4.21 us
    pallas_call x2, Pallas kernels, pick(): kernel_call(kernel, out_shape=jax.ShapeDtypeStruct((S, tokens, width), va...  3.29 us
  transfers between devices with their start and end apart: 26, of which 6 were waited for; matrix products, arithmetic and copies ran while one was open for 1% of the time, Pallas kernels for 28%

profile of v8, /device:TPU:0, one launch (start us, length us, event | category | flops | bytes accessed | tf_op | source)
XLA Modules:
  0.0 152.9 jit_solution(3732931470520502511)
XLA Ops:
  0.1 2.0 %pack.2.refs_0_ = bf16[1,2,2,128,1152]{4,3,2,1,0:T(8,128)(2,1)S(1)} custom-call(s32[3]{0:T(128)S(1)} %pad_add_fusion.place, bf16[2,128,2304]{2,1,0:T(8,128)(2,1)} %bitcast.43, bf16[2,128,2304]{2,1,0:T(8,128)(2,1)} %bitcast.45), custom_call_target="tpu_custom_call" | custom-call | bytes 2359296 | tf_op jit(solution)/shard_map/pack/pallas_call | solution.py:261
  2.8 5.8 %collective-permute-start.3 = (bf16[2,2,128,1152]{3,2,1,0:T(8,128)(2,1)S(1)}, bf16[2,2,128,1152]{3,2,1,0:T(8,128)(2,1)S(1)}, u32[]{:S(2)}, u32[]{:S(2)}) collective-permute-start(bf16[2,2,128,1152]{3,2,1,0:T(8,128)(2,1)S(1)} %bitcast.29), channel_id=1, source_target_pairs={{0,1},{2,3},{1,0},{3,2},{4,5},{6,7},{5,4},{7,6},{8,9},{10,11},{9,8... | collective-permute-start | bytes 3538952 | tf_op jit(solution)/shard_map/ppermute | solution.py:490
  8.6 1.6 %pick.2 = bf16[2,128,1152]{2,1,0:T(8,128)(2,1)S(1)} custom-call(s32[3]{0:T(128)S(1)} %pad_add_fusion.place, bf16[2,128,2304]{2,1,0:T(8,128)(2,1)} %bitcast.36), custom_call_target="tpu_custom_call" | custom-call | bytes 4718592 | tf_op jit(solution)/shard_map/pick/pallas_call | solution.py:285
  10.3 3.1 %pack.3.refs_3_ = bf16[2,2,2,128,1152]{4,3,2,1,0:T(8,128)(2,1)S(1)} custom-call(s32[3]{0:T(128)S(1)} %pad_add_fusion.place, bf16[2,128,2304]{2,1,0:T(8,128)(2,1)} %bitcast.44, bf16[2,128,2304]{2,1,0:T(8,128)(2,1)} %bitcast.46, bf16[1,2,2,128,1152]{4,3,2,1,0:T(8,128)(2,1)S(1)} %pack.2.refs_0_), custom_call_target="tpu_custom_call" | custom-call | bytes 2359296 | tf_op jit(solution)/shard_map/pack/pallas_call | solution.py:261
  13.5 0.8 collective-permute-start.7
  14.3 2.0 %collective-permute-start.6 = (bf16[256,1152]{1,0:T(8,128)(2,1)S(1)}, bf16[256,1152]{1,0:T(8,128)(2,1)S(1)}, u32[]{:S(2)}, u32[]{:S(2)}) collective-permute-start(bf16[256,1152]{1,0:T(8,128)(2,1)S(1)} %bitcast.31), channel_id=1, source_target_pairs={{0,1},{3,2},{4,5},{7,6},{8,9},{11,10},{12,13},{15,14},{16,17},{19,... | collective-permute-start | bytes 1769480 | tf_op jit(solution)/shard_map/ppermute | solution.py:490
  16.3 18.8 %collective-permute-done.3 = bf16[2,2,128,1152]{3,2,1,0:T(8,128)(2,1)S(1)} collective-permute-done((bf16[2,2,128,1152]{3,2,1,0:T(8,128)(2,1)S(1)}, bf16[2,2,128,1152]{3,2,1,0:T(8,128)(2,1)S(1)}, u32[]{:S(2)}, u32[]{:S(2)}) %collective-permute-start.3) | collective-permute-done | bytes 1179680 | tf_op jit(solution)/shard_map/ppermute | solution.py:490
  35.3 0.8 collective-permute-start.10
  36.1 2.8 %collective-permute-start.9 = (bf16[2,2,2,128,1152]{4,3,2,1,0:T(8,128)(2,1)S(1)}, bf16[2,2,2,128,1152]{4,3,2,1,0:T(8,128)(2,1)S(1)}, u32[]{:S(2)}, u32[]{:S(2)}) collective-permute-start(bf16[2,2,2,128,1152]{4,3,2,1,0:T(8,128)(2,1)S(1)} %pad_maximum_fusion.refs_4_.refs_5_), channel_id=1, source_target_pairs={{0,4},{8,12},{4,0},{12,8},{1,5},{9,13},{5,1},{13,9},{2,6},{10,14},... | collective-permute-start | bytes 7077896 | tf_op jit(solution)/shard_map/ppermute | solution.py:490
  39.0 1.6 %pick.3 = bf16[2,128,1152]{2,1,0:T(8,128)(2,1)S(1)} custom-call(s32[3]{0:T(128)S(1)} %pad_add_fusion.place, bf16[2,128,2304]{2,1,0:T(8,128)(2,1)} %bitcast.37), custom_call_target="tpu_custom_call" | custom-call | bytes 4718592 | tf_op jit(solution)/shard_map/pick/pallas_call | solution.py:285
  41.6 4.2 %collective-permute-start.2 = (bf16[384,1152]{1,0:T(8,128)(2,1)S(1)}, bf16[384,1152]{1,0:T(8,128)(2,1)S(1)}, u32[]{:S(2)}, u32[]{:S(2)}) collective-permute-start(bf16[384,1152]{1,0:T(8,128)(2,1)S(1)} %pad_maximum_fusion.3), channel_id=1, source_target_pairs={{0,1},{2,3},{1,0},{3,2},{4,5},{6,7},{5,4},{7,6},{8,9},{10,11},{9,8... | collective-permute-start | bytes 2654216 | tf_op jit(solution)/shard_map/ppermute | solution.py:490
  48.0 1.3 collective-permute-start.11
  49.9 1.3 collective-permute-start.17
  51.3 5.6 %rows.4 = (f32[128,1152]{1,0:T(8,128)S(1)}, bf16[128,1152]{1,0:T(8,128)(2,1)S(1)}, bf16[128,128]{1,0:T(8,128)(2,1)S(1)}) custom-call(s32[3]{0:T(128)S(1)} %pad_add_fusion.place, s32[9]{0:T(128)S(1)} %bitcast.32, s32[18]{0:T(128)S(1)} %copy-done.1, bf16[2,128,2304]{2,1,0:T(8,128)(2,1)} %bitcast.38, ...), custom_call_target="tpu_custom_call" | custom-call | flops 868220928 | bytes 7962624 | tf_op jit(solution)/shard_map/rows/pallas_call | solution.py:343
  56.9 30.8 %collective-permute-done.11.rest_ref.stats_ref = bf16[144,1152]{1,0:T(8,128)(2,1)S(1)} collective-permute-done((bf16[144,1152]{1,0:T(8,128)(2,1)S(1)}, bf16[144,1152]{1,0:T(8,128)(2,1)S(1)}, u32[]{:S(2)}, u32[]{:S(2)}) %collective-permute-start.11) | collective-permute-done | bytes 331808 | tf_op jit(solution)/shard_map/ppermute | solution.py:490
  87.7 1.1 merge.2
  88.8 2.1 %collective-permute-start.14 = (bf16[128,1152]{1,0:T(8,128)(2,1)S(1)}, bf16[128,1152]{1,0:T(8,128)(2,1)S(1)}, u32[]{:S(2)}, u32[]{:S(2)}) collective-permute-start(bf16[128,1152]{1,0:T(8,128)(2,1)S(1)} %merge.2), channel_id=1, source_target_pairs={{0,16},{16,0},{1,17},{17,1},{2,18},{18,2},{3,19},{19,3},{4,20},{20... | collective-permute-start | bytes 884744 | tf_op jit(solution)/shard_map/ppermute | solution.py:490
  91.2 6.1 %rows.5 = (f32[128,1152]{1,0:T(8,128)S(1)}, bf16[128,1152]{1,0:T(8,128)(2,1)S(1)}, bf16[128,128]{1,0:T(8,128)(2,1)S(1)}) custom-call(s32[3]{0:T(128)S(1)} %pad_add_fusion.place, s32[9]{0:T(128)S(1)} %bitcast.33, s32[18]{0:T(128)S(1)} %copy-done.1, bf16[2,128,2304]{2,1,0:T(8,128)(2,1)} %bitcast.39, ...), custom_call_target="tpu_custom_call" | custom-call | flops 868220928 | bytes 7962624 | tf_op jit(solution)/shard_map/rows/pallas_call | solution.py:343
  97.3 1.1 merge.3
  99.0 2.1 %product.2 = bf16[128,3072]{1,0:T(8,128)(2,1)S(1)} custom-call(bf16[128,1152]{1,0:T(8,128)(2,1)S(1)} %collective-permute-done.14.rows_ref, bf16[2,1152,3072]{2,1,0:T(8,128)(2,1)S(1)} %bitcast.27), custom_call_target="tpu_custom_call" | custom-call | flops 3623878656 | bytes 28311552 | tf_op jit(solution)/shard_map/product/pallas_call | solution.py:449
  101.1 1.6 %collective-permute-start.25 = (bf16[128,3072]{1,0:T(8,128)(2,1)S(1)}, bf16[128,3072]{1,0:T(8,128)(2,1)S(1)}, u32[]{:S(2)}, u32[]{:S(2)}) collective-permute-start(bf16[128,3072]{1,0:T(8,128)(2,1)S(1)} %product.2), channel_id=1, source_target_pairs={{0,16},{16,0},{1,17},{17,1},{2,18},{18,2},{3,19},{19,3},{4,20},{20... | collective-permute-start | bytes 2359304 | tf_op jit(solution)/shard_map/ppermute | solution.py:490
  104.4 5.8 %collective-permute-done.16.q_ref = bf16[384,1152]{1,0:T(8,128)(2,1)S(1)} collective-permute-done((bf16[384,1152]{1,0:T(8,128)(2,1)S(1)}, bf16[384,1152]{1,0:T(8,128)(2,1)S(1)}, u32[]{:S(2)}, u32[]{:S(2)}) %collective-permute-start.16) | collective-permute-done | bytes 884768 | tf_op jit(solution)/shard_map/ppermute | solution.py:490
  111.7 7.7 %collective-permute-done.25.other_ref = bf16[128,3072]{1,0:T(8,128)(2,1)S(1)} collective-permute-done((bf16[128,3072]{1,0:T(8,128)(2,1)S(1)}, bf16[128,3072]{1,0:T(8,128)(2,1)S(1)}, u32[]{:S(2)}, u32[]{:S(2)}) %collective-permute-start.25) | collective-permute-done | bytes 786464 | tf_op jit(solution)/shard_map/ppermute | solution.py:490
  120.9 2.1 %product.3 = bf16[128,3072]{1,0:T(8,128)(2,1)S(1)} custom-call(bf16[128,1152]{1,0:T(8,128)(2,1)S(1)} %collective-permute-done.22.rows_ref, bf16[2,1152,3072]{2,1,0:T(8,128)(2,1)S(1)} %bitcast.27), custom_call_target="tpu_custom_call" | custom-call | flops 3623878656 | bytes 28311552 | tf_op jit(solution)/shard_map/product/pallas_call | solution.py:449
  123.0 1.4 collective-permute-start.23
  124.5 1.3 collective-permute-start.24
  126.4 1.3 collective-permute-start.21
  127.7 5.6 %rows.6 = (f32[128,1152]{1,0:T(8,128)S(1)}, bf16[128,1152]{1,0:T(8,128)(2,1)S(1)}, bf16[128,128]{1,0:T(8,128)(2,1)S(1)}) custom-call(s32[3]{0:T(128)S(1)} %pad_add_fusion.place, s32[9]{0:T(128)S(1)} %bitcast.34, s32[18]{0:T(128)S(1)} %copy-done.1, bf16[2,128,2304]{2,1,0:T(8,128)(2,1)} %bitcast.40, ...), custom_call_target="tpu_custom_call" | custom-call | flops 868220928 | bytes 7962624 | tf_op jit(solution)/shard_map/rows/pallas_call | solution.py:343
  133.3 6.0 %collective-permute-done.24.rest_ref.stats_ref = bf16[144,1152]{1,0:T(8,128)(2,1)S(1)} collective-permute-done((bf16[144,1152]{1,0:T(8,128)(2,1)S(1)}, bf16[144,1152]{1,0:T(8,128)(2,1)S(1)}, u32[]{:S(2)}, u32[]{:S(2)}) %collective-permute-start.24) | collective-permute-done | bytes 331808 | tf_op jit(solution)/shard_map/ppermute | solution.py:490
  139.3 4.0 %project.2.refs_0_ = bf16[2,128,3072]{2,1,0:T(8,128)(2,1)} custom-call(s32[3]{0:T(128)S(1)} %pad_add_fusion.place, f32[128,1152]{1,0:T(8,128)S(1)} %get-tuple-element.55.base_ref, bf16[128,1152]{1,0:T(8,128)(2,1)S(1)} %get-tuple-element.56.row_ref, bf16[128,128]{1,0:T(8,128)(2,1)S(1)} %get-tuple-element.57.sums_ref, ...), custom_call_target="tpu_custom_call" | custom-call | flops 905969664 | bytes 7077888 | tf_op jit(solution)/shard_map/project/pallas_call | solution.py:414
  143.3 5.6 %rows.7 = (f32[128,1152]{1,0:T(8,128)S(1)}, bf16[128,1152]{1,0:T(8,128)(2,1)S(1)}, bf16[128,128]{1,0:T(8,128)(2,1)S(1)}) custom-call(s32[3]{0:T(128)S(1)} %pad_add_fusion.place, s32[9]{0:T(128)S(1)} %bitcast.35, s32[18]{0:T(128)S(1)} %copy-done.1, bf16[2,128,2304]{2,1,0:T(8,128)(2,1)} %bitcast.41, ...), custom_call_target="tpu_custom_call" | custom-call | flops 868220928 | bytes 7962624 | tf_op jit(solution)/shard_map/rows/pallas_call | solution.py:343
  148.9 4.0 %project.3 = bf16[2,128,3072]{2,1,0:T(8,128)(2,1)} custom-call(s32[3]{0:T(128)S(1)} %pad_add_fusion.place, f32[128,1152]{1,0:T(8,128)S(1)} %get-tuple-element.62.base_ref, bf16[128,1152]{1,0:T(8,128)(2,1)S(1)} %get-tuple-element.63.row_ref, bf16[128,128]{1,0:T(8,128)(2,1)S(1)} %get-tuple-element.64.sums_ref, ...), custom_call_target="tpu_custom_call", output_to_operand_aliasing={{}: (8, {})} | custom-call | flops 905969664 | bytes 7077888 | tf_op jit(solution)/shard_map/project/pallas_call | solution.py:414
  (64 shorter events, 10.8 us)
Async XLA Ops:
  2.1 14.2 %collective-permute-start.1 = (bf16[2,2,128,1152]{3,2,1,0:T(8,128)(2,1)S(1)}, bf16[2,2,128,1152]{3,2,1,0:T(8,128)(2,1)S(1)}, u32[]{:S(2)}, u32[]{:S(2)}) collective-permute-start(bf16[2,2,128,1152]{3,2,1,0:T(8,128)(2,1)S(1)} %bitcast.28), channel_id=1, source_target_pairs={{1,2},{2,1},{5,6},{6,5},{9,10},{10,9},{13,14},{14,13},{17,18},{18,... | collective-permute-start | bytes 3538952 | tf_op jit(solution)/shard_map/ppermute | solution.py:490
  2.8 32.2 %collective-permute-start.3 = (bf16[2,2,128,1152]{3,2,1,0:T(8,128)(2,1)S(1)}, bf16[2,2,128,1152]{3,2,1,0:T(8,128)(2,1)S(1)}, u32[]{:S(2)}, u32[]{:S(2)}) collective-permute-start(bf16[2,2,128,1152]{3,2,1,0:T(8,128)(2,1)S(1)} %bitcast.29), channel_id=1, source_target_pairs={{0,1},{2,3},{1,0},{3,2},{4,5},{6,7},{5,4},{7,6},{8,9},{10,11},{9,8... | collective-permute-start | bytes 3538952 | tf_op jit(solution)/shard_map/ppermute | solution.py:490
  13.4 27.4 %collective-permute-start = (bf16[2,2,2,128,1152]{4,3,2,1,0:T(8,128)(2,1)S(1)}, bf16[2,2,2,128,1152]{4,3,2,1,0:T(8,128)(2,1)S(1)}, u32[]{:S(2)}, u32[]{:S(2)}) collective-permute-start(bf16[2,2,2,128,1152]{4,3,2,1,0:T(8,128)(2,1)S(1)} %pack.3.refs_3_), channel_id=1, source_target_pairs={{0,4},{8,12},{4,0},{12,8},{1,5},{9,13},{5,1},{13,9},{2,6},{10,14},... | collective-permute-start | bytes 7077896 | tf_op jit(solution)/shard_map/ppermute | solution.py:490
  13.5 28.1 %collective-permute-start.7 = (bf16[2,2,2,128,1152]{4,3,2,1,0:T(8,128)(2,1)S(1)}, bf16[2,2,2,128,1152]{4,3,2,1,0:T(8,128)(2,1)S(1)}, u32[]{:S(2)}, u32[]{:S(2)}) collective-permute-start(bf16[2,2,2,128,1152]{4,3,2,1,0:T(8,128)(2,1)S(1)} %pack.3.refs_3_), channel_id=1, source_target_pairs={{4,8},{8,4},{5,9},{9,5},{6,10},{10,6},{7,11},{11,7},{20,24},{24,20... | collective-permute-start | bytes 7077896 | tf_op jit(solution)/shard_map/ppermute | solution.py:490
  14.3 32.4 %collective-permute-start.6 = (bf16[256,1152]{1,0:T(8,128)(2,1)S(1)}, bf16[256,1152]{1,0:T(8,128)(2,1)S(1)}, u32[]{:S(2)}, u32[]{:S(2)}) collective-permute-start(bf16[256,1152]{1,0:T(8,128)(2,1)S(1)} %bitcast.31), channel_id=1, source_target_pairs={{0,1},{3,2},{4,5},{7,6},{8,9},{11,10},{12,13},{15,14},{16,17},{19,... | collective-permute-start | bytes 1769480 | tf_op jit(solution)/shard_map/ppermute | solution.py:490
  35.3 14.6 %collective-permute-start.10 = (bf16[2,2,2,128,1152]{4,3,2,1,0:T(8,128)(2,1)S(1)}, bf16[2,2,2,128,1152]{4,3,2,1,0:T(8,128)(2,1)S(1)}, u32[]{:S(2)}, u32[]{:S(2)}) collective-permute-start(bf16[2,2,2,128,1152]{4,3,2,1,0:T(8,128)(2,1)S(1)} %pad_maximum_fusion.refs_4_.refs_5_), channel_id=1, source_target_pairs={{4,8},{8,4},{5,9},{9,5},{6,10},{10,6},{7,11},{11,7},{20,24},{24,20... | collective-permute-start | bytes 7077896 | tf_op jit(solution)/shard_map/ppermute | solution.py:490
  36.1 15.1 %collective-permute-start.9 = (bf16[2,2,2,128,1152]{4,3,2,1,0:T(8,128)(2,1)S(1)}, bf16[2,2,2,128,1152]{4,3,2,1,0:T(8,128)(2,1)S(1)}, u32[]{:S(2)}, u32[]{:S(2)}) collective-permute-start(bf16[2,2,2,128,1152]{4,3,2,1,0:T(8,128)(2,1)S(1)} %pad_maximum_fusion.refs_4_.refs_5_), channel_id=1, source_target_pairs={{0,4},{8,12},{4,0},{12,8},{1,5},{9,13},{5,1},{13,9},{2,6},{10,14},... | collective-permute-start | bytes 7077896 | tf_op jit(solution)/shard_map/ppermute | solution.py:490
  40.8 5.1 %collective-permute-start.4 = (bf16[1,2,128,1152]{3,2,1,0:T(8,128)(2,1)S(1)}, bf16[1,2,128,1152]{3,2,1,0:T(8,128)(2,1)S(1)}, u32[]{:S(2)}, u32[]{:S(2)}) collective-permute-start(bf16[1,2,128,1152]{3,2,1,0:T(8,128)(2,1)S(1)} %get-tuple-element.39), channel_id=1, source_target_pairs={{1,2},{2,1},{5,6},{6,5},{9,10},{10,9},{13,14},{14,13},{17,18},{18,... | collective-permute-start | bytes 1769480 | tf_op jit(solution)/shard_map/ppermute | solution.py:490
  41.6 49.3 %collective-permute-start.2 = (bf16[384,1152]{1,0:T(8,128)(2,1)S(1)}, bf16[384,1152]{1,0:T(8,128)(2,1)S(1)}, u32[]{:S(2)}, u32[]{:S(2)}) collective-permute-start(bf16[384,1152]{1,0:T(8,128)(2,1)S(1)} %pad_maximum_fusion.3), channel_id=1, source_target_pairs={{0,1},{2,3},{1,0},{3,2},{4,5},{6,7},{5,4},{7,6},{8,9},{10,11},{9,8... | collective-permute-start | bytes 2654216 | tf_op jit(solution)/shard_map/ppermute | solution.py:490
  45.8 2.2 %collective-permute-start.8 = (bf16[1,2,128,1152]{3,2,1,0:T(8,128)(2,1)S(1)}, bf16[1,2,128,1152]{3,2,1,0:T(8,128)(2,1)S(1)}, u32[]{:S(2)}, u32[]{:S(2)}) collective-permute-start(bf16[1,2,128,1152]{3,2,1,0:T(8,128)(2,1)S(1)} %get-tuple-element.42), channel_id=1, source_target_pairs={{1,2},{2,1},{5,6},{6,5},{9,10},{10,9},{13,14},{14,13},{17,18},{18,... | collective-permute-start | bytes 1769480 | tf_op jit(solution)/shard_map/ppermute | solution.py:490
  46.7 56.7 %collective-permute-start.5 = (bf16[2,2,128,1152]{3,2,1,0:T(8,128)(2,1)S(1)}, bf16[2,2,128,1152]{3,2,1,0:T(8,128)(2,1)S(1)}, u32[]{:S(2)}, u32[]{:S(2)}) collective-permute-start(bf16[2,2,128,1152]{3,2,1,0:T(8,128)(2,1)S(1)} %slice_bitcast_fusion), channel_id=1, source_target_pairs={{1,2},{2,1},{5,6},{6,5},{9,10},{10,9},{13,14},{14,13},{17,18},{18,... | collective-permute-start | bytes 3538952 | tf_op jit(solution)/shard_map/ppermute | solution.py:490
  48.0 3.2 %copy-start = (s32[1,1,1,9]{3,2,1,0:T(1,128)S(1)}, s32[1,1,1,9]{3,2,1,0:T(1,128)}, u32[]{:S(2)}) copy-start(s32[1,1,1,9]{3,2,1,0:T(1,128)} %param.9) | copy-start | bytes 112
  48.0 3.2 %copy-start.1 = (s32[18]{0:T(128)S(1)}, s32[18]{0:T(128)}, u32[]{:S(2)}) copy-start(s32[18]{0:T(128)} %reach.7) | copy-start | bytes 220
  48.0 39.7 %collective-permute-start.11 = (bf16[144,1152]{1,0:T(8,128)(2,1)S(1)}, bf16[144,1152]{1,0:T(8,128)(2,1)S(1)}, u32[]{:S(2)}, u32[]{:S(2)}) collective-permute-start(bf16[144,1152]{1,0:T(8,128)(2,1)S(1)} %edge_rows.4), channel_id=1, source_target_pairs={{1,0},{2,3},{5,4},{6,7},{9,8},{10,11},{13,12},{14,15},{17,16},{18,... | collective-permute-start | bytes 995336 | tf_op jit(solution)/shard_map/ppermute | solution.py:490
  49.9 47.4 %collective-permute-start.17 = (bf16[144,1152]{1,0:T(8,128)(2,1)S(1)}, bf16[144,1152]{1,0:T(8,128)(2,1)S(1)}, u32[]{:S(2)}, u32[]{:S(2)}) collective-permute-start(bf16[144,1152]{1,0:T(8,128)(2,1)S(1)} %edge_rows.5), channel_id=1, source_target_pairs={{1,0},{2,3},{5,4},{6,7},{9,8},{10,11},{13,12},{14,15},{17,16},{18,... | collective-permute-start | bytes 995336 | tf_op jit(solution)/shard_map/ppermute | solution.py:490
  88.8 10.2 %collective-permute-start.14 = (bf16[128,1152]{1,0:T(8,128)(2,1)S(1)}, bf16[128,1152]{1,0:T(8,128)(2,1)S(1)}, u32[]{:S(2)}, u32[]{:S(2)}) collective-permute-start(bf16[128,1152]{1,0:T(8,128)(2,1)S(1)} %merge.2), channel_id=1, source_target_pairs={{0,16},{16,0},{1,17},{17,1},{2,18},{18,2},{3,19},{19,3},{4,20},{20... | collective-permute-start | bytes 884744 | tf_op jit(solution)/shard_map/ppermute | solution.py:490
  91.0 8.0 %slice-start = ((s8[14155776]{0:T(1024)(128)(4,1)}), s8[4194304]{0:T(1024)(128)(4,1)S(1)}, s32[]{:S(2)}) async-start(s8[14155776]{0:T(1024)(128)(4,1)} %bitcast.26), calls=%async_computation | async-start | bytes 8388608
  91.0 7.9 %slice-start.1 = ((s8[14155776]{0:T(1024)(128)(4,1)}), s8[4194304]{0:T(1024)(128)(4,1)S(1)}, s32[]{:S(2)}) async-start(s8[14155776]{0:T(1024)(128)(4,1)} %bitcast.26), calls=%async_computation.1 | async-start | bytes 8388608
  91.1 7.9 %slice-start.2 = ((s8[14155776]{0:T(1024)(128)(4,1)}), s8[4194304]{0:T(1024)(128)(4,1)S(1)}, s32[]{:S(2)}) async-start(s8[14155776]{0:T(1024)(128)(4,1)} %bitcast.26), calls=%async_computation.2 | async-start | bytes 8388608
  91.1 7.9 %slice-start.3 = ((s8[14155776]{0:T(1024)(128)(4,1)}), s8[1572864]{0:T(1024)(128)(4,1)S(1)}, s32[]{:S(2)}) async-start(s8[14155776]{0:T(1024)(128)(4,1)} %bitcast.26), calls=%async_computation.3 | async-start | bytes 3145728
  91.1 19.2 %collective-permute-start.16 = (bf16[384,1152]{1,0:T(8,128)(2,1)S(1)}, bf16[384,1152]{1,0:T(8,128)(2,1)S(1)}, u32[]{:S(2)}, u32[]{:S(2)}) collective-permute-start(bf16[384,1152]{1,0:T(8,128)(2,1)S(1)} %pad_maximum_fusion.4), channel_id=1, source_target_pairs={{0,1},{2,3},{1,0},{3,2},{4,5},{6,7},{5,4},{7,6},{8,9},{10,11},{9,8... | collective-permute-start | bytes 2654216 | tf_op jit(solution)/shard_map/ppermute | solution.py:490
  98.4 11.9 %collective-permute-start.22 = (bf16[128,1152]{1,0:T(8,128)(2,1)S(1)}, bf16[128,1152]{1,0:T(8,128)(2,1)S(1)}, u32[]{:S(2)}, u32[]{:S(2)}) collective-permute-start(bf16[128,1152]{1,0:T(8,128)(2,1)S(1)} %merge.3), channel_id=1, source_target_pairs={{0,16},{16,0},{1,17},{17,1},{2,18},{18,2},{3,19},{19,3},{4,20},{20... | collective-permute-start | bytes 884744 | tf_op jit(solution)/shard_map/ppermute | solution.py:490
  101.1 18.3 %collective-permute-start.25 = (bf16[128,3072]{1,0:T(8,128)(2,1)S(1)}, bf16[128,3072]{1,0:T(8,128)(2,1)S(1)}, u32[]{:S(2)}, u32[]{:S(2)}) collective-permute-start(bf16[128,3072]{1,0:T(8,128)(2,1)S(1)} %product.2), channel_id=1, source_target_pairs={{0,16},{16,0},{1,17},{17,1},{2,18},{18,2},{3,19},{19,3},{4,20},{20... | collective-permute-start | bytes 2359304 | tf_op jit(solution)/shard_map/ppermute | solution.py:490
  102.7 8.4 %collective-permute-start.15 = (bf16[1,2,128,1152]{3,2,1,0:T(8,128)(2,1)S(1)}, bf16[1,2,128,1152]{3,2,1,0:T(8,128)(2,1)S(1)}, u32[]{:S(2)}, u32[]{:S(2)}) collective-permute-start(bf16[1,2,128,1152]{3,2,1,0:T(8,128)(2,1)S(1)} %bitcast.49), channel_id=1, source_target_pairs={{1,2},{2,1},{5,6},{6,5},{9,10},{10,9},{13,14},{14,13},{17,18},{18,... | collective-permute-start | bytes 1769480 | tf_op jit(solution)/shard_map/ppermute | solution.py:490
  103.6 20.8 %collective-permute-start.13 = (bf16[2,1,2,128,1152]{4,3,2,1,0:T(8,128)(2,1)S(1)}, bf16[2,1,2,128,1152]{4,3,2,1,0:T(8,128)(2,1)S(1)}, u32[]{:S(2)}, u32[]{:S(2)}) collective-permute-start(bf16[2,1,2,128,1152]{4,3,2,1,0:T(8,128)(2,1)S(1)} %pad_maximum_fusion.1.refs_4_.refs_5_), channel_id=1, source_target_pairs={{4,8},{8,4},{5,9},{9,5},{6,10},{10,6},{7,11},{11,7},{20,24},{24,20... | collective-permute-start | bytes 3538952 | tf_op jit(solution)/shard_map/ppermute | solution.py:490
  110.2 16.1 %collective-permute-start.12 = (bf16[2,1,2,128,1152]{4,3,2,1,0:T(8,128)(2,1)S(1)}, bf16[2,1,2,128,1152]{4,3,2,1,0:T(8,128)(2,1)S(1)}, u32[]{:S(2)}, u32[]{:S(2)}) collective-permute-start(bf16[2,1,2,128,1152]{4,3,2,1,0:T(8,128)(2,1)S(1)} %pad_maximum_fusion.1.refs_4_.refs_5_), channel_id=1, source_target_pairs={{0,4},{8,12},{4,0},{12,8},{1,5},{9,13},{5,1},{13,9},{2,6},{10,14},... | collective-permute-start | bytes 3538952 | tf_op jit(solution)/shard_map/ppermute | solution.py:490
  110.3 12.7 %collective-permute-start.20 = (bf16[1,2,128,1152]{3,2,1,0:T(8,128)(2,1)S(1)}, bf16[1,2,128,1152]{3,2,1,0:T(8,128)(2,1)S(1)}, u32[]{:S(2)}, u32[]{:S(2)}) collective-permute-start(bf16[1,2,128,1152]{3,2,1,0:T(8,128)(2,1)S(1)} %bitcast.51), channel_id=1, source_target_pairs={{1,2},{2,1},{5,6},{6,5},{9,10},{10,9},{13,14},{14,13},{17,18},{18,... | collective-permute-start | bytes 1769480 | tf_op jit(solution)/shard_map/ppermute | solution.py:490
  111.1 32.2 %collective-permute-start.18 = (bf16[2,1,2,128,1152]{4,3,2,1,0:T(8,128)(2,1)S(1)}, bf16[2,1,2,128,1152]{4,3,2,1,0:T(8,128)(2,1)S(1)}, u32[]{:S(2)}, u32[]{:S(2)}) collective-permute-start(bf16[2,1,2,128,1152]{4,3,2,1,0:T(8,128)(2,1)S(1)} %pad_maximum_fusion.2.refs_4_.refs_5_), channel_id=1, source_target_pairs={{0,4},{8,12},{4,0},{12,8},{1,5},{9,13},{5,1},{13,9},{2,6},{10,14},... | collective-permute-start | bytes 3538952 | tf_op jit(solution)/shard_map/ppermute | solution.py:490
  119.4 23.9 %collective-permute-start.19 = (bf16[2,1,2,128,1152]{4,3,2,1,0:T(8,128)(2,1)S(1)}, bf16[2,1,2,128,1152]{4,3,2,1,0:T(8,128)(2,1)S(1)}, u32[]{:S(2)}, u32[]{:S(2)}) collective-permute-start(bf16[2,1,2,128,1152]{4,3,2,1,0:T(8,128)(2,1)S(1)} %pad_maximum_fusion.2.refs_4_.refs_5_), channel_id=1, source_target_pairs={{4,8},{8,4},{5,9},{9,5},{6,10},{10,6},{7,11},{11,7},{20,24},{24,20... | collective-permute-start | bytes 3538952 | tf_op jit(solution)/shard_map/ppermute | solution.py:490
  123.0 25.9 %collective-permute-start.23 = (bf16[128,3072]{1,0:T(8,128)(2,1)S(1)}, bf16[128,3072]{1,0:T(8,128)(2,1)S(1)}, u32[]{:S(2)}, u32[]{:S(2)}) collective-permute-start(bf16[128,3072]{1,0:T(8,128)(2,1)S(1)} %product.3), channel_id=1, source_target_pairs={{0,16},{16,0},{1,17},{17,1},{2,18},{18,2},{3,19},{19,3},{4,20},{20... | collective-permute-start | bytes 2359304 | tf_op jit(solution)/shard_map/ppermute | solution.py:490
  124.5 14.9 %collective-permute-start.24 = (bf16[144,1152]{1,0:T(8,128)(2,1)S(1)}, bf16[144,1152]{1,0:T(8,128)(2,1)S(1)}, u32[]{:S(2)}, u32[]{:S(2)}) collective-permute-start(bf16[144,1152]{1,0:T(8,128)(2,1)S(1)} %edge_rows.6), channel_id=1, source_target_pairs={{1,0},{2,3},{5,4},{6,7},{9,8},{10,11},{13,12},{14,15},{17,16},{18,... | collective-permute-start | bytes 995336 | tf_op jit(solution)/shard_map/ppermute | solution.py:490
  126.4 22.5 %collective-permute-start.21 = (bf16[144,1152]{1,0:T(8,128)(2,1)S(1)}, bf16[144,1152]{1,0:T(8,128)(2,1)S(1)}, u32[]{:S(2)}, u32[]{:S(2)}) collective-permute-start(bf16[144,1152]{1,0:T(8,128)(2,1)S(1)} %edge_rows.7), channel_id=1, source_target_pairs={{1,0},{2,3},{5,4},{6,7},{9,8},{10,11},{13,12},{14,15},{17,16},{18,... | collective-permute-start | bytes 995336 | tf_op jit(solution)/shard_map/ppermute | solution.py:490

commit v9 on v8

--- a/solution.py
+++ b/solution.py
@@ -40,20 +40,24 @@
     return jnp.abs(q // group - k // group)
 
 
-def softmax_sums(scores, values):
+def softmax_sums(scores, values, scale=TO_LOG2, ones=False):
     tops = [jnp.max(functools.reduce(jnp.maximum, tiles), axis=1, keepdims=True) for tiles in scores]
     weights = [
-        [jnp.exp2((s - top) * TO_LOG2) for s in tiles] for tiles, top in zip(scores, tops)
+        [jnp.exp2(s - top if scale == 1 else (s - top) * scale) for s in tiles]
+        for tiles, top in zip(scores, tops)
     ]
-    sums = [jnp.sum(functools.reduce(jnp.add, w), axis=1, keepdims=True) for w in weights]
-    totals = [
-        dot_nn(
-            jnp.concatenate([x.astype(jnp.bfloat16) for x in w], axis=1),
-            jnp.concatenate(tiles, axis=0),
-        )
-        for w, tiles in zip(weights, values)
-    ]
-    return [top * TO_LOG2 for top in tops], totals, sums
+    totals, sums = [], []
+    for w, tiles in zip(weights, values):
+        rounded = jnp.concatenate([x.astype(jnp.bfloat16) for x in w], axis=1)
+        right = jnp.concatenate(tiles, axis=0)
+        if ones:
+            both = dot_nn(rounded, jnp.concatenate([right, jnp.ones_like(right)], axis=1))
+            totals.append(both[:, :HEAD])
+            sums.append(both[:, HEAD:])
+        else:
+            totals.append(dot_nn(rounded, right))
+            sums.append(jnp.sum(functools.reduce(jnp.add, w), axis=1, keepdims=True))
+    return [top * scale for top in tops], totals, sums
 
 
 def place_pieces(stats, values, first):
@@ -121,7 +125,9 @@
     bias_ref[frames + 1] = jnp.where(group_gap(tokens, cols_tile) == 0, 0.0, NEG)
 
 
-def rows_kernel(place, mask, reach, q_ref, *refs, heads, half, grid, cols_tile, frame_tokens):
+def rows_kernel(
+    place, mask, reach, q_ref, *refs, heads, half, grid, cols_tile, frame_tokens, split, ones
+):
     tiles = refs[:10]
     base_ref, row_ref, sums_ref, bias_ref = refs[10:]
     tokens = q_ref.shape[0]
@@ -149,7 +155,14 @@
     outer_bias = bias_ref[jnp.where(inner, none + 1, none)]
 
     def scores_of(n):
-        scores = dot_nn(q_ref[:, cuts[n]], jnp.concatenate([t[0, :, cuts[n]] for t in tiles], axis=1))
+        q, keys = q_ref[:, cuts[n]], jnp.concatenate([t[0, :, cuts[n]] for t in tiles], axis=1)
+        if split:
+            scaled = q.astype(jnp.float32) * TO_LOG2
+            high = scaled.astype(jnp.bfloat16)
+            low = (scaled - high.astype(jnp.float32)).astype(jnp.bfloat16)
+            q = jnp.concatenate([high, low], axis=1)
+            keys = jnp.concatenate([keys, keys], axis=0)
+        scores = dot_nn(q, keys)
         return [scores[:, t * tokens:(t + 1) * tokens] for t in range(10)]
 
     lse = []
@@ -160,7 +173,9 @@
         limit = reach[first_head + step * heads + n]
         window = [raw[t] + bias_ref[jnp.where(listed[t], limit, none)] for t in range(9)]
         row = [raw[3] + row_bias, raw[4] + row_bias, raw[5] + outer_bias, raw[9] + outer_bias]
-        tops, totals, weights = softmax_sums([window, row], [values[:9], values[3:6] + values[9:]])
+        tops, totals, weights = softmax_sums(
+            [window, row], [values[:9], values[3:6] + values[9:]], 1 if split else TO_LOG2, ones
+        )
         axial = totals[1] / weights[1]
         base_ref[:, c] = totals[0] / weights[0] + axial
         row_ref[:, c] = axial.astype(jnp.bfloat16)
@@ -326,7 +341,7 @@
     )(place, q, near, far)
 
 
-def rows_attend(place, mask, reach, q, tiles, sides, far, half, stream, cols_tile, frame_tokens, grid, block=3):
+def rows_attend(place, mask, reach, q, tiles, sides, far, half, stream, cols_tile, frame_tokens, grid, block=3, split=False, ones=False):
     tokens, width = far.shape[2:]
     at = stream if far.shape[0] > 1 else 0
     heads = width // HEAD
@@ -338,7 +353,8 @@
     other = pl.BlockSpec((None, None, 2, tokens, lanes), lambda g, p: (1, place_of, 0, 0, g))
     args = [x for tile, pair in zip(tiles, sides) for x in (tile, pair, pair)]
     kernel = functools.partial(
-        rows_kernel, heads=block, half=half, grid=grid, cols_tile=cols_tile, frame_tokens=frame_tokens
+        rows_kernel, heads=block, half=half, grid=grid, cols_tile=cols_tile, frame_tokens=frame_tokens,
+        split=split, ones=ones,
     )
     return kernel_call(
         kernel,
@@ -469,6 +485,9 @@
     return pairs + [(j, i) for i, j in pairs]
 
 
+STYLES = ((dict(split=True), dict(block=1)), (dict(ones=True), dict(split=True, ones=True)))
+
+
 def per_device(queries, key_states, value_states, tile_mask, frame_reach, out_weight):
     S, F, R, C, width = queries.shape
     tokens = F * R * C
@@ -512,7 +531,8 @@
         part = f"{h}" if h == 0 else f"{h}{s}"
         sides = [sent[f"pair_sides{part}"], sent[f"sides{part}"], sent[f"next_sides{part}"]]
         sent[f"rows{h}{s}"] = rows_attend(
-            place, tied(mask, after), frame_reach, q, tiles, sides, sent[f"far{h}{s}"], h, s, C, R * C, (rows, cols)
+            place, tied(mask, after), frame_reach, q, tiles, sides, sent[f"far{h}{s}"], h, s, C, R * C, (rows, cols),
+            **STYLES[h][s],
         )
 
     send("near0", own0[0], "col", col_pairs)

time: 154 us -> 157 us (1.019)
  Pallas kernels: 48.1 us -> 51.1 us
    pallas_call x4, Pallas kernels: 23 us -> 26 us  [rows_attend(): kernel_call(kernel, out_shape=(jax.ShapeDtypeStruct((tokens, width), jnp....]
  transfers between devices with their start and end apart: 26 -> 26, of which waited for: 6 -> 7; matrix products, arithmetic and copies ran while one was open for 1% -> 1% of each run, Pallas kernels for 28% -> 29%
where the time goes in v9:
time: 157 us; the launch traced here: 156 us
  waiting for transfers between devices  70.4 us (45%)
  Pallas kernels  51.1 us (33%)
  starting transfers between devices  32.7 us (21%)
    ppermute x26, waiting for transfers between devices, send(): sent[name] = lax.ppermute(tied(value, after), axis, pairs)  70.4 us
    ppermute x26, starting transfers between devices, send(): sent[name] = lax.ppermute(tied(value, after), axis, pairs)  32.7 us
    pallas_call x4, Pallas kernels, rows_attend(): kernel_call(kernel, out_shape=(jax.ShapeDtypeStruct((tokens, width), jnp....  26 us
    pallas_call x2, Pallas kernels, project(): kernel_call(functools.partial(project_kernel, cols=cols), out_shape=jax.S...  7.93 us
    pallas_call x2, Pallas kernels, pack(): kernel_call(kernel, out_shape=jax.ShapeDtypeStruct((1 + len(given), S, 2,...  5.08 us
    pallas_call x2, Pallas kernels, product(): kernel_call(product_kernel, out_shape=jax.ShapeDtypeStruct((tokens, model...  4.21 us
    pallas_call x2, Pallas kernels, pick(): kernel_call(kernel, out_shape=jax.ShapeDtypeStruct((S, tokens, width), va...  3.29 us
  transfers between devices with their start and end apart: 26, of which 7 were waited for; matrix products, arithmetic and copies ran while one was open for 1% of the time, Pallas kernels for 29%

profile of v9, /device:TPU:0, one launch (start us, length us, event | category | flops | bytes accessed | tf_op | source)
XLA Modules:
  0.0 156.0 jit_solution(16490576122709689957)
XLA Ops:
  0.1 2.0 %pack.2.refs_0_ = bf16[1,2,2,128,1152]{4,3,2,1,0:T(8,128)(2,1)S(1)} custom-call(s32[3]{0:T(128)S(1)} %pad_add_fusion.place, bf16[2,128,2304]{2,1,0:T(8,128)(2,1)} %bitcast.43, bf16[2,128,2304]{2,1,0:T(8,128)(2,1)} %bitcast.45), custom_call_target="tpu_custom_call" | custom-call | bytes 2359296 | tf_op jit(solution)/shard_map/pack/pallas_call | solution.py:276
  2.8 5.8 %collective-permute-start.3 = (bf16[2,2,128,1152]{3,2,1,0:T(8,128)(2,1)S(1)}, bf16[2,2,128,1152]{3,2,1,0:T(8,128)(2,1)S(1)}, u32[]{:S(2)}, u32[]{:S(2)}) collective-permute-start(bf16[2,2,128,1152]{3,2,1,0:T(8,128)(2,1)S(1)} %bitcast.29), channel_id=1, source_target_pairs={{0,1},{2,3},{1,0},{3,2},{4,5},{6,7},{5,4},{7,6},{8,9},{10,11},{9,8... | collective-permute-start | bytes 3538952 | tf_op jit(solution)/shard_map/ppermute | solution.py:509
  8.6 1.6 %pick.2 = bf16[2,128,1152]{2,1,0:T(8,128)(2,1)S(1)} custom-call(s32[3]{0:T(128)S(1)} %pad_add_fusion.place, bf16[2,128,2304]{2,1,0:T(8,128)(2,1)} %bitcast.36), custom_call_target="tpu_custom_call" | custom-call | bytes 4718592 | tf_op jit(solution)/shard_map/pick/pallas_call | solution.py:300
  10.3 3.1 %pack.3.refs_3_ = bf16[2,2,2,128,1152]{4,3,2,1,0:T(8,128)(2,1)S(1)} custom-call(s32[3]{0:T(128)S(1)} %pad_add_fusion.place, bf16[2,128,2304]{2,1,0:T(8,128)(2,1)} %bitcast.44, bf16[2,128,2304]{2,1,0:T(8,128)(2,1)} %bitcast.46, bf16[1,2,2,128,1152]{4,3,2,1,0:T(8,128)(2,1)S(1)} %pack.2.refs_0_), custom_call_target="tpu_custom_call" | custom-call | bytes 2359296 | tf_op jit(solution)/shard_map/pack/pallas_call | solution.py:276
  13.5 0.8 collective-permute-start.7
  14.3 2.0 %collective-permute-start.6 = (bf16[256,1152]{1,0:T(8,128)(2,1)S(1)}, bf16[256,1152]{1,0:T(8,128)(2,1)S(1)}, u32[]{:S(2)}, u32[]{:S(2)}) collective-permute-start(bf16[256,1152]{1,0:T(8,128)(2,1)S(1)} %bitcast.31), channel_id=1, source_target_pairs={{0,1},{3,2},{4,5},{7,6},{8,9},{11,10},{12,13},{15,14},{16,17},{19,... | collective-permute-start | bytes 1769480 | tf_op jit(solution)/shard_map/ppermute | solution.py:509
  16.3 18.8 %collective-permute-done.3 = bf16[2,2,128,1152]{3,2,1,0:T(8,128)(2,1)S(1)} collective-permute-done((bf16[2,2,128,1152]{3,2,1,0:T(8,128)(2,1)S(1)}, bf16[2,2,128,1152]{3,2,1,0:T(8,128)(2,1)S(1)}, u32[]{:S(2)}, u32[]{:S(2)}) %collective-permute-start.3) | collective-permute-done | bytes 1179680 | tf_op jit(solution)/shard_map/ppermute | solution.py:509
  36.1 2.8 %collective-permute-start.9 = (bf16[2,2,2,128,1152]{4,3,2,1,0:T(8,128)(2,1)S(1)}, bf16[2,2,2,128,1152]{4,3,2,1,0:T(8,128)(2,1)S(1)}, u32[]{:S(2)}, u32[]{:S(2)}) collective-permute-start(bf16[2,2,2,128,1152]{4,3,2,1,0:T(8,128)(2,1)S(1)} %pad_maximum_fusion.refs_4_.refs_5_), channel_id=1, source_target_pairs={{0,4},{8,12},{4,0},{12,8},{1,5},{9,13},{5,1},{13,9},{2,6},{10,14},... | collective-permute-start | bytes 7077896 | tf_op jit(solution)/shard_map/ppermute | solution.py:509
  39.0 1.6 %pick.3 = bf16[2,128,1152]{2,1,0:T(8,128)(2,1)S(1)} custom-call(s32[3]{0:T(128)S(1)} %pad_add_fusion.place, bf16[2,128,2304]{2,1,0:T(8,128)(2,1)} %bitcast.37), custom_call_target="tpu_custom_call" | custom-call | bytes 4718592 | tf_op jit(solution)/shard_map/pick/pallas_call | solution.py:300
  41.6 4.2 %collective-permute-start.2 = (bf16[384,1152]{1,0:T(8,128)(2,1)S(1)}, bf16[384,1152]{1,0:T(8,128)(2,1)S(1)}, u32[]{:S(2)}, u32[]{:S(2)}) collective-permute-start(bf16[384,1152]{1,0:T(8,128)(2,1)S(1)} %pad_maximum_fusion.3), channel_id=1, source_target_pairs={{0,1},{2,3},{1,0},{3,2},{4,5},{6,7},{5,4},{7,6},{8,9},{10,11},{9,8... | collective-permute-start | bytes 2654216 | tf_op jit(solution)/shard_map/ppermute | solution.py:509
  48.0 1.3 collective-permute-start.11
  49.9 1.3 collective-permute-start.17
  51.3 5.5 %rows.4 = (f32[128,1152]{1,0:T(8,128)S(1)}, bf16[128,1152]{1,0:T(8,128)(2,1)S(1)}, bf16[128,128]{1,0:T(8,128)(2,1)S(1)}) custom-call(s32[3]{0:T(128)S(1)} %pad_add_fusion.place, s32[9]{0:T(128)S(1)} %bitcast.32, s32[18]{0:T(128)S(1)} %copy-done.1, bf16[2,128,2304]{2,1,0:T(8,128)(2,1)} %bitcast.38, ...), custom_call_target="tpu_custom_call" | custom-call | flops 868220928 | bytes 7962624 | tf_op jit(solution)/shard_map/rows/pallas_call | solution.py:359
  56.8 30.9 %collective-permute-done.11.rest_ref.stats_ref = bf16[144,1152]{1,0:T(8,128)(2,1)S(1)} collective-permute-done((bf16[144,1152]{1,0:T(8,128)(2,1)S(1)}, bf16[144,1152]{1,0:T(8,128)(2,1)S(1)}, u32[]{:S(2)}, u32[]{:S(2)}) %collective-permute-start.11) | collective-permute-done | bytes 331808 | tf_op jit(solution)/shard_map/ppermute | solution.py:509
  87.7 1.1 merge.2
  88.8 2.2 %collective-permute-start.14 = (bf16[128,1152]{1,0:T(8,128)(2,1)S(1)}, bf16[128,1152]{1,0:T(8,128)(2,1)S(1)}, u32[]{:S(2)}, u32[]{:S(2)}) collective-permute-start(bf16[128,1152]{1,0:T(8,128)(2,1)S(1)} %merge.2), channel_id=1, source_target_pairs={{0,16},{16,0},{1,17},{17,1},{2,18},{18,2},{3,19},{19,3},{4,20},{20... | collective-permute-start | bytes 884744 | tf_op jit(solution)/shard_map/ppermute | solution.py:509
  91.2 9.7 %rows.5 = (f32[128,1152]{1,0:T(8,128)S(1)}, bf16[128,1152]{1,0:T(8,128)(2,1)S(1)}, bf16[128,128]{1,0:T(8,128)(2,1)S(1)}) custom-call(s32[3]{0:T(128)S(1)} %pad_add_fusion.place, s32[9]{0:T(128)S(1)} %bitcast.33, s32[18]{0:T(128)S(1)} %copy-done.1, bf16[2,128,2304]{2,1,0:T(8,128)(2,1)} %bitcast.39, ...), custom_call_target="tpu_custom_call" | custom-call | flops 868220928 | bytes 7962624 | tf_op jit(solution)/shard_map/rows/pallas_call | solution.py:359
  100.9 1.1 merge.3
  102.5 2.1 %product.2 = bf16[128,3072]{1,0:T(8,128)(2,1)S(1)} custom-call(bf16[128,1152]{1,0:T(8,128)(2,1)S(1)} %collective-permute-done.14.rows_ref, bf16[2,1152,3072]{2,1,0:T(8,128)(2,1)S(1)} %bitcast.27), custom_call_target="tpu_custom_call" | custom-call | flops 3623878656 | bytes 28311552 | tf_op jit(solution)/shard_map/product/pallas_call | solution.py:465
  104.6 1.7 %collective-permute-start.25 = (bf16[128,3072]{1,0:T(8,128)(2,1)S(1)}, bf16[128,3072]{1,0:T(8,128)(2,1)S(1)}, u32[]{:S(2)}, u32[]{:S(2)}) collective-permute-start(bf16[128,3072]{1,0:T(8,128)(2,1)S(1)} %product.2), channel_id=1, source_target_pairs={{0,16},{16,0},{1,17},{17,1},{2,18},{18,2},{3,19},{19,3},{4,20},{20... | collective-permute-start | bytes 2359304 | tf_op jit(solution)/shard_map/ppermute | solution.py:509
  108.0 2.3 %collective-permute-done.16.q_ref = bf16[384,1152]{1,0:T(8,128)(2,1)S(1)} collective-permute-done((bf16[384,1152]{1,0:T(8,128)(2,1)S(1)}, bf16[384,1152]{1,0:T(8,128)(2,1)S(1)}, u32[]{:S(2)}, u32[]{:S(2)}) %collective-permute-start.16) | collective-permute-done | bytes 884768 | tf_op jit(solution)/shard_map/ppermute | solution.py:509
  110.3 1.7 %collective-permute-done.22.rows_ref = bf16[128,1152]{1,0:T(8,128)(2,1)S(1)} collective-permute-done((bf16[128,1152]{1,0:T(8,128)(2,1)S(1)}, bf16[128,1152]{1,0:T(8,128)(2,1)S(1)}, u32[]{:S(2)}, u32[]{:S(2)}) %collective-permute-start.22) | collective-permute-done | bytes 294944 | tf_op jit(solution)/shard_map/ppermute | solution.py:509
  112.9 9.6 %collective-permute-done.25.other_ref = bf16[128,3072]{1,0:T(8,128)(2,1)S(1)} collective-permute-done((bf16[128,3072]{1,0:T(8,128)(2,1)S(1)}, bf16[128,3072]{1,0:T(8,128)(2,1)S(1)}, u32[]{:S(2)}, u32[]{:S(2)}) %collective-permute-start.25) | collective-permute-done | bytes 786464 | tf_op jit(solution)/shard_map/ppermute | solution.py:509
  124.0 2.1 %product.3 = bf16[128,3072]{1,0:T(8,128)(2,1)S(1)} custom-call(bf16[128,1152]{1,0:T(8,128)(2,1)S(1)} %collective-permute-done.22.rows_ref, bf16[2,1152,3072]{2,1,0:T(8,128)(2,1)S(1)} %bitcast.27), custom_call_target="tpu_custom_call" | custom-call | flops 3623878656 | bytes 28311552 | tf_op jit(solution)/shard_map/product/pallas_call | solution.py:465
  126.2 0.9 collective-permute-start.23
  127.0 1.3 collective-permute-start.24
  128.9 1.3 collective-permute-start.21
  130.2 5.4 %rows.6 = (f32[128,1152]{1,0:T(8,128)S(1)}, bf16[128,1152]{1,0:T(8,128)(2,1)S(1)}, bf16[128,128]{1,0:T(8,128)(2,1)S(1)}) custom-call(s32[3]{0:T(128)S(1)} %pad_add_fusion.place, s32[9]{0:T(128)S(1)} %bitcast.34, s32[18]{0:T(128)S(1)} %copy-done.1, bf16[2,128,2304]{2,1,0:T(8,128)(2,1)} %bitcast.40, ...), custom_call_target="tpu_custom_call" | custom-call | flops 868220928 | bytes 7962624 | tf_op jit(solution)/shard_map/rows/pallas_call | solution.py:359
  135.6 7.0 %collective-permute-done.24.rest_ref.stats_ref = bf16[144,1152]{1,0:T(8,128)(2,1)S(1)} collective-permute-done((bf16[144,1152]{1,0:T(8,128)(2,1)S(1)}, bf16[144,1152]{1,0:T(8,128)(2,1)S(1)}, u32[]{:S(2)}, u32[]{:S(2)}) %collective-permute-start.24) | collective-permute-done | bytes 331808 | tf_op jit(solution)/shard_map/ppermute | solution.py:509
  142.6 4.0 %project.2.refs_0_ = bf16[2,128,3072]{2,1,0:T(8,128)(2,1)} custom-call(s32[3]{0:T(128)S(1)} %pad_add_fusion.place, f32[128,1152]{1,0:T(8,128)S(1)} %get-tuple-element.55.base_ref, bf16[128,1152]{1,0:T(8,128)(2,1)S(1)} %get-tuple-element.56.row_ref, bf16[128,128]{1,0:T(8,128)(2,1)S(1)} %get-tuple-element.57.sums_ref, ...), custom_call_target="tpu_custom_call" | custom-call | flops 905969664 | bytes 7077888 | tf_op jit(solution)/shard_map/project/pallas_call | solution.py:430
  146.6 5.4 %rows.7 = (f32[128,1152]{1,0:T(8,128)S(1)}, bf16[128,1152]{1,0:T(8,128)(2,1)S(1)}, bf16[128,128]{1,0:T(8,128)(2,1)S(1)}) custom-call(s32[3]{0:T(128)S(1)} %pad_add_fusion.place, s32[9]{0:T(128)S(1)} %bitcast.35, s32[18]{0:T(128)S(1)} %copy-done.1, bf16[2,128,2304]{2,1,0:T(8,128)(2,1)} %bitcast.41, ...), custom_call_target="tpu_custom_call" | custom-call | flops 868220928 | bytes 7962624 | tf_op jit(solution)/shard_map/rows/pallas_call | solution.py:359
  152.1 4.0 %project.3 = bf16[2,128,3072]{2,1,0:T(8,128)(2,1)} custom-call(s32[3]{0:T(128)S(1)} %pad_add_fusion.place, f32[128,1152]{1,0:T(8,128)S(1)} %get-tuple-element.62.base_ref, bf16[128,1152]{1,0:T(8,128)(2,1)S(1)} %get-tuple-element.63.row_ref, bf16[128,128]{1,0:T(8,128)(2,1)S(1)} %get-tuple-element.64.sums_ref, ...), custom_call_target="tpu_custom_call", output_to_operand_aliasing={{}: (8, {})} | custom-call | flops 905969664 | bytes 7077888 | tf_op jit(solution)/shard_map/project/pallas_call | solution.py:430
  (64 shorter events, 11.0 us)
Async XLA Ops:
  2.1 14.2 %collective-permute-start.1 = (bf16[2,2,128,1152]{3,2,1,0:T(8,128)(2,1)S(1)}, bf16[2,2,128,1152]{3,2,1,0:T(8,128)(2,1)S(1)}, u32[]{:S(2)}, u32[]{:S(2)}) collective-permute-start(bf16[2,2,128,1152]{3,2,1,0:T(8,128)(2,1)S(1)} %bitcast.28), channel_id=1, source_target_pairs={{1,2},{2,1},{5,6},{6,5},{9,10},{10,9},{13,14},{14,13},{17,18},{18,... | collective-permute-start | bytes 3538952 | tf_op jit(solution)/shard_map/ppermute | solution.py:509
  2.8 32.2 %collective-permute-start.3 = (bf16[2,2,128,1152]{3,2,1,0:T(8,128)(2,1)S(1)}, bf16[2,2,128,1152]{3,2,1,0:T(8,128)(2,1)S(1)}, u32[]{:S(2)}, u32[]{:S(2)}) collective-permute-start(bf16[2,2,128,1152]{3,2,1,0:T(8,128)(2,1)S(1)} %bitcast.29), channel_id=1, source_target_pairs={{0,1},{2,3},{1,0},{3,2},{4,5},{6,7},{5,4},{7,6},{8,9},{10,11},{9,8... | collective-permute-start | bytes 3538952 | tf_op jit(solution)/shard_map/ppermute | solution.py:509
  13.4 27.4 %collective-permute-start = (bf16[2,2,2,128,1152]{4,3,2,1,0:T(8,128)(2,1)S(1)}, bf16[2,2,2,128,1152]{4,3,2,1,0:T(8,128)(2,1)S(1)}, u32[]{:S(2)}, u32[]{:S(2)}) collective-permute-start(bf16[2,2,2,128,1152]{4,3,2,1,0:T(8,128)(2,1)S(1)} %pack.3.refs_3_), channel_id=1, source_target_pairs={{0,4},{8,12},{4,0},{12,8},{1,5},{9,13},{5,1},{13,9},{2,6},{10,14},... | collective-permute-start | bytes 7077896 | tf_op jit(solution)/shard_map/ppermute | solution.py:509
  13.5 28.1 %collective-permute-start.7 = (bf16[2,2,2,128,1152]{4,3,2,1,0:T(8,128)(2,1)S(1)}, bf16[2,2,2,128,1152]{4,3,2,1,0:T(8,128)(2,1)S(1)}, u32[]{:S(2)}, u32[]{:S(2)}) collective-permute-start(bf16[2,2,2,128,1152]{4,3,2,1,0:T(8,128)(2,1)S(1)} %pack.3.refs_3_), channel_id=1, source_target_pairs={{4,8},{8,4},{5,9},{9,5},{6,10},{10,6},{7,11},{11,7},{20,24},{24,20... | collective-permute-start | bytes 7077896 | tf_op jit(solution)/shard_map/ppermute | solution.py:509
  14.3 32.4 %collective-permute-start.6 = (bf16[256,1152]{1,0:T(8,128)(2,1)S(1)}, bf16[256,1152]{1,0:T(8,128)(2,1)S(1)}, u32[]{:S(2)}, u32[]{:S(2)}) collective-permute-start(bf16[256,1152]{1,0:T(8,128)(2,1)S(1)} %bitcast.31), channel_id=1, source_target_pairs={{0,1},{3,2},{4,5},{7,6},{8,9},{11,10},{12,13},{15,14},{16,17},{19,... | collective-permute-start | bytes 1769480 | tf_op jit(solution)/shard_map/ppermute | solution.py:509
  35.3 14.6 %collective-permute-start.10 = (bf16[2,2,2,128,1152]{4,3,2,1,0:T(8,128)(2,1)S(1)}, bf16[2,2,2,128,1152]{4,3,2,1,0:T(8,128)(2,1)S(1)}, u32[]{:S(2)}, u32[]{:S(2)}) collective-permute-start(bf16[2,2,2,128,1152]{4,3,2,1,0:T(8,128)(2,1)S(1)} %pad_maximum_fusion.refs_4_.refs_5_), channel_id=1, source_target_pairs={{4,8},{8,4},{5,9},{9,5},{6,10},{10,6},{7,11},{11,7},{20,24},{24,20... | collective-permute-start | bytes 7077896 | tf_op jit(solution)/shard_map/ppermute | solution.py:509
  36.1 15.1 %collective-permute-start.9 = (bf16[2,2,2,128,1152]{4,3,2,1,0:T(8,128)(2,1)S(1)}, bf16[2,2,2,128,1152]{4,3,2,1,0:T(8,128)(2,1)S(1)}, u32[]{:S(2)}, u32[]{:S(2)}) collective-permute-start(bf16[2,2,2,128,1152]{4,3,2,1,0:T(8,128)(2,1)S(1)} %pad_maximum_fusion.refs_4_.refs_5_), channel_id=1, source_target_pairs={{0,4},{8,12},{4,0},{12,8},{1,5},{9,13},{5,1},{13,9},{2,6},{10,14},... | collective-permute-start | bytes 7077896 | tf_op jit(solution)/shard_map/ppermute | solution.py:509
  40.8 5.1 %collective-permute-start.4 = (bf16[1,2,128,1152]{3,2,1,0:T(8,128)(2,1)S(1)}, bf16[1,2,128,1152]{3,2,1,0:T(8,128)(2,1)S(1)}, u32[]{:S(2)}, u32[]{:S(2)}) collective-permute-start(bf16[1,2,128,1152]{3,2,1,0:T(8,128)(2,1)S(1)} %get-tuple-element.39), channel_id=1, source_target_pairs={{1,2},{2,1},{5,6},{6,5},{9,10},{10,9},{13,14},{14,13},{17,18},{18,... | collective-permute-start | bytes 1769480 | tf_op jit(solution)/shard_map/ppermute | solution.py:509
  41.6 49.4 %collective-permute-start.2 = (bf16[384,1152]{1,0:T(8,128)(2,1)S(1)}, bf16[384,1152]{1,0:T(8,128)(2,1)S(1)}, u32[]{:S(2)}, u32[]{:S(2)}) collective-permute-start(bf16[384,1152]{1,0:T(8,128)(2,1)S(1)} %pad_maximum_fusion.3), channel_id=1, source_target_pairs={{0,1},{2,3},{1,0},{3,2},{4,5},{6,7},{5,4},{7,6},{8,9},{10,11},{9,8... | collective-permute-start | bytes 2654216 | tf_op jit(solution)/shard_map/ppermute | solution.py:509
  45.8 2.2 %collective-permute-start.8 = (bf16[1,2,128,1152]{3,2,1,0:T(8,128)(2,1)S(1)}, bf16[1,2,128,1152]{3,2,1,0:T(8,128)(2,1)S(1)}, u32[]{:S(2)}, u32[]{:S(2)}) collective-permute-start(bf16[1,2,128,1152]{3,2,1,0:T(8,128)(2,1)S(1)} %get-tuple-element.42), channel_id=1, source_target_pairs={{1,2},{2,1},{5,6},{6,5},{9,10},{10,9},{13,14},{14,13},{17,18},{18,... | collective-permute-start | bytes 1769480 | tf_op jit(solution)/shard_map/ppermute | solution.py:509
  46.7 60.3 %collective-permute-start.5 = (bf16[2,2,128,1152]{3,2,1,0:T(8,128)(2,1)S(1)}, bf16[2,2,128,1152]{3,2,1,0:T(8,128)(2,1)S(1)}, u32[]{:S(2)}, u32[]{:S(2)}) collective-permute-start(bf16[2,2,128,1152]{3,2,1,0:T(8,128)(2,1)S(1)} %slice_bitcast_fusion), channel_id=1, source_target_pairs={{1,2},{2,1},{5,6},{6,5},{9,10},{10,9},{13,14},{14,13},{17,18},{18,... | collective-permute-start | bytes 3538952 | tf_op jit(solution)/shard_map/ppermute | solution.py:509
  48.0 3.2 %copy-start = (s32[1,1,1,9]{3,2,1,0:T(1,128)S(1)}, s32[1,1,1,9]{3,2,1,0:T(1,128)}, u32[]{:S(2)}) copy-start(s32[1,1,1,9]{3,2,1,0:T(1,128)} %param.9) | copy-start | bytes 112
  48.0 3.2 %copy-start.1 = (s32[18]{0:T(128)S(1)}, s32[18]{0:T(128)}, u32[]{:S(2)}) copy-start(s32[18]{0:T(128)} %reach.7) | copy-start | bytes 220
  48.0 39.7 %collective-permute-start.11 = (bf16[144,1152]{1,0:T(8,128)(2,1)S(1)}, bf16[144,1152]{1,0:T(8,128)(2,1)S(1)}, u32[]{:S(2)}, u32[]{:S(2)}) collective-permute-start(bf16[144,1152]{1,0:T(8,128)(2,1)S(1)} %edge_rows.4), channel_id=1, source_target_pairs={{1,0},{2,3},{5,4},{6,7},{9,8},{10,11},{13,12},{14,15},{17,16},{18,... | collective-permute-start | bytes 995336 | tf_op jit(solution)/shard_map/ppermute | solution.py:509
  49.9 50.9 %collective-permute-start.17 = (bf16[144,1152]{1,0:T(8,128)(2,1)S(1)}, bf16[144,1152]{1,0:T(8,128)(2,1)S(1)}, u32[]{:S(2)}, u32[]{:S(2)}) collective-permute-start(bf16[144,1152]{1,0:T(8,128)(2,1)S(1)} %edge_rows.5), channel_id=1, source_target_pairs={{1,0},{2,3},{5,4},{6,7},{9,8},{10,11},{13,12},{14,15},{17,16},{18,... | collective-permute-start | bytes 995336 | tf_op jit(solution)/shard_map/ppermute | solution.py:509
  88.8 13.7 %collective-permute-start.14 = (bf16[128,1152]{1,0:T(8,128)(2,1)S(1)}, bf16[128,1152]{1,0:T(8,128)(2,1)S(1)}, u32[]{:S(2)}, u32[]{:S(2)}) collective-permute-start(bf16[128,1152]{1,0:T(8,128)(2,1)S(1)} %merge.2), channel_id=1, source_target_pairs={{0,16},{16,0},{1,17},{17,1},{2,18},{18,2},{3,19},{19,3},{4,20},{20... | collective-permute-start | bytes 884744 | tf_op jit(solution)/shard_map/ppermute | solution.py:509
  91.0 11.4 %slice-start = ((s8[14155776]{0:T(1024)(128)(4,1)}), s8[4194304]{0:T(1024)(128)(4,1)S(1)}, s32[]{:S(2)}) async-start(s8[14155776]{0:T(1024)(128)(4,1)} %bitcast.26), calls=%async_computation | async-start | bytes 8388608
  91.1 11.4 %slice-start.1 = ((s8[14155776]{0:T(1024)(128)(4,1)}), s8[4194304]{0:T(1024)(128)(4,1)S(1)}, s32[]{:S(2)}) async-start(s8[14155776]{0:T(1024)(128)(4,1)} %bitcast.26), calls=%async_computation.1 | async-start | bytes 8388608
  91.1 11.4 %slice-start.2 = ((s8[14155776]{0:T(1024)(128)(4,1)}), s8[4194304]{0:T(1024)(128)(4,1)S(1)}, s32[]{:S(2)}) async-start(s8[14155776]{0:T(1024)(128)(4,1)} %bitcast.26), calls=%async_computation.2 | async-start | bytes 8388608
  91.1 11.4 %slice-start.3 = ((s8[14155776]{0:T(1024)(128)(4,1)}), s8[1572864]{0:T(1024)(128)(4,1)S(1)}, s32[]{:S(2)}) async-start(s8[14155776]{0:T(1024)(128)(4,1)} %bitcast.26), calls=%async_computation.3 | async-start | bytes 3145728
  91.1 19.1 %collective-permute-start.16 = (bf16[384,1152]{1,0:T(8,128)(2,1)S(1)}, bf16[384,1152]{1,0:T(8,128)(2,1)S(1)}, u32[]{:S(2)}, u32[]{:S(2)}) collective-permute-start(bf16[384,1152]{1,0:T(8,128)(2,1)S(1)} %pad_maximum_fusion.4), channel_id=1, source_target_pairs={{0,1},{2,3},{1,0},{3,2},{4,5},{6,7},{5,4},{7,6},{8,9},{10,11},{9,8... | collective-permute-start | bytes 2654216 | tf_op jit(solution)/shard_map/ppermute | solution.py:509
  102.0 10.0 %collective-permute-start.22 = (bf16[128,1152]{1,0:T(8,128)(2,1)S(1)}, bf16[128,1152]{1,0:T(8,128)(2,1)S(1)}, u32[]{:S(2)}, u32[]{:S(2)}) collective-permute-start(bf16[128,1152]{1,0:T(8,128)(2,1)S(1)} %merge.3), channel_id=1, source_target_pairs={{0,16},{16,0},{1,17},{17,1},{2,18},{18,2},{3,19},{19,3},{4,20},{20... | collective-permute-start | bytes 884744 | tf_op jit(solution)/shard_map/ppermute | solution.py:509
  104.6 17.9 %collective-permute-start.25 = (bf16[128,3072]{1,0:T(8,128)(2,1)S(1)}, bf16[128,3072]{1,0:T(8,128)(2,1)S(1)}, u32[]{:S(2)}, u32[]{:S(2)}) collective-permute-start(bf16[128,3072]{1,0:T(8,128)(2,1)S(1)} %product.2), channel_id=1, source_target_pairs={{0,16},{16,0},{1,17},{17,1},{2,18},{18,2},{3,19},{19,3},{4,20},{20... | collective-permute-start | bytes 2359304 | tf_op jit(solution)/shard_map/ppermute | solution.py:509
  106.3 6.5 %collective-permute-start.15 = (bf16[1,2,128,1152]{3,2,1,0:T(8,128)(2,1)S(1)}, bf16[1,2,128,1152]{3,2,1,0:T(8,128)(2,1)S(1)}, u32[]{:S(2)}, u32[]{:S(2)}) collective-permute-start(bf16[1,2,128,1152]{3,2,1,0:T(8,128)(2,1)S(1)} %bitcast.49), channel_id=1, source_target_pairs={{1,2},{2,1},{5,6},{6,5},{9,10},{10,9},{13,14},{14,13},{17,18},{18,... | collective-permute-start | bytes 1769480 | tf_op jit(solution)/shard_map/ppermute | solution.py:509
  107.2 19.8 %collective-permute-start.13 = (bf16[2,1,2,128,1152]{4,3,2,1,0:T(8,128)(2,1)S(1)}, bf16[2,1,2,128,1152]{4,3,2,1,0:T(8,128)(2,1)S(1)}, u32[]{:S(2)}, u32[]{:S(2)}) collective-permute-start(bf16[2,1,2,128,1152]{4,3,2,1,0:T(8,128)(2,1)S(1)} %pad_maximum_fusion.1.refs_4_.refs_5_), channel_id=1, source_target_pairs={{4,8},{8,4},{5,9},{9,5},{6,10},{10,6},{7,11},{11,7},{20,24},{24,20... | collective-permute-start | bytes 3538952 | tf_op jit(solution)/shard_map/ppermute | solution.py:509
  110.2 18.7 %collective-permute-start.12 = (bf16[2,1,2,128,1152]{4,3,2,1,0:T(8,128)(2,1)S(1)}, bf16[2,1,2,128,1152]{4,3,2,1,0:T(8,128)(2,1)S(1)}, u32[]{:S(2)}, u32[]{:S(2)}) collective-permute-start(bf16[2,1,2,128,1152]{4,3,2,1,0:T(8,128)(2,1)S(1)} %pad_maximum_fusion.1.refs_4_.refs_5_), channel_id=1, source_target_pairs={{0,4},{8,12},{4,0},{12,8},{1,5},{9,13},{5,1},{13,9},{2,6},{10,14},... | collective-permute-start | bytes 3538952 | tf_op jit(solution)/shard_map/ppermute | solution.py:509
  112.0 14.2 %collective-permute-start.20 = (bf16[1,2,128,1152]{3,2,1,0:T(8,128)(2,1)S(1)}, bf16[1,2,128,1152]{3,2,1,0:T(8,128)(2,1)S(1)}, u32[]{:S(2)}, u32[]{:S(2)}) collective-permute-start(bf16[1,2,128,1152]{3,2,1,0:T(8,128)(2,1)S(1)} %bitcast.51), channel_id=1, source_target_pairs={{1,2},{2,1},{5,6},{6,5},{9,10},{10,9},{13,14},{14,13},{17,18},{18,... | collective-permute-start | bytes 1769480 | tf_op jit(solution)/shard_map/ppermute | solution.py:509
  112.8 33.8 %collective-permute-start.18 = (bf16[2,1,2,128,1152]{4,3,2,1,0:T(8,128)(2,1)S(1)}, bf16[2,1,2,128,1152]{4,3,2,1,0:T(8,128)(2,1)S(1)}, u32[]{:S(2)}, u32[]{:S(2)}) collective-permute-start(bf16[2,1,2,128,1152]{4,3,2,1,0:T(8,128)(2,1)S(1)} %pad_maximum_fusion.2.refs_4_.refs_5_), channel_id=1, source_target_pairs={{0,4},{8,12},{4,0},{12,8},{1,5},{9,13},{5,1},{13,9},{2,6},{10,14},... | collective-permute-start | bytes 3538952 | tf_op jit(solution)/shard_map/ppermute | solution.py:509
  122.5 24.1 %collective-permute-start.19 = (bf16[2,1,2,128,1152]{4,3,2,1,0:T(8,128)(2,1)S(1)}, bf16[2,1,2,128,1152]{4,3,2,1,0:T(8,128)(2,1)S(1)}, u32[]{:S(2)}, u32[]{:S(2)}) collective-permute-start(bf16[2,1,2,128,1152]{4,3,2,1,0:T(8,128)(2,1)S(1)} %pad_maximum_fusion.2.refs_4_.refs_5_), channel_id=1, source_target_pairs={{4,8},{8,4},{5,9},{9,5},{6,10},{10,6},{7,11},{11,7},{20,24},{24,20... | collective-permute-start | bytes 3538952 | tf_op jit(solution)/shard_map/ppermute | solution.py:509
  126.2 25.9 %collective-permute-start.23 = (bf16[128,3072]{1,0:T(8,128)(2,1)S(1)}, bf16[128,3072]{1,0:T(8,128)(2,1)S(1)}, u32[]{:S(2)}, u32[]{:S(2)}) collective-permute-start(bf16[128,3072]{1,0:T(8,128)(2,1)S(1)} %product.3), channel_id=1, source_target_pairs={{0,16},{16,0},{1,17},{17,1},{2,18},{18,2},{3,19},{19,3},{4,20},{20... | collective-permute-start | bytes 2359304 | tf_op jit(solution)/shard_map/ppermute | solution.py:509
  127.0 15.6 %collective-permute-start.24 = (bf16[144,1152]{1,0:T(8,128)(2,1)S(1)}, bf16[144,1152]{1,0:T(8,128)(2,1)S(1)}, u32[]{:S(2)}, u32[]{:S(2)}) collective-permute-start(bf16[144,1152]{1,0:T(8,128)(2,1)S(1)} %edge_rows.6), channel_id=1, source_target_pairs={{1,0},{2,3},{5,4},{6,7},{9,8},{10,11},{13,12},{14,15},{17,16},{18,... | collective-permute-start | bytes 995336 | tf_op jit(solution)/shard_map/ppermute | solution.py:509
  128.9 23.1 %collective-permute-start.21 = (bf16[144,1152]{1,0:T(8,128)(2,1)S(1)}, bf16[144,1152]{1,0:T(8,128)(2,1)S(1)}, u32[]{:S(2)}, u32[]{:S(2)}) collective-permute-start(bf16[144,1152]{1,0:T(8,128)(2,1)S(1)} %edge_rows.7), channel_id=1, source_target_pairs={{1,0},{2,3},{5,4},{6,7},{9,8},{10,11},{13,12},{14,15},{17,16},{18,... | collective-permute-start | bytes 995336 | tf_op jit(solution)/shard_map/ppermute | solution.py:509

commit v10 on v9

--- a/solution.py
+++ b/solution.py
@@ -92,7 +92,7 @@
 
 
 def edge_kernel(place, q_ref, near_ref, far_ref, out_ref, *, heads, cols_tile, cols):
-    tokens = q_ref.shape[0]
+    tokens = q_ref.shape[1]
     inner = (place[2] > 0) & (place[2] < cols - 1)
 
     @pl.when(jnp.logical_not(inner))
@@ -102,10 +102,9 @@
     @pl.when(inner)
     def _():
         bias = jnp.where(group_gap(tokens, cols_tile) == 0, 0.0, NEG)
-        cuts = [slice(n * HEAD, (n + 1) * HEAD) for n in range(heads)]
         tiles = (near_ref, far_ref)
-        scores = [[dot_nn(q_ref[:, c], t[0, :, c]) + bias for t in tiles] for c in cuts]
-        values = [[t[1, :, c] for t in tiles] for c in cuts]
+        scores = [[dot_nn(q_ref[n], t[0, n]) + bias for t in tiles] for n in range(heads)]
+        values = [[t[1, n] for t in tiles] for n in range(heads)]
         tops, totals, weights = softmax_sums(scores, values)
         lse = [top + jnp.log2(w) for top, w in zip(tops, weights)]
         stats = place_pieces(jnp.zeros((tokens, HEAD), jnp.float32), lse, 0)
@@ -155,7 +154,7 @@
     outer_bias = bias_ref[jnp.where(inner, none + 1, none)]
 
     def scores_of(n):
-        q, keys = q_ref[:, cuts[n]], jnp.concatenate([t[0, :, cuts[n]] for t in tiles], axis=1)
+        q, keys = q_ref[:, cuts[n]], jnp.concatenate([t[0, n] for t in tiles], axis=1)
         if split:
             scaled = q.astype(jnp.float32) * TO_LOG2
             high = scaled.astype(jnp.bfloat16)
@@ -169,7 +168,7 @@
     following = scores_of(0)
     for n, c in enumerate(cuts):
         raw, following = following, scores_of(n + 1) if n + 1 < heads else None
-        values = [t[1, :, c] for t in tiles]
+        values = [t[1, n] for t in tiles]
         limit = reach[first_head + step * heads + n]
         window = [raw[t] + bias_ref[jnp.where(listed[t], limit, none)] for t in range(9)]
         row = [raw[3] + row_bias, raw[4] + row_bias, raw[5] + outer_bias, raw[9] + outer_bias]
@@ -248,16 +247,16 @@
 
 def pack(place, keys, values, half, earlier=None):
     S, tokens, width = keys.shape
-    width //= 2
-    spec = pl.BlockSpec((None, tokens, width), lambda h, s, p: (s, 0, side(half, p)))
-    block = (None, None, 2, tokens, width)
+    heads = width // 2 // HEAD
+    spec = pl.BlockSpec((None, tokens, width // 2), lambda h, s, p: (s, 0, side(half, p)))
+    block = (None, None, 2, heads, tokens, HEAD)
     given = [] if earlier is None else [earlier]
 
     def turn(k_ref, v_ref, out_ref):
-        for start in range(0, width, HEAD):
-            cut = slice(start, start + HEAD)
-            out_ref[0, :, cut] = k_ref[:, cut].T
-        out_ref[1] = v_ref[...]
+        for n in range(heads):
+            cut = slice(n * HEAD, (n + 1) * HEAD)
+            out_ref[0, n] = k_ref[:, cut].T
+            out_ref[1, n] = v_ref[:, cut]
 
     def kernel(place, k_ref, v_ref, *refs):
         out_ref = refs[-1]
@@ -275,16 +274,16 @@
 
     return kernel_call(
         kernel,
-        out_shape=jax.ShapeDtypeStruct((1 + len(given), S, 2, tokens, width), keys.dtype),
+        out_shape=jax.ShapeDtypeStruct((1 + len(given), S, 2, heads, tokens, HEAD), keys.dtype),
         grid_spec=pltpu.PrefetchScalarGridSpec(
             num_scalar_prefetch=1,
             grid=(1 + len(given), S),
-            in_specs=[spec, spec, *[pl.BlockSpec(block, lambda h, s, p: (0, s, 0, 0, 0))] * len(given)],
-            out_specs=pl.BlockSpec(block, lambda h, s, p: (h, s, 0, 0, 0)),
-        ),
-        compiler_params=params(),
-        cost_estimate=pl.CostEstimate(
-            flops=0, bytes_accessed=8 * S * tokens * width, transcendentals=0
+            in_specs=[spec, spec, *[pl.BlockSpec(block, lambda h, s, p: (0, s, 0, 0, 0, 0))] * len(given)],
+            out_specs=pl.BlockSpec(block, lambda h, s, p: (h, s, 0, 0, 0, 0)),
+        ),
+        compiler_params=params(),
+        cost_estimate=pl.CostEstimate(
+            flops=0, bytes_accessed=4 * S * tokens * width, transcendentals=0
         ),
         name="pack",
     )(place, *hbm(keys, values), *given)
@@ -292,31 +291,32 @@
 
 def pick(place, value, half):
     S, tokens, width = value.shape
-    width //= 2
+    heads = width // 2 // HEAD
 
     def kernel(place, in_ref, out_ref):
-        out_ref[...] = in_ref[...]
+        for n in range(heads):
+            out_ref[n] = in_ref[:, n * HEAD:(n + 1) * HEAD]
 
     return kernel_call(
         kernel,
-        out_shape=jax.ShapeDtypeStruct((S, tokens, width), value.dtype),
+        out_shape=jax.ShapeDtypeStruct((S, heads, tokens, HEAD), value.dtype),
         grid_spec=pltpu.PrefetchScalarGridSpec(
             num_scalar_prefetch=1,
             grid=(S,),
-            in_specs=[pl.BlockSpec((None, tokens, width), lambda s, p: (s, 0, side(half, p)))],
-            out_specs=pl.BlockSpec((None, tokens, width), lambda s, p: (s, 0, 0)),
-        ),
-        compiler_params=params(),
-        cost_estimate=pl.CostEstimate(
-            flops=0, bytes_accessed=4 * S * tokens * width, transcendentals=0
+            in_specs=[pl.BlockSpec((None, tokens, width // 2), lambda s, p: (s, 0, side(half, p)))],
+            out_specs=pl.BlockSpec((None, heads, tokens, HEAD), lambda s, p: (s, 0, 0, 0)),
+        ),
+        compiler_params=params(),
+        cost_estimate=pl.CostEstimate(
+            flops=0, bytes_accessed=2 * S * tokens * width, transcendentals=0
         ),
         name="pick",
     )(place, *hbm(value))
 
 
 def edge_attend(place, q, q_block, near, far, stream, cols_tile, cols):
-    _, _, tokens, width = far.shape
-    heads = width // HEAD
+    _, _, heads, tokens, _ = far.shape
+    width = heads * HEAD
     rows = tokens + FOLD
     return kernel_call(
         functools.partial(edge_kernel, heads=heads, cols_tile=cols_tile, cols=cols),
@@ -325,9 +325,9 @@
             num_scalar_prefetch=1,
             grid=(1,),
             in_specs=[
-                pl.BlockSpec((tokens, width), lambda g, p: (q_block, 0)),
-                pl.BlockSpec((None, 2, tokens, width), lambda g, p: (stream, 0, 0, 0)),
-                pl.BlockSpec((None, 2, tokens, width), lambda g, p: (0, 0, 0, 0)),
+                pl.BlockSpec((None, heads, tokens, HEAD), lambda g, p: (q_block, 0, 0, 0)),
+                pl.BlockSpec((None, 2, heads, tokens, HEAD), lambda g, p: (stream, 0, 0, 0, 0)),
+                pl.BlockSpec((None, 2, heads, tokens, HEAD), lambda g, p: (0, 0, 0, 0, 0)),
             ],
             out_specs=pl.BlockSpec((rows, width), lambda g, p: (0, 0)),
         ),
@@ -342,15 +342,15 @@
 
 
 def rows_attend(place, mask, reach, q, tiles, sides, far, half, stream, cols_tile, frame_tokens, grid, block=3, split=False, ones=False):
-    tokens, width = far.shape[2:]
+    heads, tokens, _ = far.shape[2:]
+    width = heads * HEAD
     at = stream if far.shape[0] > 1 else 0
-    heads = width // HEAD
     lanes = block * HEAD
     steps = heads // block
     place_of = stream if sides[0].shape[1] > 1 else 0
-    own = pl.BlockSpec((None, None, 2, tokens, lanes), lambda g, p: (half, stream, 0, 0, g))
-    near = pl.BlockSpec((None, None, 2, tokens, lanes), lambda g, p: (0, place_of, 0, 0, g))
-    other = pl.BlockSpec((None, None, 2, tokens, lanes), lambda g, p: (1, place_of, 0, 0, g))
+    own = pl.BlockSpec((None, None, 2, block, tokens, HEAD), lambda g, p: (half, stream, 0, g, 0, 0))
+    near = pl.BlockSpec((None, None, 2, block, tokens, HEAD), lambda g, p: (0, place_of, 0, g, 0, 0))
+    other = pl.BlockSpec((None, None, 2, block, tokens, HEAD), lambda g, p: (1, place_of, 0, g, 0, 0))
     args = [x for tile, pair in zip(tiles, sides) for x in (tile, pair, pair)]
     kernel = functools.partial(
         rows_kernel, heads=block, half=half, grid=grid, cols_tile=cols_tile, frame_tokens=frame_tokens,
@@ -371,7 +371,7 @@
                 SMEM,
                 pl.BlockSpec((None, tokens, lanes), lambda g, p: (stream, 0, side(half, p) * steps + g)),
                 *[own, near, other] * 3,
-                pl.BlockSpec((None, 2, tokens, lanes), lambda g, p: (at, 0, 0, g)),
+                pl.BlockSpec((None, 2, block, tokens, HEAD), lambda g, p: (at, 0, g, 0, 0)),
             ],
             out_specs=(
                 pl.BlockSpec((tokens, lanes), lambda g, p: (0, g)),
@@ -485,13 +485,13 @@
     return pairs + [(j, i) for i, j in pairs]
 
 
-STYLES = ((dict(split=True), dict(block=1)), (dict(ones=True), dict(split=True, ones=True)))
+STYLES = ((dict(split=True), dict(split=True, ones=True)), (dict(), dict(ones=True)))
 
 
 def per_device(queries, key_states, value_states, tile_mask, frame_reach, out_weight):
     S, F, R, C, width = queries.shape
     tokens = F * R * C
-    half, model = width // 2, out_weight.shape[2]
+    model = out_weight.shape[2]
     rows, cols = lax.axis_size("row"), lax.axis_size("col")
     inward = [(0, 1), (cols - 1, cols - 2)]
     outward = [(j, i) for i, j in inward]
@@ -512,19 +512,20 @@
     row_pairs, row_others = swaps(rows, 0), swaps(rows, 1)
     pair_swap = swaps(2, 0)
     own0 = pack(place, k, v, 0)
-    picked = pick(place, q, 0).reshape(S * tokens, half)
+    picked = pick(place, q, 0)
+    heads = picked.shape[1]
     own = pack(tied(place, [picked]), k, v, 1, own0)
     q1 = pick(tied(place, [own]), q, 1)
-    onward = [jnp.concatenate([own[1, s].reshape(2 * tokens, half), q1[s]]) for s in range(S)]
+    onward = [jnp.concatenate([own[1, s].reshape(2 * heads, tokens, HEAD), q1[s]]) for s in range(S)]
 
     def edge(h, s, *after):
-        rows_q, block = (sent["q0"], s) if h == 0 else (sent[f"near1{s}"], 2)
+        rows_q, block = (sent["q0"], s) if h == 0 else (sent[f"near1{s}"].reshape(3, heads, tokens, HEAD), 2)
         sent[f"part{h}{s}"] = edge_attend(
             place, tied(rows_q, after), block, sent[f"other{h}"], sent[f"far{h}{s}"], s, C, cols
         )
 
     def near1(s):
-        return sent[f"near1{s}"][:2 * tokens].reshape(1, 2, tokens, half)
+        return sent[f"near1{s}"][:2 * heads].reshape(1, 2, heads, tokens, HEAD)
 
     def rows_of(h, s, *after):
         tiles = [sent["pair_own"], own, sent["next_own"]]

time: 157 us -> 160 us (1.019)
  starting transfers between devices: 32.7 us -> 46.5 us
  waiting for transfers between devices: 70.4 us -> 63.9 us
  Pallas kernels: 51.1 us -> 47.5 us
    ppermute x26, starting transfers between devices: 32.7 us -> 46.5 us  [send(): sent[name] = lax.ppermute(tied(value, after), axis, pairs)]
    ppermute x26, waiting for transfers between devices: 70.4 us -> 63.9 us  [send(): sent[name] = lax.ppermute(tied(value, after), axis, pairs)]
    pallas_call x4, Pallas kernels: 26 us -> 22.3 us  [rows_attend(): kernel_call(kernel, out_shape=(jax.ShapeDtypeStruct((tokens, width), jnp....]
  transfers between devices with their start and end apart: 26 -> 26, of which waited for: 7 -> 5; matrix products, arithmetic and copies ran while one was open for 1% -> 1% of each run, Pallas kernels for 29% -> 23%
where the time goes in v10:
time: 160 us
  waiting for transfers between devices  63.9 us (40%)
  Pallas kernels  47.5 us (30%)
  starting transfers between devices  46.5 us (29%)
    ppermute x26, waiting for transfers between devices, send(): sent[name] = lax.ppermute(tied(value, after), axis, pairs)  63.9 us
    ppermute x26, starting transfers between devices, send(): sent[name] = lax.ppermute(tied(value, after), axis, pairs)  46.5 us
    pallas_call x4, Pallas kernels, rows_attend(): kernel_call(kernel, out_shape=(jax.ShapeDtypeStruct((tokens, width), jnp....  22.3 us
    pallas_call x2, Pallas kernels, project(): kernel_call(functools.partial(project_kernel, cols=cols), out_shape=jax.S...  7.92 us
    pallas_call x2, Pallas kernels, pack(): kernel_call(kernel, out_shape=jax.ShapeDtypeStruct((1 + len(given), S, 2,...  5.14 us
    pallas_call x2, Pallas kernels, product(): kernel_call(product_kernel, out_shape=jax.ShapeDtypeStruct((tokens, model...  4.23 us
    pallas_call x2, Pallas kernels, pick(): kernel_call(kernel, out_shape=jax.ShapeDtypeStruct((S, heads, tokens, HEA...  3.35 us
  transfers between devices with their start and end apart: 26, of which 5 were waited for; matrix products, arithmetic and copies ran while one was open for 1% of the time, Pallas kernels for 23%

profile of v10, /device:TPU:0, one launch (start us, length us, event | category | flops | bytes accessed | tf_op | source)
XLA Modules:
  0.0 159.8 jit_solution(11528720875203331022)
XLA Ops:
  0.1 1.7 %pick.2 = bf16[2,9,128,128]{3,2,1,0:T(8,128)(2,1)S(1)} custom-call(s32[3]{0:T(128)S(1)} %pad_add_fusion.place, bf16[2,128,2304]{2,1,0:T(8,128)(2,1)} %bitcast.38), custom_call_target="tpu_custom_call" | custom-call | bytes 4718592 | tf_op jit(solution)/shard_map/pick/pallas_call | solution.py:300
  1.8 2.0 %pack.2.refs_0_ = bf16[1,2,2,9,128,128]{5,4,3,2,1,0:T(8,128)(2,1)S(1)} custom-call(s32[3]{0:T(128)S(1)} %pad_add_fusion.place, bf16[2,128,2304]{2,1,0:T(8,128)(2,1)} %bitcast.45, bf16[2,128,2304]{2,1,0:T(8,128)(2,1)} %bitcast.47), custom_call_target="tpu_custom_call" | custom-call | bytes 2359296 | tf_op jit(solution)/shard_map/pack/pallas_call | solution.py:275
  3.8 3.1 %pack.3.refs_3_ = bf16[2,2,2,9,128,128]{5,4,3,2,1,0:T(8,128)(2,1)S(1)} custom-call(s32[3]{0:T(128)S(1)} %pad_add_fusion.place, bf16[2,128,2304]{2,1,0:T(8,128)(2,1)} %bitcast.46, bf16[2,128,2304]{2,1,0:T(8,128)(2,1)} %bitcast.48, bf16[1,2,2,9,128,128]{5,4,3,2,1,0:T(8,128)(2,1)S(1)} %pack.2.refs_0_), custom_call_target="tpu_custom_call" | custom-call | bytes 2359296 | tf_op jit(solution)/shard_map/pack/pallas_call | solution.py:275
  8.2 5.4 %collective-permute-start.3 = (bf16[2,2,9,128,128]{4,3,2,1,0:T(8,128)(2,1)S(1)}, bf16[2,2,9,128,128]{4,3,2,1,0:T(8,128)(2,1)S(1)}, u32[]{:S(2)}, u32[]{:S(2)}) collective-permute-start(bf16[2,2,9,128,128]{4,3,2,1,0:T(8,128)(2,1)S(1)} %bitcast.30), channel_id=1, source_target_pairs={{0,1},{2,3},{1,0},{3,2},{4,5},{6,7},{5,4},{7,6},{8,9},{10,11},{9,8... | collective-permute-start | bytes 3538952 | tf_op jit(solution)/shard_map/ppermute | solution.py:509
  13.6 0.8 collective-permute-start.7
  14.4 25.5 %collective-permute-done.3 = bf16[2,2,9,128,128]{4,3,2,1,0:T(8,128)(2,1)S(1)} collective-permute-done((bf16[2,2,9,128,128]{4,3,2,1,0:T(8,128)(2,1)S(1)}, bf16[2,2,9,128,128]{4,3,2,1,0:T(8,128)(2,1)S(1)}, u32[]{:S(2)}, u32[]{:S(2)}) %collective-permute-start.3) | collective-permute-done | bytes 1179680 | tf_op jit(solution)/shard_map/ppermute | solution.py:509
  40.1 0.8 collective-permute-start.10
  41.0 2.8 %collective-permute-start.9 = (bf16[2,2,2,9,128,128]{5,4,3,2,1,0:T(8,128)(2,1)S(1)}, bf16[2,2,2,9,128,128]{5,4,3,2,1,0:T(8,128)(2,1)S(1)}, u32[]{:S(2)}, u32[]{:S(2)}) collective-permute-start(bf16[2,2,2,9,128,128]{5,4,3,2,1,0:T(8,128)(2,1)S(1)} %pad_maximum_fusion.refs_4_.refs_5_), channel_id=1, source_target_pairs={{0,4},{8,12},{4,0},{12,8},{1,5},{9,13},{5,1},{13,9},{2,6},{10,14},... | collective-permute-start | bytes 7077896 | tf_op jit(solution)/shard_map/ppermute | solution.py:509
  43.7 3.7 %collective-permute-start.6 = (bf16[2,9,128,128]{3,2,1,0:T(8,128)(2,1)S(1)}, bf16[2,9,128,128]{3,2,1,0:T(8,128)(2,1)S(1)}, u32[]{:S(2)}, u32[]{:S(2)}) collective-permute-start(bf16[2,9,128,128]{3,2,1,0:T(8,128)(2,1)S(1)} %pick.2), channel_id=1, source_target_pairs={{0,1},{3,2},{4,5},{7,6},{8,9},{11,10},{12,13},{15,14},{16,17},{19,... | collective-permute-start | bytes 1769480 | tf_op jit(solution)/shard_map/ppermute | solution.py:509
  47.4 1.7 %pick.3 = bf16[2,9,128,128]{3,2,1,0:T(8,128)(2,1)S(1)} custom-call(s32[3]{0:T(128)S(1)} %pad_add_fusion.place, bf16[2,128,2304]{2,1,0:T(8,128)(2,1)} %bitcast.39), custom_call_target="tpu_custom_call" | custom-call | bytes 4718592 | tf_op jit(solution)/shard_map/pick/pallas_call | solution.py:300
  50.9 15.7 %collective-permute-start.2 = (bf16[27,128,128]{2,1,0:T(8,128)(2,1)S(1)}, bf16[27,128,128]{2,1,0:T(8,128)(2,1)S(1)}, u32[]{:S(2)}, u32[]{:S(2)}) collective-permute-start(bf16[27,128,128]{2,1,0:T(8,128)(2,1)S(1)} %pad_maximum_fusion.3), channel_id=1, source_target_pairs={{0,1},{2,3},{1,0},{3,2},{4,5},{6,7},{5,4},{7,6},{8,9},{10,11},{9,8... | collective-permute-start | bytes 2654216 | tf_op jit(solution)/shard_map/ppermute | solution.py:509
  68.2 1.3 collective-permute-start.11
  70.1 1.3 collective-permute-start.17
  71.4 5.4 %rows.4 = (f32[128,1152]{1,0:T(8,128)S(1)}, bf16[128,1152]{1,0:T(8,128)(2,1)S(1)}, bf16[128,128]{1,0:T(8,128)(2,1)S(1)}) custom-call(s32[3]{0:T(128)S(1)} %pad_add_fusion.place, s32[9]{0:T(128)S(1)} %bitcast.34, s32[18]{0:T(128)S(1)} %copy-done.1, bf16[2,128,2304]{2,1,0:T(8,128)(2,1)} %bitcast.40, ...), custom_call_target="tpu_custom_call" | custom-call | flops 868220928 | bytes 7962624 | tf_op jit(solution)/shard_map/rows/pallas_call | solution.py:359
  76.8 17.5 %collective-permute-done.11.rest_ref.stats_ref = bf16[144,1152]{1,0:T(8,128)(2,1)S(1)} collective-permute-done((bf16[144,1152]{1,0:T(8,128)(2,1)S(1)}, bf16[144,1152]{1,0:T(8,128)(2,1)S(1)}, u32[]{:S(2)}, u32[]{:S(2)}) %collective-permute-start.11) | collective-permute-done | bytes 331808 | tf_op jit(solution)/shard_map/ppermute | solution.py:509
  94.3 1.1 merge.2
  95.4 1.6 collective-permute-start.14
  97.2 6.0 %rows.5 = (f32[128,1152]{1,0:T(8,128)S(1)}, bf16[128,1152]{1,0:T(8,128)(2,1)S(1)}, bf16[128,128]{1,0:T(8,128)(2,1)S(1)}) custom-call(s32[3]{0:T(128)S(1)} %pad_add_fusion.place, s32[9]{0:T(128)S(1)} %bitcast.35, s32[18]{0:T(128)S(1)} %copy-done.1, bf16[2,128,2304]{2,1,0:T(8,128)(2,1)} %bitcast.41, ...), custom_call_target="tpu_custom_call" | custom-call | flops 868220928 | bytes 7962624 | tf_op jit(solution)/shard_map/rows/pallas_call | solution.py:359
  103.3 1.1 merge.3
  105.0 2.1 %product.2 = bf16[128,3072]{1,0:T(8,128)(2,1)S(1)} custom-call(bf16[128,1152]{1,0:T(8,128)(2,1)S(1)} %collective-permute-done.14.rows_ref, bf16[2,1152,3072]{2,1,0:T(8,128)(2,1)S(1)} %bitcast.28), custom_call_target="tpu_custom_call" | custom-call | flops 3623878656 | bytes 28311552 | tf_op jit(solution)/shard_map/product/pallas_call | solution.py:465
  107.1 1.6 collective-permute-start.25
  110.3 7.6 %collective-permute-done.16 = bf16[27,128,128]{2,1,0:T(8,128)(2,1)S(1)} collective-permute-done((bf16[27,128,128]{2,1,0:T(8,128)(2,1)S(1)}, bf16[27,128,128]{2,1,0:T(8,128)(2,1)S(1)}, u32[]{:S(2)}, u32[]{:S(2)}) %collective-permute-start.16) | collective-permute-done | bytes 884768 | tf_op jit(solution)/shard_map/ppermute | solution.py:509
  119.4 6.0 %collective-permute-done.25.other_ref = bf16[128,3072]{1,0:T(8,128)(2,1)S(1)} collective-permute-done((bf16[128,3072]{1,0:T(8,128)(2,1)S(1)}, bf16[128,3072]{1,0:T(8,128)(2,1)S(1)}, u32[]{:S(2)}, u32[]{:S(2)}) %collective-permute-start.25) | collective-permute-done | bytes 786464 | tf_op jit(solution)/shard_map/ppermute | solution.py:509
  126.9 2.1 %product.3 = bf16[128,3072]{1,0:T(8,128)(2,1)S(1)} custom-call(bf16[128,1152]{1,0:T(8,128)(2,1)S(1)} %collective-permute-done.22.rows_ref, bf16[2,1152,3072]{2,1,0:T(8,128)(2,1)S(1)} %bitcast.28), custom_call_target="tpu_custom_call" | custom-call | flops 3623878656 | bytes 28311552 | tf_op jit(solution)/shard_map/product/pallas_call | solution.py:465
  129.0 1.6 collective-permute-start.23
  130.6 1.3 collective-permute-start.24
  132.4 1.3 collective-permute-start.21
  133.7 5.5 %rows.6 = (f32[128,1152]{1,0:T(8,128)S(1)}, bf16[128,1152]{1,0:T(8,128)(2,1)S(1)}, bf16[128,128]{1,0:T(8,128)(2,1)S(1)}) custom-call(s32[3]{0:T(128)S(1)} %pad_add_fusion.place, s32[9]{0:T(128)S(1)} %bitcast.36, s32[18]{0:T(128)S(1)} %copy-done.1, bf16[2,128,2304]{2,1,0:T(8,128)(2,1)} %bitcast.42, ...), custom_call_target="tpu_custom_call" | custom-call | flops 868220928 | bytes 7962624 | tf_op jit(solution)/shard_map/rows/pallas_call | solution.py:359
  139.3 7.3 %collective-permute-done.24.rest_ref.stats_ref = bf16[144,1152]{1,0:T(8,128)(2,1)S(1)} collective-permute-done((bf16[144,1152]{1,0:T(8,128)(2,1)S(1)}, bf16[144,1152]{1,0:T(8,128)(2,1)S(1)}, u32[]{:S(2)}, u32[]{:S(2)}) %collective-permute-start.24) | collective-permute-done | bytes 331808 | tf_op jit(solution)/shard_map/ppermute | solution.py:509
  146.6 4.0 %project.2.refs_0_ = bf16[2,128,3072]{2,1,0:T(8,128)(2,1)} custom-call(s32[3]{0:T(128)S(1)} %pad_add_fusion.place, f32[128,1152]{1,0:T(8,128)S(1)} %get-tuple-element.55.base_ref, bf16[128,1152]{1,0:T(8,128)(2,1)S(1)} %get-tuple-element.56.row_ref, bf16[128,128]{1,0:T(8,128)(2,1)S(1)} %get-tuple-element.57.sums_ref, ...), custom_call_target="tpu_custom_call" | custom-call | flops 905969664 | bytes 7077888 | tf_op jit(solution)/shard_map/project/pallas_call | solution.py:430
  150.6 5.3 %rows.7 = (f32[128,1152]{1,0:T(8,128)S(1)}, bf16[128,1152]{1,0:T(8,128)(2,1)S(1)}, bf16[128,128]{1,0:T(8,128)(2,1)S(1)}) custom-call(s32[3]{0:T(128)S(1)} %pad_add_fusion.place, s32[9]{0:T(128)S(1)} %bitcast.37, s32[18]{0:T(128)S(1)} %copy-done.1, bf16[2,128,2304]{2,1,0:T(8,128)(2,1)} %bitcast.43, ...), custom_call_target="tpu_custom_call" | custom-call | flops 868220928 | bytes 7962624 | tf_op jit(solution)/shard_map/rows/pallas_call | solution.py:359
  155.9 4.0 %project.3 = bf16[2,128,3072]{2,1,0:T(8,128)(2,1)} custom-call(s32[3]{0:T(128)S(1)} %pad_add_fusion.place, f32[128,1152]{1,0:T(8,128)S(1)} %get-tuple-element.62.base_ref, bf16[128,1152]{1,0:T(8,128)(2,1)S(1)} %get-tuple-element.63.row_ref, bf16[128,128]{1,0:T(8,128)(2,1)S(1)} %get-tuple-element.64.sums_ref, ...), custom_call_target="tpu_custom_call", output_to_operand_aliasing={{}: (8, {})} | custom-call | flops 905969664 | bytes 7077888 | tf_op jit(solution)/shard_map/project/pallas_call | solution.py:430
  (64 shorter events, 11.3 us)
Async XLA Ops:
  6.9 42.3 %collective-permute-start = (bf16[2,2,2,9,128,128]{5,4,3,2,1,0:T(8,128)(2,1)S(1)}, bf16[2,2,2,9,128,128]{5,4,3,2,1,0:T(8,128)(2,1)S(1)}, u32[]{:S(2)}, u32[]{:S(2)}) collective-permute-start(bf16[2,2,2,9,128,128]{5,4,3,2,1,0:T(8,128)(2,1)S(1)} %pack.3.refs_3_), channel_id=1, source_target_pairs={{0,4},{8,12},{4,0},{12,8},{1,5},{9,13},{5,1},{13,9},{2,6},{10,14},... | collective-permute-start | bytes 7077896 | tf_op jit(solution)/shard_map/ppermute | solution.py:509
  7.4 7.0 %collective-permute-start.1 = (bf16[2,2,9,128,128]{4,3,2,1,0:T(8,128)(2,1)S(1)}, bf16[2,2,9,128,128]{4,3,2,1,0:T(8,128)(2,1)S(1)}, u32[]{:S(2)}, u32[]{:S(2)}) collective-permute-start(bf16[2,2,9,128,128]{4,3,2,1,0:T(8,128)(2,1)S(1)} %bitcast.29), channel_id=1, source_target_pairs={{1,2},{2,1},{5,6},{6,5},{9,10},{10,9},{13,14},{14,13},{17,18},{18,... | collective-permute-start | bytes 3538952 | tf_op jit(solution)/shard_map/ppermute | solution.py:509
  8.2 31.7 %collective-permute-start.3 = (bf16[2,2,9,128,128]{4,3,2,1,0:T(8,128)(2,1)S(1)}, bf16[2,2,9,128,128]{4,3,2,1,0:T(8,128)(2,1)S(1)}, u32[]{:S(2)}, u32[]{:S(2)}) collective-permute-start(bf16[2,2,9,128,128]{4,3,2,1,0:T(8,128)(2,1)S(1)} %bitcast.30), channel_id=1, source_target_pairs={{0,1},{2,3},{1,0},{3,2},{4,5},{6,7},{5,4},{7,6},{8,9},{10,11},{9,8... | collective-permute-start | bytes 3538952 | tf_op jit(solution)/shard_map/ppermute | solution.py:509
  13.6 36.6 %collective-permute-start.7 = (bf16[2,2,2,9,128,128]{5,4,3,2,1,0:T(8,128)(2,1)S(1)}, bf16[2,2,2,9,128,128]{5,4,3,2,1,0:T(8,128)(2,1)S(1)}, u32[]{:S(2)}, u32[]{:S(2)}) collective-permute-start(bf16[2,2,2,9,128,128]{5,4,3,2,1,0:T(8,128)(2,1)S(1)} %pack.3.refs_3_), channel_id=1, source_target_pairs={{4,8},{8,4},{5,9},{9,5},{6,10},{10,6},{7,11},{11,7},{20,24},{24,20... | collective-permute-start | bytes 7077896 | tf_op jit(solution)/shard_map/ppermute | solution.py:509
  40.1 29.9 %collective-permute-start.10 = (bf16[2,2,2,9,128,128]{5,4,3,2,1,0:T(8,128)(2,1)S(1)}, bf16[2,2,2,9,128,128]{5,4,3,2,1,0:T(8,128)(2,1)S(1)}, u32[]{:S(2)}, u32[]{:S(2)}) collective-permute-start(bf16[2,2,2,9,128,128]{5,4,3,2,1,0:T(8,128)(2,1)S(1)} %pad_maximum_fusion.refs_4_.refs_5_), channel_id=1, source_target_pairs={{4,8},{8,4},{5,9},{9,5},{6,10},{10,6},{7,11},{11,7},{20,24},{24,20... | collective-permute-start | bytes 7077896 | tf_op jit(solution)/shard_map/ppermute | solution.py:509
  41.0 30.4 %collective-permute-start.9 = (bf16[2,2,2,9,128,128]{5,4,3,2,1,0:T(8,128)(2,1)S(1)}, bf16[2,2,2,9,128,128]{5,4,3,2,1,0:T(8,128)(2,1)S(1)}, u32[]{:S(2)}, u32[]{:S(2)}) collective-permute-start(bf16[2,2,2,9,128,128]{5,4,3,2,1,0:T(8,128)(2,1)S(1)} %pad_maximum_fusion.refs_4_.refs_5_), channel_id=1, source_target_pairs={{0,4},{8,12},{4,0},{12,8},{1,5},{9,13},{5,1},{13,9},{2,6},{10,14},... | collective-permute-start | bytes 7077896 | tf_op jit(solution)/shard_map/ppermute | solution.py:509
  43.7 23.1 %collective-permute-start.6 = (bf16[2,9,128,128]{3,2,1,0:T(8,128)(2,1)S(1)}, bf16[2,9,128,128]{3,2,1,0:T(8,128)(2,1)S(1)}, u32[]{:S(2)}, u32[]{:S(2)}) collective-permute-start(bf16[2,9,128,128]{3,2,1,0:T(8,128)(2,1)S(1)} %pick.2), channel_id=1, source_target_pairs={{0,1},{3,2},{4,5},{7,6},{8,9},{11,10},{12,13},{15,14},{16,17},{19,... | collective-permute-start | bytes 1769480 | tf_op jit(solution)/shard_map/ppermute | solution.py:509
  49.2 1.7 %collective-permute-start.4 = (bf16[1,2,9,128,128]{4,3,2,1,0:T(8,128)(2,1)S(1)}, bf16[1,2,9,128,128]{4,3,2,1,0:T(8,128)(2,1)S(1)}, u32[]{:S(2)}, u32[]{:S(2)}) collective-permute-start(bf16[1,2,9,128,128]{4,3,2,1,0:T(8,128)(2,1)S(1)} %get-tuple-element.39), channel_id=1, source_target_pairs={{1,2},{2,1},{5,6},{6,5},{9,10},{10,9},{13,14},{14,13},{17,18},{18,... | collective-permute-start | bytes 1769480 | tf_op jit(solution)/shard_map/ppermute | solution.py:509
  50.1 18.0 %collective-permute-start.8 = (bf16[1,2,9,128,128]{4,3,2,1,0:T(8,128)(2,1)S(1)}, bf16[1,2,9,128,128]{4,3,2,1,0:T(8,128)(2,1)S(1)}, u32[]{:S(2)}, u32[]{:S(2)}) collective-permute-start(bf16[1,2,9,128,128]{4,3,2,1,0:T(8,128)(2,1)S(1)} %get-tuple-element.42), channel_id=1, source_target_pairs={{1,2},{2,1},{5,6},{6,5},{9,10},{10,9},{13,14},{14,13},{17,18},{18,... | collective-permute-start | bytes 1769480 | tf_op jit(solution)/shard_map/ppermute | solution.py:509
  50.9 46.1 %collective-permute-start.2 = (bf16[27,128,128]{2,1,0:T(8,128)(2,1)S(1)}, bf16[27,128,128]{2,1,0:T(8,128)(2,1)S(1)}, u32[]{:S(2)}, u32[]{:S(2)}) collective-permute-start(bf16[27,128,128]{2,1,0:T(8,128)(2,1)S(1)} %pad_maximum_fusion.3), channel_id=1, source_target_pairs={{0,1},{2,3},{1,0},{3,2},{4,5},{6,7},{5,4},{7,6},{8,9},{10,11},{9,8... | collective-permute-start | bytes 2654216 | tf_op jit(solution)/shard_map/ppermute | solution.py:509
  66.8 42.5 %collective-permute-start.5 = (bf16[2,2,9,128,128]{4,3,2,1,0:T(8,128)(2,1)S(1)}, bf16[2,2,9,128,128]{4,3,2,1,0:T(8,128)(2,1)S(1)}, u32[]{:S(2)}, u32[]{:S(2)}) collective-permute-start(bf16[2,2,9,128,128]{4,3,2,1,0:T(8,128)(2,1)S(1)} %slice_bitcast_fusion), channel_id=1, source_target_pairs={{1,2},{2,1},{5,6},{6,5},{9,10},{10,9},{13,14},{14,13},{17,18},{18,... | collective-permute-start | bytes 3538952 | tf_op jit(solution)/shard_map/ppermute | solution.py:509
  68.1 3.2 %copy-start = (s32[1,1,1,9]{3,2,1,0:T(1,128)S(1)}, s32[1,1,1,9]{3,2,1,0:T(1,128)}, u32[]{:S(2)}) copy-start(s32[1,1,1,9]{3,2,1,0:T(1,128)} %param.9) | copy-start | bytes 112
  68.1 3.2 %copy-start.1 = (s32[18]{0:T(128)S(1)}, s32[18]{0:T(128)}, u32[]{:S(2)}) copy-start(s32[18]{0:T(128)} %reach.7) | copy-start | bytes 220
  68.2 26.2 %collective-permute-start.11 = (bf16[144,1152]{1,0:T(8,128)(2,1)S(1)}, bf16[144,1152]{1,0:T(8,128)(2,1)S(1)}, u32[]{:S(2)}, u32[]{:S(2)}) collective-permute-start(bf16[144,1152]{1,0:T(8,128)(2,1)S(1)} %edge_rows.4), channel_id=1, source_target_pairs={{1,0},{2,3},{5,4},{6,7},{9,8},{10,11},{13,12},{14,15},{17,16},{18,... | collective-permute-start | bytes 995336 | tf_op jit(solution)/shard_map/ppermute | solution.py:509
  70.1 33.2 %collective-permute-start.17 = (bf16[144,1152]{1,0:T(8,128)(2,1)S(1)}, bf16[144,1152]{1,0:T(8,128)(2,1)S(1)}, u32[]{:S(2)}, u32[]{:S(2)}) collective-permute-start(bf16[144,1152]{1,0:T(8,128)(2,1)S(1)} %edge_rows.5), channel_id=1, source_target_pairs={{1,0},{2,3},{5,4},{6,7},{9,8},{10,11},{13,12},{14,15},{17,16},{18,... | collective-permute-start | bytes 995336 | tf_op jit(solution)/shard_map/ppermute | solution.py:509
  95.4 9.5 %collective-permute-start.14 = (bf16[128,1152]{1,0:T(8,128)(2,1)S(1)}, bf16[128,1152]{1,0:T(8,128)(2,1)S(1)}, u32[]{:S(2)}, u32[]{:S(2)}) collective-permute-start(bf16[128,1152]{1,0:T(8,128)(2,1)S(1)} %merge.2), channel_id=1, source_target_pairs={{0,16},{16,0},{1,17},{17,1},{2,18},{18,2},{3,19},{19,3},{4,20},{20... | collective-permute-start | bytes 884744 | tf_op jit(solution)/shard_map/ppermute | solution.py:509
  97.1 7.9 %slice-start = ((s8[14155776]{0:T(1024)(128)(4,1)}), s8[4194304]{0:T(1024)(128)(4,1)S(1)}, s32[]{:S(2)}) async-start(s8[14155776]{0:T(1024)(128)(4,1)} %bitcast.27), calls=%async_computation | async-start | bytes 8388608
  97.1 7.8 %slice-start.1 = ((s8[14155776]{0:T(1024)(128)(4,1)}), s8[4194304]{0:T(1024)(128)(4,1)S(1)}, s32[]{:S(2)}) async-start(s8[14155776]{0:T(1024)(128)(4,1)} %bitcast.27), calls=%async_computation.1 | async-start | bytes 8388608
  97.1 7.8 %slice-start.2 = ((s8[14155776]{0:T(1024)(128)(4,1)}), s8[4194304]{0:T(1024)(128)(4,1)S(1)}, s32[]{:S(2)}) async-start(s8[14155776]{0:T(1024)(128)(4,1)} %bitcast.27), calls=%async_computation.2 | async-start | bytes 8388608
  97.2 7.8 %slice-start.3 = ((s8[14155776]{0:T(1024)(128)(4,1)}), s8[1572864]{0:T(1024)(128)(4,1)S(1)}, s32[]{:S(2)}) async-start(s8[14155776]{0:T(1024)(128)(4,1)} %bitcast.27), calls=%async_computation.3 | async-start | bytes 3145728
  97.2 20.7 %collective-permute-start.16 = (bf16[27,128,128]{2,1,0:T(8,128)(2,1)S(1)}, bf16[27,128,128]{2,1,0:T(8,128)(2,1)S(1)}, u32[]{:S(2)}, u32[]{:S(2)}) collective-permute-start(bf16[27,128,128]{2,1,0:T(8,128)(2,1)S(1)} %pad_maximum_fusion.4), channel_id=1, source_target_pairs={{0,1},{2,3},{1,0},{3,2},{4,5},{6,7},{5,4},{7,6},{8,9},{10,11},{9,8... | collective-permute-start | bytes 2654216 | tf_op jit(solution)/shard_map/ppermute | solution.py:509
  104.3 13.6 %collective-permute-start.22 = (bf16[128,1152]{1,0:T(8,128)(2,1)S(1)}, bf16[128,1152]{1,0:T(8,128)(2,1)S(1)}, u32[]{:S(2)}, u32[]{:S(2)}) collective-permute-start(bf16[128,1152]{1,0:T(8,128)(2,1)S(1)} %merge.3), channel_id=1, source_target_pairs={{0,16},{16,0},{1,17},{17,1},{2,18},{18,2},{3,19},{19,3},{4,20},{20... | collective-permute-start | bytes 884744 | tf_op jit(solution)/shard_map/ppermute | solution.py:509
  107.1 18.3 %collective-permute-start.25 = (bf16[128,3072]{1,0:T(8,128)(2,1)S(1)}, bf16[128,3072]{1,0:T(8,128)(2,1)S(1)}, u32[]{:S(2)}, u32[]{:S(2)}) collective-permute-start(bf16[128,3072]{1,0:T(8,128)(2,1)S(1)} %product.2), channel_id=1, source_target_pairs={{0,16},{16,0},{1,17},{17,1},{2,18},{18,2},{3,19},{19,3},{4,20},{20... | collective-permute-start | bytes 2359304 | tf_op jit(solution)/shard_map/ppermute | solution.py:509
  108.7 10.1 %collective-permute-start.15 = (bf16[1,2,9,128,128]{4,3,2,1,0:T(8,128)(2,1)S(1)}, bf16[1,2,9,128,128]{4,3,2,1,0:T(8,128)(2,1)S(1)}, u32[]{:S(2)}, u32[]{:S(2)}) collective-permute-start(bf16[1,2,9,128,128]{4,3,2,1,0:T(8,128)(2,1)S(1)} %bitcast.51), channel_id=1, source_target_pairs={{1,2},{2,1},{5,6},{6,5},{9,10},{10,9},{13,14},{14,13},{17,18},{18,... | collective-permute-start | bytes 1769480 | tf_op jit(solution)/shard_map/ppermute | solution.py:509
  109.6 21.0 %collective-permute-start.13 = (bf16[2,1,2,9,128,128]{5,4,3,2,1,0:T(8,128)(2,1)S(1)}, bf16[2,1,2,9,128,128]{5,4,3,2,1,0:T(8,128)(2,1)S(1)}, u32[]{:S(2)}, u32[]{:S(2)}) collective-permute-start(bf16[2,1,2,9,128,128]{5,4,3,2,1,0:T(8,128)(2,1)S(1)} %pad_maximum_fusion.1.refs_4_.refs_5_), channel_id=1, source_target_pairs={{4,8},{8,4},{5,9},{9,5},{6,10},{10,6},{7,11},{11,7},{20,24},{24,20... | collective-permute-start | bytes 3538952 | tf_op jit(solution)/shard_map/ppermute | solution.py:509
  117.9 14.5 %collective-permute-start.12 = (bf16[2,1,2,9,128,128]{5,4,3,2,1,0:T(8,128)(2,1)S(1)}, bf16[2,1,2,9,128,128]{5,4,3,2,1,0:T(8,128)(2,1)S(1)}, u32[]{:S(2)}, u32[]{:S(2)}) collective-permute-start(bf16[2,1,2,9,128,128]{5,4,3,2,1,0:T(8,128)(2,1)S(1)} %pad_maximum_fusion.1.refs_4_.refs_5_), channel_id=1, source_target_pairs={{0,4},{8,12},{4,0},{12,8},{1,5},{9,13},{5,1},{13,9},{2,6},{10,14},... | collective-permute-start | bytes 3538952 | tf_op jit(solution)/shard_map/ppermute | solution.py:509
  118.0 11.0 %collective-permute-start.20 = (bf16[1,2,9,128,128]{4,3,2,1,0:T(8,128)(2,1)S(1)}, bf16[1,2,9,128,128]{4,3,2,1,0:T(8,128)(2,1)S(1)}, u32[]{:S(2)}, u32[]{:S(2)}) collective-permute-start(bf16[1,2,9,128,128]{4,3,2,1,0:T(8,128)(2,1)S(1)} %bitcast.53), channel_id=1, source_target_pairs={{1,2},{2,1},{5,6},{6,5},{9,10},{10,9},{13,14},{14,13},{17,18},{18,... | collective-permute-start | bytes 1769480 | tf_op jit(solution)/shard_map/ppermute | solution.py:509
  118.8 31.7 %collective-permute-start.18 = (bf16[2,1,2,9,128,128]{5,4,3,2,1,0:T(8,128)(2,1)S(1)}, bf16[2,1,2,9,128,128]{5,4,3,2,1,0:T(8,128)(2,1)S(1)}, u32[]{:S(2)}, u32[]{:S(2)}) collective-permute-start(bf16[2,1,2,9,128,128]{5,4,3,2,1,0:T(8,128)(2,1)S(1)} %pad_maximum_fusion.2.refs_4_.refs_5_), channel_id=1, source_target_pairs={{0,4},{8,12},{4,0},{12,8},{1,5},{9,13},{5,1},{13,9},{2,6},{10,14},... | collective-permute-start | bytes 3538952 | tf_op jit(solution)/shard_map/ppermute | solution.py:509
  125.4 25.2 %collective-permute-start.19 = (bf16[2,1,2,9,128,128]{5,4,3,2,1,0:T(8,128)(2,1)S(1)}, bf16[2,1,2,9,128,128]{5,4,3,2,1,0:T(8,128)(2,1)S(1)}, u32[]{:S(2)}, u32[]{:S(2)}) collective-permute-start(bf16[2,1,2,9,128,128]{5,4,3,2,1,0:T(8,128)(2,1)S(1)} %pad_maximum_fusion.2.refs_4_.refs_5_), channel_id=1, source_target_pairs={{4,8},{8,4},{5,9},{9,5},{6,10},{10,6},{7,11},{11,7},{20,24},{24,20... | collective-permute-start | bytes 3538952 | tf_op jit(solution)/shard_map/ppermute | solution.py:509
  129.0 26.9 %collective-permute-start.23 = (bf16[128,3072]{1,0:T(8,128)(2,1)S(1)}, bf16[128,3072]{1,0:T(8,128)(2,1)S(1)}, u32[]{:S(2)}, u32[]{:S(2)}) collective-permute-start(bf16[128,3072]{1,0:T(8,128)(2,1)S(1)} %product.3), channel_id=1, source_target_pairs={{0,16},{16,0},{1,17},{17,1},{2,18},{18,2},{3,19},{19,3},{4,20},{20... | collective-permute-start | bytes 2359304 | tf_op jit(solution)/shard_map/ppermute | solution.py:509
  130.6 16.0 %collective-permute-start.24 = (bf16[144,1152]{1,0:T(8,128)(2,1)S(1)}, bf16[144,1152]{1,0:T(8,128)(2,1)S(1)}, u32[]{:S(2)}, u32[]{:S(2)}) collective-permute-start(bf16[144,1152]{1,0:T(8,128)(2,1)S(1)} %edge_rows.6), channel_id=1, source_target_pairs={{1,0},{2,3},{5,4},{6,7},{9,8},{10,11},{13,12},{14,15},{17,16},{18,... | collective-permute-start | bytes 995336 | tf_op jit(solution)/shard_map/ppermute | solution.py:509
  132.4 23.4 %collective-permute-start.21 = (bf16[144,1152]{1,0:T(8,128)(2,1)S(1)}, bf16[144,1152]{1,0:T(8,128)(2,1)S(1)}, u32[]{:S(2)}, u32[]{:S(2)}) collective-permute-start(bf16[144,1152]{1,0:T(8,128)(2,1)S(1)} %edge_rows.7), channel_id=1, source_target_pairs={{1,0},{2,3},{5,4},{6,7},{9,8},{10,11},{13,12},{14,15},{17,16},{18,... | collective-permute-start | bytes 995336 | tf_op jit(solution)/shard_map/ppermute | solution.py:509

commit v11 on v9

--- a/solution.py
+++ b/solution.py
@@ -485,9 +485,6 @@
     return pairs + [(j, i) for i, j in pairs]
 
 
-STYLES = ((dict(split=True), dict(block=1)), (dict(ones=True), dict(split=True, ones=True)))
-
-
 def per_device(queries, key_states, value_states, tile_mask, frame_reach, out_weight):
     S, F, R, C, width = queries.shape
     tokens = F * R * C
@@ -532,7 +529,7 @@
         sides = [sent[f"pair_sides{part}"], sent[f"sides{part}"], sent[f"next_sides{part}"]]
         sent[f"rows{h}{s}"] = rows_attend(
             place, tied(mask, after), frame_reach, q, tiles, sides, sent[f"far{h}{s}"], h, s, C, R * C, (rows, cols),
-            **STYLES[h][s],
+            ones=True,
         )
 
     send("near0", own0[0], "col", col_pairs)
@@ -543,8 +540,8 @@
     send("far00", sent["near0"][:1], "col", col_others, "other0", "pair_own")
     send("far01", sent["near0"][1:], "col", col_others, "near0", "next_own")
     sent["sides0"] = jnp.stack([sent["near0"], sent["other0"]])
+    send("next_sides0", sent["sides0"], "row", row_others)
     send("pair_sides0", sent["sides0"], "row", row_pairs)
-    send("next_sides0", sent["sides0"], "row", row_others)
     send("near10", onward[0], "col", col_pairs, "other0")
     edge(0, 0)
     send("rest00", sent["part00"], "col", outward)

time: 157 us -> 153 us (0.975)
  Pallas kernels: 51.1 us -> 47.2 us
  starting transfers between devices: 32.7 us -> 34.6 us
    pallas_call x4, Pallas kernels: 26 us -> 22.1 us  [rows_attend(): kernel_call(kernel, out_shape=(jax.ShapeDtypeStruct((tokens, width), jnp....]
    ppermute x26, starting transfers between devices: 32.7 us -> 34.6 us  [send(): sent[name] = lax.ppermute(tied(value, after), axis, pairs)]
  transfers between devices with their start and end apart: 26 -> 26, of which waited for: 7 -> 6; matrix products, arithmetic and copies ran while one was open for 1% -> 1% of each run, Pallas kernels for 29% -> 27%
where the time goes in v11:
time: 153 us
  waiting for transfers between devices  69.1 us (45%)
  Pallas kernels  47.2 us (31%)
  starting transfers between devices  34.6 us (23%)
    ppermute x26, waiting for transfers between devices, send(): sent[name] = lax.ppermute(tied(value, after), axis, pairs)  69.1 us
    ppermute x26, starting transfers between devices, send(): sent[name] = lax.ppermute(tied(value, after), axis, pairs)  34.6 us
    pallas_call x4, Pallas kernels, rows_attend(): kernel_call(kernel, out_shape=(jax.ShapeDtypeStruct((tokens, width), jnp....  22.1 us
    pallas_call x2, Pallas kernels, project(): kernel_call(functools.partial(project_kernel, cols=cols), out_shape=jax.S...  7.92 us
    pallas_call x2, Pallas kernels, pack(): kernel_call(kernel, out_shape=jax.ShapeDtypeStruct((1 + len(given), S, 2,...  5.08 us
    pallas_call x2, Pallas kernels, product(): kernel_call(product_kernel, out_shape=jax.ShapeDtypeStruct((tokens, model...  4.23 us
    pallas_call x2, Pallas kernels, pick(): kernel_call(kernel, out_shape=jax.ShapeDtypeStruct((S, tokens, width), va...  3.29 us
  transfers between devices with their start and end apart: 26, of which 6 were waited for; matrix products, arithmetic and copies ran while one was open for 1% of the time, Pallas kernels for 27%

profile of v11, /device:TPU:0, one launch (start us, length us, event | category | flops | bytes accessed | tf_op | source)
XLA Modules:
  0.0 152.7 jit_solution(6285108055599139804)
XLA Ops:
  0.1 2.0 %pack.2.refs_0_ = bf16[1,2,2,128,1152]{4,3,2,1,0:T(8,128)(2,1)S(1)} custom-call(s32[3]{0:T(128)S(1)} %pad_add_fusion.place, bf16[2,128,2304]{2,1,0:T(8,128)(2,1)} %bitcast.43, bf16[2,128,2304]{2,1,0:T(8,128)(2,1)} %bitcast.45), custom_call_target="tpu_custom_call" | custom-call | bytes 2359296 | tf_op jit(solution)/shard_map/pack/pallas_call | solution.py:276
  2.8 5.8 %collective-permute-start.3 = (bf16[2,2,128,1152]{3,2,1,0:T(8,128)(2,1)S(1)}, bf16[2,2,128,1152]{3,2,1,0:T(8,128)(2,1)S(1)}, u32[]{:S(2)}, u32[]{:S(2)}) collective-permute-start(bf16[2,2,128,1152]{3,2,1,0:T(8,128)(2,1)S(1)} %bitcast.29), channel_id=1, source_target_pairs={{0,1},{2,3},{1,0},{3,2},{4,5},{6,7},{5,4},{7,6},{8,9},{10,11},{9,8... | collective-permute-start | bytes 3538952 | tf_op jit(solution)/shard_map/ppermute | solution.py:506
  8.6 1.6 %pick.2 = bf16[2,128,1152]{2,1,0:T(8,128)(2,1)S(1)} custom-call(s32[3]{0:T(128)S(1)} %pad_add_fusion.place, bf16[2,128,2304]{2,1,0:T(8,128)(2,1)} %bitcast.36), custom_call_target="tpu_custom_call" | custom-call | bytes 4718592 | tf_op jit(solution)/shard_map/pick/pallas_call | solution.py:300
  10.3 3.1 %pack.3.refs_3_ = bf16[2,2,2,128,1152]{4,3,2,1,0:T(8,128)(2,1)S(1)} custom-call(s32[3]{0:T(128)S(1)} %pad_add_fusion.place, bf16[2,128,2304]{2,1,0:T(8,128)(2,1)} %bitcast.44, bf16[2,128,2304]{2,1,0:T(8,128)(2,1)} %bitcast.46, bf16[1,2,2,128,1152]{4,3,2,1,0:T(8,128)(2,1)S(1)} %pack.2.refs_0_), custom_call_target="tpu_custom_call" | custom-call | bytes 2359296 | tf_op jit(solution)/shard_map/pack/pallas_call | solution.py:276
  13.5 0.8 collective-permute-start.7
  14.3 2.0 %collective-permute-start.6 = (bf16[256,1152]{1,0:T(8,128)(2,1)S(1)}, bf16[256,1152]{1,0:T(8,128)(2,1)S(1)}, u32[]{:S(2)}, u32[]{:S(2)}) collective-permute-start(bf16[256,1152]{1,0:T(8,128)(2,1)S(1)} %bitcast.31), channel_id=1, source_target_pairs={{0,1},{3,2},{4,5},{7,6},{8,9},{11,10},{12,13},{15,14},{16,17},{19,... | collective-permute-start | bytes 1769480 | tf_op jit(solution)/shard_map/ppermute | solution.py:506
  16.3 18.8 %collective-permute-done.3 = bf16[2,2,128,1152]{3,2,1,0:T(8,128)(2,1)S(1)} collective-permute-done((bf16[2,2,128,1152]{3,2,1,0:T(8,128)(2,1)S(1)}, bf16[2,2,128,1152]{3,2,1,0:T(8,128)(2,1)S(1)}, u32[]{:S(2)}, u32[]{:S(2)}) %collective-permute-start.3) | collective-permute-done | bytes 1179680 | tf_op jit(solution)/shard_map/ppermute | solution.py:506
  35.3 0.8 collective-permute-start.10
  36.1 2.8 %collective-permute-start.9 = (bf16[2,2,2,128,1152]{4,3,2,1,0:T(8,128)(2,1)S(1)}, bf16[2,2,2,128,1152]{4,3,2,1,0:T(8,128)(2,1)S(1)}, u32[]{:S(2)}, u32[]{:S(2)}) collective-permute-start(bf16[2,2,2,128,1152]{4,3,2,1,0:T(8,128)(2,1)S(1)} %pad_maximum_fusion.refs_4_.refs_5_), channel_id=1, source_target_pairs={{0,4},{8,12},{4,0},{12,8},{1,5},{9,13},{5,1},{13,9},{2,6},{10,14},... | collective-permute-start | bytes 7077896 | tf_op jit(solution)/shard_map/ppermute | solution.py:506
  39.0 1.6 %pick.3 = bf16[2,128,1152]{2,1,0:T(8,128)(2,1)S(1)} custom-call(s32[3]{0:T(128)S(1)} %pad_add_fusion.place, bf16[2,128,2304]{2,1,0:T(8,128)(2,1)} %bitcast.37), custom_call_target="tpu_custom_call" | custom-call | bytes 4718592 | tf_op jit(solution)/shard_map/pick/pallas_call | solution.py:300
  41.6 4.2 %collective-permute-start.2 = (bf16[384,1152]{1,0:T(8,128)(2,1)S(1)}, bf16[384,1152]{1,0:T(8,128)(2,1)S(1)}, u32[]{:S(2)}, u32[]{:S(2)}) collective-permute-start(bf16[384,1152]{1,0:T(8,128)(2,1)S(1)} %pad_maximum_fusion.3), channel_id=1, source_target_pairs={{0,1},{2,3},{1,0},{3,2},{4,5},{6,7},{5,4},{7,6},{8,9},{10,11},{9,8... | collective-permute-start | bytes 2654216 | tf_op jit(solution)/shard_map/ppermute | solution.py:506
  48.0 1.3 collective-permute-start.11
  49.9 1.3 collective-permute-start.17
  51.3 5.4 %rows.4 = (f32[128,1152]{1,0:T(8,128)S(1)}, bf16[128,1152]{1,0:T(8,128)(2,1)S(1)}, bf16[128,128]{1,0:T(8,128)(2,1)S(1)}) custom-call(s32[3]{0:T(128)S(1)} %pad_add_fusion.place, s32[9]{0:T(128)S(1)} %bitcast.32, s32[18]{0:T(128)S(1)} %copy-done.1, bf16[2,128,2304]{2,1,0:T(8,128)(2,1)} %bitcast.38, ...), custom_call_target="tpu_custom_call" | custom-call | flops 868220928 | bytes 7962624 | tf_op jit(solution)/shard_map/rows/pallas_call | solution.py:359
  56.7 31.1 %collective-permute-done.11.rest_ref.stats_ref = bf16[144,1152]{1,0:T(8,128)(2,1)S(1)} collective-permute-done((bf16[144,1152]{1,0:T(8,128)(2,1)S(1)}, bf16[144,1152]{1,0:T(8,128)(2,1)S(1)}, u32[]{:S(2)}, u32[]{:S(2)}) %collective-permute-start.11) | collective-permute-done | bytes 331808 | tf_op jit(solution)/shard_map/ppermute | solution.py:506
  87.7 1.1 merge.2
  88.8 2.4 %collective-permute-start.14 = (bf16[128,1152]{1,0:T(8,128)(2,1)S(1)}, bf16[128,1152]{1,0:T(8,128)(2,1)S(1)}, u32[]{:S(2)}, u32[]{:S(2)}) collective-permute-start(bf16[128,1152]{1,0:T(8,128)(2,1)S(1)} %merge.2), channel_id=1, source_target_pairs={{0,16},{16,0},{1,17},{17,1},{2,18},{18,2},{3,19},{19,3},{4,20},{20... | collective-permute-start | bytes 884744 | tf_op jit(solution)/shard_map/ppermute | solution.py:506
  91.4 6.0 %rows.5 = (f32[128,1152]{1,0:T(8,128)S(1)}, bf16[128,1152]{1,0:T(8,128)(2,1)S(1)}, bf16[128,128]{1,0:T(8,128)(2,1)S(1)}) custom-call(s32[3]{0:T(128)S(1)} %pad_add_fusion.place, s32[9]{0:T(128)S(1)} %bitcast.33, s32[18]{0:T(128)S(1)} %copy-done.1, bf16[2,128,2304]{2,1,0:T(8,128)(2,1)} %bitcast.39, ...), custom_call_target="tpu_custom_call" | custom-call | flops 868220928 | bytes 7962624 | tf_op jit(solution)/shard_map/rows/pallas_call | solution.py:359
  97.4 1.1 merge.3
  98.6 2.1 %product.2 = bf16[128,3072]{1,0:T(8,128)(2,1)S(1)} custom-call(bf16[128,1152]{1,0:T(8,128)(2,1)S(1)} %collective-permute-done.14.rows_ref, bf16[2,1152,3072]{2,1,0:T(8,128)(2,1)S(1)} %bitcast.27), custom_call_target="tpu_custom_call" | custom-call | flops 3623878656 | bytes 28311552 | tf_op jit(solution)/shard_map/product/pallas_call | solution.py:465
  100.7 2.1 %collective-permute-start.25 = (bf16[128,3072]{1,0:T(8,128)(2,1)S(1)}, bf16[128,3072]{1,0:T(8,128)(2,1)S(1)}, u32[]{:S(2)}, u32[]{:S(2)}) collective-permute-start(bf16[128,3072]{1,0:T(8,128)(2,1)S(1)} %product.2), channel_id=1, source_target_pairs={{0,16},{16,0},{1,17},{17,1},{2,18},{18,2},{3,19},{19,3},{4,20},{20... | collective-permute-start | bytes 2359304 | tf_op jit(solution)/shard_map/ppermute | solution.py:506
  104.4 5.8 %collective-permute-done.16.q_ref = bf16[384,1152]{1,0:T(8,128)(2,1)S(1)} collective-permute-done((bf16[384,1152]{1,0:T(8,128)(2,1)S(1)}, bf16[384,1152]{1,0:T(8,128)(2,1)S(1)}, u32[]{:S(2)}, u32[]{:S(2)}) %collective-permute-start.16) | collective-permute-done | bytes 884768 | tf_op jit(solution)/shard_map/ppermute | solution.py:506
  111.7 7.3 %collective-permute-done.25.other_ref = bf16[128,3072]{1,0:T(8,128)(2,1)S(1)} collective-permute-done((bf16[128,3072]{1,0:T(8,128)(2,1)S(1)}, bf16[128,3072]{1,0:T(8,128)(2,1)S(1)}, u32[]{:S(2)}, u32[]{:S(2)}) %collective-permute-start.25) | collective-permute-done | bytes 786464 | tf_op jit(solution)/shard_map/ppermute | solution.py:506
  120.5 2.1 %product.3 = bf16[128,3072]{1,0:T(8,128)(2,1)S(1)} custom-call(bf16[128,1152]{1,0:T(8,128)(2,1)S(1)} %collective-permute-done.22.rows_ref, bf16[2,1152,3072]{2,1,0:T(8,128)(2,1)S(1)} %bitcast.27), custom_call_target="tpu_custom_call" | custom-call | flops 3623878656 | bytes 28311552 | tf_op jit(solution)/shard_map/product/pallas_call | solution.py:465
  122.7 2.1 %collective-permute-start.23 = (bf16[128,3072]{1,0:T(8,128)(2,1)S(1)}, bf16[128,3072]{1,0:T(8,128)(2,1)S(1)}, u32[]{:S(2)}, u32[]{:S(2)}) collective-permute-start(bf16[128,3072]{1,0:T(8,128)(2,1)S(1)} %product.3), channel_id=1, source_target_pairs={{0,16},{16,0},{1,17},{17,1},{2,18},{18,2},{3,19},{19,3},{4,20},{20... | collective-permute-start | bytes 2359304 | tf_op jit(solution)/shard_map/ppermute | solution.py:506
  124.7 1.3 collective-permute-start.24
  126.6 1.3 collective-permute-start.21
  127.9 5.4 %rows.6 = (f32[128,1152]{1,0:T(8,128)S(1)}, bf16[128,1152]{1,0:T(8,128)(2,1)S(1)}, bf16[128,128]{1,0:T(8,128)(2,1)S(1)}) custom-call(s32[3]{0:T(128)S(1)} %pad_add_fusion.place, s32[9]{0:T(128)S(1)} %bitcast.34, s32[18]{0:T(128)S(1)} %copy-done.1, bf16[2,128,2304]{2,1,0:T(8,128)(2,1)} %bitcast.40, ...), custom_call_target="tpu_custom_call" | custom-call | flops 868220928 | bytes 7962624 | tf_op jit(solution)/shard_map/rows/pallas_call | solution.py:359
  133.3 6.0 %collective-permute-done.24.rest_ref.stats_ref = bf16[144,1152]{1,0:T(8,128)(2,1)S(1)} collective-permute-done((bf16[144,1152]{1,0:T(8,128)(2,1)S(1)}, bf16[144,1152]{1,0:T(8,128)(2,1)S(1)}, u32[]{:S(2)}, u32[]{:S(2)}) %collective-permute-start.24) | collective-permute-done | bytes 331808 | tf_op jit(solution)/shard_map/ppermute | solution.py:506
  139.3 4.0 %project.2.refs_0_ = bf16[2,128,3072]{2,1,0:T(8,128)(2,1)} custom-call(s32[3]{0:T(128)S(1)} %pad_add_fusion.place, f32[128,1152]{1,0:T(8,128)S(1)} %get-tuple-element.55.base_ref, bf16[128,1152]{1,0:T(8,128)(2,1)S(1)} %get-tuple-element.56.row_ref, bf16[128,128]{1,0:T(8,128)(2,1)S(1)} %get-tuple-element.57.sums_ref, ...), custom_call_target="tpu_custom_call" | custom-call | flops 905969664 | bytes 7077888 | tf_op jit(solution)/shard_map/project/pallas_call | solution.py:430
  143.3 5.4 %rows.7 = (f32[128,1152]{1,0:T(8,128)S(1)}, bf16[128,1152]{1,0:T(8,128)(2,1)S(1)}, bf16[128,128]{1,0:T(8,128)(2,1)S(1)}) custom-call(s32[3]{0:T(128)S(1)} %pad_add_fusion.place, s32[9]{0:T(128)S(1)} %bitcast.35, s32[18]{0:T(128)S(1)} %copy-done.1, bf16[2,128,2304]{2,1,0:T(8,128)(2,1)} %bitcast.41, ...), custom_call_target="tpu_custom_call" | custom-call | flops 868220928 | bytes 7962624 | tf_op jit(solution)/shard_map/rows/pallas_call | solution.py:359
  148.7 4.0 %project.3 = bf16[2,128,3072]{2,1,0:T(8,128)(2,1)} custom-call(s32[3]{0:T(128)S(1)} %pad_add_fusion.place, f32[128,1152]{1,0:T(8,128)S(1)} %get-tuple-element.62.base_ref, bf16[128,1152]{1,0:T(8,128)(2,1)S(1)} %get-tuple-element.63.row_ref, bf16[128,128]{1,0:T(8,128)(2,1)S(1)} %get-tuple-element.64.sums_ref, ...), custom_call_target="tpu_custom_call", output_to_operand_aliasing={{}: (8, {})} | custom-call | flops 905969664 | bytes 7077888 | tf_op jit(solution)/shard_map/project/pallas_call | solution.py:430
  (64 shorter events, 10.3 us)
Async XLA Ops:
  2.1 14.2 %collective-permute-start.1 = (bf16[2,2,128,1152]{3,2,1,0:T(8,128)(2,1)S(1)}, bf16[2,2,128,1152]{3,2,1,0:T(8,128)(2,1)S(1)}, u32[]{:S(2)}, u32[]{:S(2)}) collective-permute-start(bf16[2,2,128,1152]{3,2,1,0:T(8,128)(2,1)S(1)} %bitcast.28), channel_id=1, source_target_pairs={{1,2},{2,1},{5,6},{6,5},{9,10},{10,9},{13,14},{14,13},{17,18},{18,... | collective-permute-start | bytes 3538952 | tf_op jit(solution)/shard_map/ppermute | solution.py:506
  2.8 32.2 %collective-permute-start.3 = (bf16[2,2,128,1152]{3,2,1,0:T(8,128)(2,1)S(1)}, bf16[2,2,128,1152]{3,2,1,0:T(8,128)(2,1)S(1)}, u32[]{:S(2)}, u32[]{:S(2)}) collective-permute-start(bf16[2,2,128,1152]{3,2,1,0:T(8,128)(2,1)S(1)} %bitcast.29), channel_id=1, source_target_pairs={{0,1},{2,3},{1,0},{3,2},{4,5},{6,7},{5,4},{7,6},{8,9},{10,11},{9,8... | collective-permute-start | bytes 3538952 | tf_op jit(solution)/shard_map/ppermute | solution.py:506
  13.4 27.4 %collective-permute-start = (bf16[2,2,2,128,1152]{4,3,2,1,0:T(8,128)(2,1)S(1)}, bf16[2,2,2,128,1152]{4,3,2,1,0:T(8,128)(2,1)S(1)}, u32[]{:S(2)}, u32[]{:S(2)}) collective-permute-start(bf16[2,2,2,128,1152]{4,3,2,1,0:T(8,128)(2,1)S(1)} %pack.3.refs_3_), channel_id=1, source_target_pairs={{0,4},{8,12},{4,0},{12,8},{1,5},{9,13},{5,1},{13,9},{2,6},{10,14},... | collective-permute-start | bytes 7077896 | tf_op jit(solution)/shard_map/ppermute | solution.py:506
  13.5 28.1 %collective-permute-start.7 = (bf16[2,2,2,128,1152]{4,3,2,1,0:T(8,128)(2,1)S(1)}, bf16[2,2,2,128,1152]{4,3,2,1,0:T(8,128)(2,1)S(1)}, u32[]{:S(2)}, u32[]{:S(2)}) collective-permute-start(bf16[2,2,2,128,1152]{4,3,2,1,0:T(8,128)(2,1)S(1)} %pack.3.refs_3_), channel_id=1, source_target_pairs={{4,8},{8,4},{5,9},{9,5},{6,10},{10,6},{7,11},{11,7},{20,24},{24,20... | collective-permute-start | bytes 7077896 | tf_op jit(solution)/shard_map/ppermute | solution.py:506
  14.3 32.4 %collective-permute-start.6 = (bf16[256,1152]{1,0:T(8,128)(2,1)S(1)}, bf16[256,1152]{1,0:T(8,128)(2,1)S(1)}, u32[]{:S(2)}, u32[]{:S(2)}) collective-permute-start(bf16[256,1152]{1,0:T(8,128)(2,1)S(1)} %bitcast.31), channel_id=1, source_target_pairs={{0,1},{3,2},{4,5},{7,6},{8,9},{11,10},{12,13},{15,14},{16,17},{19,... | collective-permute-start | bytes 1769480 | tf_op jit(solution)/shard_map/ppermute | solution.py:506
  35.3 14.6 %collective-permute-start.10 = (bf16[2,2,2,128,1152]{4,3,2,1,0:T(8,128)(2,1)S(1)}, bf16[2,2,2,128,1152]{4,3,2,1,0:T(8,128)(2,1)S(1)}, u32[]{:S(2)}, u32[]{:S(2)}) collective-permute-start(bf16[2,2,2,128,1152]{4,3,2,1,0:T(8,128)(2,1)S(1)} %pad_maximum_fusion.refs_4_.refs_5_), channel_id=1, source_target_pairs={{4,8},{8,4},{5,9},{9,5},{6,10},{10,6},{7,11},{11,7},{20,24},{24,20... | collective-permute-start | bytes 7077896 | tf_op jit(solution)/shard_map/ppermute | solution.py:506
  36.1 15.1 %collective-permute-start.9 = (bf16[2,2,2,128,1152]{4,3,2,1,0:T(8,128)(2,1)S(1)}, bf16[2,2,2,128,1152]{4,3,2,1,0:T(8,128)(2,1)S(1)}, u32[]{:S(2)}, u32[]{:S(2)}) collective-permute-start(bf16[2,2,2,128,1152]{4,3,2,1,0:T(8,128)(2,1)S(1)} %pad_maximum_fusion.refs_4_.refs_5_), channel_id=1, source_target_pairs={{0,4},{8,12},{4,0},{12,8},{1,5},{9,13},{5,1},{13,9},{2,6},{10,14},... | collective-permute-start | bytes 7077896 | tf_op jit(solution)/shard_map/ppermute | solution.py:506
  40.8 5.1 %collective-permute-start.4 = (bf16[1,2,128,1152]{3,2,1,0:T(8,128)(2,1)S(1)}, bf16[1,2,128,1152]{3,2,1,0:T(8,128)(2,1)S(1)}, u32[]{:S(2)}, u32[]{:S(2)}) collective-permute-start(bf16[1,2,128,1152]{3,2,1,0:T(8,128)(2,1)S(1)} %get-tuple-element.39), channel_id=1, source_target_pairs={{1,2},{2,1},{5,6},{6,5},{9,10},{10,9},{13,14},{14,13},{17,18},{18,... | collective-permute-start | bytes 1769480 | tf_op jit(solution)/shard_map/ppermute | solution.py:506
  41.6 49.6 %collective-permute-start.2 = (bf16[384,1152]{1,0:T(8,128)(2,1)S(1)}, bf16[384,1152]{1,0:T(8,128)(2,1)S(1)}, u32[]{:S(2)}, u32[]{:S(2)}) collective-permute-start(bf16[384,1152]{1,0:T(8,128)(2,1)S(1)} %pad_maximum_fusion.3), channel_id=1, source_target_pairs={{0,1},{2,3},{1,0},{3,2},{4,5},{6,7},{5,4},{7,6},{8,9},{10,11},{9,8... | collective-permute-start | bytes 2654216 | tf_op jit(solution)/shard_map/ppermute | solution.py:506
  45.8 2.2 %collective-permute-start.8 = (bf16[1,2,128,1152]{3,2,1,0:T(8,128)(2,1)S(1)}, bf16[1,2,128,1152]{3,2,1,0:T(8,128)(2,1)S(1)}, u32[]{:S(2)}, u32[]{:S(2)}) collective-permute-start(bf16[1,2,128,1152]{3,2,1,0:T(8,128)(2,1)S(1)} %get-tuple-element.42), channel_id=1, source_target_pairs={{1,2},{2,1},{5,6},{6,5},{9,10},{10,9},{13,14},{14,13},{17,18},{18,... | collective-permute-start | bytes 1769480 | tf_op jit(solution)/shard_map/ppermute | solution.py:506
  46.7 56.8 %collective-permute-start.5 = (bf16[2,2,128,1152]{3,2,1,0:T(8,128)(2,1)S(1)}, bf16[2,2,128,1152]{3,2,1,0:T(8,128)(2,1)S(1)}, u32[]{:S(2)}, u32[]{:S(2)}) collective-permute-start(bf16[2,2,128,1152]{3,2,1,0:T(8,128)(2,1)S(1)} %slice_bitcast_fusion), channel_id=1, source_target_pairs={{1,2},{2,1},{5,6},{6,5},{9,10},{10,9},{13,14},{14,13},{17,18},{18,... | collective-permute-start | bytes 3538952 | tf_op jit(solution)/shard_map/ppermute | solution.py:506
  48.0 3.2 %copy-start = (s32[1,1,1,9]{3,2,1,0:T(1,128)S(1)}, s32[1,1,1,9]{3,2,1,0:T(1,128)}, u32[]{:S(2)}) copy-start(s32[1,1,1,9]{3,2,1,0:T(1,128)} %param.9) | copy-start | bytes 112
  48.0 3.2 %copy-start.1 = (s32[18]{0:T(128)S(1)}, s32[18]{0:T(128)}, u32[]{:S(2)}) copy-start(s32[18]{0:T(128)} %reach.7) | copy-start | bytes 220
  48.0 39.7 %collective-permute-start.11 = (bf16[144,1152]{1,0:T(8,128)(2,1)S(1)}, bf16[144,1152]{1,0:T(8,128)(2,1)S(1)}, u32[]{:S(2)}, u32[]{:S(2)}) collective-permute-start(bf16[144,1152]{1,0:T(8,128)(2,1)S(1)} %edge_rows.4), channel_id=1, source_target_pairs={{1,0},{2,3},{5,4},{6,7},{9,8},{10,11},{13,12},{14,15},{17,16},{18,... | collective-permute-start | bytes 995336 | tf_op jit(solution)/shard_map/ppermute | solution.py:506
  49.9 47.4 %collective-permute-start.17 = (bf16[144,1152]{1,0:T(8,128)(2,1)S(1)}, bf16[144,1152]{1,0:T(8,128)(2,1)S(1)}, u32[]{:S(2)}, u32[]{:S(2)}) collective-permute-start(bf16[144,1152]{1,0:T(8,128)(2,1)S(1)} %edge_rows.5), channel_id=1, source_target_pairs={{1,0},{2,3},{5,4},{6,7},{9,8},{10,11},{13,12},{14,15},{17,16},{18,... | collective-permute-start | bytes 995336 | tf_op jit(solution)/shard_map/ppermute | solution.py:506
  88.8 9.8 %collective-permute-start.14 = (bf16[128,1152]{1,0:T(8,128)(2,1)S(1)}, bf16[128,1152]{1,0:T(8,128)(2,1)S(1)}, u32[]{:S(2)}, u32[]{:S(2)}) collective-permute-start(bf16[128,1152]{1,0:T(8,128)(2,1)S(1)} %merge.2), channel_id=1, source_target_pairs={{0,16},{16,0},{1,17},{17,1},{2,18},{18,2},{3,19},{19,3},{4,20},{20... | collective-permute-start | bytes 884744 | tf_op jit(solution)/shard_map/ppermute | solution.py:506
  91.2 7.3 %slice-start = ((s8[14155776]{0:T(1024)(128)(4,1)}), s8[4194304]{0:T(1024)(128)(4,1)S(1)}, s32[]{:S(2)}) async-start(s8[14155776]{0:T(1024)(128)(4,1)} %bitcast.26), calls=%async_computation | async-start | bytes 8388608
  91.3 7.3 %slice-start.1 = ((s8[14155776]{0:T(1024)(128)(4,1)}), s8[4194304]{0:T(1024)(128)(4,1)S(1)}, s32[]{:S(2)}) async-start(s8[14155776]{0:T(1024)(128)(4,1)} %bitcast.26), calls=%async_computation.1 | async-start | bytes 8388608
  91.3 7.3 %slice-start.2 = ((s8[14155776]{0:T(1024)(128)(4,1)}), s8[4194304]{0:T(1024)(128)(4,1)S(1)}, s32[]{:S(2)}) async-start(s8[14155776]{0:T(1024)(128)(4,1)} %bitcast.26), calls=%async_computation.2 | async-start | bytes 8388608
  91.3 7.3 %slice-start.3 = ((s8[14155776]{0:T(1024)(128)(4,1)}), s8[1572864]{0:T(1024)(128)(4,1)S(1)}, s32[]{:S(2)}) async-start(s8[14155776]{0:T(1024)(128)(4,1)} %bitcast.26), calls=%async_computation.3 | async-start | bytes 3145728
  91.3 18.9 %collective-permute-start.16 = (bf16[384,1152]{1,0:T(8,128)(2,1)S(1)}, bf16[384,1152]{1,0:T(8,128)(2,1)S(1)}, u32[]{:S(2)}, u32[]{:S(2)}) collective-permute-start(bf16[384,1152]{1,0:T(8,128)(2,1)S(1)} %pad_maximum_fusion.4), channel_id=1, source_target_pairs={{0,1},{2,3},{1,0},{3,2},{4,5},{6,7},{5,4},{7,6},{8,9},{10,11},{9,8... | collective-permute-start | bytes 2654216 | tf_op jit(solution)/shard_map/ppermute | solution.py:506
  98.5 11.8 %collective-permute-start.22 = (bf16[128,1152]{1,0:T(8,128)(2,1)S(1)}, bf16[128,1152]{1,0:T(8,128)(2,1)S(1)}, u32[]{:S(2)}, u32[]{:S(2)}) collective-permute-start(bf16[128,1152]{1,0:T(8,128)(2,1)S(1)} %merge.3), channel_id=1, source_target_pairs={{0,16},{16,0},{1,17},{17,1},{2,18},{18,2},{3,19},{19,3},{4,20},{20... | collective-permute-start | bytes 884744 | tf_op jit(solution)/shard_map/ppermute | solution.py:506
  100.7 18.3 %collective-permute-start.25 = (bf16[128,3072]{1,0:T(8,128)(2,1)S(1)}, bf16[128,3072]{1,0:T(8,128)(2,1)S(1)}, u32[]{:S(2)}, u32[]{:S(2)}) collective-permute-start(bf16[128,3072]{1,0:T(8,128)(2,1)S(1)} %product.2), channel_id=1, source_target_pairs={{0,16},{16,0},{1,17},{17,1},{2,18},{18,2},{3,19},{19,3},{4,20},{20... | collective-permute-start | bytes 2359304 | tf_op jit(solution)/shard_map/ppermute | solution.py:506
  102.8 8.4 %collective-permute-start.15 = (bf16[1,2,128,1152]{3,2,1,0:T(8,128)(2,1)S(1)}, bf16[1,2,128,1152]{3,2,1,0:T(8,128)(2,1)S(1)}, u32[]{:S(2)}, u32[]{:S(2)}) collective-permute-start(bf16[1,2,128,1152]{3,2,1,0:T(8,128)(2,1)S(1)} %bitcast.49), channel_id=1, source_target_pairs={{1,2},{2,1},{5,6},{6,5},{9,10},{10,9},{13,14},{14,13},{17,18},{18,... | collective-permute-start | bytes 1769480 | tf_op jit(solution)/shard_map/ppermute | solution.py:506
  103.7 21.0 %collective-permute-start.13 = (bf16[2,1,2,128,1152]{4,3,2,1,0:T(8,128)(2,1)S(1)}, bf16[2,1,2,128,1152]{4,3,2,1,0:T(8,128)(2,1)S(1)}, u32[]{:S(2)}, u32[]{:S(2)}) collective-permute-start(bf16[2,1,2,128,1152]{4,3,2,1,0:T(8,128)(2,1)S(1)} %pad_maximum_fusion.1.refs_4_.refs_5_), channel_id=1, source_target_pairs={{4,8},{8,4},{5,9},{9,5},{6,10},{10,6},{7,11},{11,7},{20,24},{24,20... | collective-permute-start | bytes 3538952 | tf_op jit(solution)/shard_map/ppermute | solution.py:506
  110.2 16.4 %collective-permute-start.12 = (bf16[2,1,2,128,1152]{4,3,2,1,0:T(8,128)(2,1)S(1)}, bf16[2,1,2,128,1152]{4,3,2,1,0:T(8,128)(2,1)S(1)}, u32[]{:S(2)}, u32[]{:S(2)}) collective-permute-start(bf16[2,1,2,128,1152]{4,3,2,1,0:T(8,128)(2,1)S(1)} %pad_maximum_fusion.1.refs_4_.refs_5_), channel_id=1, source_target_pairs={{0,4},{8,12},{4,0},{12,8},{1,5},{9,13},{5,1},{13,9},{2,6},{10,14},... | collective-permute-start | bytes 3538952 | tf_op jit(solution)/shard_map/ppermute | solution.py:506
  110.3 12.4 %collective-permute-start.20 = (bf16[1,2,128,1152]{3,2,1,0:T(8,128)(2,1)S(1)}, bf16[1,2,128,1152]{3,2,1,0:T(8,128)(2,1)S(1)}, u32[]{:S(2)}, u32[]{:S(2)}) collective-permute-start(bf16[1,2,128,1152]{3,2,1,0:T(8,128)(2,1)S(1)} %bitcast.51), channel_id=1, source_target_pairs={{1,2},{2,1},{5,6},{6,5},{9,10},{10,9},{13,14},{14,13},{17,18},{18,... | collective-permute-start | bytes 1769480 | tf_op jit(solution)/shard_map/ppermute | solution.py:506
  111.1 32.2 %collective-permute-start.18 = (bf16[2,1,2,128,1152]{4,3,2,1,0:T(8,128)(2,1)S(1)}, bf16[2,1,2,128,1152]{4,3,2,1,0:T(8,128)(2,1)S(1)}, u32[]{:S(2)}, u32[]{:S(2)}) collective-permute-start(bf16[2,1,2,128,1152]{4,3,2,1,0:T(8,128)(2,1)S(1)} %pad_maximum_fusion.2.refs_4_.refs_5_), channel_id=1, source_target_pairs={{0,4},{8,12},{4,0},{12,8},{1,5},{9,13},{5,1},{13,9},{2,6},{10,14},... | collective-permute-start | bytes 3538952 | tf_op jit(solution)/shard_map/ppermute | solution.py:506
  119.0 24.3 %collective-permute-start.19 = (bf16[2,1,2,128,1152]{4,3,2,1,0:T(8,128)(2,1)S(1)}, bf16[2,1,2,128,1152]{4,3,2,1,0:T(8,128)(2,1)S(1)}, u32[]{:S(2)}, u32[]{:S(2)}) collective-permute-start(bf16[2,1,2,128,1152]{4,3,2,1,0:T(8,128)(2,1)S(1)} %pad_maximum_fusion.2.refs_4_.refs_5_), channel_id=1, source_target_pairs={{4,8},{8,4},{5,9},{9,5},{6,10},{10,6},{7,11},{11,7},{20,24},{24,20... | collective-permute-start | bytes 3538952 | tf_op jit(solution)/shard_map/ppermute | solution.py:506
  122.7 26.0 %collective-permute-start.23 = (bf16[128,3072]{1,0:T(8,128)(2,1)S(1)}, bf16[128,3072]{1,0:T(8,128)(2,1)S(1)}, u32[]{:S(2)}, u32[]{:S(2)}) collective-permute-start(bf16[128,3072]{1,0:T(8,128)(2,1)S(1)} %product.3), channel_id=1, source_target_pairs={{0,16},{16,0},{1,17},{17,1},{2,18},{18,2},{3,19},{19,3},{4,20},{20... | collective-permute-start | bytes 2359304 | tf_op jit(solution)/shard_map/ppermute | solution.py:506
  124.7 14.6 %collective-permute-start.24 = (bf16[144,1152]{1,0:T(8,128)(2,1)S(1)}, bf16[144,1152]{1,0:T(8,128)(2,1)S(1)}, u32[]{:S(2)}, u32[]{:S(2)}) collective-permute-start(bf16[144,1152]{1,0:T(8,128)(2,1)S(1)} %edge_rows.6), channel_id=1, source_target_pairs={{1,0},{2,3},{5,4},{6,7},{9,8},{10,11},{13,12},{14,15},{17,16},{18,... | collective-permute-start | bytes 995336 | tf_op jit(solution)/shard_map/ppermute | solution.py:506
  126.6 22.1 %collective-permute-start.21 = (bf16[144,1152]{1,0:T(8,128)(2,1)S(1)}, bf16[144,1152]{1,0:T(8,128)(2,1)S(1)}, u32[]{:S(2)}, u32[]{:S(2)}) collective-permute-start(bf16[144,1152]{1,0:T(8,128)(2,1)S(1)} %edge_rows.7), channel_id=1, source_target_pairs={{1,0},{2,3},{5,4},{6,7},{9,8},{10,11},{13,12},{14,15},{17,16},{18,... | collective-permute-start | bytes 995336 | tf_op jit(solution)/shard_map/ppermute | solution.py:506

commit v12 on v11

--- a/solution.py
+++ b/solution.py
@@ -529,7 +529,7 @@
         sides = [sent[f"pair_sides{part}"], sent[f"sides{part}"], sent[f"next_sides{part}"]]
         sent[f"rows{h}{s}"] = rows_attend(
             place, tied(mask, after), frame_reach, q, tiles, sides, sent[f"far{h}{s}"], h, s, C, R * C, (rows, cols),
-            ones=True,
+            ones=True, block=3 if h == 0 else 9,
         )
 
     send("near0", own0[0], "col", col_pairs)

time: 153 us -> 153 us (level)
  transfers between devices with their start and end apart: 26 -> 26, of which waited for: 6 -> 6; matrix products, arithmetic and copies ran while one was open for 1% -> 1% of each run, Pallas kernels for 27% -> 26%
where the time goes in v12:
time: 153 us; the launch traced here: 152 us
  waiting for transfers between devices  69.7 us (46%)
  Pallas kernels  45.9 us (30%)
  starting transfers between devices  34.6 us (23%)
    ppermute x26, waiting for transfers between devices, send(): sent[name] = lax.ppermute(tied(value, after), axis, pairs)  69.7 us
    ppermute x26, starting transfers between devices, send(): sent[name] = lax.ppermute(tied(value, after), axis, pairs)  34.6 us
    pallas_call x4, Pallas kernels, rows_attend(): kernel_call(kernel, out_shape=(jax.ShapeDtypeStruct((tokens, width), jnp....  20.8 us
    pallas_call x2, Pallas kernels, project(): kernel_call(functools.partial(project_kernel, cols=cols), out_shape=jax.S...  7.92 us
    pallas_call x2, Pallas kernels, pack(): kernel_call(kernel, out_shape=jax.ShapeDtypeStruct((1 + len(given), S, 2,...  5.08 us
    pallas_call x2, Pallas kernels, product(): kernel_call(product_kernel, out_shape=jax.ShapeDtypeStruct((tokens, model...  4.23 us
    pallas_call x2, Pallas kernels, pick(): kernel_call(kernel, out_shape=jax.ShapeDtypeStruct((S, tokens, width), va...  3.29 us
  transfers between devices with their start and end apart: 26, of which 6 were waited for; matrix products, arithmetic and copies ran while one was open for 1% of the time, Pallas kernels for 26%

profile of v12, /device:TPU:0, one launch (start us, length us, event | category | flops | bytes accessed | tf_op | source)
XLA Modules:
  0.0 152.0 jit_solution(7788401792308310384)
XLA Ops:
  0.1 2.0 %pack.2.refs_0_ = bf16[1,2,2,128,1152]{4,3,2,1,0:T(8,128)(2,1)S(1)} custom-call(s32[3]{0:T(128)S(1)} %pad_add_fusion.place, bf16[2,128,2304]{2,1,0:T(8,128)(2,1)} %bitcast.43, bf16[2,128,2304]{2,1,0:T(8,128)(2,1)} %bitcast.45), custom_call_target="tpu_custom_call" | custom-call | bytes 2359296 | tf_op jit(solution)/shard_map/pack/pallas_call | solution.py:276
  2.8 5.8 %collective-permute-start.3 = (bf16[2,2,128,1152]{3,2,1,0:T(8,128)(2,1)S(1)}, bf16[2,2,128,1152]{3,2,1,0:T(8,128)(2,1)S(1)}, u32[]{:S(2)}, u32[]{:S(2)}) collective-permute-start(bf16[2,2,128,1152]{3,2,1,0:T(8,128)(2,1)S(1)} %bitcast.29), channel_id=1, source_target_pairs={{0,1},{2,3},{1,0},{3,2},{4,5},{6,7},{5,4},{7,6},{8,9},{10,11},{9,8... | collective-permute-start | bytes 3538952 | tf_op jit(solution)/shard_map/ppermute | solution.py:506
  8.6 1.6 %pick.2 = bf16[2,128,1152]{2,1,0:T(8,128)(2,1)S(1)} custom-call(s32[3]{0:T(128)S(1)} %pad_add_fusion.place, bf16[2,128,2304]{2,1,0:T(8,128)(2,1)} %bitcast.36), custom_call_target="tpu_custom_call" | custom-call | bytes 4718592 | tf_op jit(solution)/shard_map/pick/pallas_call | solution.py:300
  10.3 3.1 %pack.3.refs_3_ = bf16[2,2,2,128,1152]{4,3,2,1,0:T(8,128)(2,1)S(1)} custom-call(s32[3]{0:T(128)S(1)} %pad_add_fusion.place, bf16[2,128,2304]{2,1,0:T(8,128)(2,1)} %bitcast.44, bf16[2,128,2304]{2,1,0:T(8,128)(2,1)} %bitcast.46, bf16[1,2,2,128,1152]{4,3,2,1,0:T(8,128)(2,1)S(1)} %pack.2.refs_0_), custom_call_target="tpu_custom_call" | custom-call | bytes 2359296 | tf_op jit(solution)/shard_map/pack/pallas_call | solution.py:276
  13.5 0.8 collective-permute-start.7
  14.3 2.0 %collective-permute-start.6 = (bf16[256,1152]{1,0:T(8,128)(2,1)S(1)}, bf16[256,1152]{1,0:T(8,128)(2,1)S(1)}, u32[]{:S(2)}, u32[]{:S(2)}) collective-permute-start(bf16[256,1152]{1,0:T(8,128)(2,1)S(1)} %bitcast.31), channel_id=1, source_target_pairs={{0,1},{3,2},{4,5},{7,6},{8,9},{11,10},{12,13},{15,14},{16,17},{19,... | collective-permute-start | bytes 1769480 | tf_op jit(solution)/shard_map/ppermute | solution.py:506
  16.3 18.8 %collective-permute-done.3 = bf16[2,2,128,1152]{3,2,1,0:T(8,128)(2,1)S(1)} collective-permute-done((bf16[2,2,128,1152]{3,2,1,0:T(8,128)(2,1)S(1)}, bf16[2,2,128,1152]{3,2,1,0:T(8,128)(2,1)S(1)}, u32[]{:S(2)}, u32[]{:S(2)}) %collective-permute-start.3) | collective-permute-done | bytes 1179680 | tf_op jit(solution)/shard_map/ppermute | solution.py:506
  35.3 0.8 collective-permute-start.10
  36.1 2.8 %collective-permute-start.9 = (bf16[2,2,2,128,1152]{4,3,2,1,0:T(8,128)(2,1)S(1)}, bf16[2,2,2,128,1152]{4,3,2,1,0:T(8,128)(2,1)S(1)}, u32[]{:S(2)}, u32[]{:S(2)}) collective-permute-start(bf16[2,2,2,128,1152]{4,3,2,1,0:T(8,128)(2,1)S(1)} %pad_maximum_fusion.refs_4_.refs_5_), channel_id=1, source_target_pairs={{0,4},{8,12},{4,0},{12,8},{1,5},{9,13},{5,1},{13,9},{2,6},{10,14},... | collective-permute-start | bytes 7077896 | tf_op jit(solution)/shard_map/ppermute | solution.py:506
  39.0 1.6 %pick.3 = bf16[2,128,1152]{2,1,0:T(8,128)(2,1)S(1)} custom-call(s32[3]{0:T(128)S(1)} %pad_add_fusion.place, bf16[2,128,2304]{2,1,0:T(8,128)(2,1)} %bitcast.37), custom_call_target="tpu_custom_call" | custom-call | bytes 4718592 | tf_op jit(solution)/shard_map/pick/pallas_call | solution.py:300
  41.6 4.2 %collective-permute-start.2 = (bf16[384,1152]{1,0:T(8,128)(2,1)S(1)}, bf16[384,1152]{1,0:T(8,128)(2,1)S(1)}, u32[]{:S(2)}, u32[]{:S(2)}) collective-permute-start(bf16[384,1152]{1,0:T(8,128)(2,1)S(1)} %pad_maximum_fusion.3), channel_id=1, source_target_pairs={{0,1},{2,3},{1,0},{3,2},{4,5},{6,7},{5,4},{7,6},{8,9},{10,11},{9,8... | collective-permute-start | bytes 2654216 | tf_op jit(solution)/shard_map/ppermute | solution.py:506
  48.0 1.3 collective-permute-start.11
  49.9 1.3 collective-permute-start.17
  51.3 5.4 %rows.4 = (f32[128,1152]{1,0:T(8,128)S(1)}, bf16[128,1152]{1,0:T(8,128)(2,1)S(1)}, bf16[128,128]{1,0:T(8,128)(2,1)S(1)}) custom-call(s32[3]{0:T(128)S(1)} %pad_add_fusion.place, s32[9]{0:T(128)S(1)} %bitcast.32, s32[18]{0:T(128)S(1)} %copy-done.1, bf16[2,128,2304]{2,1,0:T(8,128)(2,1)} %bitcast.38, ...), custom_call_target="tpu_custom_call" | custom-call | flops 868220928 | bytes 7962624 | tf_op jit(solution)/shard_map/rows/pallas_call | solution.py:359
  56.7 31.1 %collective-permute-done.11.rest_ref.stats_ref = bf16[144,1152]{1,0:T(8,128)(2,1)S(1)} collective-permute-done((bf16[144,1152]{1,0:T(8,128)(2,1)S(1)}, bf16[144,1152]{1,0:T(8,128)(2,1)S(1)}, u32[]{:S(2)}, u32[]{:S(2)}) %collective-permute-start.11) | collective-permute-done | bytes 331808 | tf_op jit(solution)/shard_map/ppermute | solution.py:506
  87.7 1.1 merge.2
  88.8 2.4 %collective-permute-start.14 = (bf16[128,1152]{1,0:T(8,128)(2,1)S(1)}, bf16[128,1152]{1,0:T(8,128)(2,1)S(1)}, u32[]{:S(2)}, u32[]{:S(2)}) collective-permute-start(bf16[128,1152]{1,0:T(8,128)(2,1)S(1)} %merge.2), channel_id=1, source_target_pairs={{0,16},{16,0},{1,17},{17,1},{2,18},{18,2},{3,19},{19,3},{4,20},{20... | collective-permute-start | bytes 884744 | tf_op jit(solution)/shard_map/ppermute | solution.py:506
  91.4 6.0 %rows.5 = (f32[128,1152]{1,0:T(8,128)S(1)}, bf16[128,1152]{1,0:T(8,128)(2,1)S(1)}, bf16[128,128]{1,0:T(8,128)(2,1)S(1)}) custom-call(s32[3]{0:T(128)S(1)} %pad_add_fusion.place, s32[9]{0:T(128)S(1)} %bitcast.33, s32[18]{0:T(128)S(1)} %copy-done.1, bf16[2,128,2304]{2,1,0:T(8,128)(2,1)} %bitcast.39, ...), custom_call_target="tpu_custom_call" | custom-call | flops 868220928 | bytes 7962624 | tf_op jit(solution)/shard_map/rows/pallas_call | solution.py:359
  97.4 1.1 merge.3
  98.6 2.1 %product.2 = bf16[128,3072]{1,0:T(8,128)(2,1)S(1)} custom-call(bf16[128,1152]{1,0:T(8,128)(2,1)S(1)} %collective-permute-done.14.rows_ref, bf16[2,1152,3072]{2,1,0:T(8,128)(2,1)S(1)} %bitcast.27), custom_call_target="tpu_custom_call" | custom-call | flops 3623878656 | bytes 28311552 | tf_op jit(solution)/shard_map/product/pallas_call | solution.py:465
  100.7 2.1 %collective-permute-start.25 = (bf16[128,3072]{1,0:T(8,128)(2,1)S(1)}, bf16[128,3072]{1,0:T(8,128)(2,1)S(1)}, u32[]{:S(2)}, u32[]{:S(2)}) collective-permute-start(bf16[128,3072]{1,0:T(8,128)(2,1)S(1)} %product.2), channel_id=1, source_target_pairs={{0,16},{16,0},{1,17},{17,1},{2,18},{18,2},{3,19},{19,3},{4,20},{20... | collective-permute-start | bytes 2359304 | tf_op jit(solution)/shard_map/ppermute | solution.py:506
  104.4 5.8 %collective-permute-done.16.q_ref = bf16[384,1152]{1,0:T(8,128)(2,1)S(1)} collective-permute-done((bf16[384,1152]{1,0:T(8,128)(2,1)S(1)}, bf16[384,1152]{1,0:T(8,128)(2,1)S(1)}, u32[]{:S(2)}, u32[]{:S(2)}) %collective-permute-start.16) | collective-permute-done | bytes 884768 | tf_op jit(solution)/shard_map/ppermute | solution.py:506
  111.7 7.3 %collective-permute-done.25.other_ref = bf16[128,3072]{1,0:T(8,128)(2,1)S(1)} collective-permute-done((bf16[128,3072]{1,0:T(8,128)(2,1)S(1)}, bf16[128,3072]{1,0:T(8,128)(2,1)S(1)}, u32[]{:S(2)}, u32[]{:S(2)}) %collective-permute-start.25) | collective-permute-done | bytes 786464 | tf_op jit(solution)/shard_map/ppermute | solution.py:506
  120.5 2.1 %product.3 = bf16[128,3072]{1,0:T(8,128)(2,1)S(1)} custom-call(bf16[128,1152]{1,0:T(8,128)(2,1)S(1)} %collective-permute-done.22.rows_ref, bf16[2,1152,3072]{2,1,0:T(8,128)(2,1)S(1)} %bitcast.27), custom_call_target="tpu_custom_call" | custom-call | flops 3623878656 | bytes 28311552 | tf_op jit(solution)/shard_map/product/pallas_call | solution.py:465
  122.7 2.1 %collective-permute-start.23 = (bf16[128,3072]{1,0:T(8,128)(2,1)S(1)}, bf16[128,3072]{1,0:T(8,128)(2,1)S(1)}, u32[]{:S(2)}, u32[]{:S(2)}) collective-permute-start(bf16[128,3072]{1,0:T(8,128)(2,1)S(1)} %product.3), channel_id=1, source_target_pairs={{0,16},{16,0},{1,17},{17,1},{2,18},{18,2},{3,19},{19,3},{4,20},{20... | collective-permute-start | bytes 2359304 | tf_op jit(solution)/shard_map/ppermute | solution.py:506
  124.7 1.3 collective-permute-start.24
  126.6 1.3 collective-permute-start.21
  127.9 4.7 %rows.6 = (f32[128,1152]{1,0:T(8,128)S(1)}, bf16[128,1152]{1,0:T(8,128)(2,1)S(1)}, bf16[128,128]{1,0:T(8,128)(2,1)S(1)}) custom-call(s32[3]{0:T(128)S(1)} %pad_add_fusion.place, s32[9]{0:T(128)S(1)} %bitcast.34, s32[18]{0:T(128)S(1)} %copy-done.1, bf16[2,128,2304]{2,1,0:T(8,128)(2,1)} %bitcast.40, ...), custom_call_target="tpu_custom_call" | custom-call | flops 868220928 | bytes 7962624 | tf_op jit(solution)/shard_map/rows/pallas_call | solution.py:359
  132.7 6.7 %collective-permute-done.24.rest_ref.stats_ref = bf16[144,1152]{1,0:T(8,128)(2,1)S(1)} collective-permute-done((bf16[144,1152]{1,0:T(8,128)(2,1)S(1)}, bf16[144,1152]{1,0:T(8,128)(2,1)S(1)}, u32[]{:S(2)}, u32[]{:S(2)}) %collective-permute-start.24) | collective-permute-done | bytes 331808 | tf_op jit(solution)/shard_map/ppermute | solution.py:506
  139.3 4.0 %project.2.refs_0_ = bf16[2,128,3072]{2,1,0:T(8,128)(2,1)} custom-call(s32[3]{0:T(128)S(1)} %pad_add_fusion.place, f32[128,1152]{1,0:T(8,128)S(1)} %get-tuple-element.55.base_ref, bf16[128,1152]{1,0:T(8,128)(2,1)S(1)} %get-tuple-element.56.row_ref, bf16[128,128]{1,0:T(8,128)(2,1)S(1)} %get-tuple-element.57.sums_ref, ...), custom_call_target="tpu_custom_call" | custom-call | flops 905969664 | bytes 7077888 | tf_op jit(solution)/shard_map/project/pallas_call | solution.py:430
  143.3 4.7 %rows.7 = (f32[128,1152]{1,0:T(8,128)S(1)}, bf16[128,1152]{1,0:T(8,128)(2,1)S(1)}, bf16[128,128]{1,0:T(8,128)(2,1)S(1)}) custom-call(s32[3]{0:T(128)S(1)} %pad_add_fusion.place, s32[9]{0:T(128)S(1)} %bitcast.35, s32[18]{0:T(128)S(1)} %copy-done.1, bf16[2,128,2304]{2,1,0:T(8,128)(2,1)} %bitcast.41, ...), custom_call_target="tpu_custom_call" | custom-call | flops 868220928 | bytes 7962624 | tf_op jit(solution)/shard_map/rows/pallas_call | solution.py:359
  148.1 4.0 %project.3 = bf16[2,128,3072]{2,1,0:T(8,128)(2,1)} custom-call(s32[3]{0:T(128)S(1)} %pad_add_fusion.place, f32[128,1152]{1,0:T(8,128)S(1)} %get-tuple-element.62.base_ref, bf16[128,1152]{1,0:T(8,128)(2,1)S(1)} %get-tuple-element.63.row_ref, bf16[128,128]{1,0:T(8,128)(2,1)S(1)} %get-tuple-element.64.sums_ref, ...), custom_call_target="tpu_custom_call", output_to_operand_aliasing={{}: (8, {})} | custom-call | flops 905969664 | bytes 7077888 | tf_op jit(solution)/shard_map/project/pallas_call | solution.py:430
  (64 shorter events, 10.3 us)
Async XLA Ops:
  2.1 14.2 %collective-permute-start.1 = (bf16[2,2,128,1152]{3,2,1,0:T(8,128)(2,1)S(1)}, bf16[2,2,128,1152]{3,2,1,0:T(8,128)(2,1)S(1)}, u32[]{:S(2)}, u32[]{:S(2)}) collective-permute-start(bf16[2,2,128,1152]{3,2,1,0:T(8,128)(2,1)S(1)} %bitcast.28), channel_id=1, source_target_pairs={{1,2},{2,1},{5,6},{6,5},{9,10},{10,9},{13,14},{14,13},{17,18},{18,... | collective-permute-start | bytes 3538952 | tf_op jit(solution)/shard_map/ppermute | solution.py:506
  2.8 32.2 %collective-permute-start.3 = (bf16[2,2,128,1152]{3,2,1,0:T(8,128)(2,1)S(1)}, bf16[2,2,128,1152]{3,2,1,0:T(8,128)(2,1)S(1)}, u32[]{:S(2)}, u32[]{:S(2)}) collective-permute-start(bf16[2,2,128,1152]{3,2,1,0:T(8,128)(2,1)S(1)} %bitcast.29), channel_id=1, source_target_pairs={{0,1},{2,3},{1,0},{3,2},{4,5},{6,7},{5,4},{7,6},{8,9},{10,11},{9,8... | collective-permute-start | bytes 3538952 | tf_op jit(solution)/shard_map/ppermute | solution.py:506
  13.4 27.4 %collective-permute-start = (bf16[2,2,2,128,1152]{4,3,2,1,0:T(8,128)(2,1)S(1)}, bf16[2,2,2,128,1152]{4,3,2,1,0:T(8,128)(2,1)S(1)}, u32[]{:S(2)}, u32[]{:S(2)}) collective-permute-start(bf16[2,2,2,128,1152]{4,3,2,1,0:T(8,128)(2,1)S(1)} %pack.3.refs_3_), channel_id=1, source_target_pairs={{0,4},{8,12},{4,0},{12,8},{1,5},{9,13},{5,1},{13,9},{2,6},{10,14},... | collective-permute-start | bytes 7077896 | tf_op jit(solution)/shard_map/ppermute | solution.py:506
  13.5 28.1 %collective-permute-start.7 = (bf16[2,2,2,128,1152]{4,3,2,1,0:T(8,128)(2,1)S(1)}, bf16[2,2,2,128,1152]{4,3,2,1,0:T(8,128)(2,1)S(1)}, u32[]{:S(2)}, u32[]{:S(2)}) collective-permute-start(bf16[2,2,2,128,1152]{4,3,2,1,0:T(8,128)(2,1)S(1)} %pack.3.refs_3_), channel_id=1, source_target_pairs={{4,8},{8,4},{5,9},{9,5},{6,10},{10,6},{7,11},{11,7},{20,24},{24,20... | collective-permute-start | bytes 7077896 | tf_op jit(solution)/shard_map/ppermute | solution.py:506
  14.3 32.4 %collective-permute-start.6 = (bf16[256,1152]{1,0:T(8,128)(2,1)S(1)}, bf16[256,1152]{1,0:T(8,128)(2,1)S(1)}, u32[]{:S(2)}, u32[]{:S(2)}) collective-permute-start(bf16[256,1152]{1,0:T(8,128)(2,1)S(1)} %bitcast.31), channel_id=1, source_target_pairs={{0,1},{3,2},{4,5},{7,6},{8,9},{11,10},{12,13},{15,14},{16,17},{19,... | collective-permute-start | bytes 1769480 | tf_op jit(solution)/shard_map/ppermute | solution.py:506
  35.3 14.6 %collective-permute-start.10 = (bf16[2,2,2,128,1152]{4,3,2,1,0:T(8,128)(2,1)S(1)}, bf16[2,2,2,128,1152]{4,3,2,1,0:T(8,128)(2,1)S(1)}, u32[]{:S(2)}, u32[]{:S(2)}) collective-permute-start(bf16[2,2,2,128,1152]{4,3,2,1,0:T(8,128)(2,1)S(1)} %pad_maximum_fusion.refs_4_.refs_5_), channel_id=1, source_target_pairs={{4,8},{8,4},{5,9},{9,5},{6,10},{10,6},{7,11},{11,7},{20,24},{24,20... | collective-permute-start | bytes 7077896 | tf_op jit(solution)/shard_map/ppermute | solution.py:506
  36.1 15.1 %collective-permute-start.9 = (bf16[2,2,2,128,1152]{4,3,2,1,0:T(8,128)(2,1)S(1)}, bf16[2,2,2,128,1152]{4,3,2,1,0:T(8,128)(2,1)S(1)}, u32[]{:S(2)}, u32[]{:S(2)}) collective-permute-start(bf16[2,2,2,128,1152]{4,3,2,1,0:T(8,128)(2,1)S(1)} %pad_maximum_fusion.refs_4_.refs_5_), channel_id=1, source_target_pairs={{0,4},{8,12},{4,0},{12,8},{1,5},{9,13},{5,1},{13,9},{2,6},{10,14},... | collective-permute-start | bytes 7077896 | tf_op jit(solution)/shard_map/ppermute | solution.py:506
  40.8 5.1 %collective-permute-start.4 = (bf16[1,2,128,1152]{3,2,1,0:T(8,128)(2,1)S(1)}, bf16[1,2,128,1152]{3,2,1,0:T(8,128)(2,1)S(1)}, u32[]{:S(2)}, u32[]{:S(2)}) collective-permute-start(bf16[1,2,128,1152]{3,2,1,0:T(8,128)(2,1)S(1)} %get-tuple-element.39), channel_id=1, source_target_pairs={{1,2},{2,1},{5,6},{6,5},{9,10},{10,9},{13,14},{14,13},{17,18},{18,... | collective-permute-start | bytes 1769480 | tf_op jit(solution)/shard_map/ppermute | solution.py:506
  41.6 49.6 %collective-permute-start.2 = (bf16[384,1152]{1,0:T(8,128)(2,1)S(1)}, bf16[384,1152]{1,0:T(8,128)(2,1)S(1)}, u32[]{:S(2)}, u32[]{:S(2)}) collective-permute-start(bf16[384,1152]{1,0:T(8,128)(2,1)S(1)} %pad_maximum_fusion.3), channel_id=1, source_target_pairs={{0,1},{2,3},{1,0},{3,2},{4,5},{6,7},{5,4},{7,6},{8,9},{10,11},{9,8... | collective-permute-start | bytes 2654216 | tf_op jit(solution)/shard_map/ppermute | solution.py:506
  45.8 2.2 %collective-permute-start.8 = (bf16[1,2,128,1152]{3,2,1,0:T(8,128)(2,1)S(1)}, bf16[1,2,128,1152]{3,2,1,0:T(8,128)(2,1)S(1)}, u32[]{:S(2)}, u32[]{:S(2)}) collective-permute-start(bf16[1,2,128,1152]{3,2,1,0:T(8,128)(2,1)S(1)} %get-tuple-element.42), channel_id=1, source_target_pairs={{1,2},{2,1},{5,6},{6,5},{9,10},{10,9},{13,14},{14,13},{17,18},{18,... | collective-permute-start | bytes 1769480 | tf_op jit(solution)/shard_map/ppermute | solution.py:506
  46.7 56.8 %collective-permute-start.5 = (bf16[2,2,128,1152]{3,2,1,0:T(8,128)(2,1)S(1)}, bf16[2,2,128,1152]{3,2,1,0:T(8,128)(2,1)S(1)}, u32[]{:S(2)}, u32[]{:S(2)}) collective-permute-start(bf16[2,2,128,1152]{3,2,1,0:T(8,128)(2,1)S(1)} %slice_bitcast_fusion), channel_id=1, source_target_pairs={{1,2},{2,1},{5,6},{6,5},{9,10},{10,9},{13,14},{14,13},{17,18},{18,... | collective-permute-start | bytes 3538952 | tf_op jit(solution)/shard_map/ppermute | solution.py:506
  48.0 3.2 %copy-start = (s32[1,1,1,9]{3,2,1,0:T(1,128)S(1)}, s32[1,1,1,9]{3,2,1,0:T(1,128)}, u32[]{:S(2)}) copy-start(s32[1,1,1,9]{3,2,1,0:T(1,128)} %param.9) | copy-start | bytes 112
  48.0 3.2 %copy-start.1 = (s32[18]{0:T(128)S(1)}, s32[18]{0:T(128)}, u32[]{:S(2)}) copy-start(s32[18]{0:T(128)} %reach.7) | copy-start | bytes 220
  48.0 39.7 %collective-permute-start.11 = (bf16[144,1152]{1,0:T(8,128)(2,1)S(1)}, bf16[144,1152]{1,0:T(8,128)(2,1)S(1)}, u32[]{:S(2)}, u32[]{:S(2)}) collective-permute-start(bf16[144,1152]{1,0:T(8,128)(2,1)S(1)} %edge_rows.4), channel_id=1, source_target_pairs={{1,0},{2,3},{5,4},{6,7},{9,8},{10,11},{13,12},{14,15},{17,16},{18,... | collective-permute-start | bytes 995336 | tf_op jit(solution)/shard_map/ppermute | solution.py:506
  49.9 47.4 %collective-permute-start.17 = (bf16[144,1152]{1,0:T(8,128)(2,1)S(1)}, bf16[144,1152]{1,0:T(8,128)(2,1)S(1)}, u32[]{:S(2)}, u32[]{:S(2)}) collective-permute-start(bf16[144,1152]{1,0:T(8,128)(2,1)S(1)} %edge_rows.5), channel_id=1, source_target_pairs={{1,0},{2,3},{5,4},{6,7},{9,8},{10,11},{13,12},{14,15},{17,16},{18,... | collective-permute-start | bytes 995336 | tf_op jit(solution)/shard_map/ppermute | solution.py:506
  88.8 9.8 %collective-permute-start.14 = (bf16[128,1152]{1,0:T(8,128)(2,1)S(1)}, bf16[128,1152]{1,0:T(8,128)(2,1)S(1)}, u32[]{:S(2)}, u32[]{:S(2)}) collective-permute-start(bf16[128,1152]{1,0:T(8,128)(2,1)S(1)} %merge.2), channel_id=1, source_target_pairs={{0,16},{16,0},{1,17},{17,1},{2,18},{18,2},{3,19},{19,3},{4,20},{20... | collective-permute-start | bytes 884744 | tf_op jit(solution)/shard_map/ppermute | solution.py:506
  91.2 7.3 %slice-start = ((s8[14155776]{0:T(1024)(128)(4,1)}), s8[4194304]{0:T(1024)(128)(4,1)S(1)}, s32[]{:S(2)}) async-start(s8[14155776]{0:T(1024)(128)(4,1)} %bitcast.26), calls=%async_computation | async-start | bytes 8388608
  91.3 7.3 %slice-start.1 = ((s8[14155776]{0:T(1024)(128)(4,1)}), s8[4194304]{0:T(1024)(128)(4,1)S(1)}, s32[]{:S(2)}) async-start(s8[14155776]{0:T(1024)(128)(4,1)} %bitcast.26), calls=%async_computation.1 | async-start | bytes 8388608
  91.3 7.3 %slice-start.2 = ((s8[14155776]{0:T(1024)(128)(4,1)}), s8[4194304]{0:T(1024)(128)(4,1)S(1)}, s32[]{:S(2)}) async-start(s8[14155776]{0:T(1024)(128)(4,1)} %bitcast.26), calls=%async_computation.2 | async-start | bytes 8388608
  91.3 7.3 %slice-start.3 = ((s8[14155776]{0:T(1024)(128)(4,1)}), s8[1572864]{0:T(1024)(128)(4,1)S(1)}, s32[]{:S(2)}) async-start(s8[14155776]{0:T(1024)(128)(4,1)} %bitcast.26), calls=%async_computation.3 | async-start | bytes 3145728
  91.3 18.9 %collective-permute-start.16 = (bf16[384,1152]{1,0:T(8,128)(2,1)S(1)}, bf16[384,1152]{1,0:T(8,128)(2,1)S(1)}, u32[]{:S(2)}, u32[]{:S(2)}) collective-permute-start(bf16[384,1152]{1,0:T(8,128)(2,1)S(1)} %pad_maximum_fusion.4), channel_id=1, source_target_pairs={{0,1},{2,3},{1,0},{3,2},{4,5},{6,7},{5,4},{7,6},{8,9},{10,11},{9,8... | collective-permute-start | bytes 2654216 | tf_op jit(solution)/shard_map/ppermute | solution.py:506
  98.5 11.8 %collective-permute-start.22 = (bf16[128,1152]{1,0:T(8,128)(2,1)S(1)}, bf16[128,1152]{1,0:T(8,128)(2,1)S(1)}, u32[]{:S(2)}, u32[]{:S(2)}) collective-permute-start(bf16[128,1152]{1,0:T(8,128)(2,1)S(1)} %merge.3), channel_id=1, source_target_pairs={{0,16},{16,0},{1,17},{17,1},{2,18},{18,2},{3,19},{19,3},{4,20},{20... | collective-permute-start | bytes 884744 | tf_op jit(solution)/shard_map/ppermute | solution.py:506
  100.7 18.3 %collective-permute-start.25 = (bf16[128,3072]{1,0:T(8,128)(2,1)S(1)}, bf16[128,3072]{1,0:T(8,128)(2,1)S(1)}, u32[]{:S(2)}, u32[]{:S(2)}) collective-permute-start(bf16[128,3072]{1,0:T(8,128)(2,1)S(1)} %product.2), channel_id=1, source_target_pairs={{0,16},{16,0},{1,17},{17,1},{2,18},{18,2},{3,19},{19,3},{4,20},{20... | collective-permute-start | bytes 2359304 | tf_op jit(solution)/shard_map/ppermute | solution.py:506
  102.8 8.4 %collective-permute-start.15 = (bf16[1,2,128,1152]{3,2,1,0:T(8,128)(2,1)S(1)}, bf16[1,2,128,1152]{3,2,1,0:T(8,128)(2,1)S(1)}, u32[]{:S(2)}, u32[]{:S(2)}) collective-permute-start(bf16[1,2,128,1152]{3,2,1,0:T(8,128)(2,1)S(1)} %bitcast.49), channel_id=1, source_target_pairs={{1,2},{2,1},{5,6},{6,5},{9,10},{10,9},{13,14},{14,13},{17,18},{18,... | collective-permute-start | bytes 1769480 | tf_op jit(solution)/shard_map/ppermute | solution.py:506
  103.7 21.0 %collective-permute-start.13 = (bf16[2,1,2,128,1152]{4,3,2,1,0:T(8,128)(2,1)S(1)}, bf16[2,1,2,128,1152]{4,3,2,1,0:T(8,128)(2,1)S(1)}, u32[]{:S(2)}, u32[]{:S(2)}) collective-permute-start(bf16[2,1,2,128,1152]{4,3,2,1,0:T(8,128)(2,1)S(1)} %pad_maximum_fusion.1.refs_4_.refs_5_), channel_id=1, source_target_pairs={{4,8},{8,4},{5,9},{9,5},{6,10},{10,6},{7,11},{11,7},{20,24},{24,20... | collective-permute-start | bytes 3538952 | tf_op jit(solution)/shard_map/ppermute | solution.py:506
  110.2 16.4 %collective-permute-start.12 = (bf16[2,1,2,128,1152]{4,3,2,1,0:T(8,128)(2,1)S(1)}, bf16[2,1,2,128,1152]{4,3,2,1,0:T(8,128)(2,1)S(1)}, u32[]{:S(2)}, u32[]{:S(2)}) collective-permute-start(bf16[2,1,2,128,1152]{4,3,2,1,0:T(8,128)(2,1)S(1)} %pad_maximum_fusion.1.refs_4_.refs_5_), channel_id=1, source_target_pairs={{0,4},{8,12},{4,0},{12,8},{1,5},{9,13},{5,1},{13,9},{2,6},{10,14},... | collective-permute-start | bytes 3538952 | tf_op jit(solution)/shard_map/ppermute | solution.py:506
  110.3 12.4 %collective-permute-start.20 = (bf16[1,2,128,1152]{3,2,1,0:T(8,128)(2,1)S(1)}, bf16[1,2,128,1152]{3,2,1,0:T(8,128)(2,1)S(1)}, u32[]{:S(2)}, u32[]{:S(2)}) collective-permute-start(bf16[1,2,128,1152]{3,2,1,0:T(8,128)(2,1)S(1)} %bitcast.51), channel_id=1, source_target_pairs={{1,2},{2,1},{5,6},{6,5},{9,10},{10,9},{13,14},{14,13},{17,18},{18,... | collective-permute-start | bytes 1769480 | tf_op jit(solution)/shard_map/ppermute | solution.py:506
  111.1 32.2 %collective-permute-start.18 = (bf16[2,1,2,128,1152]{4,3,2,1,0:T(8,128)(2,1)S(1)}, bf16[2,1,2,128,1152]{4,3,2,1,0:T(8,128)(2,1)S(1)}, u32[]{:S(2)}, u32[]{:S(2)}) collective-permute-start(bf16[2,1,2,128,1152]{4,3,2,1,0:T(8,128)(2,1)S(1)} %pad_maximum_fusion.2.refs_4_.refs_5_), channel_id=1, source_target_pairs={{0,4},{8,12},{4,0},{12,8},{1,5},{9,13},{5,1},{13,9},{2,6},{10,14},... | collective-permute-start | bytes 3538952 | tf_op jit(solution)/shard_map/ppermute | solution.py:506
  119.0 24.3 %collective-permute-start.19 = (bf16[2,1,2,128,1152]{4,3,2,1,0:T(8,128)(2,1)S(1)}, bf16[2,1,2,128,1152]{4,3,2,1,0:T(8,128)(2,1)S(1)}, u32[]{:S(2)}, u32[]{:S(2)}) collective-permute-start(bf16[2,1,2,128,1152]{4,3,2,1,0:T(8,128)(2,1)S(1)} %pad_maximum_fusion.2.refs_4_.refs_5_), channel_id=1, source_target_pairs={{4,8},{8,4},{5,9},{9,5},{6,10},{10,6},{7,11},{11,7},{20,24},{24,20... | collective-permute-start | bytes 3538952 | tf_op jit(solution)/shard_map/ppermute | solution.py:506
  122.7 25.4 %collective-permute-start.23 = (bf16[128,3072]{1,0:T(8,128)(2,1)S(1)}, bf16[128,3072]{1,0:T(8,128)(2,1)S(1)}, u32[]{:S(2)}, u32[]{:S(2)}) collective-permute-start(bf16[128,3072]{1,0:T(8,128)(2,1)S(1)} %product.3), channel_id=1, source_target_pairs={{0,16},{16,0},{1,17},{17,1},{2,18},{18,2},{3,19},{19,3},{4,20},{20... | collective-permute-start | bytes 2359304 | tf_op jit(solution)/shard_map/ppermute | solution.py:506
  124.7 14.6 %collective-permute-start.24 = (bf16[144,1152]{1,0:T(8,128)(2,1)S(1)}, bf16[144,1152]{1,0:T(8,128)(2,1)S(1)}, u32[]{:S(2)}, u32[]{:S(2)}) collective-permute-start(bf16[144,1152]{1,0:T(8,128)(2,1)S(1)} %edge_rows.6), channel_id=1, source_target_pairs={{1,0},{2,3},{5,4},{6,7},{9,8},{10,11},{13,12},{14,15},{17,16},{18,... | collective-permute-start | bytes 995336 | tf_op jit(solution)/shard_map/ppermute | solution.py:506
  126.6 21.4 %collective-permute-start.21 = (bf16[144,1152]{1,0:T(8,128)(2,1)S(1)}, bf16[144,1152]{1,0:T(8,128)(2,1)S(1)}, u32[]{:S(2)}, u32[]{:S(2)}) collective-permute-start(bf16[144,1152]{1,0:T(8,128)(2,1)S(1)} %edge_rows.7), channel_id=1, source_target_pairs={{1,0},{2,3},{5,4},{6,7},{9,8},{10,11},{13,12},{14,15},{17,16},{18,... | collective-permute-start | bytes 995336 | tf_op jit(solution)/shard_map/ppermute | solution.py:506
